TPU v7x, 32 devices: a whole 2x2x4 slice. The times are simulated.
32 devices in a mesh: parts: 2 (over y), rows: 4 (over z), layer: 4 (over x, core).
Axes of the slice: x: 2, y: 2, z: 4, core: 2. Of those that a mesh axis runs over, the one named last changes fastest.
Arguments:
- query_hidden: bfloat16 [4, 384, 6144], P('layer', 'rows'), may hold values from -6 to 6
- query_model: bfloat16 [4, 384, 4096], P('layer', 'rows'), may hold values from -6 to 6
- train_hidden: bfloat16 [4, 320, 6144], P('layer', ('parts', 'rows')), parts along dimension 1, may hold values from -0.009765625 to 0.009765625
- train_model: bfloat16 [4, 320, 4096], P('layer', ('parts', 'rows')), parts along dimension 1, may hold values from -0.01171875 to 0.01171875
- hidden_basis: bfloat16 [4, 6144, 6144], P('layer', 'rows'), may hold values from -0.078125 to 0.078125
- model_basis: bfloat16 [4, 4096, 4096], P('layer', 'rows'), may hold values from -0.09375 to 0.09375
- hidden_eigen: float32 [4, 6144], P('layer', 'rows'), may hold values from 0.05 to 5
- model_eigen: float32 [4, 4096], P('layer', 'rows'), may hold values from 0.05 to 5
Outputs:
- scores: float32 [40, 48], P(('parts', 'rows'), 'layer'), parts along dimension 0
There are 2 independent parts, one for each index of `parts`. A program takes and returns all parts, laid end to end along the dimension named above; an argument that names none is the same for every part. Nothing has to cross between parts.
All inputs are finite; a program needn't handle non-finite values.
Results may differ from a plain program's by a relative error of at most 0.0041.
Values may be sent and summed in bfloat16 or wider, within the bound.
No kernel may reach another device: no remote copies, remote signals or barrier semaphores. Data moves between devices by JAX's collectives and lax.ppermute only.
A program may use at most 128 MiB of HBM per device.

v0:
```python
import jax
import jax.numpy as jnp
from jax import lax
from jax.sharding import PartitionSpec as P

RANK = 8


damping = 0.1


def per_device(
    query_hidden,
    query_model,
    train_hidden,
    train_model,
    hidden_basis,
    model_basis,
    hidden_eigen,
    model_eigen,
):
    rows_count = lax.axis_size("rows")
    hidden_base = hidden_basis[0]
    model_base = model_basis[0]
    hidden_share = hidden_base.shape[0]
    model_share = model_base.shape[0]
    stacked = hidden_share + model_share
    columns = query_hidden.shape[1] * rows_count
    hidden_part = jnp.einsum(
        "eh,qh->eq",
        hidden_base,
        lax.all_gather(query_hidden[0], "rows", axis=0, tiled=True),
        preferred_element_type=jnp.float32,
    )
    model_part = jnp.einsum(
        "eh,qh->eq",
        model_base,
        lax.all_gather(query_model[0], "rows", axis=0, tiled=True),
        preferred_element_type=jnp.float32,
    )
    rotated_block = jnp.concatenate([hidden_part, model_part], axis=0)
    inverse = jnp.concatenate([1.0 / (hidden_eigen[0] + damping), 1.0 / (model_eigen[0] + damping)])
    scaled = (inverse[:, None] * rotated_block).astype(jnp.bfloat16)
    store_hidden = train_hidden[0]
    store_model = train_model[0]
    segment = lax.all_gather(scaled, "rows", axis=0, tiled=True)
    shards = segment.shape[0] // stacked
    blocks = segment.reshape(shards, stacked, segment.shape[1])
    hidden_rows = blocks[:, :hidden_share].reshape(shards * hidden_share, segment.shape[1])
    model_rows = blocks[:, hidden_share:].reshape(shards * model_share, segment.shape[1])
    hidden_gram = jnp.dot(store_hidden, hidden_rows, preferred_element_type=jnp.float32)
    model_gram = jnp.dot(store_model, model_rows, preferred_element_type=jnp.float32)
    train_count = store_hidden.shape[0] // RANK
    query_count = columns // RANK
    partial_value = jnp.einsum(
        "isqr,isqr->iq",
        hidden_gram.reshape(train_count, RANK, query_count, RANK),
        model_gram.reshape(train_count, RANK, query_count, RANK),
    )
    return lax.psum_scatter(partial_value, "layer", scatter_dimension=1, tiled=True)


def solution(mesh):
    placed = (
        P("layer", "rows", None),
        P("layer", "rows", None),
        P("layer", ("parts", "rows"), None),
        P("layer", ("parts", "rows"), None),
        P("layer", "rows", None),
        P("layer", "rows", None),
        P("layer", "rows"),
        P("layer", "rows"),
    )
    return jax.shard_map(
        per_device,
        mesh=mesh,
        in_specs=placed,
        out_specs=P(("parts", "rows"), "layer"),
        check_vma=False,
    )
```

profile of v0, /device:TPU:0, one launch (start us, length us, event | category | flops | bytes accessed | tf_op | source)
XLA Modules:
  0.0 346.1 jit_solution(13637529683287418049)
XLA Ops:
  6.5 0.7 all-gather.10.cloned.1.call-update
  7.3 0.0 all-gather.8.cloned.1.call-start
  7.3 0.7 all-gather.8.cloned.1.call-update
  8.0 0.0 all-gather.6.cloned.1.call-start
  8.1 0.7 divide_reduce_fusion
  8.8 0.7 add_divide_fusion
  9.5 65.7 %all-gather.10.cloned.1.call-done = bf16[1,384,4096]{2,1,0:T(8,128)(2,1)} async-done(((bf16[1,96,4096]{2,1,0:T(8,128)(2,1)}), bf16[1,384,4096]{2,1,0:T(8,128)(2,1)}) %all-gather.10.cloned.1.call-update) | async-done | bytes 3145744 | tf_op jit(solution)/shard_map/all_gather | solution.py:38
  75.2 7.9 %fusion.2 = f32[1024,384]{1,0:T(8,128)S(1)} fusion(bf16[1,1024,4096]{2,1,0:T(8,128)(2,1)} %param.13, bf16[1,384,4096]{2,1,0:T(8,128)(2,1)} %all-gather.10.cloned.1.call-done), kind=kOutput, calls=%fused_computation.2 | convolution fusion | flops 3221225472 | bytes 13107200 | tf_op jit(solution)/shard_map/eh,qh->eq/dot_general | solution.py:35
  83.0 81.8 %all-gather.8.cloned.1.call-done = bf16[1,384,6144]{2,1,0:T(8,128)(2,1)} async-done(((bf16[1,96,6144]{2,1,0:T(8,128)(2,1)}), bf16[1,384,6144]{2,1,0:T(8,128)(2,1)}) %all-gather.8.cloned.1.call-update) | async-done | bytes 4718608 | tf_op jit(solution)/shard_map/all_gather | solution.py:32
  164.8 14.5 %fusion = f32[1536,384]{1,0:T(8,128)S(1)} fusion(bf16[1,1536,6144]{2,1,0:T(8,128)(2,1)} %param.12, bf16[1,384,6144]{2,1,0:T(8,128)(2,1)} %all-gather.8.cloned.1.call-done), kind=kOutput, calls=%fused_computation | convolution fusion | flops 7247757312 | bytes 25952256 | tf_op jit(solution)/shard_map/eh,qh->eq/dot_general | solution.py:29
  179.3 0.0 copy-start.2
  179.3 1.8 fusion.5
  181.1 0.0 all-gather.6.cloned.1.call-update
  181.1 0.6 dynamic-slice
  182.4 138.4 %all-gather.6.cloned.1.call-done = bf16[10240,384]{1,0:T(8,128)(2,1)} async-done(((bf16[2560,384]{1,0:T(8,128)(2,1)}), bf16[10240,384]{1,0:T(8,128)(2,1)}) %all-gather.6.cloned.1.call-update) | async-done | bytes 7864336 | tf_op jit(solution)/shard_map/all_gather | solution.py:46
  320.8 2.8 slice.8
  323.6 4.0 %slice.9 = bf16[4,1024,384]{2,1,0:T(8,128)(2,1)} slice(bf16[4,2560,384]{2,1,0:T(8,128)(2,1)} %bitcast.38), slice={[0:4], [1536:2560], [0:384]} | slice | bytes 6291456 | tf_op jit(solution)/shard_map/slice | solution.py:50
  327.6 0.8 convolution_bitcast_fusion.1
  328.3 0.5 reshape.26
  328.9 2.4 convolution_bitcast_fusion
  331.3 0.5 reshape.28
  331.8 0.2 multiply_reduce_fusion
  332.0 6.8 %all-reduce = f32[5,48]{1,0:T(8,128)S(1)} all-reduce(f32[5,48]{1,0:T(8,128)S(1)} %multiply_reduce_fusion), channel_id=4, replica_groups=mesh['parts'=2,'rows'=4,'layer'=4] {'layer'}, use_global_device_ids=true, to_apply=%region_0.0.clone | all-reduce | flops 240 | bytes 1920
  338.9 0.7 constant_dynamic-slice_fusion
  (7 shorter events, 0.0 us)
Async XLA Ops:
  6.5 321.0 %copy-start = (bf16[1,40,6144]{2,1,0:T(8,128)(2,1)S(1)}, bf16[1,40,6144]{2,1,0:T(8,128)(2,1)}, u32[]{:S(2)}) copy-start(bf16[1,40,6144]{2,1,0:T(8,128)(2,1)} %param.10) | copy-start | bytes 1474564
  6.5 68.6 %all-gather.10.cloned.1.call-start = ((), (), s32[]{:S(2)}) async-start(), calls=%async_computation.2 | async-start | bytes 3932160 | tf_op jit(solution)/shard_map/all_gather | solution.py:38
  7.3 157.6 %all-gather.8.cloned.1.call-start = ((), (), s32[]{:S(2)}) async-start(), calls=%async_computation.1 | async-start | bytes 5898240 | tf_op jit(solution)/shard_map/all_gather | solution.py:32
  8.0 312.8 %all-gather.6.cloned.1.call-start = ((), (), s32[]{:S(2)}) async-start(), calls=%async_computation | async-start | bytes 9830400 | tf_op jit(solution)/shard_map/all_gather | solution.py:46
  179.3 1.8 copy-start.2
  327.5 1.3 copy-start.1
Sparse Core Ops, SparseCore 0:
  8.9 66.1 all-gather.9
  76.7 88.0 all-gather.7
  181.2 139.5 all-gather.5
where the time goes:
time: 346 us
  waiting for transfers between devices  287 us (83%)
  matrix products  25.5 us (7%)
  between operations  13.9 us (4%)
  local copies, waits for them, and re-layouts  9.09 us (3%)
  blocking collectives  6.85 us (2%)
    all_gather x1, waiting for transfers between devices, per_device(): segment = lax.all_gather(scaled, 'rows', axis=0, tiled=True)  138 us
    all_gather x1, waiting for transfers between devices, per_device(): lax.all_gather(query_hidden[0], 'rows', axis=0, tiled=True)  81.8 us
    all_gather x1, waiting for transfers between devices, per_device(): lax.all_gather(query_model[0], 'rows', axis=0, tiled=True)  65.7 us
    dot_general x1, matrix products, per_device(): jnp.einsum('eh,qh->eq', hidden_base, lax.all_gather(query_hidden[0], 'row...  14.5 us
    dot_general x1, matrix products, per_device(): jnp.einsum('eh,qh->eq', model_base, lax.all_gather(query_model[0], 'rows'...  7.88 us
  transfers between devices with their start and end apart: 3, of which 3 were waited for; matrix products, arithmetic and copies ran while one was open for 3% of the time, Pallas kernels for 0%

commit v1 on v0

v1 whole, which is shorter than its diff:
```python
import jax
import jax.numpy as jnp
from jax import lax
from jax.sharding import PartitionSpec as P

RANK = 8


damping = 0.1


def shift(value, axis, by):
    size = lax.axis_size(axis)
    return lax.ppermute(value, axis, [(i, (i + by) % size) for i in range(size)])


def per_device(
    query_hidden,
    query_model,
    train_hidden,
    train_model,
    hidden_basis,
    model_basis,
    hidden_eigen,
    model_eigen,
):
    rows = lax.axis_size("rows")
    parts = lax.axis_size("parts")
    layers = lax.axis_size("layer")
    row = lax.axis_index("rows")
    part = lax.axis_index("parts")
    hidden_share = hidden_basis.shape[1]
    model_share = model_basis.shape[1]
    held = train_hidden.shape[1]
    columns = query_hidden.shape[1] // parts
    queries = query_hidden.shape[1] * rows // RANK

    own_model = lax.dynamic_slice_in_dim(query_model[0], part * columns, columns, 0)
    own_hidden = lax.dynamic_slice_in_dim(query_hidden[0], part * columns, columns, 0)

    def directions_of(owner):
        return jnp.concatenate(
            [
                lax.dynamic_slice_in_dim(train_hidden[0], owner * hidden_share, hidden_share, 1),
                lax.dynamic_slice_in_dim(train_model[0], owner * model_share, model_share, 1),
            ],
            axis=1,
        )

    blocks = [directions_of(row)]
    for k in range(1, rows):
        blocks.append(shift(directions_of((row + k) % rows), "rows", k))
    store = jnp.concatenate(blocks, axis=0)
    stores = jnp.concatenate([store] + [shift(store, "parts", j) for j in range(1, parts)], axis=0)

    all_model = lax.all_gather(own_model, "rows", axis=0, tiled=True)
    all_hidden = lax.all_gather(own_hidden, "rows", axis=0, tiled=True)

    def gram(basis, eigen, gathered, train):
        rotated = jnp.einsum("eh,qh->eq", basis, gathered, preferred_element_type=jnp.float32)
        scaled = (rotated * (1.0 / (eigen + damping))[:, None]).astype(jnp.bfloat16)
        return jnp.dot(train, scaled, preferred_element_type=jnp.float32)

    model_gram = gram(model_basis[0], model_eigen[0], all_model, stores[:, hidden_share:])
    hidden_gram = gram(hidden_basis[0], hidden_eigen[0], all_hidden, stores[:, :hidden_share])

    def summed(partial):
        partial = partial.reshape(parts, rows, held, columns * rows)
        total = partial[:, 0]
        for k in range(1, rows):
            total = total + shift(partial[:, k].astype(jnp.bfloat16), "rows", -k).astype(jnp.float32)
        return total

    product = summed(model_gram) * summed(hidden_gram)
    examples = held // RANK
    by_column = product.reshape(parts, examples, RANK, rows * columns).sum(axis=2)
    if columns % RANK == 0:
        by_query = by_column.reshape(parts, examples, rows, 1, columns // RANK, RANK).sum(axis=-1)
        mine = lax.broadcasted_iota(jnp.int32, (1, 1, 1, parts, 1), 3) == part
        partial_value = jnp.where(mine, by_query, 0.0).reshape(parts, examples, queries)
    else:
        place = jnp.arange(rows * columns)
        place = (place // columns) * (columns * parts) + part * columns + place % columns
        pick = (place[:, None] // RANK == jnp.arange(queries)[None, :]).astype(jnp.float32)
        partial_value = jnp.einsum("pic,cq->piq", by_column, pick, precision=lax.Precision.HIGHEST)
    partial_value = jnp.stack(
        [lax.dynamic_index_in_dim(partial_value, (part - j) % parts, 0, False) for j in range(parts)]
    )
    whole = lax.psum(partial_value, ("parts", "layer"))
    here = lax.dynamic_index_in_dim(whole, part, 0, False)
    width = queries // layers
    return lax.dynamic_slice_in_dim(here, lax.axis_index("layer") * width, width, 1)


def solution(mesh):
    placed = (
        P("layer", "rows", None),
        P("layer", "rows", None),
        P("layer", ("parts", "rows"), None),
        P("layer", ("parts", "rows"), None),
        P("layer", "rows", None),
        P("layer", "rows", None),
        P("layer", "rows"),
        P("layer", "rows"),
    )
    return jax.shard_map(
        per_device,
        mesh=mesh,
        in_specs=placed,
        out_specs=P(("parts", "rows"), "layer"),
        check_vma=False,
    )
```

time: 346 us -> 153 us (0.44)
  waiting for transfers between devices: 287 us -> 71.2 us
  starting transfers between devices: 0.08 us -> 27.4 us
  matrix products: 25.5 us -> 19 us
  blocking collectives: 6.85 us -> 12.6 us
    all_gather x3 -> x2, waiting for transfers between devices: 286 us -> 31.7 us  [the longest x1 31.6 us: per_device(): all_hidden = lax.all_gather(own_hidden, 'rows', axis=0, tiled=True)]
    ppermute x0 -> x10, waiting for transfers between devices: none -> 39.5 us  [shift(): lax.ppermute(value, axis, [(i, (i + by) % size) for i in range(size)])]
    ppermute x0 -> x10, starting transfers between devices: none -> 27.3 us  [shift(): lax.ppermute(value, axis, [(i, (i + by) % size) for i in range(size)])]
    psum x0 -> x1, blocking collectives: none -> 12.6 us  [per_device(): whole = lax.psum(partial_value, ('parts', 'layer'))]
    unnamed x1 -> x0, blocking collectives: 6.85 us -> none
    slice x2 -> x0, local copies, waits for them, and re-layouts: 6.76 us -> none  [the longest x1 3.95 us: per_device(): blocks[:, hidden_share:].reshape(shards * model_share, segment.shape[1])]
    dot_general x4 -> x2, matrix products: 25.5 us -> 19 us  [gram(): return jnp.dot(train, scaled, preferred_element_type=jnp.float32)]
    dynamic_slice x0 -> x6, local copies, waits for them, and re-layouts: none -> 3.92 us  [the longest x1 1.88 us: per_device(): lax.dynamic_slice_in_dim(query_model[0], part * columns, columns, 0)]
  transfers between devices with their start and end apart: 3 -> 12, of which waited for: 3 -> 7; matrix products, arithmetic and copies ran while one was open for 3% -> 16% of each run, Pallas kernels for 0% -> 0%
where the time goes in v1:
time: 153 us
  waiting for transfers between devices  71.2 us (47%)
  starting transfers between devices  27.4 us (18%)
  matrix products  19 us (12%)
  between operations  13.7 us (9%)
  blocking collectives  12.6 us (8%)
  local copies, waits for them, and re-layouts  8.04 us (5%)
    ppermute x10, waiting for transfers between devices, shift(): lax.ppermute(value, axis, [(i, (i + by) % size) for i in range(size)])  39.5 us
    all_gather x1, waiting for transfers between devices, per_device(): all_hidden = lax.all_gather(own_hidden, 'rows', axis=0, tiled=True)  31.6 us
    ppermute x10, starting transfers between devices, shift(): lax.ppermute(value, axis, [(i, (i + by) % size) for i in range(size)])  27.3 us
    dot_general x2, matrix products, gram(): return jnp.dot(train, scaled, preferred_element_type=jnp.float32)  19 us
    psum x1, blocking collectives, per_device(): whole = lax.psum(partial_value, ('parts', 'layer'))  12.6 us
  transfers between devices with their start and end apart: 12, of which 7 were waited for; matrix products, arithmetic and copies ran while one was open for 16% of the time, Pallas kernels for 0%

profile of v1, /device:TPU:0, one launch (start us, length us, event | category | flops | bytes accessed | tf_op | source)
XLA Modules:
  0.0 152.9 jit_solution(9440619426883737905)
XLA Ops:
  6.5 1.9 %constant_dynamic-slice_fusion.4 = bf16[1,48,4096]{2,1,0:T(8,128)(2,1)} fusion(bf16[1,96,4096]{2,1,0:T(8,128)(2,1)} %param.9, s32[]{:T(128)S(6)} %select_n.84), kind=kLoop, calls=%fused_computation.59 | loop fusion | bytes 786436 | tf_op jit(solution)/shard_map/dynamic_slice | solution.py:38
  8.6 1.0 dynamic-slice_bitcast_fusion.4
  9.7 3.1 %collective-permute-start = (bf16[40,2560]{1,0:T(8,128)(2,1)S(1)}, bf16[40,2560]{1,0:T(8,128)(2,1)S(1)}, u32[]{:S(2)}, u32[]{:S(2)}) collective-permute-start(bf16[40,2560]{1,0:T(8,128)(2,1)S(1)} %pad_maximum_fusion.1), channel_id=1, source_target_pairs={{0,4},{4,8},{8,12},{12,0},{1,5},{5,9},{9,13},{13,1},{2,6},{6,10},{... | collective-permute-start | bytes 614408 | tf_op jit(solution)/shard_map/ppermute | solution.py:14
  12.8 2.7 %collective-permute-start.1 = (bf16[40,2560]{1,0:T(8,128)(2,1)S(1)}, bf16[40,2560]{1,0:T(8,128)(2,1)S(1)}, u32[]{:S(2)}, u32[]{:S(2)}) collective-permute-start(bf16[40,2560]{1,0:T(8,128)(2,1)S(1)} %pad_maximum_fusion.2), channel_id=1, source_target_pairs={{0,8},{4,12},{8,0},{12,4},{1,9},{5,13},{9,1},{13,5},{2,10},{6,14},... | collective-permute-start | bytes 614408 | tf_op jit(solution)/shard_map/ppermute | solution.py:14
  15.5 0.9 constant_dynamic-slice_fusion.3
  16.4 1.4 collective-permute-start.2
  18.5 2.3 %collective-permute-done = bf16[40,2560]{1,0:T(8,128)(2,1)S(1)} collective-permute-done((bf16[40,2560]{1,0:T(8,128)(2,1)S(1)}, bf16[40,2560]{1,0:T(8,128)(2,1)S(1)}, u32[]{:S(2)}, u32[]{:S(2)}) %collective-permute-start) | collective-permute-done | bytes 204832 | tf_op jit(solution)/shard_map/ppermute | solution.py:14
  20.8 17.7 %collective-permute-done.1 = bf16[40,2560]{1,0:T(8,128)(2,1)S(1)} collective-permute-done((bf16[40,2560]{1,0:T(8,128)(2,1)S(1)}, bf16[40,2560]{1,0:T(8,128)(2,1)S(1)}, u32[]{:S(2)}, u32[]{:S(2)}) %collective-permute-start.1) | collective-permute-done | bytes 204832 | tf_op jit(solution)/shard_map/ppermute | solution.py:14
  38.6 1.6 %collective-permute-start.3 = (bf16[160,2560]{1,0:T(8,128)(2,1)S(1)}, bf16[160,2560]{1,0:T(8,128)(2,1)S(1)}, u32[]{:S(2)}, u32[]{:S(2)}) collective-permute-start(bf16[160,2560]{1,0:T(8,128)(2,1)S(1)} %pad_maximum_fusion), channel_id=1, source_target_pairs={{0,16},{16,0},{1,17},{17,1},{2,18},{18,2},{3,19},{19,3},{4,20},{20... | collective-permute-start | bytes 2457608 | tf_op jit(solution)/shard_map/ppermute | solution.py:14
  40.8 0.7 constant_dynamic-update-slice_fusion.2
  41.6 0.7 constant_dynamic-update-slice_fusion.1
  42.2 15.2 %collective-permute-done.3 = bf16[160,2560]{1,0:T(8,128)(2,1)S(1)} collective-permute-done((bf16[160,2560]{1,0:T(8,128)(2,1)S(1)}, bf16[160,2560]{1,0:T(8,128)(2,1)S(1)}, u32[]{:S(2)}, u32[]{:S(2)}) %collective-permute-start.3) | collective-permute-done | bytes 819232 | tf_op jit(solution)/shard_map/ppermute | solution.py:14
  57.5 1.0 constant_dynamic-update-slice_fusion
  58.5 7.3 %fusion.24 = f32[320,192]{1,0:T(8,128)S(1)} fusion(bf16[1,1024,4096]{2,1,0:T(8,128)(2,1)} %param.13, bf16[1,192,4096]{2,1,0:T(8,128)(2,1)} %all-gather.5.cloned.1.call-done, bf16[320,2560]{1,0:T(8,128)(2,1)} %constant_dynamic-update-slice_fusion, f32[1024]{0:T(1024)S(1)} %bitcast.106), kind=kOutput, calls=%fused_computation.10 | convolution fusion | flops 1736835072 | bytes 10866688 | tf_op jit(solution)/shard_map/dot_general | solution.py:62
  65.8 6.1 %collective-permute-start.4 = (bf16[2,40,192]{2,1,0:T(8,128)(2,1)S(1)}, bf16[2,40,192]{2,1,0:T(8,128)(2,1)S(1)}, u32[]{:S(2)}, u32[]{:S(2)}) collective-permute-start(bf16[2,40,192]{2,1,0:T(8,128)(2,1)S(1)} %get-tuple-element.13), channel_id=1, source_target_pairs={{0,12},{4,0},{8,4},{12,8},{1,13},{5,1},{9,5},{13,9},{2,14},{6,2},{... | collective-permute-start | bytes 92168 | tf_op jit(solution)/shard_map/ppermute | solution.py:14
  71.9 10.0 %collective-permute-start.5 = (bf16[2,40,192]{2,1,0:T(8,128)(2,1)S(1)}, bf16[2,40,192]{2,1,0:T(8,128)(2,1)S(1)}, u32[]{:S(2)}, u32[]{:S(2)}) collective-permute-start(bf16[2,40,192]{2,1,0:T(8,128)(2,1)S(1)} %get-tuple-element.15), channel_id=1, source_target_pairs={{0,8},{4,12},{8,0},{12,4},{1,9},{5,13},{9,1},{13,5},{2,10},{6,14},... | collective-permute-start | bytes 92168 | tf_op jit(solution)/shard_map/ppermute | solution.py:14
  81.9 31.6 %all-gather.7.cloned.1.call-done = bf16[1,192,6144]{2,1,0:T(8,128)(2,1)} async-done(((bf16[1,48,6144]{2,1,0:T(8,128)(2,1)}), bf16[1,192,6144]{2,1,0:T(8,128)(2,1)}) %all-gather.7.cloned.1.call-update) | async-done | bytes 2359312 | tf_op jit(solution)/shard_map/all_gather | solution.py:57
  113.6 11.7 %fusion.29 = f32[320,192]{1,0:T(8,128)S(1)} fusion(bf16[1,1536,6144]{2,1,0:T(8,128)(2,1)} %param.12, bf16[1,192,6144]{2,1,0:T(8,128)(2,1)} %all-gather.7.cloned.1.call-done, bf16[320,2560]{1,0:T(8,128)(2,1)} %constant_dynamic-update-slice_fusion, f32[1536]{0:T(1024)S(1)} %divide_reduce_fusion), kind=kOutput, calls=%fused_computation.11 | convolution fusion | flops 3813212160 | bytes 22468608 | tf_op jit(solution)/shard_map/dot_general | solution.py:62
  125.4 0.9 collective-permute-start.7
  126.3 1.5 collective-permute-start.9
  128.0 1.4 collective-permute-done.7
  129.4 1.9 %collective-permute-done.8 = bf16[2,40,192]{2,1,0:T(8,128)(2,1)S(1)} collective-permute-done((bf16[2,40,192]{2,1,0:T(8,128)(2,1)S(1)}, bf16[2,40,192]{2,1,0:T(8,128)(2,1)S(1)}, u32[]{:S(2)}, u32[]{:S(2)}) %collective-permute-start.8) | collective-permute-done | bytes 30752 | tf_op jit(solution)/shard_map/ppermute | solution.py:14
  131.3 0.9 collective-permute-done.9
  132.8 12.6 %psum.7 = f32[2,5,48]{2,0,1:T(2,128)S(1)} all-reduce(f32[2,5,48]{2,0,1:T(2,128)S(1)} %pad_maximum_fusion.4), channel_id=1, replica_groups=mesh['parts'=2,'rows'=4,'layer'=4] {'parts','layer'}, use_global_device_ids=true, to_apply=%region_2.3 | all-reduce | flops 480 | bytes 3840 | tf_op jit(solution)/shard_map/psum | solution.py:89
  (45 shorter events, 3.1 us)
Async XLA Ops:
  6.5 8.9 %copy-start = (bf16[1,96,6144]{2,1,0:T(8,128)(2,1)S(1)}, bf16[1,96,6144]{2,1,0:T(8,128)(2,1)}, u32[]{:S(2)}) copy-start(bf16[1,96,6144]{2,1,0:T(8,128)(2,1)} %param.8) | copy-start | bytes 3538948
  6.5 3.1 %copy-start.1 = (bf16[1,40,6144]{2,1,0:T(8,128)(2,1)S(1)}, bf16[1,40,6144]{2,1,0:T(8,128)(2,1)}, u32[]{:S(2)}) copy-start(bf16[1,40,6144]{2,1,0:T(8,128)(2,1)} %param.10) | copy-start | bytes 1474564
  6.5 51.9 %all-gather.5.cloned.1.call-start = ((), (), s32[]{:S(2)}) async-start(), calls=%async_computation | async-start | bytes 1966080 | tf_op jit(solution)/shard_map/all_gather | solution.py:56
  8.5 105.1 %all-gather.7.cloned.1.call-start = ((), (), s32[]{:S(2)}) async-start(), calls=%async_computation.1 | async-start | bytes 2949120 | tf_op jit(solution)/shard_map/all_gather | solution.py:57
  9.7 8.1 %copy-start.2 = (f32[1,1536]{1,0:T(1,128)S(1)}, f32[1,1536]{1,0:T(1,128)}, u32[]{:S(2)}) copy-start(f32[1,1536]{1,0:T(1,128)} %param.14) | copy-start | bytes 18436
  9.7 8.8 %copy-start.3 = (f32[1,1024]{1,0:T(1,128)S(1)}, f32[1,1024]{1,0:T(1,128)}, u32[]{:S(2)}) copy-start(f32[1,1024]{1,0:T(1,128)} %param.15) | copy-start | bytes 12292
  9.7 11.1 %collective-permute-start = (bf16[40,2560]{1,0:T(8,128)(2,1)S(1)}, bf16[40,2560]{1,0:T(8,128)(2,1)S(1)}, u32[]{:S(2)}, u32[]{:S(2)}) collective-permute-start(bf16[40,2560]{1,0:T(8,128)(2,1)S(1)} %pad_maximum_fusion.1), channel_id=1, source_target_pairs={{0,4},{4,8},{8,12},{12,0},{1,5},{5,9},{9,13},{13,1},{2,6},{6,10},{... | collective-permute-start | bytes 614408 | tf_op jit(solution)/shard_map/ppermute | solution.py:14
  12.8 25.7 %collective-permute-start.1 = (bf16[40,2560]{1,0:T(8,128)(2,1)S(1)}, bf16[40,2560]{1,0:T(8,128)(2,1)S(1)}, u32[]{:S(2)}, u32[]{:S(2)}) collective-permute-start(bf16[40,2560]{1,0:T(8,128)(2,1)S(1)} %pad_maximum_fusion.2), channel_id=1, source_target_pairs={{0,8},{4,12},{8,0},{12,4},{1,9},{5,13},{9,1},{13,5},{2,10},{6,14},... | collective-permute-start | bytes 614408 | tf_op jit(solution)/shard_map/ppermute | solution.py:14
  16.4 22.1 %collective-permute-start.2 = (bf16[40,2560]{1,0:T(8,128)(2,1)S(1)}, bf16[40,2560]{1,0:T(8,128)(2,1)S(1)}, u32[]{:S(2)}, u32[]{:S(2)}) collective-permute-start(bf16[40,2560]{1,0:T(8,128)(2,1)S(1)} %pad_maximum_fusion.3), channel_id=1, source_target_pairs={{0,12},{4,0},{8,4},{12,8},{1,13},{5,1},{9,5},{13,9},{2,14},{6,2},{... | collective-permute-start | bytes 614408 | tf_op jit(solution)/shard_map/ppermute | solution.py:14
  38.6 18.9 %collective-permute-start.3 = (bf16[160,2560]{1,0:T(8,128)(2,1)S(1)}, bf16[160,2560]{1,0:T(8,128)(2,1)S(1)}, u32[]{:S(2)}, u32[]{:S(2)}) collective-permute-start(bf16[160,2560]{1,0:T(8,128)(2,1)S(1)} %pad_maximum_fusion), channel_id=1, source_target_pairs={{0,16},{16,0},{1,17},{17,1},{2,18},{18,2},{3,19},{19,3},{4,20},{20... | collective-permute-start | bytes 2457608 | tf_op jit(solution)/shard_map/ppermute | solution.py:14
  65.8 60.5 %collective-permute-start.4 = (bf16[2,40,192]{2,1,0:T(8,128)(2,1)S(1)}, bf16[2,40,192]{2,1,0:T(8,128)(2,1)S(1)}, u32[]{:S(2)}, u32[]{:S(2)}) collective-permute-start(bf16[2,40,192]{2,1,0:T(8,128)(2,1)S(1)} %get-tuple-element.13), channel_id=1, source_target_pairs={{0,12},{4,0},{8,4},{12,8},{1,13},{5,1},{9,5},{13,9},{2,14},{6,2},{... | collective-permute-start | bytes 92168 | tf_op jit(solution)/shard_map/ppermute | solution.py:14
  71.9 56.1 %collective-permute-start.5 = (bf16[2,40,192]{2,1,0:T(8,128)(2,1)S(1)}, bf16[2,40,192]{2,1,0:T(8,128)(2,1)S(1)}, u32[]{:S(2)}, u32[]{:S(2)}) collective-permute-start(bf16[2,40,192]{2,1,0:T(8,128)(2,1)S(1)} %get-tuple-element.15), channel_id=1, source_target_pairs={{0,8},{4,12},{8,0},{12,4},{1,9},{5,13},{9,1},{13,5},{2,10},{6,14},... | collective-permute-start | bytes 92168 | tf_op jit(solution)/shard_map/ppermute | solution.py:14
  81.9 46.0 %collective-permute-start.6 = (bf16[2,40,192]{2,1,0:T(8,128)(2,1)S(1)}, bf16[2,40,192]{2,1,0:T(8,128)(2,1)S(1)}, u32[]{:S(2)}, u32[]{:S(2)}) collective-permute-start(bf16[2,40,192]{2,1,0:T(8,128)(2,1)S(1)} %get-tuple-element.14), channel_id=1, source_target_pairs={{0,4},{4,8},{8,12},{12,0},{1,5},{5,9},{9,13},{13,1},{2,6},{6,10},{... | collective-permute-start | bytes 92168 | tf_op jit(solution)/shard_map/ppermute | solution.py:14
  125.4 4.1 %collective-permute-start.7 = (bf16[2,40,192]{2,1,0:T(8,128)(2,1)S(1)}, bf16[2,40,192]{2,1,0:T(8,128)(2,1)S(1)}, u32[]{:S(2)}, u32[]{:S(2)}) collective-permute-start(bf16[2,40,192]{2,1,0:T(8,128)(2,1)S(1)} %get-tuple-element.16), channel_id=1, source_target_pairs={{0,12},{4,0},{8,4},{12,8},{1,13},{5,1},{9,5},{13,9},{2,14},{6,2},{... | collective-permute-start | bytes 92168 | tf_op jit(solution)/shard_map/ppermute | solution.py:14
  126.3 5.1 %collective-permute-start.8 = (bf16[2,40,192]{2,1,0:T(8,128)(2,1)S(1)}, bf16[2,40,192]{2,1,0:T(8,128)(2,1)S(1)}, u32[]{:S(2)}, u32[]{:S(2)}) collective-permute-start(bf16[2,40,192]{2,1,0:T(8,128)(2,1)S(1)} %get-tuple-element.18), channel_id=1, source_target_pairs={{0,8},{4,12},{8,0},{12,4},{1,9},{5,13},{9,1},{13,5},{2,10},{6,14},... | collective-permute-start | bytes 92168 | tf_op jit(solution)/shard_map/ppermute | solution.py:14
  126.3 5.9 %collective-permute-start.9 = (bf16[2,40,192]{2,1,0:T(8,128)(2,1)S(1)}, bf16[2,40,192]{2,1,0:T(8,128)(2,1)S(1)}, u32[]{:S(2)}, u32[]{:S(2)}) collective-permute-start(bf16[2,40,192]{2,1,0:T(8,128)(2,1)S(1)} %get-tuple-element.17), channel_id=1, source_target_pairs={{0,4},{4,8},{8,12},{12,0},{1,5},{5,9},{9,13},{13,1},{2,6},{6,10},{... | collective-permute-start | bytes 92168 | tf_op jit(solution)/shard_map/ppermute | solution.py:14
Sparse Core Ops, SparseCore 0:
  8.9 49.4 all-gather.4
  60.0 53.5 all-gather.6

commit v2 on v1

v2 whole, which is shorter than its diff:
```python
import jax
import jax.numpy as jnp
from jax import lax
from jax.experimental import pallas as pl
from jax.experimental.pallas import tpu as pltpu
from jax.sharding import PartitionSpec as P

RANK = 8


damping = 0.1

VMEM_LIMIT = 56 * 1024 * 1024


def shift(value, axis, by):
    size = lax.axis_size(axis)
    return lax.ppermute(value, axis, [(i, (i + by) % size) for i in range(size)])


def along(value, by):
    size = lax.axis_size("rows")
    return lax.ppermute(value, "rows", [(i, i + by) for i in range(size) if 0 <= i + by < size])


def high_low(value):
    high = value.astype(jnp.bfloat16)
    low = (value - high.astype(jnp.float32)).astype(jnp.bfloat16)
    return high, low


def project_kernel(
    split, train_ref, basis_hidden_ref, basis_model_ref, eigen_hidden_ref, eigen_model_ref, out_ref, scaled_hidden, scaled_model
):
    step = pl.program_id(0)
    count = train_ref.shape[0]
    share = basis_hidden_ref.shape[0]

    @pl.when(step == 0)
    def _():
        for train, eigen, scaled in (
            (train_ref[:, :share], eigen_hidden_ref, scaled_hidden),
            (train_ref[:, share:], eigen_model_ref, scaled_model),
        ):
            inverse = 1.0 / (eigen[...] + damping)
            high, low = high_low(train.astype(jnp.float32) * inverse)
            scaled[:count, :] = high
            scaled[count:, :] = low

    def project(scaled, basis):
        both = jnp.dot(scaled[...], basis[...], preferred_element_type=jnp.float32)
        high, low = high_low(both[:count] + both[count:])
        out_ref[:count, :] = high
        out_ref[count:, :] = low

    @pl.when(step < split)
    def _():
        project(scaled_hidden, basis_hidden_ref)

    @pl.when(step >= split)
    def _():
        project(scaled_model, basis_model_ref)


def project(train, hidden_basis, model_basis, hidden_eigen, model_eigen):
    count = train.shape[0]
    hidden_share, hidden_width = hidden_basis.shape
    model_share, model_width = model_basis.shape
    tile = 512
    split = hidden_width // tile

    def whole(shape):
        return pl.BlockSpec(shape, lambda i: (0, 0))

    return pl.pallas_call(
        lambda *refs: project_kernel(split, *refs),
        grid=(split + model_width // tile,),
        in_specs=[
            whole(train.shape),
            pl.BlockSpec((hidden_share, tile), lambda i: (0, jnp.minimum(i, split - 1))),
            pl.BlockSpec((model_share, tile), lambda i: (0, jnp.maximum(i - split, 0))),
            whole(hidden_eigen.shape),
            whole(model_eigen.shape),
        ],
        out_specs=pl.BlockSpec((2 * count, tile), lambda i: (0, i)),
        out_shape=jax.ShapeDtypeStruct((2 * count, hidden_width + model_width), jnp.bfloat16),
        scratch_shapes=[
            pltpu.VMEM((2 * count, hidden_share), jnp.bfloat16),
            pltpu.VMEM((2 * count, model_share), jnp.bfloat16),
        ],
        compiler_params=pltpu.CompilerParams(vmem_limit_bytes=VMEM_LIMIT),
        cost_estimate=pl.CostEstimate(
            flops=4 * count * (hidden_share * hidden_width + model_share * model_width),
            bytes_accessed=2 * (hidden_share * hidden_width + model_share * model_width),
            transcendentals=0,
        ),
    )(train, hidden_basis, model_basis, hidden_eigen, model_eigen)


def gram_kernel(split, places, projected_ref, *refs):
    query_refs, gram_ref, query = refs[:-2], refs[-2], refs[-1]
    step = pl.program_id(0)
    count = gram_ref.shape[1]
    columns = query_refs[0].shape[0]
    for place, group in enumerate(places):
        rows = query_refs[group[0]][...]
        for other in group[1:]:
            rows = rows + query_refs[other][...]
        if len(places) > 1:
            place = lax.rem(lax.axis_index("rows") + place, len(places))
        query[pl.ds(pl.multiple_of(place * columns, columns), columns), :] = rows
    both = lax.dot_general(
        projected_ref[...], query[...], (((1,), (1,)), ((), ())), preferred_element_type=jnp.float32
    )
    term = both[:count] + both[count:]
    first = jnp.logical_or(step == 0, step == split)

    @pl.when(first)
    def _():
        gram_ref[0] = term

    @pl.when(jnp.logical_not(first))
    def _():
        gram_ref[0] += term


def grams(projected, queries, places, hidden_width):
    count, width = projected.shape[0] // 2, projected.shape[1]
    columns = queries[0].shape[0]
    held = len(places) * columns
    tile = 1024
    split = hidden_width // tile
    return pl.pallas_call(
        lambda *refs: gram_kernel(split, places, *refs),
        grid=(width // tile,),
        in_specs=[pl.BlockSpec((2 * count, tile), lambda i: (0, i))]
        + [pl.BlockSpec((columns, tile), lambda i: (0, i)) for _ in queries],
        out_specs=pl.BlockSpec((1, count, held), lambda i: (jnp.where(i < split, 0, 1), 0, 0)),
        out_shape=jax.ShapeDtypeStruct((2, count, held), jnp.float32),
        scratch_shapes=[pltpu.VMEM((held, tile), jnp.bfloat16)],
        compiler_params=pltpu.CompilerParams(vmem_limit_bytes=VMEM_LIMIT),
        cost_estimate=pl.CostEstimate(flops=1, bytes_accessed=4 * count * width, transcendentals=0),
    )(projected, *queries)


def exchange(partial):
    total = partial[:, :, 0]
    for k in range(1, lax.axis_size("rows")):
        total = total + shift(partial[:, :, k].astype(jnp.bfloat16), "rows", -k).astype(jnp.float32)
    return total


def along_four(query, projected, hidden_width, blocked):
    row = lax.axis_index("rows")
    columns = query.shape[0]
    after, before = [query], [query]
    for step in range(3):
        if step == 2:
            projected, after[2], before[2] = lax.optimization_barrier((projected, after[2], before[2]))
        after.append(along(after[-1], -1))
        before.append(along(before[-1], 1))
    most = grams(projected, [query, after[1], after[2], before[2], before[1]], ((0,), (1,), (2, 3), (4,)), hidden_width)
    total = exchange(blocked(most))

    total, last_after, last_before = lax.optimization_barrier((total, after[3], before[3]))
    partial = blocked(grams(projected, [last_after, last_before], ((0, 1),), hidden_width))
    first = jnp.where(row == 3, partial[:, :, 0], 0.0)
    final = jnp.where(row == 0, partial[:, :, 0], 0.0)
    for k in range(1, 4):
        ends = [(0, (0 - k) % 4), (3, (3 - k) % 4)]
        part = lax.ppermute(partial[:, :, k].astype(jnp.bfloat16), "rows", ends).astype(jnp.float32)
        source = (row + k) % 4
        first = first + jnp.where(source == 3, part, 0.0)
        final = final + jnp.where(source == 0, part, 0.0)
    between = jnp.zeros(first.shape[:-1] + (2 * columns,), jnp.float32)
    return total + jnp.concatenate([first, between, final], axis=-1)


def per_device(
    query_hidden,
    query_model,
    train_hidden,
    train_model,
    hidden_basis,
    model_basis,
    hidden_eigen,
    model_eigen,
):
    rows = lax.axis_size("rows")
    parts = lax.axis_size("parts")
    layers = lax.axis_size("layer")
    row = lax.axis_index("rows")
    part = lax.axis_index("parts")
    hidden_share, hidden_width = hidden_basis.shape[1:]
    model_share = model_basis.shape[1]
    held = train_hidden.shape[1]
    columns = query_hidden.shape[1] // parts
    queries = query_hidden.shape[1] * rows // RANK

    def directions_of(owner):
        return jnp.concatenate(
            [
                lax.dynamic_slice_in_dim(train_hidden[0], owner * hidden_share, hidden_share, 1),
                lax.dynamic_slice_in_dim(train_model[0], owner * model_share, model_share, 1),
            ],
            axis=1,
        )

    blocks = [directions_of(row)]
    for k in range(1, rows):
        blocks.append(shift(directions_of((row + k) % rows), "rows", k))
    store = jnp.concatenate(blocks, axis=0)
    stores = jnp.concatenate([store] + [shift(store, "parts", j) for j in range(1, parts)], axis=0)

    query = jnp.concatenate(
        [
            lax.dynamic_slice_in_dim(query_hidden[0], part * columns, columns, 0),
            lax.dynamic_slice_in_dim(query_model[0], part * columns, columns, 0),
        ],
        axis=1,
    )

    def blocked(partial):
        return partial.reshape(2, parts, rows, held, partial.shape[-1])

    if rows == 4:
        projected = project(stores, hidden_basis[0], model_basis[0], hidden_eigen, model_eigen)
        total = along_four(query, projected, hidden_width, blocked)
    else:
        every = lax.all_gather(query, "rows", axis=0, tiled=True)

        def gram(basis, eigen, gathered, train):
            rotated = jnp.einsum("eh,qh->eq", basis, gathered, preferred_element_type=jnp.float32)
            scaled = (rotated * (1.0 / (eigen + damping))[:, None]).astype(jnp.bfloat16)
            return jnp.dot(train, scaled, preferred_element_type=jnp.float32)

        hidden_gram = gram(hidden_basis[0], hidden_eigen[0], every[:, :hidden_width], stores[:, :hidden_share])
        model_gram = gram(model_basis[0], model_eigen[0], every[:, hidden_width:], stores[:, hidden_share:])
        total = exchange(blocked(jnp.stack([hidden_gram, model_gram])))

    product = total[0] * total[1]
    examples = held // RANK
    by_column = product.reshape(parts, examples, RANK, rows * columns).sum(axis=2)
    if columns % RANK == 0:
        by_query = by_column.reshape(parts, examples, rows, 1, columns // RANK, RANK).sum(axis=-1)
        mine = lax.broadcasted_iota(jnp.int32, (1, 1, 1, parts, 1), 3) == part
        scores = jnp.where(mine, by_query, 0.0).reshape(parts, examples, queries)
    else:
        place = jnp.arange(rows * columns)
        place = (place // columns) * (columns * parts) + part * columns + place % columns
        pick = (place[:, None] // RANK == jnp.arange(queries)[None, :]).astype(jnp.float32)
        scores = jnp.einsum("pic,cq->piq", by_column, pick, precision=lax.Precision.HIGHEST)

    kept = scores[0]
    for j in range(1, parts):
        kept = kept + shift(scores[j], "parts", -j)
    layer = lax.axis_index("layer")
    width = queries // layers

    def queries_of(owner):
        return lax.dynamic_slice_in_dim(kept, owner * width, width, 1)

    result = queries_of(layer)
    for k in range(1, layers):
        result = result + shift(queries_of((layer + k) % layers), "layer", k)
    return result


def solution(mesh):
    placed = (
        P("layer", "rows", None),
        P("layer", "rows", None),
        P("layer", ("parts", "rows"), None),
        P("layer", ("parts", "rows"), None),
        P("layer", "rows", None),
        P("layer", "rows", None),
        P("layer", "rows"),
        P("layer", "rows"),
    )
    return jax.shard_map(
        per_device,
        mesh=mesh,
        in_specs=placed,
        out_specs=P(("parts", "rows"), "layer"),
        check_vma=False,
    )
```

time: 153 us -> 172 us (1.12)
  Pallas kernels: 0 us -> 53.5 us
  starting transfers between devices: 27.4 us -> 52.2 us
  waiting for transfers between devices: 71.2 us -> 51.9 us
  matrix products: 19 us -> 0 us
  between operations: 13.7 us -> 0.43 us
  blocking collectives: 12.6 us -> 0 us
  other arithmetic: 1.08 us -> 5.22 us
    pallas_call x0 -> x3, Pallas kernels: none -> 53.5 us  [the longest x1 30.3 us: project(): pl.pallas_call(lambda *refs: project_kernel(split, *refs), grid=(split +...]
    ppermute x0 -> x9, starting transfers between devices: none -> 36 us  [the longest x6 26.4 us: along(): lax.ppermute(value, 'rows', [(i, i + by) for i in range(size) if 0 <= i +...]
    all_gather x2 -> x0, waiting for transfers between devices: 31.7 us -> none  [the longest x1 31.6 us: per_device(): all_hidden = lax.all_gather(own_hidden, 'rows', axis=0, tiled=True)]
    dot_general x2 -> x0, matrix products: 19 us -> none  [gram(): return jnp.dot(train, scaled, preferred_element_type=jnp.float32)]
    psum x1 -> x0, blocking collectives: 12.6 us -> none  [per_device(): whole = lax.psum(partial_value, ('parts', 'layer'))]
    ppermute x10 -> x11, starting transfers between devices: 27.3 us -> 16.2 us  [shift(): lax.ppermute(value, axis, [(i, (i + by) % size) for i in range(size)])]
    ppermute x10 -> x11, waiting for transfers between devices: 39.5 us -> 46.3 us  [shift(): lax.ppermute(value, axis, [(i, (i + by) % size) for i in range(size)])]
    ppermute x0 -> x9, waiting for transfers between devices: none -> 5.62 us  [the longest x3 5.61 us: along_four(): lax.ppermute(partial[:, :, k].astype(jnp.bfloat16), 'rows', ends)]
  transfers between devices with their start and end apart: 12 -> 20, of which waited for: 7 -> 10; matrix products, arithmetic and copies ran while one was open for 16% -> 2% of each run, Pallas kernels for 0% -> 25%
where the time goes in v2:
time: 172 us; the launch traced here: 170 us
  Pallas kernels  53.5 us (31%)
  starting transfers between devices  52.2 us (30%)
  waiting for transfers between devices  51.9 us (30%)
  local copies, waits for them, and re-layouts  7.15 us (4%)
  other arithmetic  5.22 us (3%)
    ppermute x11, waiting for transfers between devices, shift(): lax.ppermute(value, axis, [(i, (i + by) % size) for i in range(size)])  46.3 us
    pallas_call x1, Pallas kernels, project(): pl.pallas_call(lambda *refs: project_kernel(split, *refs), grid=(split +...  30.3 us
    ppermute x6, starting transfers between devices, along(): lax.ppermute(value, 'rows', [(i, i + by) for i in range(size) if 0 <= i +...  26.4 us
    pallas_call x2, Pallas kernels, grams(): pl.pallas_call(lambda *refs: gram_kernel(split, places, *refs), grid=(wid...  23.2 us
    ppermute x11, starting transfers between devices, shift(): lax.ppermute(value, axis, [(i, (i + by) % size) for i in range(size)])  16.2 us
    ppermute x3, starting transfers between devices, along_four(): lax.ppermute(partial[:, :, k].astype(jnp.bfloat16), 'rows', ends)  9.69 us
    ppermute x3, waiting for transfers between devices, along_four(): lax.ppermute(partial[:, :, k].astype(jnp.bfloat16), 'rows', ends)  5.61 us
    unnamed x21, local copies, waits for them, and re-layouts  4.38 us
  transfers between devices with their start and end apart: 20, of which 10 were waited for; matrix products, arithmetic and copies ran while one was open for 2% of the time, Pallas kernels for 25%

profile of v2, /device:TPU:0, one launch (start us, length us, event | category | flops | bytes accessed | tf_op | source)
XLA Modules:
  0.0 170.4 jit_solution(11544772913978483585)
XLA Ops:
  2.4 1.3 collective-permute-start.4
  3.7 6.5 %collective-permute-start.6 = (bf16[48,10240]{1,0:T(8,128)(2,1)S(1)}, bf16[48,10240]{1,0:T(8,128)(2,1)}, u32[]{:S(2)}, u32[]{:S(2)}) collective-permute-start(bf16[48,10240]{1,0:T(8,128)(2,1)S(1)} %pad_maximum_fusion.refs_1_), channel_id=1, source_target_pairs={{0,4},{4,8},{8,12},{1,5},{5,9},{9,13},{2,6},{6,10},{10,14},{3,7},{... | collective-permute-start | bytes 2949128 | tf_op jit(solution)/shard_map/ppermute | solution.py:23
  13.8 3.0 %collective-permute-start.2 = (bf16[40,2560]{1,0:T(8,128)(2,1)S(1)}, bf16[40,2560]{1,0:T(8,128)(2,1)S(1)}, u32[]{:S(2)}, u32[]{:S(2)}) collective-permute-start(bf16[40,2560]{1,0:T(8,128)(2,1)S(1)} %pad_maximum_fusion.4), channel_id=1, source_target_pairs={{0,12},{4,0},{8,4},{12,8},{1,13},{5,1},{9,5},{13,9},{2,14},{6,2},{... | collective-permute-start | bytes 614408 | tf_op jit(solution)/shard_map/ppermute | solution.py:18
  16.8 20.1 %collective-permute-done = bf16[40,2560]{1,0:T(8,128)(2,1)S(1)} collective-permute-done((bf16[40,2560]{1,0:T(8,128)(2,1)S(1)}, bf16[40,2560]{1,0:T(8,128)(2,1)S(1)}, u32[]{:S(2)}, u32[]{:S(2)}) %collective-permute-start) | collective-permute-done | bytes 204832 | tf_op jit(solution)/shard_map/ppermute | solution.py:18
  36.9 7.7 %collective-permute-done.1 = bf16[40,2560]{1,0:T(8,128)(2,1)S(1)} collective-permute-done((bf16[40,2560]{1,0:T(8,128)(2,1)S(1)}, bf16[40,2560]{1,0:T(8,128)(2,1)S(1)}, u32[]{:S(2)}, u32[]{:S(2)}) %collective-permute-start.1) | collective-permute-done | bytes 204832 | tf_op jit(solution)/shard_map/ppermute | solution.py:18
  44.7 1.6 collective-permute-start.3
  46.4 1.3 collective-permute-start.5
  47.7 7.6 %collective-permute-start.7 = (bf16[48,10240]{1,0:T(8,128)(2,1)}, bf16[48,10240]{1,0:T(8,128)(2,1)S(1)}, u32[]{:S(2)}, u32[]{:S(2)}) collective-permute-start(bf16[48,10240]{1,0:T(8,128)(2,1)} %collective-permute-done.6.refs_5_), channel_id=1, source_target_pairs={{0,4},{4,8},{8,12},{1,5},{5,9},{9,13},{2,6},{6,10},{10,14},{3,7},{... | collective-permute-start | bytes 2949128 | tf_op jit(solution)/shard_map/ppermute | solution.py:23
  55.3 7.5 %collective-permute-done.3 = bf16[160,2560]{1,0:T(8,128)(2,1)S(1)} collective-permute-done((bf16[160,2560]{1,0:T(8,128)(2,1)S(1)}, bf16[160,2560]{1,0:T(8,128)(2,1)S(1)}, u32[]{:S(2)}, u32[]{:S(2)}) %collective-permute-start.3) | collective-permute-done | bytes 819232 | tf_op jit(solution)/shard_map/ppermute | solution.py:18
  64.0 30.3 %shard_map.82.refs_0_ = bf16[640,10240]{1,0:T(8,128)(2,1)} custom-call(bf16[320,2560]{1,0:T(8,128)(2,1)} %copy-done.8, bf16[1536,6144]{1,0:T(8,128)(2,1)} %bitcast.74, bf16[1024,4096]{1,0:T(8,128)(2,1)} %bitcast.75, f32[1,1536]{1,0:T(1,128)} %refs_3_.1, f32[1,1024]{1,0:T(1,128)} %refs_4_.1), custom_call_target="tpu_custom_call" | custom-call | flops 17448304640 | bytes 27262976 | tf_op jit(solution)/shard_map/pallas_call | solution.py:75
  95.6 8.4 %collective-permute-start.12 = (bf16[48,10240]{1,0:T(8,128)(2,1)S(1)}, bf16[48,10240]{1,0:T(8,128)(2,1)S(1)}, u32[]{:S(2)}, u32[]{:S(2)}) collective-permute-start(bf16[48,10240]{1,0:T(8,128)(2,1)S(1)} %collective-permute-done.7.refs_4_), channel_id=1, source_target_pairs={{0,4},{4,8},{8,12},{1,5},{5,9},{9,13},{2,6},{6,10},{10,14},{3,7},{... | collective-permute-start | bytes 2949128 | tf_op jit(solution)/shard_map/ppermute | solution.py:23
  104.0 12.2 %shard_map.83 = f32[2,320,192]{2,1,0:T(8,128)} custom-call(bf16[640,10240]{1,0:T(8,128)(2,1)} %shard_map.82.refs_0_, bf16[48,10240]{1,0:T(8,128)(2,1)} %copy-done.1, bf16[48,10240]{1,0:T(8,128)(2,1)} %copy-done.2, bf16[48,10240]{1,0:T(8,128)(2,1)} %copy-done.3, bf16[48,10240]{1,0:T(8,128)(2,1)} %copy-done.4, bf16[48,10240]{1,0:T(8,128)(2,1)} %collective-permute-done.6.refs_5_), custom_call_target="tpu_custom_call" | custom-call | flops 1 | bytes 13107200 | tf_op jit(solution)/shard_map/pallas_call | solution.py:133
  117.3 2.0 %collective-permute-start.10 = (bf16[2,2,40,192]{3,2,1,0:T(8,128)(2,1)S(1)}, bf16[2,2,40,192]{3,2,1,0:T(8,128)(2,1)S(1)}, u32[]{:S(2)}, u32[]{:S(2)}) collective-permute-start(bf16[2,2,40,192]{3,2,1,0:T(8,128)(2,1)S(1)} %get-tuple-element.24), channel_id=1, source_target_pairs={{0,4},{4,8},{8,12},{12,0},{1,5},{5,9},{9,13},{13,1},{2,6},{6,10},{... | collective-permute-start | bytes 184328 | tf_op jit(solution)/shard_map/ppermute | solution.py:18
  119.3 1.9 %collective-permute-start.8 = (bf16[2,2,40,192]{3,2,1,0:T(8,128)(2,1)S(1)}, bf16[2,2,40,192]{3,2,1,0:T(8,128)(2,1)S(1)}, u32[]{:S(2)}, u32[]{:S(2)}) collective-permute-start(bf16[2,2,40,192]{3,2,1,0:T(8,128)(2,1)S(1)} %get-tuple-element.23), channel_id=1, source_target_pairs={{0,12},{4,0},{8,4},{12,8},{1,13},{5,1},{9,5},{13,9},{2,14},{6,2},{... | collective-permute-start | bytes 184328 | tf_op jit(solution)/shard_map/ppermute | solution.py:18
  122.1 5.3 %collective-permute-done.10 = bf16[2,2,40,192]{3,2,1,0:T(8,128)(2,1)S(1)} collective-permute-done((bf16[2,2,40,192]{3,2,1,0:T(8,128)(2,1)S(1)}, bf16[2,2,40,192]{3,2,1,0:T(8,128)(2,1)S(1)}, u32[]{:S(2)}, u32[]{:S(2)}) %collective-permute-start.10) | collective-permute-done | bytes 61472 | tf_op jit(solution)/shard_map/ppermute | solution.py:18
  127.4 2.4 %collective-permute-done.9 = bf16[2,2,40,192]{3,2,1,0:T(8,128)(2,1)S(1)} collective-permute-done((bf16[2,2,40,192]{3,2,1,0:T(8,128)(2,1)S(1)}, bf16[2,2,40,192]{3,2,1,0:T(8,128)(2,1)S(1)}, u32[]{:S(2)}, u32[]{:S(2)}) %collective-permute-start.9) | collective-permute-done | bytes 61472 | tf_op jit(solution)/shard_map/ppermute | solution.py:18
  132.7 11.0 %shard_map.84 = f32[2,320,48]{2,1,0:T(8,128)} custom-call(bf16[640,10240]{1,0:T(8,128)(2,1)} %shard_map.82.refs_0_, bf16[48,10240]{1,0:T(8,128)(2,1)} %copy-done.5, bf16[48,10240]{1,0:T(8,128)(2,1)} %copy-done.6), custom_call_target="tpu_custom_call" | custom-call | flops 1 | bytes 13107200 | tf_op jit(solution)/shard_map/pallas_call | solution.py:133
  144.7 6.5 %collective-permute-start.13 = (bf16[2,2,40,48]{3,2,1,0:T(8,128)(2,1)S(1)}, bf16[2,2,40,48]{3,2,1,0:T(8,128)(2,1)S(1)}, u32[]{:S(2)}, u32[]{:S(2)}) collective-permute-start(bf16[2,2,40,48]{3,2,1,0:T(8,128)(2,1)S(1)} %get-tuple-element.31), channel_id=1, source_target_pairs={{0,12},{12,8},{1,13},{13,9},{2,14},{14,10},{3,15},{15,11},{16,28},... | collective-permute-start | bytes 46088 | tf_op jit(solution)/shard_map/ppermute | solution.py:171
  152.5 1.9 %collective-permute-start.15 = (bf16[2,2,40,48]{3,2,1,0:T(8,128)(2,1)S(1)}, bf16[2,2,40,48]{3,2,1,0:T(8,128)(2,1)S(1)}, u32[]{:S(2)}, u32[]{:S(2)}) collective-permute-start(bf16[2,2,40,48]{3,2,1,0:T(8,128)(2,1)S(1)} %get-tuple-element.30), channel_id=1, source_target_pairs={{0,4},{12,0},{1,5},{13,1},{2,6},{14,2},{3,7},{15,3},{16,20},{28,16... | collective-permute-start | bytes 46088 | tf_op jit(solution)/shard_map/ppermute | solution.py:171
  154.6 5.6 %collective-permute-done.15 = bf16[2,2,40,48]{3,2,1,0:T(8,128)(2,1)S(1)} collective-permute-done((bf16[2,2,40,48]{3,2,1,0:T(8,128)(2,1)S(1)}, bf16[2,2,40,48]{3,2,1,0:T(8,128)(2,1)S(1)}, u32[]{:S(2)}, u32[]{:S(2)}) %collective-permute-start.15) | collective-permute-done | bytes 15392 | tf_op jit(solution)/shard_map/ppermute | solution.py:171
  161.8 1.5 collective-permute-start.16
  163.4 2.0 %collective-permute-done.16 = f32[5,48]{1,0:T(8,128)S(1)} collective-permute-done((f32[5,48]{1,0:T(8,128)S(1)}, f32[5,48]{1,0:T(8,128)S(1)}, u32[]{:S(2)}, u32[]{:S(2)}) %collective-permute-start.16) | collective-permute-done | bytes 992 | tf_op jit(solution)/shard_map/ppermute | solution.py:18
  165.5 1.5 collective-permute-start.18
  167.0 1.4 collective-permute-start.19
  (72 shorter events, 19.6 us)
Async XLA Ops:
  2.4 14.4 %copy-start.1 = (bf16[48,10240]{1,0:T(8,128)(2,1)}, bf16[48,10240]{1,0:T(8,128)(2,1)S(1)}, u32[]{:S(2)}) copy-start(bf16[48,10240]{1,0:T(8,128)(2,1)S(1)} %pad_maximum_fusion.refs_1_) | copy-start | bytes 2949124
  2.4 43.9 %collective-permute-start.4 = (bf16[48,10240]{1,0:T(8,128)(2,1)S(1)}, bf16[48,10240]{1,0:T(8,128)(2,1)S(1)}, u32[]{:S(2)}, u32[]{:S(2)}) collective-permute-start(bf16[48,10240]{1,0:T(8,128)(2,1)S(1)} %pad_maximum_fusion.refs_1_), channel_id=1, source_target_pairs={{4,0},{8,4},{12,8},{5,1},{9,5},{13,9},{6,2},{10,6},{14,10},{7,3},{... | collective-permute-start | bytes 2949128 | tf_op jit(solution)/shard_map/ppermute | solution.py:23
  3.7 43.9 %collective-permute-start.6 = (bf16[48,10240]{1,0:T(8,128)(2,1)S(1)}, bf16[48,10240]{1,0:T(8,128)(2,1)}, u32[]{:S(2)}, u32[]{:S(2)}) collective-permute-start(bf16[48,10240]{1,0:T(8,128)(2,1)S(1)} %pad_maximum_fusion.refs_1_), channel_id=1, source_target_pairs={{0,4},{4,8},{8,12},{1,5},{5,9},{9,13},{2,6},{6,10},{10,14},{3,7},{... | collective-permute-start | bytes 2949128 | tf_op jit(solution)/shard_map/ppermute | solution.py:23
  11.5 25.5 %collective-permute-start = (bf16[40,2560]{1,0:T(8,128)(2,1)S(1)}, bf16[40,2560]{1,0:T(8,128)(2,1)S(1)}, u32[]{:S(2)}, u32[]{:S(2)}) collective-permute-start(bf16[40,2560]{1,0:T(8,128)(2,1)S(1)} %pad_maximum_fusion.2), channel_id=1, source_target_pairs={{0,4},{4,8},{8,12},{12,0},{1,5},{5,9},{9,13},{13,1},{2,6},{6,10},{... | collective-permute-start | bytes 614408 | tf_op jit(solution)/shard_map/ppermute | solution.py:18
  12.7 31.9 %collective-permute-start.1 = (bf16[40,2560]{1,0:T(8,128)(2,1)S(1)}, bf16[40,2560]{1,0:T(8,128)(2,1)S(1)}, u32[]{:S(2)}, u32[]{:S(2)}) collective-permute-start(bf16[40,2560]{1,0:T(8,128)(2,1)S(1)} %pad_maximum_fusion.3), channel_id=1, source_target_pairs={{0,8},{4,12},{8,0},{12,4},{1,9},{5,13},{9,1},{13,5},{2,10},{6,14},... | collective-permute-start | bytes 614408 | tf_op jit(solution)/shard_map/ppermute | solution.py:18
  13.8 30.8 %collective-permute-start.2 = (bf16[40,2560]{1,0:T(8,128)(2,1)S(1)}, bf16[40,2560]{1,0:T(8,128)(2,1)S(1)}, u32[]{:S(2)}, u32[]{:S(2)}) collective-permute-start(bf16[40,2560]{1,0:T(8,128)(2,1)S(1)} %pad_maximum_fusion.4), channel_id=1, source_target_pairs={{0,12},{4,0},{8,4},{12,8},{1,13},{5,1},{9,5},{13,9},{2,14},{6,2},{... | collective-permute-start | bytes 614408 | tf_op jit(solution)/shard_map/ppermute | solution.py:18
  44.7 18.1 %collective-permute-start.3 = (bf16[160,2560]{1,0:T(8,128)(2,1)S(1)}, bf16[160,2560]{1,0:T(8,128)(2,1)S(1)}, u32[]{:S(2)}, u32[]{:S(2)}) collective-permute-start(bf16[160,2560]{1,0:T(8,128)(2,1)S(1)} %pad_maximum_fusion.1), channel_id=1, source_target_pairs={{0,16},{16,0},{1,17},{17,1},{2,18},{18,2},{3,19},{19,3},{4,20},{20... | collective-permute-start | bytes 2457608 | tf_op jit(solution)/shard_map/ppermute | solution.py:18
  46.3 47.9 %copy-start.2 = (bf16[48,10240]{1,0:T(8,128)(2,1)}, bf16[48,10240]{1,0:T(8,128)(2,1)S(1)}, u32[]{:S(2)}) copy-start(bf16[48,10240]{1,0:T(8,128)(2,1)S(1)} %collective-permute-done.4.refs_2_) | copy-start | bytes 2949124
  46.4 47.9 %collective-permute-start.5 = (bf16[48,10240]{1,0:T(8,128)(2,1)S(1)}, bf16[48,10240]{1,0:T(8,128)(2,1)S(1)}, u32[]{:S(2)}, u32[]{:S(2)}) collective-permute-start(bf16[48,10240]{1,0:T(8,128)(2,1)S(1)} %collective-permute-done.4.refs_2_), channel_id=1, source_target_pairs={{4,0},{8,4},{12,8},{5,1},{9,5},{13,9},{6,2},{10,6},{14,10},{7,3},{... | collective-permute-start | bytes 2949128 | tf_op jit(solution)/shard_map/ppermute | solution.py:23
  47.7 46.6 %collective-permute-start.7 = (bf16[48,10240]{1,0:T(8,128)(2,1)}, bf16[48,10240]{1,0:T(8,128)(2,1)S(1)}, u32[]{:S(2)}, u32[]{:S(2)}) collective-permute-start(bf16[48,10240]{1,0:T(8,128)(2,1)} %collective-permute-done.6.refs_5_), channel_id=1, source_target_pairs={{0,4},{4,8},{8,12},{1,5},{5,9},{9,13},{2,6},{6,10},{10,14},{3,7},{... | collective-permute-start | bytes 2949128 | tf_op jit(solution)/shard_map/ppermute | solution.py:23
  94.3 9.7 %copy-start.3 = (bf16[48,10240]{1,0:T(8,128)(2,1)}, bf16[48,10240]{1,0:T(8,128)(2,1)S(1)}, u32[]{:S(2)}) copy-start(bf16[48,10240]{1,0:T(8,128)(2,1)S(1)} %collective-permute-done.5.refs_3_) | copy-start | bytes 2949124
  94.3 9.7 %copy-start.4 = (bf16[48,10240]{1,0:T(8,128)(2,1)}, bf16[48,10240]{1,0:T(8,128)(2,1)S(1)}, u32[]{:S(2)}) copy-start(bf16[48,10240]{1,0:T(8,128)(2,1)S(1)} %collective-permute-done.7.refs_4_) | copy-start | bytes 2949124
  94.3 36.5 %collective-permute-start.11 = (bf16[48,10240]{1,0:T(8,128)(2,1)S(1)}, bf16[48,10240]{1,0:T(8,128)(2,1)S(1)}, u32[]{:S(2)}, u32[]{:S(2)}) collective-permute-start(bf16[48,10240]{1,0:T(8,128)(2,1)S(1)} %collective-permute-done.5.refs_3_), channel_id=1, source_target_pairs={{4,0},{8,4},{12,8},{5,1},{9,5},{13,9},{6,2},{10,6},{14,10},{7,3},{... | collective-permute-start | bytes 2949128 | tf_op jit(solution)/shard_map/ppermute | solution.py:23
  95.6 35.2 %collective-permute-start.12 = (bf16[48,10240]{1,0:T(8,128)(2,1)S(1)}, bf16[48,10240]{1,0:T(8,128)(2,1)S(1)}, u32[]{:S(2)}, u32[]{:S(2)}) collective-permute-start(bf16[48,10240]{1,0:T(8,128)(2,1)S(1)} %collective-permute-done.7.refs_4_), channel_id=1, source_target_pairs={{0,4},{4,8},{8,12},{1,5},{5,9},{9,13},{2,6},{6,10},{10,14},{3,7},{... | collective-permute-start | bytes 2949128 | tf_op jit(solution)/shard_map/ppermute | solution.py:23
  117.3 10.1 %collective-permute-start.10 = (bf16[2,2,40,192]{3,2,1,0:T(8,128)(2,1)S(1)}, bf16[2,2,40,192]{3,2,1,0:T(8,128)(2,1)S(1)}, u32[]{:S(2)}, u32[]{:S(2)}) collective-permute-start(bf16[2,2,40,192]{3,2,1,0:T(8,128)(2,1)S(1)} %get-tuple-element.24), channel_id=1, source_target_pairs={{0,4},{4,8},{8,12},{12,0},{1,5},{5,9},{9,13},{13,1},{2,6},{6,10},{... | collective-permute-start | bytes 184328 | tf_op jit(solution)/shard_map/ppermute | solution.py:18
  119.3 8.1 %collective-permute-start.8 = (bf16[2,2,40,192]{3,2,1,0:T(8,128)(2,1)S(1)}, bf16[2,2,40,192]{3,2,1,0:T(8,128)(2,1)S(1)}, u32[]{:S(2)}, u32[]{:S(2)}) collective-permute-start(bf16[2,2,40,192]{3,2,1,0:T(8,128)(2,1)S(1)} %get-tuple-element.23), channel_id=1, source_target_pairs={{0,12},{4,0},{8,4},{12,8},{1,13},{5,1},{9,5},{13,9},{2,14},{6,2},{... | collective-permute-start | bytes 184328 | tf_op jit(solution)/shard_map/ppermute | solution.py:18
  121.2 8.6 %collective-permute-start.9 = (bf16[2,2,40,192]{3,2,1,0:T(8,128)(2,1)S(1)}, bf16[2,2,40,192]{3,2,1,0:T(8,128)(2,1)S(1)}, u32[]{:S(2)}, u32[]{:S(2)}) collective-permute-start(bf16[2,2,40,192]{3,2,1,0:T(8,128)(2,1)S(1)} %get-tuple-element.25), channel_id=1, source_target_pairs={{0,8},{4,12},{8,0},{12,4},{1,9},{5,13},{9,1},{13,5},{2,10},{6,14},... | collective-permute-start | bytes 184328 | tf_op jit(solution)/shard_map/ppermute | solution.py:18
  144.7 9.9 %collective-permute-start.13 = (bf16[2,2,40,48]{3,2,1,0:T(8,128)(2,1)S(1)}, bf16[2,2,40,48]{3,2,1,0:T(8,128)(2,1)S(1)}, u32[]{:S(2)}, u32[]{:S(2)}) collective-permute-start(bf16[2,2,40,48]{3,2,1,0:T(8,128)(2,1)S(1)} %get-tuple-element.31), channel_id=1, source_target_pairs={{0,12},{12,8},{1,13},{13,9},{2,14},{14,10},{3,15},{15,11},{16,28},... | collective-permute-start | bytes 46088 | tf_op jit(solution)/shard_map/ppermute | solution.py:171
  151.2 3.4 %collective-permute-start.14 = (bf16[2,2,40,48]{3,2,1,0:T(8,128)(2,1)S(1)}, bf16[2,2,40,48]{3,2,1,0:T(8,128)(2,1)S(1)}, u32[]{:S(2)}, u32[]{:S(2)}) collective-permute-start(bf16[2,2,40,48]{3,2,1,0:T(8,128)(2,1)S(1)} %get-tuple-element.32), channel_id=1, source_target_pairs={{0,8},{12,4},{1,9},{13,5},{2,10},{14,6},{3,11},{15,7},{16,24},{28,... | collective-permute-start | bytes 46088 | tf_op jit(solution)/shard_map/ppermute | solution.py:171
  152.5 7.7 %collective-permute-start.15 = (bf16[2,2,40,48]{3,2,1,0:T(8,128)(2,1)S(1)}, bf16[2,2,40,48]{3,2,1,0:T(8,128)(2,1)S(1)}, u32[]{:S(2)}, u32[]{:S(2)}) collective-permute-start(bf16[2,2,40,48]{3,2,1,0:T(8,128)(2,1)S(1)} %get-tuple-element.30), channel_id=1, source_target_pairs={{0,4},{12,0},{1,5},{13,1},{2,6},{14,2},{3,7},{15,3},{16,20},{28,16... | collective-permute-start | bytes 46088 | tf_op jit(solution)/shard_map/ppermute | solution.py:171
  161.8 3.6 %collective-permute-start.16 = (f32[5,48]{1,0:T(8,128)S(1)}, f32[5,48]{1,0:T(8,128)S(1)}, u32[]{:S(2)}, u32[]{:S(2)}) collective-permute-start(f32[5,48]{1,0:T(8,128)S(1)} %squeeze.14), channel_id=1, source_target_pairs={{0,16},{16,0},{1,17},{17,1},{2,18},{18,2},{3,19},{19,3},{4,20},{20... | collective-permute-start | bytes 2888 | tf_op jit(solution)/shard_map/ppermute | solution.py:18
  165.5 3.0 %collective-permute-start.17 = (f32[5,12]{1,0:T(8,128)S(1)}, f32[5,12]{1,0:T(8,128)S(1)}, u32[]{:S(2)}, u32[]{:S(2)}) collective-permute-start(f32[5,12]{1,0:T(8,128)S(1)} %get-tuple-element.35), channel_id=1, source_target_pairs={{0,1},{1,2},{2,3},{3,0},{4,5},{5,6},{6,7},{7,4},{8,9},{9,10},{10,1... | collective-permute-start | bytes 728 | tf_op jit(solution)/shard_map/ppermute | solution.py:18
  165.5 3.7 %collective-permute-start.18 = (f32[5,12]{1,0:T(8,128)S(1)}, f32[5,12]{1,0:T(8,128)S(1)}, u32[]{:S(2)}, u32[]{:S(2)}) collective-permute-start(f32[5,12]{1,0:T(8,128)S(1)} %get-tuple-element.37), channel_id=1, source_target_pairs={{0,2},{1,3},{2,0},{3,1},{4,6},{5,7},{6,4},{7,5},{8,10},{9,11},{10,... | collective-permute-start | bytes 728 | tf_op jit(solution)/shard_map/ppermute | solution.py:18
  167.0 2.7 %collective-permute-start.19 = (f32[5,12]{1,0:T(8,128)S(1)}, f32[5,12]{1,0:T(8,128)S(1)}, u32[]{:S(2)}, u32[]{:S(2)}) collective-permute-start(f32[5,12]{1,0:T(8,128)S(1)} %get-tuple-element.36), channel_id=1, source_target_pairs={{0,3},{1,0},{2,1},{3,2},{4,7},{5,4},{6,5},{7,6},{8,11},{9,8},{10,9... | collective-permute-start | bytes 728 | tf_op jit(solution)/shard_map/ppermute | solution.py:18
  (5 other events, 13.4 us)

commit v3 on v1

v3 whole, which is shorter than its diff:
```python
import jax
import jax.numpy as jnp
from jax import lax
from jax.experimental import pallas as pl
from jax.experimental.pallas import tpu as pltpu
from jax.sharding import PartitionSpec as P

RANK = 8


damping = 0.1

VMEM_LIMIT = 24 * 1024 * 1024


def shift(value, axis, by):
    size = lax.axis_size(axis)
    return lax.ppermute(value, axis, [(i, (i + by) % size) for i in range(size)])


def along(value, by):
    size = lax.axis_size("rows")
    return lax.ppermute(value, "rows", [(i, i + by) for i in range(size) if 0 <= i + by < size])


def rotate_kernel(basis_ref, eigen_ref, *refs):
    query_refs, out_ref, total = refs[:-2], refs[-2], refs[-1]
    step = pl.program_id(1)
    blocks = [ref[...] for ref in query_refs]
    query = blocks[0] if len(blocks) == 1 else jnp.concatenate(blocks, axis=0)
    term = lax.dot_general(
        query, basis_ref[...], (((1,), (1,)), ((), ())), preferred_element_type=jnp.float32
    )

    @pl.when(step == 0)
    def _():
        total[...] = term

    @pl.when(step != 0)
    def _():
        total[...] += term

    @pl.when(step == pl.num_programs(1) - 1)
    def _():
        out_ref[...] = (total[...] * (1.0 / (eigen_ref[...] + damping))).astype(jnp.bfloat16)


def rotate(basis, eigen, queries, start):
    share, width = basis.shape
    columns = queries[0].shape[0]
    held = columns * len(queries)
    tile, depth = 512, 2048
    first = start // depth
    return pl.pallas_call(
        rotate_kernel,
        grid=(share // tile, width // depth),
        in_specs=[
            pl.BlockSpec((tile, depth), lambda e, k: (e, k)),
            pl.BlockSpec((1, tile), lambda e, k: (0, e)),
        ]
        + [pl.BlockSpec((columns, depth), lambda e, k: (0, first + k)) for _ in queries],
        out_specs=pl.BlockSpec((held, tile), lambda e, k: (0, e)),
        out_shape=jax.ShapeDtypeStruct((held, share), jnp.bfloat16),
        scratch_shapes=[pltpu.VMEM((held, tile), jnp.float32)],
        compiler_params=pltpu.CompilerParams(vmem_limit_bytes=VMEM_LIMIT),
        cost_estimate=pl.CostEstimate(flops=1, bytes_accessed=1, transcendentals=0),
    )(
        pltpu.with_memory_space_constraint(basis, pltpu.HBM),
        eigen,
        *[pltpu.with_memory_space_constraint(query, pltpu.VMEM) for query in queries],
    )


def grams(stores, rotated, places):
    columns = rotated[0][0].shape[0]
    share = rotated[0][0].shape[1]
    count = stores.shape[0]
    held = columns * places

    def kernel(stores_ref, *refs):
        hidden_refs, model_refs = refs[:places], refs[places : 2 * places]
        gram_ref, sent_ref, hidden, model = refs[2 * places :]
        for place in range(places):
            where = place if places == 1 else lax.rem(lax.axis_index("rows") + place, places)
            rows = pl.ds(pl.multiple_of(where * columns, columns), columns)
            hidden[rows, :] = hidden_refs[place][...]
            model[rows, :] = model_refs[place][...]
        for side, (store, query) in enumerate(((stores_ref[:, :share], hidden), (stores_ref[:, share:], model))):
            gram = lax.dot_general(
                store, query[...], (((1,), (1,)), ((), ())), preferred_element_type=jnp.float32
            )
            gram_ref[side] = gram
            sent_ref[side] = gram.astype(jnp.bfloat16)

    return pl.pallas_call(
        kernel,
        out_shape=[
            jax.ShapeDtypeStruct((2, count, held), jnp.float32),
            jax.ShapeDtypeStruct((2, count, held), jnp.bfloat16),
        ],
        scratch_shapes=[pltpu.VMEM((held, side.shape[1]), jnp.bfloat16) for side in (rotated[0][0], rotated[1][0])],
        compiler_params=pltpu.CompilerParams(vmem_limit_bytes=VMEM_LIMIT),
        cost_estimate=pl.CostEstimate(
            flops=2 * count * held * stores.shape[1], bytes_accessed=2 * stores.size, transcendentals=0
        ),
    )(stores, *rotated[0], *rotated[1])


def exchange(partial, sent):
    total = partial[:, :, 0]
    for k in range(1, lax.axis_size("rows")):
        total = total + shift(sent[:, :, k], "rows", -k).astype(jnp.float32)
    return total


def along_four(query, bases, eigens, stores, blocked):
    row = lax.axis_index("rows")
    columns = query.shape[0]
    width = bases[0].shape[1]

    def rotated(*queries):
        return [rotate(bases[side], eigens[side], queries, start) for side, start in enumerate((0, width))]

    after, before = along(query, -1), along(query, 1)
    own = rotated(query)
    own, after, before = lax.optimization_barrier((own, after, before))
    after_two, before_two = along(after, -1), along(before, 1)
    near = rotated(after, before)
    near, after_two, before_two = lax.optimization_barrier((near, after_two, before_two))
    two = [jnp.where(row < 2, after_two[:, s], before_two[:, s]) for s in (slice(0, width), slice(width, None))]
    three = [lax.ppermute(side, "rows", [(1, 0), (2, 3)]) for side in two]
    far = [rotate(bases[side], eigens[side], [two[side]], 0) for side in range(2)]
    most = [[own[s], near[s][:columns], far[s], near[s][columns:]] for s in range(2)]
    partial, sent = grams(stores, most, 4)
    total = exchange(blocked(partial), blocked(sent))

    total, three = lax.optimization_barrier((total, three))
    last = [rotate(bases[side], eigens[side], [three[side]], 0) for side in range(2)]
    partial, sent = grams(stores, [[side] for side in last], 1)
    partial, sent = blocked(partial), blocked(sent)
    first = jnp.where(row == 3, partial[:, :, 0], 0.0)
    final = jnp.where(row == 0, partial[:, :, 0], 0.0)
    for k in range(1, 4):
        ends = [(0, (0 - k) % 4), (3, (3 - k) % 4)]
        part = lax.ppermute(sent[:, :, k], "rows", ends).astype(jnp.float32)
        source = (row + k) % 4
        first = first + jnp.where(source == 3, part, 0.0)
        final = final + jnp.where(source == 0, part, 0.0)
    between = jnp.zeros(first.shape[:-1] + (2 * columns,), jnp.float32)
    return total + jnp.concatenate([first, between, final], axis=-1)


def per_device(
    query_hidden,
    query_model,
    train_hidden,
    train_model,
    hidden_basis,
    model_basis,
    hidden_eigen,
    model_eigen,
):
    rows = lax.axis_size("rows")
    parts = lax.axis_size("parts")
    layers = lax.axis_size("layer")
    row = lax.axis_index("rows")
    part = lax.axis_index("parts")
    hidden_share = hidden_basis.shape[1]
    model_share = model_basis.shape[1]
    held = train_hidden.shape[1]
    columns = query_hidden.shape[1] // parts
    queries = query_hidden.shape[1] * rows // RANK

    def directions_of(owner):
        return jnp.concatenate(
            [
                lax.dynamic_slice_in_dim(train_hidden[0], owner * hidden_share, hidden_share, 1),
                lax.dynamic_slice_in_dim(train_model[0], owner * model_share, model_share, 1),
            ],
            axis=1,
        )

    blocks = [directions_of(row)]
    for k in range(1, rows):
        blocks.append(shift(directions_of((row + k) % rows), "rows", k))
    store = jnp.concatenate(blocks, axis=0)
    stores = jnp.concatenate([store] + [shift(store, "parts", j) for j in range(1, parts)], axis=0)

    query = jnp.concatenate(
        [lax.dynamic_slice_in_dim(side[0], part * columns, columns, 0) for side in (query_hidden, query_model)],
        axis=1,
    )

    def blocked(partial):
        return partial.reshape(2, parts, rows, held, partial.shape[-1])

    if rows == 4:
        total = along_four(query, [hidden_basis[0], model_basis[0]], [hidden_eigen, model_eigen], stores, blocked)
    else:
        every = lax.all_gather(query, "rows", axis=0, tiled=True)
        width = hidden_basis.shape[2]

        def gram(basis, eigen, gathered, train):
            rotated = jnp.einsum("eh,qh->eq", basis, gathered, preferred_element_type=jnp.float32)
            scaled = (rotated * (1.0 / (eigen + damping))[:, None]).astype(jnp.bfloat16)
            return jnp.dot(train, scaled, preferred_element_type=jnp.float32)

        hidden_gram = gram(hidden_basis[0], hidden_eigen[0], every[:, :width], stores[:, :hidden_share])
        model_gram = gram(model_basis[0], model_eigen[0], every[:, width:], stores[:, hidden_share:])
        both = blocked(jnp.stack([hidden_gram, model_gram]))
        total = exchange(both, both.astype(jnp.bfloat16))

    product = total[0] * total[1]
    examples = held // RANK
    by_column = product.reshape(parts, examples, RANK, rows * columns).sum(axis=2)
    if columns % RANK == 0:
        by_query = by_column.reshape(parts, examples, rows, 1, columns // RANK, RANK).sum(axis=-1)
        mine = lax.broadcasted_iota(jnp.int32, (1, 1, 1, parts, 1), 3) == part
        scores = jnp.where(mine, by_query, 0.0).reshape(parts, examples, queries)
    else:
        place = jnp.arange(rows * columns)
        place = (place // columns) * (columns * parts) + part * columns + place % columns
        pick = (place[:, None] // RANK == jnp.arange(queries)[None, :]).astype(jnp.float32)
        scores = jnp.einsum("pic,cq->piq", by_column, pick, precision=lax.Precision.HIGHEST)

    kept = scores[0]
    for j in range(1, parts):
        kept = kept + shift(scores[j], "parts", -j)
    layer = lax.axis_index("layer")
    width = queries // layers

    def queries_of(owner):
        return lax.dynamic_slice_in_dim(kept, owner * width, width, 1)

    result = queries_of(layer)
    for k in range(1, layers):
        result = result + shift(queries_of((layer + k) % layers), "layer", k)
    return result


def solution(mesh):
    placed = (
        P("layer", "rows", None),
        P("layer", "rows", None),
        P("layer", ("parts", "rows"), None),
        P("layer", ("parts", "rows"), None),
        P("layer", "rows", None),
        P("layer", "rows", None),
        P("layer", "rows"),
        P("layer", "rows"),
    )
    return jax.shard_map(
        per_device,
        mesh=mesh,
        in_specs=placed,
        out_specs=P(("parts", "rows"), "layer"),
        check_vma=False,
    )
```

time: 153 us -> 161 us (1.052)
  Pallas kernels: 0 us -> 73 us
  waiting for transfers between devices: 71.2 us -> 30 us
  starting transfers between devices: 27.4 us -> 46.6 us
  matrix products: 19 us -> 0 us
  between operations: 13.7 us -> 0.47 us
  blocking collectives: 12.6 us -> 0 us
  other arithmetic: 1.08 us -> 4.47 us
  local copies, waits for them, and re-layouts: 8.04 us -> 5.72 us
    pallas_call x0 -> x10, Pallas kernels: none -> 73 us  [the longest x8 71.7 us: rotate(): pl.pallas_call(rotate_kernel, grid=(share // tile, width // depth), in_sp...]
    all_gather x2 -> x0, waiting for transfers between devices: 31.7 us -> none  [the longest x1 31.6 us: per_device(): all_hidden = lax.all_gather(own_hidden, 'rows', axis=0, tiled=True)]
    ppermute x0 -> x9, starting transfers between devices: none -> 28.9 us  [the longest x4 16.8 us: along(): lax.ppermute(value, 'rows', [(i, i + by) for i in range(size) if 0 <= i +...]
    dot_general x2 -> x0, matrix products: 19 us -> none  [gram(): return jnp.dot(train, scaled, preferred_element_type=jnp.float32)]
    ppermute x10 -> x11, waiting for transfers between devices: 39.5 us -> 23.9 us  [shift(): lax.ppermute(value, axis, [(i, (i + by) % size) for i in range(size)])]
    psum x1 -> x0, blocking collectives: 12.6 us -> none  [per_device(): whole = lax.psum(partial_value, ('parts', 'layer'))]
    ppermute x10 -> x11, starting transfers between devices: 27.3 us -> 17.7 us  [shift(): lax.ppermute(value, axis, [(i, (i + by) % size) for i in range(size)])]
    ppermute x0 -> x9, waiting for transfers between devices: none -> 6.1 us  [the longest x3 5.61 us: along_four(): part = lax.ppermute(sent[:, :, k], 'rows', ends).astype(jnp.float32)]
  transfers between devices with their start and end apart: 12 -> 20, of which waited for: 7 -> 8; matrix products, arithmetic and copies ran while one was open for 16% -> 4% of each run, Pallas kernels for 0% -> 27%
where the time goes in v3:
time: 161 us; the launch traced here: 160 us
  Pallas kernels  73 us (45%)
  starting transfers between devices  46.6 us (29%)
  waiting for transfers between devices  30 us (19%)
  local copies, waits for them, and re-layouts  5.72 us (4%)
  other arithmetic  4.47 us (3%)
    pallas_call x8, Pallas kernels, rotate(): pl.pallas_call(rotate_kernel, grid=(share // tile, width // depth), in_sp...  71.7 us
    ppermute x11, waiting for transfers between devices, shift(): lax.ppermute(value, axis, [(i, (i + by) % size) for i in range(size)])  23.9 us
    ppermute x11, starting transfers between devices, shift(): lax.ppermute(value, axis, [(i, (i + by) % size) for i in range(size)])  17.7 us
    ppermute x4, starting transfers between devices, along(): lax.ppermute(value, 'rows', [(i, i + by) for i in range(size) if 0 <= i +...  16.8 us
    ppermute x3, starting transfers between devices, along_four(): part = lax.ppermute(sent[:, :, k], 'rows', ends).astype(jnp.float32)  9.47 us
    ppermute x3, waiting for transfers between devices, along_four(): part = lax.ppermute(sent[:, :, k], 'rows', ends).astype(jnp.float32)  5.61 us
  transfers between devices with their start and end apart: 20, of which 8 were waited for; matrix products, arithmetic and copies ran while one was open for 4% of the time, Pallas kernels for 27%

profile of v3, /device:TPU:0, one launch (start us, length us, event | category | flops | bytes accessed | tf_op | source)
XLA Modules:
  0.0 160.1 jit_solution(8179469788838053810)
XLA Ops:
  1.5 1.3 collective-permute-start.4
  2.8 6.6 %collective-permute-start.5 = (bf16[48,10240]{1,0:T(8,128)(2,1)S(1)}, bf16[48,10240]{1,0:T(8,128)(2,1)}, u32[]{:S(2)}, u32[]{:S(2)}) collective-permute-start(bf16[48,10240]{1,0:T(8,128)(2,1)S(1)} %pad_maximum_fusion.refs_0_), channel_id=1, source_target_pairs={{0,4},{4,8},{8,12},{1,5},{5,9},{9,13},{2,6},{6,10},{10,14},{3,7},{... | collective-permute-start | bytes 2949128 | tf_op jit(solution)/shard_map/ppermute | solution.py:23
  15.4 2.9 %collective-permute-start.2 = (bf16[40,2560]{1,0:T(8,128)(2,1)}, bf16[40,2560]{1,0:T(8,128)(2,1)}, u32[]{:S(2)}, u32[]{:S(2)}) collective-permute-start(bf16[40,2560]{1,0:T(8,128)(2,1)} %pad_maximum_fusion.4), channel_id=1, source_target_pairs={{0,12},{4,0},{8,4},{12,8},{1,13},{5,1},{9,5},{13,9},{2,14},{6,2},{... | collective-permute-start | bytes 614408 | tf_op jit(solution)/shard_map/ppermute | solution.py:18
  18.4 12.1 %shard_map.82.refs_0_ = bf16[48,1536]{1,0:T(8,128)(2,1)S(1)} custom-call(bf16[1536,6144]{1,0:T(8,128)(2,1)} %bitcast.76, f32[1,1536]{1,0:T(1,128)S(1)} %copy-done.1, bf16[48,10240]{1,0:T(8,128)(2,1)S(1)} %pad_maximum_fusion.refs_0_), custom_call_target="tpu_custom_call" | custom-call | flops 1 | bytes 1 | tf_op jit(solution)/shard_map/pallas_call | solution.py:54
  30.5 5.8 %shard_map.83.refs_4_ = bf16[48,1024]{1,0:T(8,128)(2,1)S(1)} custom-call(bf16[1024,4096]{1,0:T(8,128)(2,1)} %bitcast.80, f32[1,1024]{1,0:T(1,128)S(1)} %copy-done.2, bf16[48,10240]{1,0:T(8,128)(2,1)S(1)} %pad_maximum_fusion.refs_0_), custom_call_target="tpu_custom_call" | custom-call | flops 1 | bytes 1 | tf_op jit(solution)/shard_map/pallas_call | solution.py:54
  36.3 7.4 %collective-permute-done.1 = bf16[40,2560]{1,0:T(8,128)(2,1)S(1)} collective-permute-done((bf16[40,2560]{1,0:T(8,128)(2,1)}, bf16[40,2560]{1,0:T(8,128)(2,1)S(1)}, u32[]{:S(2)}, u32[]{:S(2)}) %collective-permute-start.1) | collective-permute-done | bytes 204832 | tf_op jit(solution)/shard_map/ppermute | solution.py:18
  44.8 1.6 collective-permute-start.3
  48.6 7.7 %collective-permute-start.7 = (bf16[48,10240]{1,0:T(8,128)(2,1)}, bf16[48,10240]{1,0:T(8,128)(2,1)S(1)}, u32[]{:S(2)}, u32[]{:S(2)}) collective-permute-start(bf16[48,10240]{1,0:T(8,128)(2,1)} %collective-permute-done.5.refs_1_), channel_id=1, source_target_pairs={{0,4},{4,8},{8,12},{1,5},{5,9},{9,13},{2,6},{6,10},{10,14},{3,7},{... | collective-permute-start | bytes 2949128 | tf_op jit(solution)/shard_map/ppermute | solution.py:23
  57.3 12.3 %shard_map.84 = bf16[96,1536]{1,0:T(8,128)(2,1)S(1)} custom-call(bf16[1536,6144]{1,0:T(8,128)(2,1)} %bitcast.77, f32[1,1536]{1,0:T(1,128)S(1)} %copy-done.1, bf16[48,10240]{1,0:T(8,128)(2,1)S(1)} %collective-permute-done.4.refs_0_, bf16[48,10240]{1,0:T(8,128)(2,1)} %collective-permute-done.5.refs_1_), custom_call_target="tpu_custom_call" | custom-call | flops 1 | bytes 1 | tf_op jit(solution)/shard_map/pallas_call | solution.py:54
  69.6 5.9 %shard_map.85 = bf16[96,1024]{1,0:T(8,128)(2,1)S(1)} custom-call(bf16[1024,4096]{1,0:T(8,128)(2,1)} %bitcast.81, f32[1,1024]{1,0:T(1,128)S(1)} %copy-done.2, bf16[48,10240]{1,0:T(8,128)(2,1)S(1)} %collective-permute-done.4.refs_0_, bf16[48,10240]{1,0:T(8,128)(2,1)} %collective-permute-done.5.refs_1_), custom_call_target="tpu_custom_call" | custom-call | flops 1 | bytes 1 | tf_op jit(solution)/shard_map/pallas_call | solution.py:54
  76.2 12.1 %shard_map.86.refs_2_ = bf16[48,1536]{1,0:T(8,128)(2,1)S(1)} custom-call(bf16[1536,6144]{1,0:T(8,128)(2,1)} %bitcast.78, f32[1,1536]{1,0:T(1,128)S(1)} %copy-done.1, bf16[48,6144]{1,0:T(8,128)(2,1)S(1)} %slice_select_fusion.refs_0_), custom_call_target="tpu_custom_call" | custom-call | flops 1 | bytes 1 | tf_op jit(solution)/shard_map/pallas_call | solution.py:54
  89.6 5.7 %shard_map.87.refs_6_ = bf16[48,1024]{1,0:T(8,128)(2,1)S(1)} custom-call(bf16[1024,4096]{1,0:T(8,128)(2,1)} %bitcast.82, f32[1,1024]{1,0:T(1,128)S(1)} %copy-done.2, bf16[48,4096]{1,0:T(8,128)(2,1)S(1)} %slice_select_fusion.1.refs_0_), custom_call_target="tpu_custom_call" | custom-call | flops 1 | bytes 1 | tf_op jit(solution)/shard_map/pallas_call | solution.py:54
  97.4 2.7 %collective-permute-start.10 = (bf16[2,2,40,192]{3,2,1,0:T(8,128)(2,1)S(1)}, bf16[2,2,40,192]{3,2,1,0:T(8,128)(2,1)S(1)}, u32[]{:S(2)}, u32[]{:S(2)}) collective-permute-start(bf16[2,2,40,192]{3,2,1,0:T(8,128)(2,1)S(1)} %get-tuple-element.42), channel_id=1, source_target_pairs={{0,4},{4,8},{8,12},{12,0},{1,5},{5,9},{9,13},{13,1},{2,6},{6,10},{... | collective-permute-start | bytes 184328 | tf_op jit(solution)/shard_map/ppermute | solution.py:18
  100.2 3.2 %collective-permute-start.9 = (bf16[2,2,40,192]{3,2,1,0:T(8,128)(2,1)S(1)}, bf16[2,2,40,192]{3,2,1,0:T(8,128)(2,1)S(1)}, u32[]{:S(2)}, u32[]{:S(2)}) collective-permute-start(bf16[2,2,40,192]{3,2,1,0:T(8,128)(2,1)S(1)} %get-tuple-element.43), channel_id=1, source_target_pairs={{0,8},{4,12},{8,0},{12,4},{1,9},{5,13},{9,1},{13,5},{2,10},{6,14},... | collective-permute-start | bytes 184328 | tf_op jit(solution)/shard_map/ppermute | solution.py:18
  103.3 2.8 %collective-permute-start.8 = (bf16[2,2,40,192]{3,2,1,0:T(8,128)(2,1)S(1)}, bf16[2,2,40,192]{3,2,1,0:T(8,128)(2,1)S(1)}, u32[]{:S(2)}, u32[]{:S(2)}) collective-permute-start(bf16[2,2,40,192]{3,2,1,0:T(8,128)(2,1)S(1)} %get-tuple-element.41), channel_id=1, source_target_pairs={{0,12},{4,0},{8,4},{12,8},{1,13},{5,1},{9,5},{13,9},{2,14},{6,2},{... | collective-permute-start | bytes 184328 | tf_op jit(solution)/shard_map/ppermute | solution.py:18
  106.3 10.5 %collective-permute-done.8 = bf16[2,2,40,192]{3,2,1,0:T(8,128)(2,1)S(1)} collective-permute-done((bf16[2,2,40,192]{3,2,1,0:T(8,128)(2,1)S(1)}, bf16[2,2,40,192]{3,2,1,0:T(8,128)(2,1)S(1)}, u32[]{:S(2)}, u32[]{:S(2)}) %collective-permute-start.8) | collective-permute-done | bytes 61472 | tf_op jit(solution)/shard_map/ppermute | solution.py:18
  116.8 12.1 %shard_map.89.refs_0_ = bf16[48,1536]{1,0:T(8,128)(2,1)S(1)} custom-call(bf16[1536,6144]{1,0:T(8,128)(2,1)} %bitcast.79, f32[1,1536]{1,0:T(1,128)S(1)} %copy-done.1, bf16[48,6144]{1,0:T(8,128)(2,1)S(1)} %collective-permute-done.11.refs_0_), custom_call_target="tpu_custom_call" | custom-call | flops 1 | bytes 1 | tf_op jit(solution)/shard_map/pallas_call | solution.py:54
  128.9 5.7 %shard_map.90.refs_1_ = bf16[48,1024]{1,0:T(8,128)(2,1)S(1)} custom-call(bf16[1024,4096]{1,0:T(8,128)(2,1)} %bitcast.83, f32[1,1024]{1,0:T(1,128)S(1)} %copy-done.2, bf16[48,4096]{1,0:T(8,128)(2,1)S(1)} %collective-permute-done.12.refs_0_), custom_call_target="tpu_custom_call" | custom-call | flops 1 | bytes 1 | tf_op jit(solution)/shard_map/pallas_call | solution.py:54
  135.2 6.3 %collective-permute-start.13 = (bf16[2,2,40,48]{3,2,1,0:T(8,128)(2,1)S(1)}, bf16[2,2,40,48]{3,2,1,0:T(8,128)(2,1)S(1)}, u32[]{:S(2)}, u32[]{:S(2)}) collective-permute-start(bf16[2,2,40,48]{3,2,1,0:T(8,128)(2,1)S(1)} %get-tuple-element.53), channel_id=1, source_target_pairs={{0,12},{12,8},{1,13},{13,9},{2,14},{14,10},{3,15},{15,11},{16,28},... | collective-permute-start | bytes 46088 | tf_op jit(solution)/shard_map/ppermute | solution.py:145
  142.8 1.9 %collective-permute-start.15 = (bf16[2,2,40,48]{3,2,1,0:T(8,128)(2,1)S(1)}, bf16[2,2,40,48]{3,2,1,0:T(8,128)(2,1)S(1)}, u32[]{:S(2)}, u32[]{:S(2)}) collective-permute-start(bf16[2,2,40,48]{3,2,1,0:T(8,128)(2,1)S(1)} %get-tuple-element.52), channel_id=1, source_target_pairs={{0,4},{12,0},{1,5},{13,1},{2,6},{14,2},{3,7},{15,3},{16,20},{28,16... | collective-permute-start | bytes 46088 | tf_op jit(solution)/shard_map/ppermute | solution.py:145
  144.9 5.6 %collective-permute-done.15 = bf16[2,2,40,48]{3,2,1,0:T(8,128)(2,1)S(1)} collective-permute-done((bf16[2,2,40,48]{3,2,1,0:T(8,128)(2,1)S(1)}, bf16[2,2,40,48]{3,2,1,0:T(8,128)(2,1)S(1)}, u32[]{:S(2)}, u32[]{:S(2)}) %collective-permute-start.15) | collective-permute-done | bytes 15392 | tf_op jit(solution)/shard_map/ppermute | solution.py:145
  151.8 3.0 %collective-permute-done.16 = f32[5,48]{1,0:T(8,128)S(1)} collective-permute-done((f32[5,48]{1,0:T(8,128)S(1)}, f32[5,48]{1,0:T(8,128)S(1)}, u32[]{:S(2)}, u32[]{:S(2)}) %collective-permute-start.16) | collective-permute-done | bytes 992 | tf_op jit(solution)/shard_map/ppermute | solution.py:18
  154.9 1.6 collective-permute-start.18
  156.6 1.9 %collective-permute-done.18 = f32[5,12]{1,0:T(8,128)S(1)} collective-permute-done((f32[5,12]{1,0:T(8,128)S(1)}, f32[5,12]{1,0:T(8,128)S(1)}, u32[]{:S(2)}, u32[]{:S(2)}) %collective-permute-start.18) | collective-permute-done | bytes 272 | tf_op jit(solution)/shard_map/ppermute | solution.py:18
  (73 shorter events, 21.0 us)
Async XLA Ops:
  1.4 8.0 %copy-start.4 = (bf16[1,40,4096]{2,1,0:T(8,128)(2,1)S(1)}, bf16[1,40,4096]{2,1,0:T(8,128)(2,1)}, u32[]{:S(2)}) copy-start(bf16[1,40,4096]{2,1,0:T(8,128)(2,1)} %param.11) | copy-start | bytes 983044
  1.5 16.9 %copy-start.1 = (f32[1,1536]{1,0:T(1,128)S(1)}, f32[1,1536]{1,0:T(1,128)}, u32[]{:S(2)}) copy-start(f32[1,1536]{1,0:T(1,128)} %eigen_ref.14) | copy-start | bytes 18436
  1.5 45.8 %collective-permute-start.4 = (bf16[48,10240]{1,0:T(8,128)(2,1)S(1)}, bf16[48,10240]{1,0:T(8,128)(2,1)S(1)}, u32[]{:S(2)}, u32[]{:S(2)}) collective-permute-start(bf16[48,10240]{1,0:T(8,128)(2,1)S(1)} %pad_maximum_fusion.refs_0_), channel_id=1, source_target_pairs={{4,0},{8,4},{12,8},{5,1},{9,5},{13,9},{6,2},{10,6},{14,10},{7,3},{... | collective-permute-start | bytes 2949128 | tf_op jit(solution)/shard_map/ppermute | solution.py:23
  2.8 44.5 %collective-permute-start.5 = (bf16[48,10240]{1,0:T(8,128)(2,1)S(1)}, bf16[48,10240]{1,0:T(8,128)(2,1)}, u32[]{:S(2)}, u32[]{:S(2)}) collective-permute-start(bf16[48,10240]{1,0:T(8,128)(2,1)S(1)} %pad_maximum_fusion.refs_0_), channel_id=1, source_target_pairs={{0,4},{4,8},{8,12},{1,5},{5,9},{9,13},{2,6},{6,10},{10,14},{3,7},{... | collective-permute-start | bytes 2949128 | tf_op jit(solution)/shard_map/ppermute | solution.py:23
  11.9 24.4 %collective-permute-start = (bf16[40,2560]{1,0:T(8,128)(2,1)}, bf16[40,2560]{1,0:T(8,128)(2,1)}, u32[]{:S(2)}, u32[]{:S(2)}) collective-permute-start(bf16[40,2560]{1,0:T(8,128)(2,1)} %pad_maximum_fusion.2), channel_id=1, source_target_pairs={{0,4},{4,8},{8,12},{12,0},{1,5},{5,9},{9,13},{13,1},{2,6},{6,10},{... | collective-permute-start | bytes 614408 | tf_op jit(solution)/shard_map/ppermute | solution.py:18
  13.7 30.0 %collective-permute-start.1 = (bf16[40,2560]{1,0:T(8,128)(2,1)}, bf16[40,2560]{1,0:T(8,128)(2,1)S(1)}, u32[]{:S(2)}, u32[]{:S(2)}) collective-permute-start(bf16[40,2560]{1,0:T(8,128)(2,1)} %pad_maximum_fusion.3), channel_id=1, source_target_pairs={{0,8},{4,12},{8,0},{12,4},{1,9},{5,13},{9,1},{13,5},{2,10},{6,14},... | collective-permute-start | bytes 614408 | tf_op jit(solution)/shard_map/ppermute | solution.py:18
  15.4 28.2 %collective-permute-start.2 = (bf16[40,2560]{1,0:T(8,128)(2,1)}, bf16[40,2560]{1,0:T(8,128)(2,1)}, u32[]{:S(2)}, u32[]{:S(2)}) collective-permute-start(bf16[40,2560]{1,0:T(8,128)(2,1)} %pad_maximum_fusion.4), channel_id=1, source_target_pairs={{0,12},{4,0},{8,4},{12,8},{1,13},{5,1},{9,5},{13,9},{2,14},{6,2},{... | collective-permute-start | bytes 614408 | tf_op jit(solution)/shard_map/ppermute | solution.py:18
  18.4 12.1 %copy-start.2 = (f32[1,1024]{1,0:T(1,128)S(1)}, f32[1,1024]{1,0:T(1,128)}, u32[]{:S(2)}) copy-start(f32[1,1024]{1,0:T(1,128)} %eigen_ref.15) | copy-start | bytes 12292
  30.5 5.8 %copy-start.3 = (bf16[40,1024]{1,0:T(8,128)(2,1)S(1)}, bf16[40,1024]{1,0:T(8,128)(2,1)}, u32[]{:S(2)}) copy-start(bf16[40,1024]{1,0:T(8,128)(2,1)} %get-tuple-element.46) | copy-start | bytes 245764
  44.8 30.8 %collective-permute-start.3 = (bf16[160,2560]{1,0:T(8,128)(2,1)S(1)}, bf16[160,2560]{1,0:T(8,128)(2,1)S(1)}, u32[]{:S(2)}, u32[]{:S(2)}) collective-permute-start(bf16[160,2560]{1,0:T(8,128)(2,1)S(1)} %pad_maximum_fusion.1), channel_id=1, source_target_pairs={{0,16},{16,0},{1,17},{17,1},{2,18},{18,2},{3,19},{19,3},{4,20},{20... | collective-permute-start | bytes 2457608 | tf_op jit(solution)/shard_map/ppermute | solution.py:18
  47.3 28.3 %collective-permute-start.6 = (bf16[48,10240]{1,0:T(8,128)(2,1)S(1)}, bf16[48,10240]{1,0:T(8,128)(2,1)S(1)}, u32[]{:S(2)}, u32[]{:S(2)}) collective-permute-start(bf16[48,10240]{1,0:T(8,128)(2,1)S(1)} %collective-permute-done.4.refs_0_), channel_id=1, source_target_pairs={{4,0},{8,4},{12,8},{5,1},{9,5},{13,9},{6,2},{10,6},{14,10},{7,3},{... | collective-permute-start | bytes 2949128 | tf_op jit(solution)/shard_map/ppermute | solution.py:23
  48.6 27.5 %collective-permute-start.7 = (bf16[48,10240]{1,0:T(8,128)(2,1)}, bf16[48,10240]{1,0:T(8,128)(2,1)S(1)}, u32[]{:S(2)}, u32[]{:S(2)}) collective-permute-start(bf16[48,10240]{1,0:T(8,128)(2,1)} %collective-permute-done.5.refs_1_), channel_id=1, source_target_pairs={{0,4},{4,8},{8,12},{1,5},{5,9},{9,13},{2,6},{6,10},{10,14},{3,7},{... | collective-permute-start | bytes 2949128 | tf_op jit(solution)/shard_map/ppermute | solution.py:23
  88.3 28.5 %collective-permute-start.11 = (bf16[48,6144]{1,0:T(8,128)(2,1)S(1)}, bf16[48,6144]{1,0:T(8,128)(2,1)S(1)}, u32[]{:S(2)}, u32[]{:S(2)}) collective-permute-start(bf16[48,6144]{1,0:T(8,128)(2,1)S(1)} %slice_select_fusion.refs_0_), channel_id=1, source_target_pairs={{4,0},{8,12},{5,1},{9,13},{6,2},{10,14},{7,3},{11,15},{20,16},{24,... | collective-permute-start | bytes 1769480 | tf_op jit(solution)/shard_map/ppermute | solution.py:131
  95.4 21.4 %collective-permute-start.12 = (bf16[48,4096]{1,0:T(8,128)(2,1)S(1)}, bf16[48,4096]{1,0:T(8,128)(2,1)S(1)}, u32[]{:S(2)}, u32[]{:S(2)}) collective-permute-start(bf16[48,4096]{1,0:T(8,128)(2,1)S(1)} %slice_select_fusion.1.refs_0_), channel_id=1, source_target_pairs={{4,0},{8,12},{5,1},{9,13},{6,2},{10,14},{7,3},{11,15},{20,16},{24,... | collective-permute-start | bytes 1179656 | tf_op jit(solution)/shard_map/ppermute | solution.py:131
  97.4 8.8 %collective-permute-start.10 = (bf16[2,2,40,192]{3,2,1,0:T(8,128)(2,1)S(1)}, bf16[2,2,40,192]{3,2,1,0:T(8,128)(2,1)S(1)}, u32[]{:S(2)}, u32[]{:S(2)}) collective-permute-start(bf16[2,2,40,192]{3,2,1,0:T(8,128)(2,1)S(1)} %get-tuple-element.42), channel_id=1, source_target_pairs={{0,4},{4,8},{8,12},{12,0},{1,5},{5,9},{9,13},{13,1},{2,6},{6,10},{... | collective-permute-start | bytes 184328 | tf_op jit(solution)/shard_map/ppermute | solution.py:18
  100.2 6.1 %collective-permute-start.9 = (bf16[2,2,40,192]{3,2,1,0:T(8,128)(2,1)S(1)}, bf16[2,2,40,192]{3,2,1,0:T(8,128)(2,1)S(1)}, u32[]{:S(2)}, u32[]{:S(2)}) collective-permute-start(bf16[2,2,40,192]{3,2,1,0:T(8,128)(2,1)S(1)} %get-tuple-element.43), channel_id=1, source_target_pairs={{0,8},{4,12},{8,0},{12,4},{1,9},{5,13},{9,1},{13,5},{2,10},{6,14},... | collective-permute-start | bytes 184328 | tf_op jit(solution)/shard_map/ppermute | solution.py:18
  103.3 13.4 %collective-permute-start.8 = (bf16[2,2,40,192]{3,2,1,0:T(8,128)(2,1)S(1)}, bf16[2,2,40,192]{3,2,1,0:T(8,128)(2,1)S(1)}, u32[]{:S(2)}, u32[]{:S(2)}) collective-permute-start(bf16[2,2,40,192]{3,2,1,0:T(8,128)(2,1)S(1)} %get-tuple-element.41), channel_id=1, source_target_pairs={{0,12},{4,0},{8,4},{12,8},{1,13},{5,1},{9,5},{13,9},{2,14},{6,2},{... | collective-permute-start | bytes 184328 | tf_op jit(solution)/shard_map/ppermute | solution.py:18
  135.2 9.7 %collective-permute-start.13 = (bf16[2,2,40,48]{3,2,1,0:T(8,128)(2,1)S(1)}, bf16[2,2,40,48]{3,2,1,0:T(8,128)(2,1)S(1)}, u32[]{:S(2)}, u32[]{:S(2)}) collective-permute-start(bf16[2,2,40,48]{3,2,1,0:T(8,128)(2,1)S(1)} %get-tuple-element.53), channel_id=1, source_target_pairs={{0,12},{12,8},{1,13},{13,9},{2,14},{14,10},{3,15},{15,11},{16,28},... | collective-permute-start | bytes 46088 | tf_op jit(solution)/shard_map/ppermute | solution.py:145
  141.5 3.4 %collective-permute-start.14 = (bf16[2,2,40,48]{3,2,1,0:T(8,128)(2,1)S(1)}, bf16[2,2,40,48]{3,2,1,0:T(8,128)(2,1)S(1)}, u32[]{:S(2)}, u32[]{:S(2)}) collective-permute-start(bf16[2,2,40,48]{3,2,1,0:T(8,128)(2,1)S(1)} %get-tuple-element.54), channel_id=1, source_target_pairs={{0,8},{12,4},{1,9},{13,5},{2,10},{14,6},{3,11},{15,7},{16,24},{28,... | collective-permute-start | bytes 46088 | tf_op jit(solution)/shard_map/ppermute | solution.py:145
  142.8 7.7 %collective-permute-start.15 = (bf16[2,2,40,48]{3,2,1,0:T(8,128)(2,1)S(1)}, bf16[2,2,40,48]{3,2,1,0:T(8,128)(2,1)S(1)}, u32[]{:S(2)}, u32[]{:S(2)}) collective-permute-start(bf16[2,2,40,48]{3,2,1,0:T(8,128)(2,1)S(1)} %get-tuple-element.52), channel_id=1, source_target_pairs={{0,4},{12,0},{1,5},{13,1},{2,6},{14,2},{3,7},{15,3},{16,20},{28,16... | collective-permute-start | bytes 46088 | tf_op jit(solution)/shard_map/ppermute | solution.py:145
  151.2 3.6 %collective-permute-start.16 = (f32[5,48]{1,0:T(8,128)S(1)}, f32[5,48]{1,0:T(8,128)S(1)}, u32[]{:S(2)}, u32[]{:S(2)}) collective-permute-start(f32[5,48]{1,0:T(8,128)S(1)} %squeeze.57), channel_id=1, source_target_pairs={{0,16},{16,0},{1,17},{17,1},{2,18},{18,2},{3,19},{19,3},{4,20},{20... | collective-permute-start | bytes 2888 | tf_op jit(solution)/shard_map/ppermute | solution.py:18
  154.9 1.7 %collective-permute-start.19 = (f32[5,12]{1,0:T(8,128)S(1)}, f32[5,12]{1,0:T(8,128)S(1)}, u32[]{:S(2)}, u32[]{:S(2)}) collective-permute-start(f32[5,12]{1,0:T(8,128)S(1)} %get-tuple-element.58), channel_id=1, source_target_pairs={{0,3},{1,0},{2,1},{3,2},{4,7},{5,4},{6,5},{7,6},{8,11},{9,8},{10,9... | collective-permute-start | bytes 728 | tf_op jit(solution)/shard_map/ppermute | solution.py:18
  154.9 3.7 %collective-permute-start.18 = (f32[5,12]{1,0:T(8,128)S(1)}, f32[5,12]{1,0:T(8,128)S(1)}, u32[]{:S(2)}, u32[]{:S(2)}) collective-permute-start(f32[5,12]{1,0:T(8,128)S(1)} %get-tuple-element.59), channel_id=1, source_target_pairs={{0,2},{1,3},{2,0},{3,1},{4,6},{5,7},{6,4},{7,5},{8,10},{9,11},{10,... | collective-permute-start | bytes 728 | tf_op jit(solution)/shard_map/ppermute | solution.py:18
  156.4 3.0 %collective-permute-start.17 = (f32[5,12]{1,0:T(8,128)S(1)}, f32[5,12]{1,0:T(8,128)S(1)}, u32[]{:S(2)}, u32[]{:S(2)}) collective-permute-start(f32[5,12]{1,0:T(8,128)S(1)} %get-tuple-element.57), channel_id=1, source_target_pairs={{0,1},{1,2},{2,3},{3,0},{4,5},{5,6},{6,7},{7,4},{8,9},{9,10},{10,1... | collective-permute-start | bytes 728 | tf_op jit(solution)/shard_map/ppermute | solution.py:18
  (1 other events, 1.4 us)

commit v4 on v1

v4 whole, which is shorter than its diff:
```python
import jax
import jax.numpy as jnp
from jax import lax
from jax.experimental import pallas as pl
from jax.experimental.pallas import tpu as pltpu
from jax.sharding import PartitionSpec as P

RANK = 8


damping = 0.1

VMEM_LIMIT = 24 * 1024 * 1024
STREAMS = 4
TILE = 512
DEPTH = 2048


def along(value, by):
    size = lax.axis_size("rows")
    return lax.ppermute(value, "rows", [(i, i + by) for i in range(size) if 0 <= i + by < size])


def rotate(bases, eigens, queries):
    columns = queries[0].shape[0]
    held = columns * len(queries)
    part = TILE // STREAMS
    depths = [basis.shape[1] // DEPTH for basis in bases]
    steps = [basis.shape[0] // TILE * depth for basis, depth in zip(bases, depths)]

    def place(side, i):
        i = jnp.minimum(i, steps[0] - 1) if side == 0 else jnp.maximum(i - steps[0], 0)
        return lax.div(i, depths[side]), lax.rem(i, depths[side])

    def basis_spec(side, stream):
        def index(i):
            tile, k = place(side, i)
            return tile * STREAMS + stream, k

        return pl.BlockSpec((part, DEPTH), index)

    def row_spec(side, height):
        return pl.BlockSpec((height, TILE), lambda i: (0, place(side, i)[0]))

    def query_index(i):
        return 0, jnp.where(i < steps[0], place(0, i)[1], depths[0] + place(1, i)[1])

    def kernel(*refs):
        basis_refs = refs[:STREAMS], refs[STREAMS : 2 * STREAMS]
        eigen_refs = refs[2 * STREAMS : 2 * STREAMS + 2]
        query_refs = refs[2 * STREAMS + 2 : -3]
        out_refs, total = refs[-3:-1], refs[-1]
        step = pl.program_id(0)
        blocks = [ref[...] for ref in query_refs]
        query = blocks[0] if len(blocks) == 1 else jnp.concatenate(blocks, axis=0)

        def one(side):
            k = place(side, step)[1]
            for stream, ref in enumerate(basis_refs[side]):
                where = slice(stream * part, (stream + 1) * part)
                term = lax.dot_general(
                    query, ref[...], (((1,), (1,)), ((), ())), preferred_element_type=jnp.float32
                )
                total[:, where] = jnp.where(k == 0, 0.0, total[:, where]) + term

            @pl.when(k == depths[side] - 1)
            def _():
                scale = 1.0 / (eigen_refs[side][...] + damping)
                out_refs[side][...] = (total[...] * scale).astype(jnp.bfloat16)

        @pl.when(step < steps[0])
        def _():
            one(0)

        @pl.when(step >= steps[0])
        def _():
            one(1)

    constrain = pltpu.with_memory_space_constraint
    return pl.pallas_call(
        kernel,
        grid=(sum(steps),),
        in_specs=[basis_spec(side, stream) for side in range(2) for stream in range(STREAMS)]
        + [row_spec(side, 1) for side in range(2)]
        + [pl.BlockSpec((columns, DEPTH), query_index) for _ in queries],
        out_specs=[row_spec(side, held) for side in range(2)],
        out_shape=[jax.ShapeDtypeStruct((held, basis.shape[0]), jnp.bfloat16) for basis in bases],
        scratch_shapes=[pltpu.VMEM((held, TILE), jnp.float32)],
        compiler_params=pltpu.CompilerParams(vmem_limit_bytes=VMEM_LIMIT),
        cost_estimate=pl.CostEstimate(flops=1, bytes_accessed=1, transcendentals=0),
    )(
        *[constrain(basis, pltpu.HBM) for basis in bases for _ in range(STREAMS)],
        *eigens,
        *[constrain(query, pltpu.VMEM) for query in queries],
    )


def grams(stores, near, two, three, rows):
    shares = [side.shape[1] for side in near]
    columns = two[0].shape[0]
    held = stores[0].shape[0] // rows
    count = len(stores)

    def kernel(*refs):
        store_refs, (out_ref, *queries) = refs[:count], refs[count + 6 :]
        row = lax.axis_index("rows")
        for side in range(2):
            near_ref, two_ref, three_ref = refs[count + side : count + 6 : 2]
            query = queries[side]

            def put(row_of, block, query=query):
                where = pl.multiple_of(row_of * columns, columns)
                query[pl.ds(where, columns), :] = block

            put(row, near_ref[:columns, :])
            put(lax.rem(row + 1, rows), near_ref[columns : 2 * columns, :])
            put(lax.rem(row + 3, rows), near_ref[2 * columns :, :])
            put(lax.rem(row + 2, rows), two_ref[...])

            @pl.when(row == 0)
            def _(put=put, three_ref=three_ref):
                put(3, three_ref[...])

            @pl.when(row == 3)
            def _(put=put, three_ref=three_ref):
                put(0, three_ref[...])

            begin = side * shares[0]
            for j, store_ref in enumerate(store_refs):
                gram = lax.dot_general(
                    store_ref[:, begin : begin + shares[side]],
                    query[...],
                    (((1,), (1,)), ((), ())),
                    preferred_element_type=jnp.float32,
                ).astype(jnp.bfloat16)
                for owner in range(rows):
                    out_ref[owner, side, j] = gram[owner * held : (owner + 1) * held]

    return pl.pallas_call(
        kernel,
        out_shape=jax.ShapeDtypeStruct((rows, 2, count, held, columns * rows), jnp.bfloat16),
        scratch_shapes=[pltpu.VMEM((columns * rows, share), jnp.bfloat16) for share in shares],
        compiler_params=pltpu.CompilerParams(vmem_limit_bytes=VMEM_LIMIT),
        cost_estimate=pl.CostEstimate(flops=1, bytes_accessed=1, transcendentals=0),
    )(*stores, *near, *two, *three)


def along_four(query, bases, eigens, stores):
    row = lax.axis_index("rows")
    after, before = along(query, -1), along(query, 1)
    after_two, before_two = along(after, -1), along(before, 1)
    near = rotate(bases, eigens, [query, after, before])
    near, after_two, before_two = lax.optimization_barrier((near, after_two, before_two))
    two = jnp.where(row < 2, after_two, before_two)
    three = lax.ppermute(two, "rows", [(1, 0), (2, 3)])
    two = rotate(bases, eigens, [two])
    two, three = lax.optimization_barrier((two, three))
    return grams(stores, near, two, rotate(bases, eigens, [three]), 4)


def per_device(
    query_hidden,
    query_model,
    train_hidden,
    train_model,
    hidden_basis,
    model_basis,
    hidden_eigen,
    model_eigen,
):
    rows = lax.axis_size("rows")
    parts = lax.axis_size("parts")
    layers = lax.axis_size("layer")
    part = lax.axis_index("parts")
    held = train_hidden.shape[1]
    columns = query_hidden.shape[1] // parts
    queries = query_hidden.shape[1] * rows // RANK
    bases = [hidden_basis[0], model_basis[0]]
    eigens = [hidden_eigen, model_eigen]
    share = bases[0].shape[0]
    width = bases[0].shape[1]

    query = jnp.concatenate(
        [lax.dynamic_slice_in_dim(side[0], part * columns, columns, 0) for side in (query_hidden, query_model)],
        axis=1,
    )

    by_owner = jnp.concatenate(
        [side[0].reshape(held, rows, -1).transpose(1, 0, 2) for side in (train_hidden, train_model)], axis=2
    )
    store = lax.all_to_all(by_owner, "rows", 0, 0, tiled=True).reshape(rows * held, -1)
    stores = [store]
    for j in range(1, parts):
        stores.append(lax.ppermute(store, "parts", [(i, (i + j) % parts) for i in range(parts)]))

    if rows == 4:
        partial = along_four(query, bases, eigens, stores)
    else:
        every = lax.all_gather(query, "rows", axis=0, tiled=True)
        sides = []
        for basis, eigen, gathered, begin in zip(bases, eigens, (every[:, :width], every[:, width:]), (0, share)):
            rotated = jnp.einsum("eh,qh->eq", basis, gathered, preferred_element_type=jnp.float32)
            scaled = (rotated * (1.0 / (eigen[0] + damping))[:, None]).astype(jnp.bfloat16)
            sides.append(
                [
                    jnp.dot(one[:, begin : begin + basis.shape[0]], scaled, preferred_element_type=jnp.float32)
                    for one in stores
                ]
            )
        partial = jnp.array(sides).astype(jnp.bfloat16)
        partial = partial.reshape(2, parts, rows, held, rows * columns).transpose(2, 0, 1, 3, 4)

    received = lax.all_to_all(partial, "rows", 0, 0, tiled=True)
    total = received.astype(jnp.float32).sum(axis=0)
    product = total[0] * total[1]
    examples = held // RANK
    by_column = product.reshape(parts, examples, RANK, rows * columns).sum(axis=2)
    if columns % RANK == 0:
        by_query = by_column.reshape(parts, examples, rows, 1, columns // RANK, RANK).sum(axis=-1)
        mine = lax.broadcasted_iota(jnp.int32, (1, 1, 1, parts, 1), 3) == part
        scores = jnp.where(mine, by_query, 0.0).reshape(parts, examples, queries)
    else:
        place = jnp.arange(rows * columns)
        place = (place // columns) * (columns * parts) + part * columns + place % columns
        pick = (place[:, None] // RANK == jnp.arange(queries)[None, :]).astype(jnp.float32)
        scores = jnp.einsum("pic,cq->piq", by_column, pick, precision=lax.Precision.HIGHEST)

    scores = jnp.stack([lax.dynamic_index_in_dim(scores, (part - j) % parts, 0, False) for j in range(parts)])
    scores = scores.reshape(parts, examples, layers, queries // layers).transpose(0, 2, 1, 3)
    scores = scores.reshape(parts * layers, examples, queries // layers)
    return lax.all_to_all(scores, ("parts", "layer"), 0, 0, tiled=True).sum(axis=0)


def solution(mesh):
    placed = (
        P("layer", "rows", None),
        P("layer", "rows", None),
        P("layer", ("parts", "rows"), None),
        P("layer", ("parts", "rows"), None),
        P("layer", "rows", None),
        P("layer", "rows", None),
        P("layer", "rows"),
        P("layer", "rows"),
    )
    return jax.shard_map(
        per_device,
        mesh=mesh,
        in_specs=placed,
        out_specs=P(("parts", "rows"), "layer"),
        check_vma=False,
    )
```

time: 153 us -> 136 us (0.89)
  Pallas kernels: 0 us -> 57.2 us
  waiting for transfers between devices: 71.2 us -> 35.3 us
  matrix products: 19 us -> 0 us
  between operations: 13.7 us -> 0.28 us
  blocking collectives: 12.6 us -> 7.41 us
  local copies, waits for them, and re-layouts: 8.04 us -> 3.63 us
  other arithmetic: 1.08 us -> 3.42 us
    pallas_call x0 -> x4, Pallas kernels: none -> 57.2 us  [the longest x3 55.4 us: rotate(): pl.pallas_call(kernel, grid=(sum(steps),), in_specs=[basis_spec(side, str...]
    all_gather x2 -> x0, waiting for transfers between devices: 31.7 us -> none  [the longest x1 31.6 us: per_device(): all_hidden = lax.all_gather(own_hidden, 'rows', axis=0, tiled=True)]
    ppermute x10 -> x6, waiting for transfers between devices: 39.5 us -> 18.9 us  [the longest x4 18.9 us: along(): lax.ppermute(value, 'rows', [(i, i + by) for i in range(size) if 0 <= i +...]
    dot_general x2 -> x0, matrix products: 19 us -> none  [gram(): return jnp.dot(train, scaled, preferred_element_type=jnp.float32)]
    all_to_all x0 -> x2, waiting for transfers between devices: none -> 16.4 us  [the longest x1 9.25 us: per_device(): lax.all_to_all(by_owner, 'rows', 0, 0, tiled=True).reshape(rows * held, -1)]
    psum x1 -> x0, blocking collectives: 12.6 us -> none  [per_device(): whole = lax.psum(partial_value, ('parts', 'layer'))]
    all_to_all x0 -> x2, starting transfers between devices: none -> 9.85 us  [the longest x1 5.83 us: per_device(): received = lax.all_to_all(partial, 'rows', 0, 0, tiled=True)]
    ppermute x10 -> x6, starting transfers between devices: 27.3 us -> 17.6 us  [the longest x4 14.8 us: along(): lax.ppermute(value, 'rows', [(i, i + by) for i in range(size) if 0 <= i +...]
  transfers between devices with their start and end apart: 12 -> 8, of which waited for: 7 -> 3; matrix products, arithmetic and copies ran while one was open for 16% -> 2% of each run, Pallas kernels for 0% -> 41%
where the time goes in v4:
time: 136 us; the launch traced here: 135 us
  Pallas kernels  57.2 us (42%)
  waiting for transfers between devices  35.3 us (26%)
  starting transfers between devices  27.4 us (20%)
  blocking collectives  7.41 us (5%)
  local copies, waits for them, and re-layouts  3.63 us (3%)
  other arithmetic  3.42 us (3%)
    pallas_call x3, Pallas kernels, rotate(): pl.pallas_call(kernel, grid=(sum(steps),), in_specs=[basis_spec(side, str...  55.4 us
    ppermute x4, waiting for transfers between devices, along(): lax.ppermute(value, 'rows', [(i, i + by) for i in range(size) if 0 <= i +...  18.9 us
    ppermute x4, starting transfers between devices, along(): lax.ppermute(value, 'rows', [(i, i + by) for i in range(size) if 0 <= i +...  14.8 us
    all_to_all x1, waiting for transfers between devices, per_device(): lax.all_to_all(by_owner, 'rows', 0, 0, tiled=True).reshape(rows * held, -1)  9.25 us
    all_to_all x1, blocking collectives, per_device(): lax.all_to_all(scores, ('parts', 'layer'), 0, 0, tiled=True).sum(axis=0)  7.41 us
    all_to_all x1, waiting for transfers between devices, per_device(): received = lax.all_to_all(partial, 'rows', 0, 0, tiled=True)  7.13 us
    all_to_all x1, starting transfers between devices, per_device(): received = lax.all_to_all(partial, 'rows', 0, 0, tiled=True)  5.83 us
    all_to_all x1, starting transfers between devices, per_device(): lax.all_to_all(by_owner, 'rows', 0, 0, tiled=True).reshape(rows * held, -1)  4.02 us
  transfers between devices with their start and end apart: 8, of which 3 were waited for; matrix products, arithmetic and copies ran while one was open for 2% of the time, Pallas kernels for 41%

profile of v4, /device:TPU:0, one launch (start us, length us, event | category | flops | bytes accessed | tf_op | source)
XLA Modules:
  0.0 134.6 jit_solution(18409234601568502254)
XLA Ops:
  0.0 1.3 copy-done
  1.3 1.1 dynamic-slice_bitcast_fusion.1
  2.5 1.4 %collective-permute-start.1 = (bf16[48,10240]{1,0:T(8,128)(2,1)S(1)}, bf16[48,10240]{1,0:T(8,128)(2,1)}, u32[]{:S(2)}, u32[]{:S(2)}) collective-permute-start(bf16[48,10240]{1,0:T(8,128)(2,1)S(1)} %pad_maximum_fusion.refs_10_), channel_id=1, source_target_pairs={{4,0},{8,4},{12,8},{5,1},{9,5},{13,9},{6,2},{10,6},{14,10},{7,3},{... | collective-permute-start | bytes 2949128 | tf_op jit(solution)/shard_map/ppermute | solution.py:21
  3.9 6.6 %collective-permute-start.2 = (bf16[48,10240]{1,0:T(8,128)(2,1)S(1)}, bf16[48,10240]{1,0:T(8,128)(2,1)}, u32[]{:S(2)}, u32[]{:S(2)}) collective-permute-start(bf16[48,10240]{1,0:T(8,128)(2,1)S(1)} %pad_maximum_fusion.refs_10_), channel_id=1, source_target_pairs={{0,4},{4,8},{8,12},{1,5},{5,9},{9,13},{2,6},{6,10},{10,14},{3,7},{... | collective-permute-start | bytes 2949128 | tf_op jit(solution)/shard_map/ppermute | solution.py:21
  10.5 18.9 %collective-permute-done.1.refs_11_ = bf16[48,10240]{1,0:T(8,128)(2,1)} collective-permute-done((bf16[48,10240]{1,0:T(8,128)(2,1)S(1)}, bf16[48,10240]{1,0:T(8,128)(2,1)}, u32[]{:S(2)}, u32[]{:S(2)}) %collective-permute-start.1) | collective-permute-done | bytes 983072 | tf_op jit(solution)/shard_map/ppermute | solution.py:21
  29.4 1.3 collective-permute-start.3
  30.7 5.5 %collective-permute-start.4 = (bf16[48,10240]{1,0:T(8,128)(2,1)}, bf16[48,10240]{1,0:T(8,128)(2,1)}, u32[]{:S(2)}, u32[]{:S(2)}) collective-permute-start(bf16[48,10240]{1,0:T(8,128)(2,1)} %collective-permute-done.2.refs_12_), channel_id=1, source_target_pairs={{0,4},{4,8},{8,12},{1,5},{5,9},{9,13},{2,6},{6,10},{10,14},{3,7},{... | collective-permute-start | bytes 2949128 | tf_op jit(solution)/shard_map/ppermute | solution.py:21
  36.2 0.4 reshape_squeeze.6
  36.7 0.2 reshape_squeeze.7
  37.0 0.9 pad_maximum_fusion.1
  38.0 4.0 %all-to-all-start = ((bf16[4,40,2560]{2,1,0:T(8,128)(2,1)}), bf16[4,40,2560]{2,1,0:T(8,128)(2,1)S(1)}, u32[]{:S(2)}, u32[]{:S(2)}) async-start(bf16[4,40,2560]{2,1,0:T(8,128)(2,1)} %pad_maximum_fusion.1), calls=%async_computation | async-start | bytes 1638400 | tf_op jit(solution)/shard_map/all_to_all | solution.py:191
  42.0 18.9 %shard_map.82 = (bf16[144,1536]{1,0:T(8,128)(2,1)S(1)}, bf16[144,1024]{1,0:T(8,128)(2,1)S(1)}) custom-call(bf16[1536,6144]{1,0:T(8,128)(2,1)} %bitcast.23, bf16[1536,6144]{1,0:T(8,128)(2,1)} %bitcast.24, bf16[1536,6144]{1,0:T(8,128)(2,1)} %bitcast.25, bf16[1536,6144]{1,0:T(8,128)(2,1)} %bitcast.26, bf16[1024,4096]{1,0:T(8,128)(2,1)} %bitcast.35, ...), custom_call_target="tpu_custom_call" | custom-call | flops 1 | bytes 1 | tf_op jit(solution)/shard_map/pallas_call | solution.py:80
  61.0 1.4 %broadcast_select_fusion.refs_10_ = bf16[48,10240]{1,0:T(8,128)(2,1)S(1)} fusion(bf16[48,10240]{1,0:T(8,128)(2,1)} %collective-permute-done.3, bf16[48,10240]{1,0:T(8,128)(2,1)} %collective-permute-done.4, pred[]{:T(512)S(6)} %lt.25), kind=kLoop, calls=%fused_computation.1 | loop fusion | flops 491520 | bytes 2949121 | tf_op jit(solution)/shard_map/jit(_where)/select_n | solution.py:154
  62.4 1.3 collective-permute-start.5
  63.7 9.3 %all-to-all-done = bf16[4,40,2560]{2,1,0:T(8,128)(2,1)S(1)} async-done(((bf16[4,40,2560]{2,1,0:T(8,128)(2,1)}), bf16[4,40,2560]{2,1,0:T(8,128)(2,1)S(1)}, u32[]{:S(2)}, u32[]{:S(2)}) %all-to-all-start) | async-done | bytes 819232 | tf_op jit(solution)/shard_map/all_to_all | solution.py:191
  72.9 1.5 %collective-permute-start = (bf16[160,2560]{1,0:T(8,128)(2,1)S(1)}, bf16[160,2560]{1,0:T(8,128)(2,1)S(1)}, u32[]{:S(2)}, u32[]{:S(2)}) collective-permute-start(bf16[160,2560]{1,0:T(8,128)(2,1)S(1)} %bitcast.21), channel_id=1, source_target_pairs={{0,16},{16,0},{1,17},{17,1},{2,18},{18,2},{3,19},{19,3},{4,20},{20... | collective-permute-start | bytes 2457608 | tf_op jit(solution)/shard_map/ppermute | solution.py:194
  74.5 18.1 %shard_map.83 = (bf16[48,1536]{1,0:T(8,128)(2,1)S(1)}, bf16[48,1024]{1,0:T(8,128)(2,1)S(1)}) custom-call(bf16[1536,6144]{1,0:T(8,128)(2,1)} %bitcast.27, bf16[1536,6144]{1,0:T(8,128)(2,1)} %bitcast.28, bf16[1536,6144]{1,0:T(8,128)(2,1)} %bitcast.29, bf16[1536,6144]{1,0:T(8,128)(2,1)} %bitcast.30, bf16[1024,4096]{1,0:T(8,128)(2,1)} %bitcast.39, ...), custom_call_target="tpu_custom_call" | custom-call | flops 1 | bytes 1 | tf_op jit(solution)/shard_map/pallas_call | solution.py:80
  92.6 18.4 %shard_map.84 = (bf16[48,1536]{1,0:T(8,128)(2,1)S(1)}, bf16[48,1024]{1,0:T(8,128)(2,1)S(1)}) custom-call(bf16[1536,6144]{1,0:T(8,128)(2,1)} %bitcast.31, bf16[1536,6144]{1,0:T(8,128)(2,1)} %bitcast.32, bf16[1536,6144]{1,0:T(8,128)(2,1)} %bitcast.33, bf16[1536,6144]{1,0:T(8,128)(2,1)} %bitcast.34, bf16[1024,4096]{1,0:T(8,128)(2,1)} %bitcast.43, ...), custom_call_target="tpu_custom_call" | custom-call | flops 1 | bytes 1 | tf_op jit(solution)/shard_map/pallas_call | solution.py:80
  111.0 1.7 %shard_map.85 = bf16[4,2,2,40,192]{4,3,2,1,0:T(8,128)(2,1)} custom-call(bf16[160,2560]{1,0:T(8,128)(2,1)S(1)} %bitcast.22, bf16[160,2560]{1,0:T(8,128)(2,1)S(1)} %collective-permute-done.refs_1_, bf16[144,1536]{1,0:T(8,128)(2,1)S(1)} %get-tuple-element.20.refs_2_, bf16[144,1024]{1,0:T(8,128)(2,1)S(1)} %copy-done.2, ...), custom_call_target="tpu_custom_call" | custom-call | flops 1 | bytes 1 | tf_op jit(solution)/shard_map/pallas_call | solution.py:139
  112.7 5.8 %all-to-all-start.1 = ((bf16[4,2,2,40,192]{4,3,2,1,0:T(8,128)(2,1)}), bf16[4,2,2,40,192]{4,3,2,1,0:T(8,128)(2,1)S(1)}, u32[]{:S(2)}, u32[]{:S(2)}) async-start(bf16[4,2,2,40,192]{4,3,2,1,0:T(8,128)(2,1)} %shard_map.85), calls=%async_computation.1 | async-start | bytes 655360 | tf_op jit(solution)/shard_map/all_to_all | solution.py:213
  118.8 7.1 %all-to-all-done.1 = bf16[4,2,2,40,192]{4,3,2,1,0:T(8,128)(2,1)S(1)} async-done(((bf16[4,2,2,40,192]{4,3,2,1,0:T(8,128)(2,1)}), bf16[4,2,2,40,192]{4,3,2,1,0:T(8,128)(2,1)S(1)}, u32[]{:S(2)}, u32[]{:S(2)}) %all-to-all-start.1) | async-done | bytes 245792 | tf_op jit(solution)/shard_map/all_to_all | solution.py:213
  126.1 0.1 reduce_sum.38
  126.6 7.4 %all_to_all.15 = f32[8,5,12]{2,1,0:T(8,128)S(1)} all-to-all(f32[8,5,12]{2,1,0:T(8,128)S(1)} %reshape.28), channel_id=1, replica_groups=mesh['parts'=2,'rows'=4,'layer'=4] {'parts','layer'}, dimensions={0} | all-to-all | bytes 3840 | tf_op jit(solution)/shard_map/all_to_all | solution.py:231
  134.0 0.6 reduce_sum.39
  (37 shorter events, 1.1 us)
Async XLA Ops:
  0.0 1.3 copy-start
  1.3 34.9 %copy-start.5 = (bf16[1,40,6144]{2,1,0:T(8,128)(2,1)S(1)}, bf16[1,40,6144]{2,1,0:T(8,128)(2,1)}, u32[]{:S(2)}) copy-start(bf16[1,40,6144]{2,1,0:T(8,128)(2,1)} %param.10) | copy-start | bytes 1474564
  2.4 34.3 %copy-start.6 = (bf16[1,40,4096]{2,1,0:T(8,128)(2,1)S(1)}, bf16[1,40,4096]{2,1,0:T(8,128)(2,1)}, u32[]{:S(2)}) copy-start(bf16[1,40,4096]{2,1,0:T(8,128)(2,1)} %param.11) | copy-start | bytes 983044
  2.5 26.9 %collective-permute-start.1 = (bf16[48,10240]{1,0:T(8,128)(2,1)S(1)}, bf16[48,10240]{1,0:T(8,128)(2,1)}, u32[]{:S(2)}, u32[]{:S(2)}) collective-permute-start(bf16[48,10240]{1,0:T(8,128)(2,1)S(1)} %pad_maximum_fusion.refs_10_), channel_id=1, source_target_pairs={{4,0},{8,4},{12,8},{5,1},{9,5},{13,9},{6,2},{10,6},{14,10},{7,3},{... | collective-permute-start | bytes 2949128 | tf_op jit(solution)/shard_map/ppermute | solution.py:21
  3.9 26.8 %collective-permute-start.2 = (bf16[48,10240]{1,0:T(8,128)(2,1)S(1)}, bf16[48,10240]{1,0:T(8,128)(2,1)}, u32[]{:S(2)}, u32[]{:S(2)}) collective-permute-start(bf16[48,10240]{1,0:T(8,128)(2,1)S(1)} %pad_maximum_fusion.refs_10_), channel_id=1, source_target_pairs={{0,4},{4,8},{8,12},{1,5},{5,9},{9,13},{2,6},{6,10},{10,14},{3,7},{... | collective-permute-start | bytes 2949128 | tf_op jit(solution)/shard_map/ppermute | solution.py:21
  29.4 31.6 %collective-permute-start.3 = (bf16[48,10240]{1,0:T(8,128)(2,1)}, bf16[48,10240]{1,0:T(8,128)(2,1)}, u32[]{:S(2)}, u32[]{:S(2)}) collective-permute-start(bf16[48,10240]{1,0:T(8,128)(2,1)} %collective-permute-done.1.refs_11_), channel_id=1, source_target_pairs={{4,0},{8,4},{12,8},{5,1},{9,5},{13,9},{6,2},{10,6},{14,10},{7,3},{... | collective-permute-start | bytes 2949128 | tf_op jit(solution)/shard_map/ppermute | solution.py:21
  30.7 30.3 %collective-permute-start.4 = (bf16[48,10240]{1,0:T(8,128)(2,1)}, bf16[48,10240]{1,0:T(8,128)(2,1)}, u32[]{:S(2)}, u32[]{:S(2)}) collective-permute-start(bf16[48,10240]{1,0:T(8,128)(2,1)} %collective-permute-done.2.refs_12_), channel_id=1, source_target_pairs={{0,4},{4,8},{8,12},{1,5},{5,9},{9,13},{2,6},{6,10},{10,14},{3,7},{... | collective-permute-start | bytes 2949128 | tf_op jit(solution)/shard_map/ppermute | solution.py:21
  36.9 5.1 %copy-start.3 = (f32[1,1536]{1,0:T(1,128)S(1)}, f32[1,1536]{1,0:T(1,128)}, u32[]{:S(2)}) copy-start(f32[1,1536]{1,0:T(1,128)} %refs_8_.5) | copy-start | bytes 18436
  36.9 5.1 %copy-start.4 = (f32[1,1024]{1,0:T(1,128)S(1)}, f32[1,1024]{1,0:T(1,128)}, u32[]{:S(2)}) copy-start(f32[1,1024]{1,0:T(1,128)} %refs_9_.5) | copy-start | bytes 12292
  38.0 35.0 %all-to-all-start = ((bf16[4,40,2560]{2,1,0:T(8,128)(2,1)}), bf16[4,40,2560]{2,1,0:T(8,128)(2,1)S(1)}, u32[]{:S(2)}, u32[]{:S(2)}) async-start(bf16[4,40,2560]{2,1,0:T(8,128)(2,1)} %pad_maximum_fusion.1), calls=%async_computation | async-start | bytes 1638400 | tf_op jit(solution)/shard_map/all_to_all | solution.py:191
  60.9 1.4 %copy-start.1 = (bf16[144,1024]{1,0:T(8,128)(2,1)}, bf16[144,1024]{1,0:T(8,128)(2,1)S(1)}, u32[]{:S(2)}) copy-start(bf16[144,1024]{1,0:T(8,128)(2,1)S(1)} %get-tuple-element.21.refs_3_) | copy-start | bytes 884740
  62.4 30.2 %collective-permute-start.5 = (bf16[48,10240]{1,0:T(8,128)(2,1)S(1)}, bf16[48,10240]{1,0:T(8,128)(2,1)}, u32[]{:S(2)}, u32[]{:S(2)}) collective-permute-start(bf16[48,10240]{1,0:T(8,128)(2,1)S(1)} %broadcast_select_fusion.refs_10_), channel_id=1, source_target_pairs={{4,0},{8,12},{5,1},{9,13},{6,2},{10,14},{7,3},{11,15},{20,16},{24,... | collective-permute-start | bytes 2949128 | tf_op jit(solution)/shard_map/ppermute | solution.py:155
  72.9 38.1 %collective-permute-start = (bf16[160,2560]{1,0:T(8,128)(2,1)S(1)}, bf16[160,2560]{1,0:T(8,128)(2,1)S(1)}, u32[]{:S(2)}, u32[]{:S(2)}) collective-permute-start(bf16[160,2560]{1,0:T(8,128)(2,1)S(1)} %bitcast.21), channel_id=1, source_target_pairs={{0,16},{16,0},{1,17},{17,1},{2,18},{18,2},{3,19},{19,3},{4,20},{20... | collective-permute-start | bytes 2457608 | tf_op jit(solution)/shard_map/ppermute | solution.py:194
  92.6 18.4 %copy-start.2 = (bf16[144,1024]{1,0:T(8,128)(2,1)S(1)}, bf16[144,1024]{1,0:T(8,128)(2,1)}, u32[]{:S(2)}) copy-start(bf16[144,1024]{1,0:T(8,128)(2,1)} %copy-done.1) | copy-start | bytes 884740
  112.7 13.1 %all-to-all-start.1 = ((bf16[4,2,2,40,192]{4,3,2,1,0:T(8,128)(2,1)}), bf16[4,2,2,40,192]{4,3,2,1,0:T(8,128)(2,1)S(1)}, u32[]{:S(2)}, u32[]{:S(2)}) async-start(bf16[4,2,2,40,192]{4,3,2,1,0:T(8,128)(2,1)} %shard_map.85), calls=%async_computation.1 | async-start | bytes 655360 | tf_op jit(solution)/shard_map/all_to_all | solution.py:213

commit v5 on v4

v5 whole, which is shorter than its diff:
```python
import jax
import jax.numpy as jnp
from jax import lax
from jax.experimental import pallas as pl
from jax.experimental.pallas import tpu as pltpu
from jax.sharding import PartitionSpec as P

RANK = 8


damping = 0.1

VMEM_LIMIT = 16 * 1024 * 1024
TILE = 256


def along(value, by):
    size = lax.axis_size("rows")
    return lax.ppermute(value, "rows", [(i, i + by) for i in range(size) if 0 <= i + by < size])


def rotate(bases, eigens, queries, keep=False, kept=False):
    columns = queries[0].shape[0]
    held = columns * len(queries)
    count = len(queries)

    def kernel(*refs):
        basis_refs, eigen_refs, query_refs = refs[:2], refs[2:4], refs[4 : 4 + count]
        out_refs = refs[4 + count : 6 + count]
        here_refs = basis_refs if kept else refs[6 + count : 8 + count]
        query, *semaphores = refs[6 + count if kept else 8 + count :]
        tiles = [(side, tile) for side in range(2) for tile in range(basis_refs[side].shape[0] // TILE)]
        copies = []
        if not kept:
            for at, (side, tile) in enumerate(tiles):
                where = slice(tile * TILE, (tile + 1) * TILE)
                copies.append(
                    pltpu.make_async_copy(basis_refs[side].at[where], here_refs[side].at[where], semaphores[0].at[at])
                )
                copies[-1].start()
        for place, ref in enumerate(query_refs):
            query[place * columns : (place + 1) * columns, :] = ref[...]
        begins = (0, basis_refs[0].shape[1], query.shape[1])
        for at, (side, tile) in enumerate(tiles):
            where = slice(tile * TILE, (tile + 1) * TILE)
            if not kept:
                copies[at].wait()
            rotated = lax.dot_general(
                here_refs[side][where, :],
                query[:, begins[side] : begins[side + 1]],
                (((1,), (1,)), ((), ())),
                preferred_element_type=jnp.float32,
            )
            scale = 1.0 / (eigen_refs[side][where, :] + damping)
            out_refs[side][where, :] = (rotated * scale).astype(jnp.bfloat16)

    constrain = pltpu.with_memory_space_constraint
    in_vmem = pl.BlockSpec(memory_space=pltpu.VMEM)
    here = [pltpu.VMEM(basis.shape, basis.dtype) for basis in bases]
    copies = sum(basis.shape[0] for basis in bases) // TILE
    return pl.pallas_call(
        kernel,
        in_specs=[in_vmem if kept else pl.BlockSpec(memory_space=pltpu.HBM)] * 2 + [in_vmem] * (2 + count),
        out_specs=[in_vmem] * (4 if keep else 2),
        out_shape=[jax.ShapeDtypeStruct((basis.shape[0], held), jnp.bfloat16) for basis in bases]
        + (here if keep else []),
        scratch_shapes=([] if keep or kept else here)
        + [pltpu.VMEM((held, sum(basis.shape[1] for basis in bases)), jnp.bfloat16)]
        + ([] if kept else [pltpu.SemaphoreType.DMA((copies,))]),
        compiler_params=pltpu.CompilerParams(
            vmem_limit_bytes=VMEM_LIMIT if keep or kept else VMEM_LIMIT + 28 * 1024 * 1024
        ),
        cost_estimate=pl.CostEstimate(flops=1, bytes_accessed=1, transcendentals=0),
    )(
        *[constrain(basis, pltpu.VMEM if kept else pltpu.HBM) for basis in bases],
        *[constrain(one, pltpu.VMEM) for one in (*eigens, *queries)],
    )


def grams(stores, near, two, three, rows):
    shares = [side.shape[0] for side in near]
    columns = two[0].shape[1]
    held = stores[0].shape[0] // rows
    count = len(stores)

    def kernel(*refs):
        store_refs, out_ref = refs[:count], refs[count + 6]
        row = lax.axis_index("rows")
        for side in range(2):
            near_ref, two_ref, three_ref = refs[count + side : count + 6 : 2]
            begin = side * shares[0]
            for j, store_ref in enumerate(store_refs):
                store = store_ref[:, begin : begin + shares[side]]
                close, far, last = (
                    jnp.dot(store, ref[...], preferred_element_type=jnp.float32)
                    for ref in (near_ref, two_ref, three_ref)
                )
                own, after, before = (close[:, p * columns : (p + 1) * columns] for p in range(3))
                after = jnp.where(row == 3, last, after)
                before = jnp.where(row == 0, last, before)
                ring = [own, after, far, before]
                blocks = []
                for c in range(rows):
                    block = ring[c]
                    for r in range(1, rows):
                        block = jnp.where(row == r, ring[(c - r) % rows], block)
                    blocks.append(block)
                gram = jnp.concatenate(blocks, axis=1).astype(jnp.bfloat16)
                for owner in range(rows):
                    out_ref[owner, side, j] = gram[owner * held : (owner + 1) * held]

    return pl.pallas_call(
        kernel,
        out_shape=jax.ShapeDtypeStruct((rows, 2, count, held, columns * rows), jnp.bfloat16),
        compiler_params=pltpu.CompilerParams(vmem_limit_bytes=VMEM_LIMIT),
        cost_estimate=pl.CostEstimate(flops=1, bytes_accessed=1, transcendentals=0),
    )(*stores, *near, *two, *three)


def along_four(query, bases, eigens, stores):
    row = lax.axis_index("rows")
    eigens = [eigen.reshape(-1, 1) for eigen in eigens]
    after, before = along(query, -1), along(query, 1)
    after_two, before_two = along(after, -1), along(before, 1)
    near = rotate(bases, eigens, [query, after, before])
    near, after_two, before_two = lax.optimization_barrier((near, after_two, before_two))
    two = jnp.where(row < 2, after_two, before_two)
    three = lax.ppermute(two, "rows", [(1, 0), (2, 3)])
    *two, hidden_here, model_here = rotate(bases, eigens, [two], keep=True)
    two, three = lax.optimization_barrier((two, three))
    return grams(stores, near, two, rotate([hidden_here, model_here], eigens, [three], kept=True), 4)


def per_device(
    query_hidden,
    query_model,
    train_hidden,
    train_model,
    hidden_basis,
    model_basis,
    hidden_eigen,
    model_eigen,
):
    rows = lax.axis_size("rows")
    parts = lax.axis_size("parts")
    layers = lax.axis_size("layer")
    part = lax.axis_index("parts")
    held = train_hidden.shape[1]
    columns = query_hidden.shape[1] // parts
    queries = query_hidden.shape[1] * rows // RANK
    bases = [hidden_basis[0], model_basis[0]]
    eigens = [hidden_eigen, model_eigen]
    share = bases[0].shape[0]
    width = bases[0].shape[1]

    query = jnp.concatenate(
        [lax.dynamic_slice_in_dim(side[0], part * columns, columns, 0) for side in (query_hidden, query_model)],
        axis=1,
    )

    by_owner = jnp.concatenate(
        [side[0].reshape(held, rows, -1).transpose(1, 0, 2) for side in (train_hidden, train_model)], axis=2
    )
    store = lax.all_to_all(by_owner, "rows", 0, 0, tiled=True).reshape(rows * held, -1)
    stores = [store]
    for j in range(1, parts):
        stores.append(lax.ppermute(store, "parts", [(i, (i + j) % parts) for i in range(parts)]))

    if rows == 4:
        partial = along_four(query, bases, eigens, stores)
    else:
        every = lax.all_gather(query, "rows", axis=0, tiled=True)
        sides = []
        for basis, eigen, gathered, begin in zip(bases, eigens, (every[:, :width], every[:, width:]), (0, share)):
            rotated = jnp.einsum("eh,qh->eq", basis, gathered, preferred_element_type=jnp.float32)
            scaled = (rotated * (1.0 / (eigen[0] + damping))[:, None]).astype(jnp.bfloat16)
            sides.append(
                [
                    jnp.dot(one[:, begin : begin + basis.shape[0]], scaled, preferred_element_type=jnp.float32)
                    for one in stores
                ]
            )
        partial = jnp.array(sides).astype(jnp.bfloat16)
        partial = partial.reshape(2, parts, rows, held, rows * columns).transpose(2, 0, 1, 3, 4)

    received = lax.all_to_all(partial, "rows", 0, 0, tiled=True)
    total = received.astype(jnp.float32).sum(axis=0)
    product = total[0] * total[1]
    examples = held // RANK
    by_column = product.reshape(parts, examples, RANK, rows * columns).sum(axis=2)
    if columns % RANK == 0:
        by_query = by_column.reshape(parts, examples, rows, 1, columns // RANK, RANK).sum(axis=-1)
        mine = lax.broadcasted_iota(jnp.int32, (1, 1, 1, parts, 1), 3) == part
        scores = jnp.where(mine, by_query, 0.0).reshape(parts, examples, queries)
    else:
        place = jnp.arange(rows * columns)
        place = (place // columns) * (columns * parts) + part * columns + place % columns
        pick = (place[:, None] // RANK == jnp.arange(queries)[None, :]).astype(jnp.float32)
        scores = jnp.einsum("pic,cq->piq", by_column, pick, precision=lax.Precision.HIGHEST)

    scores = jnp.stack([lax.dynamic_index_in_dim(scores, (part - j) % parts, 0, False) for j in range(parts)])
    scores = scores.reshape(parts, examples, layers, queries // layers).transpose(0, 2, 1, 3)
    scores = scores.reshape(parts * layers, examples, queries // layers)
    return lax.all_to_all(scores, ("parts", "layer"), 0, 0, tiled=True).sum(axis=0)


def solution(mesh):
    placed = (
        P("layer", "rows", None),
        P("layer", "rows", None),
        P("layer", ("parts", "rows"), None),
        P("layer", ("parts", "rows"), None),
        P("layer", "rows", None),
        P("layer", "rows", None),
        P("layer", "rows"),
        P("layer", "rows"),
    )
    return jax.shard_map(
        per_device,
        mesh=mesh,
        in_specs=placed,
        out_specs=P(("parts", "rows"), "layer"),
        check_vma=False,
    )
```

time: 136 us -> 129 us (0.949)
  Pallas kernels: 57.2 us -> 49.7 us
  waiting for transfers between devices: 35.3 us -> 32.2 us
  local copies, waits for them, and re-layouts: 3.63 us -> 6.09 us
    pallas_call x3, Pallas kernels: 55.4 us -> 46.2 us  [rotate(): pl.pallas_call(kernel, in_specs=[in_vmem if kept else pl.BlockSpec(memory...]
    all_to_all x1, waiting for transfers between devices: 9.25 us -> 6.09 us  [per_device(): lax.all_to_all(by_owner, 'rows', 0, 0, tiled=True).reshape(rows * held, -1)]
    unnamed x14 -> x24, local copies, waits for them, and re-layouts: 1.3 us -> 3.25 us
    pallas_call x1, Pallas kernels: 1.72 us -> 3.49 us  [grams(): pl.pallas_call(kernel, out_shape=jax.ShapeDtypeStruct((rows, 2, count, he...]
  transfers between devices with their start and end apart: 8 -> 8, of which waited for: 3 -> 3; matrix products, arithmetic and copies ran while one was open for 2% -> 4% of each run, Pallas kernels for 41% -> 36%
where the time goes in v5:
time: 129 us; the launch traced here: 128 us
  Pallas kernels  49.7 us (39%)
  waiting for transfers between devices  32.2 us (25%)
  starting transfers between devices  27.8 us (22%)
  blocking collectives  7.41 us (6%)
  local copies, waits for them, and re-layouts  6.09 us (5%)
  other arithmetic  4.52 us (4%)
    pallas_call x3, Pallas kernels, rotate(): pl.pallas_call(kernel, in_specs=[in_vmem if kept else pl.BlockSpec(memory...  46.2 us
    ppermute x4, waiting for transfers between devices, along(): lax.ppermute(value, 'rows', [(i, i + by) for i in range(size) if 0 <= i +...  19 us
    ppermute x4, starting transfers between devices, along(): lax.ppermute(value, 'rows', [(i, i + by) for i in range(size) if 0 <= i +...  14.8 us
    all_to_all x1, blocking collectives, per_device(): lax.all_to_all(scores, ('parts', 'layer'), 0, 0, tiled=True).sum(axis=0)  7.41 us
    all_to_all x1, waiting for transfers between devices, per_device(): received = lax.all_to_all(partial, 'rows', 0, 0, tiled=True)  7.13 us
    all_to_all x1, waiting for transfers between devices, per_device(): lax.all_to_all(by_owner, 'rows', 0, 0, tiled=True).reshape(rows * held, -1)  6.09 us
    all_to_all x1, starting transfers between devices, per_device(): received = lax.all_to_all(partial, 'rows', 0, 0, tiled=True)  5.84 us
    all_to_all x1, starting transfers between devices, per_device(): lax.all_to_all(by_owner, 'rows', 0, 0, tiled=True).reshape(rows * held, -1)  4.19 us
  transfers between devices with their start and end apart: 8, of which 3 were waited for; matrix products, arithmetic and copies ran while one was open for 4% of the time, Pallas kernels for 36%

profile of v5, /device:TPU:0, one launch (start us, length us, event | category | flops | bytes accessed | tf_op | source)
XLA Modules:
  0.0 128.0 jit_solution(9900808772265979617)
XLA Ops:
  0.0 1.3 copy-done
  1.3 1.1 dynamic-slice_bitcast_fusion.1
  2.5 1.4 %collective-permute-start.1 = (bf16[48,10240]{1,0:T(8,128)(2,1)S(1)}, bf16[48,10240]{1,0:T(8,128)(2,1)}, u32[]{:S(2)}, u32[]{:S(2)}) collective-permute-start(bf16[48,10240]{1,0:T(8,128)(2,1)S(1)} %pad_maximum_fusion.refs_4_), channel_id=1, source_target_pairs={{4,0},{8,4},{12,8},{5,1},{9,5},{13,9},{6,2},{10,6},{14,10},{7,3},{... | collective-permute-start | bytes 2949128 | tf_op jit(solution)/shard_map/ppermute | solution.py:19
  3.9 6.5 %collective-permute-start.2 = (bf16[48,10240]{1,0:T(8,128)(2,1)S(1)}, bf16[48,10240]{1,0:T(8,128)(2,1)}, u32[]{:S(2)}, u32[]{:S(2)}) collective-permute-start(bf16[48,10240]{1,0:T(8,128)(2,1)S(1)} %pad_maximum_fusion.refs_4_), channel_id=1, source_target_pairs={{0,4},{4,8},{8,12},{1,5},{5,9},{9,13},{2,6},{6,10},{10,14},{3,7},{... | collective-permute-start | bytes 2949128 | tf_op jit(solution)/shard_map/ppermute | solution.py:19
  10.4 19.0 %collective-permute-done.1.refs_5_ = bf16[48,10240]{1,0:T(8,128)(2,1)} collective-permute-done((bf16[48,10240]{1,0:T(8,128)(2,1)S(1)}, bf16[48,10240]{1,0:T(8,128)(2,1)}, u32[]{:S(2)}, u32[]{:S(2)}) %collective-permute-start.1) | collective-permute-done | bytes 983072 | tf_op jit(solution)/shard_map/ppermute | solution.py:19
  29.4 1.3 %collective-permute-start.3 = (bf16[48,10240]{1,0:T(8,128)(2,1)}, bf16[48,10240]{1,0:T(8,128)(2,1)}, u32[]{:S(2)}, u32[]{:S(2)}) collective-permute-start(bf16[48,10240]{1,0:T(8,128)(2,1)} %collective-permute-done.1.refs_5_), channel_id=1, source_target_pairs={{4,0},{8,4},{12,8},{5,1},{9,5},{13,9},{6,2},{10,6},{14,10},{7,3},{... | collective-permute-start | bytes 2949128 | tf_op jit(solution)/shard_map/ppermute | solution.py:19
  30.7 5.6 %collective-permute-start.4 = (bf16[48,10240]{1,0:T(8,128)(2,1)}, bf16[48,10240]{1,0:T(8,128)(2,1)}, u32[]{:S(2)}, u32[]{:S(2)}) collective-permute-start(bf16[48,10240]{1,0:T(8,128)(2,1)} %collective-permute-done.2.refs_6_), channel_id=1, source_target_pairs={{0,4},{4,8},{8,12},{1,5},{5,9},{9,13},{2,6},{6,10},{10,14},{3,7},{... | collective-permute-start | bytes 2949128 | tf_op jit(solution)/shard_map/ppermute | solution.py:19
  36.3 0.4 reshape_squeeze.6
  37.1 1.0 pad_maximum_fusion.1
  38.1 4.2 %all-to-all-start = ((bf16[4,40,2560]{2,1,0:T(8,128)(2,1)}), bf16[4,40,2560]{2,1,0:T(8,128)(2,1)}, u32[]{:S(2)}, u32[]{:S(2)}) async-start(bf16[4,40,2560]{2,1,0:T(8,128)(2,1)} %pad_maximum_fusion.1), calls=%async_computation | async-start | bytes 1638400 | tf_op jit(solution)/shard_map/all_to_all | solution.py:164
  42.8 19.3 %shard_map.82 = (bf16[1536,144]{1,0:T(8,128)(2,1)S(1)}, bf16[1024,144]{1,0:T(8,128)(2,1)S(1)}) custom-call(bf16[1536,6144]{1,0:T(8,128)(2,1)} %bitcast.23, bf16[1024,4096]{1,0:T(8,128)(2,1)} %bitcast.25, f32[1536,1]{1,0:T(8,128)S(1)} %copy.22.refs_2_, f32[1024,1]{1,0:T(8,128)S(1)} %copy.23.refs_3_, bf16[48,10240]{1,0:T(8,128)(2,1)S(1)} %pad_maximum_fusion.refs_4_, ...), custom_call_target="tpu_custom_call" | custom-call | flops 1 | bytes 1 | tf_op jit(solution)/shard_map/pallas_call | solution.py:61
  62.1 0.9 copy-done.4
  63.0 2.5 %broadcast_select_fusion.refs_4_ = bf16[48,10240]{1,0:T(8,128)(2,1)} fusion(bf16[48,10240]{1,0:T(8,128)(2,1)} %collective-permute-done.3, bf16[48,10240]{1,0:T(8,128)(2,1)} %collective-permute-done.4, pred[]{:T(512)S(6)} %lt.25), kind=kLoop, calls=%fused_computation.1 | loop fusion | flops 491520 | bytes 2949121 | tf_op jit(solution)/shard_map/jit(_where)/select_n | solution.py:127
  65.5 1.5 %collective-permute-start.5 = (bf16[48,10240]{1,0:T(8,128)(2,1)}, bf16[48,10240]{1,0:T(8,128)(2,1)}, u32[]{:S(2)}, u32[]{:S(2)}) collective-permute-start(bf16[48,10240]{1,0:T(8,128)(2,1)} %broadcast_select_fusion.refs_4_), channel_id=1, source_target_pairs={{4,0},{8,12},{5,1},{9,13},{6,2},{10,14},{7,3},{11,15},{20,16},{24,... | collective-permute-start | bytes 2949128 | tf_op jit(solution)/shard_map/ppermute | solution.py:128
  67.0 6.1 %all-to-all-done = bf16[4,40,2560]{2,1,0:T(8,128)(2,1)} async-done(((bf16[4,40,2560]{2,1,0:T(8,128)(2,1)}), bf16[4,40,2560]{2,1,0:T(8,128)(2,1)}, u32[]{:S(2)}, u32[]{:S(2)}) %all-to-all-start) | async-done | bytes 819232 | tf_op jit(solution)/shard_map/all_to_all | solution.py:164
  73.1 1.5 %collective-permute-start = (bf16[160,2560]{1,0:T(8,128)(2,1)}, bf16[160,2560]{1,0:T(8,128)(2,1)S(1)}, u32[]{:S(2)}, u32[]{:S(2)}) collective-permute-start(bf16[160,2560]{1,0:T(8,128)(2,1)} %bitcast.2.refs_0_), channel_id=1, source_target_pairs={{0,16},{16,0},{1,17},{17,1},{2,18},{18,2},{3,19},{19,3},{4,20},{20... | collective-permute-start | bytes 2457608 | tf_op jit(solution)/shard_map/ppermute | solution.py:167
  74.6 1.0 copy-done.3
  75.6 18.5 %shard_map.83 = (bf16[1536,48]{1,0:T(8,128)(2,1)S(1)}, bf16[1024,48]{1,0:T(8,128)(2,1)S(1)}, bf16[1536,6144]{1,0:T(8,128)(2,1)S(1)}, bf16[1024,4096]{1,0:T(8,128)(2,1)S(1)}) custom-call(bf16[1536,6144]{1,0:T(8,128)(2,1)} %bitcast.24, bf16[1024,4096]{1,0:T(8,128)(2,1)} %bitcast.26, f32[1536,1]{1,0:T(8,128)S(1)} %copy.22.refs_2_, f32[1024,1]{1,0:T(8,128)S(1)} %copy-done.3, ...), custom_call_target="tpu_custom_call" | custom-call | flops 1 | bytes 1 | tf_op jit(solution)/shard_map/pallas_call | solution.py:61
  94.1 8.5 %shard_map.84 = (bf16[1536,48]{1,0:T(8,128)(2,1)S(1)}, bf16[1024,48]{1,0:T(8,128)(2,1)S(1)}) custom-call(bf16[1536,6144]{1,0:T(8,128)(2,1)S(1)} %get-tuple-element.30.refs_0_, bf16[1024,4096]{1,0:T(8,128)(2,1)S(1)} %get-tuple-element.31.refs_1_, f32[1536,1]{1,0:T(8,128)S(1)} %copy.22.refs_2_, f32[1024,1]{1,0:T(8,128)S(1)} %copy-done.3, ...), custom_call_target="tpu_custom_call" | custom-call | flops 1 | bytes 1 | tf_op jit(solution)/shard_map/pallas_call | solution.py:61
  102.6 3.5 %shard_map.85 = bf16[4,2,2,40,192]{4,3,2,1,0:T(8,128)(2,1)} custom-call(bf16[160,2560]{1,0:T(8,128)(2,1)} %bitcast.2.refs_0_, bf16[160,2560]{1,0:T(8,128)(2,1)S(1)} %collective-permute-done.refs_1_, bf16[1536,144]{1,0:T(8,128)(2,1)S(1)} %copy-done.5, bf16[1024,144]{1,0:T(8,128)(2,1)S(1)} %copy-done.7, bf16[1536,48]{1,0:T(8,128)(2,1)S(1)} %get-tuple-element.28.refs_4_, ...), custom_call_target="tpu_custom_call" | custom-call | flops 1 | bytes 1 | tf_op jit(solution)/shard_map/pallas_call | solution.py:112
  106.1 5.8 %all-to-all-start.1 = ((bf16[4,2,2,40,192]{4,3,2,1,0:T(8,128)(2,1)}), bf16[4,2,2,40,192]{4,3,2,1,0:T(8,128)(2,1)S(1)}, u32[]{:S(2)}, u32[]{:S(2)}) async-start(bf16[4,2,2,40,192]{4,3,2,1,0:T(8,128)(2,1)} %shard_map.85), calls=%async_computation.1 | async-start | bytes 655360 | tf_op jit(solution)/shard_map/all_to_all | solution.py:186
  112.1 7.1 %all-to-all-done.1 = bf16[4,2,2,40,192]{4,3,2,1,0:T(8,128)(2,1)S(1)} async-done(((bf16[4,2,2,40,192]{4,3,2,1,0:T(8,128)(2,1)}), bf16[4,2,2,40,192]{4,3,2,1,0:T(8,128)(2,1)S(1)}, u32[]{:S(2)}, u32[]{:S(2)}) %all-to-all-start.1) | async-done | bytes 245792 | tf_op jit(solution)/shard_map/all_to_all | solution.py:186
  120.0 7.4 %all_to_all.15 = f32[8,5,12]{2,1,0:T(8,128)S(1)} all-to-all(f32[8,5,12]{2,1,0:T(8,128)S(1)} %reshape.36), channel_id=1, replica_groups=mesh['parts'=2,'rows'=4,'layer'=4] {'parts','layer'}, dimensions={0} | all-to-all | bytes 3840 | tf_op jit(solution)/shard_map/all_to_all | solution.py:204
  127.4 0.6 reduce_sum.39
  (49 shorter events, 1.9 us)
Async XLA Ops:
  0.0 1.3 copy-start
  1.3 35.0 %copy-start.8 = (bf16[1,40,6144]{2,1,0:T(8,128)(2,1)S(1)}, bf16[1,40,6144]{2,1,0:T(8,128)(2,1)}, u32[]{:S(2)}) copy-start(bf16[1,40,6144]{2,1,0:T(8,128)(2,1)} %param.10) | copy-start | bytes 1474564
  2.4 34.3 %copy-start.9 = (bf16[1,40,4096]{2,1,0:T(8,128)(2,1)S(1)}, bf16[1,40,4096]{2,1,0:T(8,128)(2,1)}, u32[]{:S(2)}) copy-start(bf16[1,40,4096]{2,1,0:T(8,128)(2,1)} %param.11) | copy-start | bytes 983044
  2.5 26.9 %collective-permute-start.1 = (bf16[48,10240]{1,0:T(8,128)(2,1)S(1)}, bf16[48,10240]{1,0:T(8,128)(2,1)}, u32[]{:S(2)}, u32[]{:S(2)}) collective-permute-start(bf16[48,10240]{1,0:T(8,128)(2,1)S(1)} %pad_maximum_fusion.refs_4_), channel_id=1, source_target_pairs={{4,0},{8,4},{12,8},{5,1},{9,5},{13,9},{6,2},{10,6},{14,10},{7,3},{... | collective-permute-start | bytes 2949128 | tf_op jit(solution)/shard_map/ppermute | solution.py:19
  3.9 26.8 %collective-permute-start.2 = (bf16[48,10240]{1,0:T(8,128)(2,1)S(1)}, bf16[48,10240]{1,0:T(8,128)(2,1)}, u32[]{:S(2)}, u32[]{:S(2)}) collective-permute-start(bf16[48,10240]{1,0:T(8,128)(2,1)S(1)} %pad_maximum_fusion.refs_4_), channel_id=1, source_target_pairs={{0,4},{4,8},{8,12},{1,5},{5,9},{9,13},{2,6},{6,10},{10,14},{3,7},{... | collective-permute-start | bytes 2949128 | tf_op jit(solution)/shard_map/ppermute | solution.py:19
  29.4 33.6 %collective-permute-start.3 = (bf16[48,10240]{1,0:T(8,128)(2,1)}, bf16[48,10240]{1,0:T(8,128)(2,1)}, u32[]{:S(2)}, u32[]{:S(2)}) collective-permute-start(bf16[48,10240]{1,0:T(8,128)(2,1)} %collective-permute-done.1.refs_5_), channel_id=1, source_target_pairs={{4,0},{8,4},{12,8},{5,1},{9,5},{13,9},{6,2},{10,6},{14,10},{7,3},{... | collective-permute-start | bytes 2949128 | tf_op jit(solution)/shard_map/ppermute | solution.py:19
  30.7 32.3 %collective-permute-start.4 = (bf16[48,10240]{1,0:T(8,128)(2,1)}, bf16[48,10240]{1,0:T(8,128)(2,1)}, u32[]{:S(2)}, u32[]{:S(2)}) collective-permute-start(bf16[48,10240]{1,0:T(8,128)(2,1)} %collective-permute-done.2.refs_6_), channel_id=1, source_target_pairs={{0,4},{4,8},{8,12},{1,5},{5,9},{9,13},{2,6},{6,10},{10,14},{3,7},{... | collective-permute-start | bytes 2949128 | tf_op jit(solution)/shard_map/ppermute | solution.py:19
  36.9 5.3 %copy-start.10 = (f32[1,1536]{1,0:T(1,128)S(1)}, f32[1,1536]{1,0:T(1,128)}, u32[]{:S(2)}) copy-start(f32[1,1536]{1,0:T(1,128)} %param.14) | copy-start | bytes 18436
  37.1 5.5 %copy-start.11 = (f32[1,1024]{1,0:T(1,128)S(1)}, f32[1,1024]{1,0:T(1,128)}, u32[]{:S(2)}) copy-start(f32[1,1024]{1,0:T(1,128)} %param.15) | copy-start | bytes 12292
  38.1 35.0 %all-to-all-start = ((bf16[4,40,2560]{2,1,0:T(8,128)(2,1)}), bf16[4,40,2560]{2,1,0:T(8,128)(2,1)}, u32[]{:S(2)}, u32[]{:S(2)}) async-start(bf16[4,40,2560]{2,1,0:T(8,128)(2,1)} %pad_maximum_fusion.1), calls=%async_computation | async-start | bytes 1638400 | tf_op jit(solution)/shard_map/all_to_all | solution.py:164
  42.8 19.3 %copy-start.2 = (f32[1024,1]{1,0:T(8,128)}, f32[1024,1]{1,0:T(8,128)S(1)}, u32[]{:S(2)}) copy-start(f32[1024,1]{1,0:T(8,128)S(1)} %copy.23.refs_3_) | copy-start | bytes 12292
  62.1 0.9 copy-start.4
  63.0 10.0 %copy-start.6 = (bf16[1024,144]{1,0:T(8,128)(2,1)}, bf16[1024,144]{1,0:T(8,128)(2,1)S(1)}, u32[]{:S(2)}) copy-start(bf16[1024,144]{1,0:T(8,128)(2,1)S(1)} %get-tuple-element.23.refs_3_) | copy-start | bytes 884740
  65.5 28.6 %collective-permute-start.5 = (bf16[48,10240]{1,0:T(8,128)(2,1)}, bf16[48,10240]{1,0:T(8,128)(2,1)}, u32[]{:S(2)}, u32[]{:S(2)}) collective-permute-start(bf16[48,10240]{1,0:T(8,128)(2,1)} %broadcast_select_fusion.refs_4_), channel_id=1, source_target_pairs={{4,0},{8,12},{5,1},{9,13},{6,2},{10,14},{7,3},{11,15},{20,16},{24,... | collective-permute-start | bytes 2949128 | tf_op jit(solution)/shard_map/ppermute | solution.py:128
  73.1 29.5 %collective-permute-start = (bf16[160,2560]{1,0:T(8,128)(2,1)}, bf16[160,2560]{1,0:T(8,128)(2,1)S(1)}, u32[]{:S(2)}, u32[]{:S(2)}) collective-permute-start(bf16[160,2560]{1,0:T(8,128)(2,1)} %bitcast.2.refs_0_), channel_id=1, source_target_pairs={{0,16},{16,0},{1,17},{17,1},{2,18},{18,2},{3,19},{19,3},{4,20},{20... | collective-permute-start | bytes 2457608 | tf_op jit(solution)/shard_map/ppermute | solution.py:167
  74.6 1.0 copy-start.3
  94.1 8.5 %copy-start.5 = (bf16[1536,144]{1,0:T(8,128)(2,1)S(1)}, bf16[1536,144]{1,0:T(8,128)(2,1)}, u32[]{:S(2)}) copy-start(bf16[1536,144]{1,0:T(8,128)(2,1)} %copy-done.4) | copy-start | bytes 1327108
  94.1 8.5 %copy-start.7 = (bf16[1024,144]{1,0:T(8,128)(2,1)S(1)}, bf16[1024,144]{1,0:T(8,128)(2,1)}, u32[]{:S(2)}) copy-start(bf16[1024,144]{1,0:T(8,128)(2,1)} %copy-done.6) | copy-start | bytes 884740
  102.6 25.4 %copy-start.1 = (bf16[1,96,6144]{2,1,0:T(8,128)(2,1)S(1)}, bf16[1,96,6144]{2,1,0:T(8,128)(2,1)}, u32[]{:S(2)}) copy-start(bf16[1,96,6144]{2,1,0:T(8,128)(2,1)} %param.8) | copy-start | bytes 3538948
  106.1 13.1 %all-to-all-start.1 = ((bf16[4,2,2,40,192]{4,3,2,1,0:T(8,128)(2,1)}), bf16[4,2,2,40,192]{4,3,2,1,0:T(8,128)(2,1)S(1)}, u32[]{:S(2)}, u32[]{:S(2)}) async-start(bf16[4,2,2,40,192]{4,3,2,1,0:T(8,128)(2,1)} %shard_map.85), calls=%async_computation.1 | async-start | bytes 655360 | tf_op jit(solution)/shard_map/all_to_all | solution.py:186

commit v6 on v5

v6 whole, which is shorter than its diff:
```python
import jax
import jax.numpy as jnp
from jax import lax
from jax.experimental import pallas as pl
from jax.experimental.pallas import tpu as pltpu
from jax.sharding import PartitionSpec as P

RANK = 8


damping = 0.1

VMEM_LIMIT = 16 * 1024 * 1024
TILE = 256


def along(value, by):
    size = lax.axis_size("rows")
    return lax.ppermute(value, "rows", [(i, i + by) for i in range(size) if 0 <= i + by < size])


def rotate(bases, eigens, queries, keep=False, kept=False):
    columns = queries[0].shape[0]
    held = columns * len(queries)
    count = len(queries)

    def kernel(*refs):
        basis_refs, eigen_refs, query_refs = refs[:2], refs[2:4], refs[4 : 4 + count]
        out_refs = refs[4 + count : 6 + count]
        here_refs = basis_refs if kept else refs[6 + count : 8 + count]
        query, *semaphores = refs[6 + count if kept else 8 + count :]
        tiles = [(side, tile) for side in range(2) for tile in range(basis_refs[side].shape[0] // TILE)]
        copies = []
        if not kept:
            for at, (side, tile) in enumerate(tiles):
                where = slice(tile * TILE, (tile + 1) * TILE)
                copies.append(
                    pltpu.make_async_copy(basis_refs[side].at[where], here_refs[side].at[where], semaphores[0].at[at])
                )
                copies[-1].start()
        for place, ref in enumerate(query_refs):
            query[place * columns : (place + 1) * columns, :] = ref[...]
        begins = (0, basis_refs[0].shape[1], query.shape[1])
        for at, (side, tile) in enumerate(tiles):
            where = slice(tile * TILE, (tile + 1) * TILE)
            if not kept:
                copies[at].wait()
            rotated = lax.dot_general(
                here_refs[side][where, :],
                query[:, begins[side] : begins[side + 1]],
                (((1,), (1,)), ((), ())),
                preferred_element_type=jnp.float32,
            )
            scale = 1.0 / (eigen_refs[side][where, :] + damping)
            out_refs[side][where, :] = (rotated * scale).astype(jnp.bfloat16)

    constrain = pltpu.with_memory_space_constraint
    in_vmem = pl.BlockSpec(memory_space=pltpu.VMEM)
    here = [pltpu.VMEM(basis.shape, basis.dtype) for basis in bases]
    copies = sum(basis.shape[0] for basis in bases) // TILE
    return pl.pallas_call(
        kernel,
        in_specs=[in_vmem if kept else pl.BlockSpec(memory_space=pltpu.HBM)] * 2 + [in_vmem] * (2 + count),
        out_specs=[in_vmem] * (4 if keep else 2),
        out_shape=[jax.ShapeDtypeStruct((basis.shape[0], held), jnp.bfloat16) for basis in bases]
        + (here if keep else []),
        scratch_shapes=([] if keep or kept else here)
        + [pltpu.VMEM((held, sum(basis.shape[1] for basis in bases)), jnp.bfloat16)]
        + ([] if kept else [pltpu.SemaphoreType.DMA((copies,))]),
        compiler_params=pltpu.CompilerParams(
            vmem_limit_bytes=VMEM_LIMIT if keep or kept else VMEM_LIMIT + 28 * 1024 * 1024
        ),
        cost_estimate=pl.CostEstimate(flops=1, bytes_accessed=1, transcendentals=0),
    )(
        *[constrain(basis, pltpu.VMEM if kept else pltpu.HBM) for basis in bases],
        *[constrain(one, pltpu.VMEM) for one in (*eigens, *queries)],
    )


def packed_width(examples, columns):
    return -(-examples * columns // 128) * 128


def grams(stores, blocks, offsets, base=None):
    rows, parts = lax.axis_size("rows"), lax.axis_size("parts")
    shares = [side.shape[0] for side in blocks[0]]
    columns = blocks[0][0].shape[1] // len(offsets[0])
    count = len(stores)
    held = stores[0].shape[0] // rows
    examples = held // RANK
    width = packed_width(examples, columns)

    def kernel(*refs):
        store_refs, block_refs, out_ref = refs[:count], refs[count : count + 2 * len(blocks)], refs[-1]
        row, part = lax.axis_index("rows"), lax.axis_index("parts")
        if base is not None:
            base_ref = refs[-2]
            out_ref[...] = base_ref[...]

        def write():
            for at, block_offsets in enumerate(offsets):
                for j, store_ref in enumerate(store_refs):
                    sides = []
                    for side, begin in enumerate((0, shares[0])):
                        store = store_ref[:, begin : begin + shares[side]]
                        sides.append(
                            jnp.dot(store, block_refs[2 * at + side][...], preferred_element_type=jnp.float32)
                        )
                    owner_part = lax.rem(part + parts - j, parts)
                    for place, offset in enumerate(block_offsets):
                        shard = lax.rem(row + offset, rows) if base is None else jnp.where(row == 0, rows - 1, 0)
                        for owner in range(rows):
                            packed = []
                            for gram in sides:
                                pieces = [
                                    gram[
                                        owner * held + i * RANK : owner * held + (i + 1) * RANK,
                                        place * columns : (place + 1) * columns,
                                    ]
                                    for i in range(examples)
                                ]
                                fill = width - examples * columns
                                if fill:
                                    pieces.append(jnp.zeros((RANK, fill), jnp.float32))
                                packed.append(jnp.concatenate(pieces, axis=1))
                            out_ref[owner_part, owner, shard] = jnp.concatenate(packed, axis=0).astype(jnp.bfloat16)

        if base is None:
            write()
        else:
            pl.when(jnp.logical_or(row == 0, row == rows - 1))(write)

    operands = [*stores, *[side for block in blocks for side in block]]
    return pl.pallas_call(
        kernel,
        out_shape=jax.ShapeDtypeStruct((parts, rows, rows, 2 * RANK, width), jnp.bfloat16),
        compiler_params=pltpu.CompilerParams(vmem_limit_bytes=VMEM_LIMIT),
        cost_estimate=pl.CostEstimate(flops=1, bytes_accessed=1, transcendentals=0),
    )(*operands, *([] if base is None else [base]))


def along_four(query, bases, eigens, by_owner):
    row = lax.axis_index("rows")
    columns = query.shape[0]
    eigens = [eigen.reshape(-1, 1) for eigen in eigens]
    after, before = along(query, -1), along(query, 1)
    store = to_owners(by_owner)
    *own, hidden_here, model_here = rotate(bases, eigens, [query], keep=True)
    bases = [hidden_here, model_here]
    own, store, after, before = lax.optimization_barrier((own, store, after, before))
    stores = to_parts(store)
    after_two, before_two = along(after, -1), along(before, 1)
    near = rotate(bases, eigens, [after, before], kept=True)
    near, stores, after_two, before_two = lax.optimization_barrier((near, stores, after_two, before_two))
    two = jnp.where(row < 2, after_two, before_two)
    three = lax.ppermute(two, "rows", [(1, 0), (2, 3)])
    far = rotate(bases, eigens, [two], kept=True)
    base = grams(stores, [own, near, far], [(0,), (1, 3), (2,)])
    base, three = lax.optimization_barrier((base, three))
    return grams(stores, [rotate(bases, eigens, [three], kept=True)], [(3,)], base)


def to_owners(by_owner):
    received = lax.all_to_all(by_owner, "rows", 0, 0, tiled=True)
    return received.reshape(-1, received.shape[-1])


def to_parts(store):
    parts = lax.axis_size("parts")
    return [store] + [
        lax.ppermute(store, "parts", [(i, (i + j) % parts) for i in range(parts)]) for j in range(1, parts)
    ]


def per_device(
    query_hidden,
    query_model,
    train_hidden,
    train_model,
    hidden_basis,
    model_basis,
    hidden_eigen,
    model_eigen,
):
    rows = lax.axis_size("rows")
    parts = lax.axis_size("parts")
    layers = lax.axis_size("layer")
    part = lax.axis_index("parts")
    held = train_hidden.shape[1]
    examples = held // RANK
    columns = query_hidden.shape[1] // parts
    width = query_hidden.shape[1] * rows // RANK // layers
    bases = [hidden_basis[0], model_basis[0]]
    eigens = [hidden_eigen, model_eigen]
    share = bases[0].shape[0]
    depth = bases[0].shape[1]

    query = jnp.concatenate(
        [lax.dynamic_slice_in_dim(side[0], part * columns, columns, 0) for side in (query_hidden, query_model)],
        axis=1,
    )
    by_owner = jnp.concatenate(
        [side[0].reshape(held, rows, -1).transpose(1, 0, 2) for side in (train_hidden, train_model)], axis=2
    )
    if rows == 4:
        partial = along_four(query, bases, eigens, by_owner)
    else:
        stores = to_parts(to_owners(by_owner))
        every = lax.all_gather(query, "rows", axis=0, tiled=True)
        sides = []
        for basis, eigen, gathered, begin in zip(bases, eigens, (every[:, :depth], every[:, depth:]), (0, share)):
            rotated = jnp.einsum("eh,qh->eq", basis, gathered, preferred_element_type=jnp.float32)
            scaled = (rotated * (1.0 / (eigen[0] + damping))[:, None]).astype(jnp.bfloat16)
            sides.append(
                [
                    jnp.dot(one[:, begin : begin + basis.shape[0]], scaled, preferred_element_type=jnp.float32)
                    for one in stores
                ]
            )
        partial = jnp.array(sides).reshape(2, parts, rows, examples, RANK, layers, rows // layers * columns)
        partial = partial.transpose(1, 2, 5, 0, 4, 3, 6).reshape(parts, rows, layers, 2 * RANK, -1)
        fill = packed_width(examples, rows // layers * columns) - partial.shape[-1]
        partial = jnp.pad(partial.astype(jnp.bfloat16), [(0, 0)] * 4 + [(0, fill)])
        partial = jnp.stack([lax.dynamic_index_in_dim(partial, (part - j) % parts, 0, False) for j in range(parts)])

    received = lax.all_to_all(
        partial.reshape((parts * rows * layers,) + partial.shape[3:]), ("parts", "rows", "layer"), 0, 0, tiled=True
    )
    gram = received.astype(jnp.float32).reshape(parts, rows, layers, 2, RANK, -1).sum(axis=1)
    by_column = (gram[:, :, 0] * gram[:, :, 1]).sum(axis=(1, 2))[:, : examples * width * RANK // parts]
    by_column = by_column.reshape(parts, examples, rows // layers, columns).transpose(1, 2, 0, 3)
    return by_column.reshape(examples, width, RANK).sum(axis=2)


def solution(mesh):
    placed = (
        P("layer", "rows", None),
        P("layer", "rows", None),
        P("layer", ("parts", "rows"), None),
        P("layer", ("parts", "rows"), None),
        P("layer", "rows", None),
        P("layer", "rows", None),
        P("layer", "rows"),
        P("layer", "rows"),
    )
    return jax.shard_map(
        per_device,
        mesh=mesh,
        in_specs=placed,
        out_specs=P(("parts", "rows"), "layer"),
        check_vma=False,
    )
```

time: 129 us -> 131 us (1.016)
  local copies, waits for them, and re-layouts: 6.09 us -> 28.5 us
  waiting for transfers between devices: 32.2 us -> 9.8 us
  blocking collectives: 7.41 us -> 13.7 us
  Pallas kernels: 49.7 us -> 47.2 us
  starting transfers between devices: 27.8 us -> 26.2 us
    unnamed x24 -> x56, local copies, waits for them, and re-layouts: 3.25 us -> 24.9 us
    ppermute x4, waiting for transfers between devices: 19 us -> 0.45 us  [along(): lax.ppermute(value, 'rows', [(i, i + by) for i in range(size) if 0 <= i +...]
    all_to_all x2 -> x1, waiting for transfers between devices: 13.2 us -> 0.01 us  [to_owners(): received = lax.all_to_all(by_owner, 'rows', 0, 0, tiled=True)]
    ppermute x1, waiting for transfers between devices: 0.01 us -> 9.34 us  [along_four(): three = lax.ppermute(two, 'rows', [(1, 0), (2, 3)])]
    all_to_all x1, blocking collectives: 7.41 us -> 13.7 us  [per_device(): lax.all_to_all(partial.reshape((parts * rows * layers,) + partial.shape[3...]
    all_to_all x2 -> x1, starting transfers between devices: 10 us -> 6.32 us  [to_owners(): received = lax.all_to_all(by_owner, 'rows', 0, 0, tiled=True)]
    pallas_call x3 -> x4, Pallas kernels: 46.2 us -> 42.7 us  [rotate(): pl.pallas_call(kernel, in_specs=[in_vmem if kept else pl.BlockSpec(memory...]
    another operation x4, local copies, waits for them, and re-layouts: 0.77 us -> 2.89 us  [per_device(): side[0].reshape(held, rows, -1).transpose(1, 0, 2)]
  transfers between devices with their start and end apart: 8 -> 7, of which waited for: 3 -> 2; matrix products, arithmetic and copies ran while one was open for 4% -> 1% of each run, Pallas kernels for 36% -> 28%
where the time goes in v6:
time: 131 us; the launch traced here: 130 us
  Pallas kernels  47.2 us (36%)
  local copies, waits for them, and re-layouts  28.5 us (22%)
  starting transfers between devices  26.2 us (20%)
  blocking collectives  13.7 us (10%)
  waiting for transfers between devices  9.8 us (7%)
  other arithmetic  4.25 us (3%)
    pallas_call x4, Pallas kernels, rotate(): pl.pallas_call(kernel, in_specs=[in_vmem if kept else pl.BlockSpec(memory...  42.7 us
    unnamed x56, local copies, waits for them, and re-layouts  24.9 us
    ppermute x4, starting transfers between devices, along(): lax.ppermute(value, 'rows', [(i, i + by) for i in range(size) if 0 <= i +...  16.8 us
    all_to_all x1, blocking collectives, per_device(): lax.all_to_all(partial.reshape((parts * rows * layers,) + partial.shape[3...  13.7 us
    ppermute x1, waiting for transfers between devices, along_four(): three = lax.ppermute(two, 'rows', [(1, 0), (2, 3)])  9.34 us
    all_to_all x1, starting transfers between devices, to_owners(): received = lax.all_to_all(by_owner, 'rows', 0, 0, tiled=True)  6.32 us
    pallas_call x2, Pallas kernels, grams(): pl.pallas_call(kernel, out_shape=jax.ShapeDtypeStruct((parts, rows, rows,...  4.54 us
    another operation x4, local copies, waits for them, and re-layouts, per_device(): side[0].reshape(held, rows, -1).transpose(1, 0, 2)  2.89 us
  transfers between devices with their start and end apart: 7, of which 2 were waited for; matrix products, arithmetic and copies ran while one was open for 1% of the time, Pallas kernels for 28%

profile of v6, /device:TPU:0, one launch (start us, length us, event | category | flops | bytes accessed | tf_op | source)
XLA Modules:
  0.0 130.1 jit_solution(13158270865120068833)
XLA Ops:
  0.0 1.3 %reshape_squeeze.7 = bf16[40,4,1024]{2,1,0:T(4,128)(2,1)S(1)} reshape(bf16[1,40,4096]{2,1,0:T(8,128)(2,1)} %param.11) | data formatting | bytes 655360 | tf_op jit(solution)/shard_map/reshape;squeeze | solution.py:203
  1.4 1.4 %reshape_squeeze.6 = bf16[40,4,1536]{2,1,0:T(4,128)(2,1)S(1)} reshape(bf16[1,40,6144]{2,1,0:T(8,128)(2,1)} %param.10) | data formatting | bytes 983040 | tf_op jit(solution)/shard_map/reshape;squeeze | solution.py:203
  3.9 6.3 %all-to-all-start = ((bf16[4,40,2560]{2,1,0:T(8,128)(2,1)}), bf16[4,40,2560]{2,1,0:T(8,128)(2,1)S(1)}, u32[]{:S(2)}, u32[]{:S(2)}) async-start(bf16[4,40,2560]{2,1,0:T(8,128)(2,1)} %pad_maximum_fusion.1), calls=%async_computation | async-start | bytes 1638400 | tf_op jit(solution)/shard_map/all_to_all | solution.py:164
  10.3 1.1 pad_maximum_fusion.refs_4_
  11.4 4.9 %collective-permute-start.1 = (bf16[48,10240]{1,0:T(8,128)(2,1)}, bf16[48,10240]{1,0:T(8,128)(2,1)}, u32[]{:S(2)}, u32[]{:S(2)}) collective-permute-start(bf16[48,10240]{1,0:T(8,128)(2,1)} %pad_maximum_fusion.refs_4_), channel_id=1, source_target_pairs={{0,4},{4,8},{8,12},{1,5},{5,9},{9,13},{2,6},{6,10},{10,14},{3,7},{... | collective-permute-start | bytes 2949128 | tf_op jit(solution)/shard_map/ppermute | solution.py:19
  16.3 1.3 collective-permute-start
  18.1 18.5 %shard_map.82 = (bf16[1536,48]{1,0:T(8,128)(2,1)S(1)}, bf16[1024,48]{1,0:T(8,128)(2,1)S(1)}, bf16[1536,6144]{1,0:T(8,128)(2,1)S(1)}, bf16[1024,4096]{1,0:T(8,128)(2,1)S(1)}) custom-call(bf16[1536,6144]{1,0:T(8,128)(2,1)} %bitcast.28, bf16[1024,4096]{1,0:T(8,128)(2,1)} %bitcast.29, f32[1536,1]{1,0:T(8,128)S(1)} %copy.22.refs_2_, f32[1024,1]{1,0:T(8,128)S(1)} %copy.23.refs_3_, ...), custom_call_target="tpu_custom_call" | custom-call | flops 1 | bytes 1 | tf_op jit(solution)/shard_map/pallas_call | solution.py:61
  36.6 6.4 %copy-done.2 = bf16[1536,6144]{1,0:T(8,128)(2,1)} copy-done((bf16[1536,6144]{1,0:T(8,128)(2,1)}, bf16[1536,6144]{1,0:T(8,128)(2,1)S(1)}, u32[]{:S(2)}) %copy-start.2) | copy-done | bytes 18874392
  43.0 3.4 %copy-done.4 = bf16[1024,4096]{1,0:T(8,128)(2,1)} copy-done((bf16[1024,4096]{1,0:T(8,128)(2,1)}, bf16[1024,4096]{1,0:T(8,128)(2,1)S(1)}, u32[]{:S(2)}) %copy-start.4) | copy-done | bytes 8388632
  46.9 1.3 collective-permute-start.3
  48.2 9.4 %collective-permute-start.4 = (bf16[48,10240]{1,0:T(8,128)(2,1)}, bf16[48,10240]{1,0:T(8,128)(2,1)}, u32[]{:S(2)}, u32[]{:S(2)}) collective-permute-start(bf16[48,10240]{1,0:T(8,128)(2,1)} %collective-permute-done.1.refs_5_), channel_id=1, source_target_pairs={{0,4},{4,8},{8,12},{1,5},{5,9},{9,13},{2,6},{6,10},{10,14},{3,7},{... | collective-permute-start | bytes 2949128 | tf_op jit(solution)/shard_map/ppermute | solution.py:19
  57.6 1.5 %collective-permute-start.2 = (bf16[160,2560]{1,0:T(8,128)(2,1)S(1)}, bf16[160,2560]{1,0:T(8,128)(2,1)}, u32[]{:S(2)}, u32[]{:S(2)}) collective-permute-start(bf16[160,2560]{1,0:T(8,128)(2,1)S(1)} %bitcast.24), channel_id=1, source_target_pairs={{0,16},{16,0},{1,17},{17,1},{2,18},{18,2},{3,19},{19,3},{4,20},{20... | collective-permute-start | bytes 2457608 | tf_op jit(solution)/shard_map/ppermute | solution.py:171
  59.1 6.4 %copy-done.3 = bf16[1536,6144]{1,0:T(8,128)(2,1)S(1)} copy-done((bf16[1536,6144]{1,0:T(8,128)(2,1)S(1)}, bf16[1536,6144]{1,0:T(8,128)(2,1)}, u32[]{:S(2)}) %copy-start.3) | copy-done | bytes 18874392
  65.4 3.4 %copy-done.5 = bf16[1024,4096]{1,0:T(8,128)(2,1)S(1)} copy-done((bf16[1024,4096]{1,0:T(8,128)(2,1)S(1)}, bf16[1024,4096]{1,0:T(8,128)(2,1)}, u32[]{:S(2)}) %copy-start.5) | copy-done | bytes 8388632
  68.8 8.7 %shard_map.83 = (bf16[1536,96]{1,0:T(8,128)(2,1)S(1)}, bf16[1024,96]{1,0:T(8,128)(2,1)S(1)}) custom-call(bf16[1536,6144]{1,0:T(8,128)(2,1)S(1)} %copy-done.3, bf16[1024,4096]{1,0:T(8,128)(2,1)S(1)} %copy-done.5, f32[1536,1]{1,0:T(8,128)S(1)} %copy.22.refs_2_, f32[1024,1]{1,0:T(8,128)S(1)} %copy.23.refs_3_, bf16[48,10240]{1,0:T(8,128)(2,1)} %collective-permute-done.refs_4_, ...), custom_call_target="tpu_custom_call" | custom-call | flops 1 | bytes 1 | tf_op jit(solution)/shard_map/pallas_call | solution.py:61
  79.0 1.5 %broadcast_select_fusion.refs_4_ = bf16[48,10240]{1,0:T(8,128)(2,1)S(1)} fusion(bf16[48,10240]{1,0:T(8,128)(2,1)} %collective-permute-done.3, bf16[48,10240]{1,0:T(8,128)(2,1)} %collective-permute-done.4, pred[]{:T(512)S(6)} %lt.8), kind=kLoop, calls=%fused_computation.1 | loop fusion | flops 491520 | bytes 2949121 | tf_op jit(solution)/shard_map/jit(_where)/select_n | solution.py:155
  80.5 1.6 %collective-permute-start.5 = (bf16[48,10240]{1,0:T(8,128)(2,1)S(1)}, bf16[48,10240]{1,0:T(8,128)(2,1)}, u32[]{:S(2)}, u32[]{:S(2)}) collective-permute-start(bf16[48,10240]{1,0:T(8,128)(2,1)S(1)} %broadcast_select_fusion.refs_4_), channel_id=1, source_target_pairs={{4,0},{8,12},{5,1},{9,13},{6,2},{10,14},{7,3},{11,15},{20,16},{24,... | collective-permute-start | bytes 2949128 | tf_op jit(solution)/shard_map/ppermute | solution.py:156
  82.1 7.2 %shard_map.84 = (bf16[1536,48]{1,0:T(8,128)(2,1)S(1)}, bf16[1024,48]{1,0:T(8,128)(2,1)S(1)}) custom-call(bf16[1536,6144]{1,0:T(8,128)(2,1)S(1)} %copy-done.3, bf16[1024,4096]{1,0:T(8,128)(2,1)S(1)} %copy-done.5, f32[1536,1]{1,0:T(8,128)S(1)} %copy.22.refs_2_, f32[1024,1]{1,0:T(8,128)S(1)} %copy-done.7, bf16[48,10240]{1,0:T(8,128)(2,1)S(1)} %broadcast_select_fusion.refs_4_), custom_call_target="tpu_custom_call" | custom-call | flops 1 | bytes 1 | tf_op jit(solution)/shard_map/pallas_call | solution.py:61
  90.0 1.2 copy-done.10
  93.1 2.6 %shard_map.85.refs_4_ = bf16[2,4,4,16,256]{4,3,2,1,0:T(8,128)(2,1)S(1)} custom-call(bf16[160,2560]{1,0:T(8,128)(2,1)S(1)} %bitcast.25, bf16[160,2560]{1,0:T(8,128)(2,1)} %collective-permute-done.2.refs_1_, bf16[1536,48]{1,0:T(8,128)(2,1)S(1)} %get-tuple-element.39.refs_2_, bf16[1024,48]{1,0:T(8,128)(2,1)S(1)} %copy-done.15, bf16[1536,96]{1,0:T(8,128)(2,1)S(1)} %copy-done.13, ...), custom_call_target="tpu_custom_call" | custom-call | flops 1 | bytes 1 | tf_op jit(solution)/shard_map/pallas_call | solution.py:134
  95.7 9.3 %collective-permute-done.5.refs_4_ = bf16[48,10240]{1,0:T(8,128)(2,1)} collective-permute-done((bf16[48,10240]{1,0:T(8,128)(2,1)S(1)}, bf16[48,10240]{1,0:T(8,128)(2,1)}, u32[]{:S(2)}, u32[]{:S(2)}) %collective-permute-start.5) | collective-permute-done | bytes 983072 | tf_op jit(solution)/shard_map/ppermute | solution.py:156
  105.1 8.4 %shard_map.86 = (bf16[1536,48]{1,0:T(8,128)(2,1)S(1)}, bf16[1024,48]{1,0:T(8,128)(2,1)S(1)}) custom-call(bf16[1536,6144]{1,0:T(8,128)(2,1)S(1)} %bitcast.23, bf16[1024,4096]{1,0:T(8,128)(2,1)S(1)} %copy-done.5, f32[1536,1]{1,0:T(8,128)S(1)} %copy.22.refs_2_, f32[1024,1]{1,0:T(8,128)S(1)} %copy-done.8, bf16[48,10240]{1,0:T(8,128)(2,1)} %collective-permute-done.5.refs_4_), custom_call_target="tpu_custom_call" | custom-call | flops 1 | bytes 1 | tf_op jit(solution)/shard_map/pallas_call | solution.py:61
  113.5 1.9 %shard_map.87 = bf16[2,4,4,16,256]{4,3,2,1,0:T(8,128)(2,1)S(1)} custom-call(bf16[160,2560]{1,0:T(8,128)(2,1)S(1)} %bitcast.26, bf16[160,2560]{1,0:T(8,128)(2,1)} %collective-permute-done.2.refs_1_, bf16[1536,48]{1,0:T(8,128)(2,1)S(1)} %get-tuple-element.48.refs_2_, bf16[1024,48]{1,0:T(8,128)(2,1)S(1)} %get-tuple-element.49.refs_3_, ...), custom_call_target="tpu_custom_call" | custom-call | flops 1 | bytes 1 | tf_op jit(solution)/shard_map/pallas_call | solution.py:134
  115.4 13.7 %all_to_all.10 = bf16[32,16,256]{2,1,0:T(8,128)(2,1)S(1)} all-to-all(bf16[32,16,256]{2,1,0:T(8,128)(2,1)S(1)} %bitcast.27), channel_id=1, replica_groups=mesh['parts'=2,'rows'=4,'layer'=4] {'parts','rows','layer'}, dimensions={0} | all-to-all | bytes 524288 | tf_op jit(solution)/shard_map/all_to_all | solution.py:226
  (71 shorter events, 7.2 us)
Async XLA Ops:
  0.0 10.2 %copy-start = (bf16[1,96,6144]{2,1,0:T(8,128)(2,1)S(1)}, bf16[1,96,6144]{2,1,0:T(8,128)(2,1)}, u32[]{:S(2)}) copy-start(bf16[1,96,6144]{2,1,0:T(8,128)(2,1)} %param.8) | copy-start | bytes 3538948
  2.8 7.4 %copy-start.20 = (bf16[1,96,4096]{2,1,0:T(8,128)(2,1)S(1)}, bf16[1,96,4096]{2,1,0:T(8,128)(2,1)}, u32[]{:S(2)}) copy-start(bf16[1,96,4096]{2,1,0:T(8,128)(2,1)} %param.9) | copy-start | bytes 2359300
  3.9 43.0 %all-to-all-start = ((bf16[4,40,2560]{2,1,0:T(8,128)(2,1)}), bf16[4,40,2560]{2,1,0:T(8,128)(2,1)S(1)}, u32[]{:S(2)}, u32[]{:S(2)}) async-start(bf16[4,40,2560]{2,1,0:T(8,128)(2,1)} %pad_maximum_fusion.1), calls=%async_computation | async-start | bytes 1638400 | tf_op jit(solution)/shard_map/all_to_all | solution.py:164
  10.2 7.4 %copy-start.22 = (f32[1,1024]{1,0:T(1,128)S(1)}, f32[1,1024]{1,0:T(1,128)}, u32[]{:S(2)}) copy-start(f32[1,1024]{1,0:T(1,128)} %param.15) | copy-start | bytes 12292
  10.2 7.6 %copy-start.21 = (f32[1,1536]{1,0:T(1,128)S(1)}, f32[1,1536]{1,0:T(1,128)}, u32[]{:S(2)}) copy-start(f32[1,1536]{1,0:T(1,128)} %param.14) | copy-start | bytes 18436
  11.4 35.1 %collective-permute-start.1 = (bf16[48,10240]{1,0:T(8,128)(2,1)}, bf16[48,10240]{1,0:T(8,128)(2,1)}, u32[]{:S(2)}, u32[]{:S(2)}) collective-permute-start(bf16[48,10240]{1,0:T(8,128)(2,1)} %pad_maximum_fusion.refs_4_), channel_id=1, source_target_pairs={{0,4},{4,8},{8,12},{1,5},{5,9},{9,13},{2,6},{6,10},{10,14},{3,7},{... | collective-permute-start | bytes 2949128 | tf_op jit(solution)/shard_map/ppermute | solution.py:19
  16.3 30.6 %collective-permute-start = (bf16[48,10240]{1,0:T(8,128)(2,1)}, bf16[48,10240]{1,0:T(8,128)(2,1)}, u32[]{:S(2)}, u32[]{:S(2)}) collective-permute-start(bf16[48,10240]{1,0:T(8,128)(2,1)} %pad_maximum_fusion.refs_4_), channel_id=1, source_target_pairs={{4,0},{8,4},{12,8},{5,1},{9,5},{13,9},{6,2},{10,6},{14,10},{7,3},{... | collective-permute-start | bytes 2949128 | tf_op jit(solution)/shard_map/ppermute | solution.py:19
  17.8 41.3 %copy-start.6 = (f32[1024,1]{1,0:T(8,128)}, f32[1024,1]{1,0:T(8,128)S(1)}, u32[]{:S(2)}) copy-start(f32[1024,1]{1,0:T(8,128)S(1)} %copy.23.refs_3_) | copy-start | bytes 12292
  46.4 31.1 %copy-start.14 = (bf16[1024,48]{1,0:T(8,128)(2,1)}, bf16[1024,48]{1,0:T(8,128)(2,1)S(1)}, u32[]{:S(2)}) copy-start(bf16[1024,48]{1,0:T(8,128)(2,1)S(1)} %get-tuple-element.40.refs_3_) | copy-start | bytes 294916
  46.9 30.6 %copy-start.9 = (bf16[4,40,2560]{2,1,0:T(8,128)(2,1)}, bf16[4,40,2560]{2,1,0:T(8,128)(2,1)S(1)}, u32[]{:S(2)}) copy-start(bf16[4,40,2560]{2,1,0:T(8,128)(2,1)S(1)} %all-to-all-done) | copy-start | bytes 2457604
  46.9 32.1 %collective-permute-start.3 = (bf16[48,10240]{1,0:T(8,128)(2,1)}, bf16[48,10240]{1,0:T(8,128)(2,1)}, u32[]{:S(2)}, u32[]{:S(2)}) collective-permute-start(bf16[48,10240]{1,0:T(8,128)(2,1)} %collective-permute-done.refs_4_), channel_id=1, source_target_pairs={{4,0},{8,4},{12,8},{5,1},{9,5},{13,9},{6,2},{10,6},{14,10},{7,3},{... | collective-permute-start | bytes 2949128 | tf_op jit(solution)/shard_map/ppermute | solution.py:19
  48.2 30.8 %collective-permute-start.4 = (bf16[48,10240]{1,0:T(8,128)(2,1)}, bf16[48,10240]{1,0:T(8,128)(2,1)}, u32[]{:S(2)}, u32[]{:S(2)}) collective-permute-start(bf16[48,10240]{1,0:T(8,128)(2,1)} %collective-permute-done.1.refs_5_), channel_id=1, source_target_pairs={{0,4},{4,8},{8,12},{1,5},{5,9},{9,13},{2,6},{6,10},{10,14},{3,7},{... | collective-permute-start | bytes 2949128 | tf_op jit(solution)/shard_map/ppermute | solution.py:19
  57.6 21.4 %collective-permute-start.2 = (bf16[160,2560]{1,0:T(8,128)(2,1)S(1)}, bf16[160,2560]{1,0:T(8,128)(2,1)}, u32[]{:S(2)}, u32[]{:S(2)}) collective-permute-start(bf16[160,2560]{1,0:T(8,128)(2,1)S(1)} %bitcast.24), channel_id=1, source_target_pairs={{0,16},{16,0},{1,17},{17,1},{2,18},{18,2},{3,19},{19,3},{4,20},{20... | collective-permute-start | bytes 2457608 | tf_op jit(solution)/shard_map/ppermute | solution.py:171
  79.0 26.1 %slice-start = ((s8[18874368]{0:T(1024)(128)(4,1)}), s8[4194304]{0:T(1024)(128)(4,1)S(1)}, s32[]{:S(2)}) async-start(s8[18874368]{0:T(1024)(128)(4,1)} %bitcast.22), calls=%async_computation.2 | async-start | bytes 8388608
  80.5 9.5 %copy-start.13 = (bf16[1536,96]{1,0:T(8,128)(2,1)S(1)}, bf16[1536,96]{1,0:T(8,128)(2,1)}, u32[]{:S(2)}) copy-start(bf16[1536,96]{1,0:T(8,128)(2,1)} %copy-done.12) | copy-start | bytes 884740
  80.5 9.5 %copy-start.15 = (bf16[1024,48]{1,0:T(8,128)(2,1)S(1)}, bf16[1024,48]{1,0:T(8,128)(2,1)}, u32[]{:S(2)}) copy-start(bf16[1024,48]{1,0:T(8,128)(2,1)} %copy-done.14) | copy-start | bytes 294916
  80.5 24.6 %slice-start.1 = ((s8[18874368]{0:T(1024)(128)(4,1)}), s8[4194304]{0:T(1024)(128)(4,1)S(1)}, s32[]{:S(2)}) async-start(s8[18874368]{0:T(1024)(128)(4,1)} %bitcast.22), calls=%async_computation.3 | async-start | bytes 8388608
  80.5 24.6 %slice-start.2 = ((s8[18874368]{0:T(1024)(128)(4,1)}), s8[4194304]{0:T(1024)(128)(4,1)S(1)}, s32[]{:S(2)}) async-start(s8[18874368]{0:T(1024)(128)(4,1)} %bitcast.22), calls=%async_computation.4 | async-start | bytes 8388608
  80.5 24.6 %slice-start.3 = ((s8[18874368]{0:T(1024)(128)(4,1)}), s8[4194304]{0:T(1024)(128)(4,1)S(1)}, s32[]{:S(2)}) async-start(s8[18874368]{0:T(1024)(128)(4,1)} %bitcast.22), calls=%async_computation.5 | async-start | bytes 8388608
  80.5 24.6 %slice-start.4 = ((s8[18874368]{0:T(1024)(128)(4,1)}), s8[2097152]{0:T(1024)(128)(4,1)S(1)}, s32[]{:S(2)}) async-start(s8[18874368]{0:T(1024)(128)(4,1)} %bitcast.22), calls=%async_computation.6 | async-start | bytes 4194304
  80.5 24.6 %collective-permute-start.5 = (bf16[48,10240]{1,0:T(8,128)(2,1)S(1)}, bf16[48,10240]{1,0:T(8,128)(2,1)}, u32[]{:S(2)}, u32[]{:S(2)}) collective-permute-start(bf16[48,10240]{1,0:T(8,128)(2,1)S(1)} %broadcast_select_fusion.refs_4_), channel_id=1, source_target_pairs={{4,0},{8,12},{5,1},{9,13},{6,2},{10,14},{7,3},{11,15},{20,16},{24,... | collective-permute-start | bytes 2949128 | tf_op jit(solution)/shard_map/ppermute | solution.py:156
  90.0 15.1 %copy-start.8 = (f32[1024,1]{1,0:T(8,128)S(1)}, f32[1024,1]{1,0:T(8,128)}, u32[]{:S(2)}) copy-start(f32[1024,1]{1,0:T(8,128)} %copy-done.6) | copy-start | bytes 12292
  95.7 17.8 %copy-start.11 = (bf16[4,40,2560]{2,1,0:T(8,128)(2,1)S(1)}, bf16[4,40,2560]{2,1,0:T(8,128)(2,1)}, u32[]{:S(2)}) copy-start(bf16[4,40,2560]{2,1,0:T(8,128)(2,1)} %copy-done.9) | copy-start | bytes 2457604
  113.5 16.5 %copy-start.1 = (bf16[1,96,6144]{2,1,0:T(8,128)(2,1)S(1)}, bf16[1,96,6144]{2,1,0:T(8,128)(2,1)}, u32[]{:S(2)}) copy-start(bf16[1,96,6144]{2,1,0:T(8,128)(2,1)} %param.8) | copy-start | bytes 3538948
  (11 other events, 28.0 us)

commit v7 on v6

--- a/solution.py
+++ b/solution.py
@@ -12,6 +12,7 @@
 
 VMEM_LIMIT = 16 * 1024 * 1024
 TILE = 256
+AHEAD = 3
 
 
 def along(value, by):
@@ -19,56 +20,78 @@
     return lax.ppermute(value, "rows", [(i, i + by) for i in range(size) if 0 <= i + by < size])
 
 
-def rotate(bases, eigens, queries, keep=False, kept=False):
+def rotate(bases, eigens, queries, begins, keep=False, kept=False):
+    groups = [query if isinstance(query, tuple) else (query,) for query in queries]
+    queries = [query for group in groups for query in group]
     columns = queries[0].shape[0]
-    held = columns * len(queries)
-    count = len(queries)
+    held = columns * len(groups)
+    count, sides = len(queries), len(bases)
+    tiles = [(side, tile) for side in range(sides) for tile in range(bases[side].shape[0] // TILE)]
 
     def kernel(*refs):
-        basis_refs, eigen_refs, query_refs = refs[:2], refs[2:4], refs[4 : 4 + count]
-        out_refs = refs[4 + count : 6 + count]
-        here_refs = basis_refs if kept else refs[6 + count : 8 + count]
-        query, *semaphores = refs[6 + count if kept else 8 + count :]
-        tiles = [(side, tile) for side in range(2) for tile in range(basis_refs[side].shape[0] // TILE)]
-        copies = []
+        refs = list(refs)
+        take = lambda many: [refs.pop(0) for _ in range(many)]
+        basis_refs, eigen_refs, query_refs, out_refs = take(sides), take(sides), take(count), take(sides)
+        here_refs = take(sides) if keep else []
+        query = take(1)[0]
+        slots = None if keep or kept else take(1)[0]
+        semaphores = None if kept else take(1)[0]
+
+        def block(at):
+            side, tile = tiles[at]
+            where = slice(tile * TILE, (tile + 1) * TILE)
+            if kept:
+                return basis_refs[side].at[where]
+            if keep:
+                return here_refs[side].at[where]
+            return slots.at[at % AHEAD, :, : basis_refs[side].shape[1]]
+
+        def copy(at):
+            side, tile = tiles[at]
+            where = slice(tile * TILE, (tile + 1) * TILE)
+            return pltpu.make_async_copy(basis_refs[side].at[where], block(at), semaphores.at[at])
+
         if not kept:
-            for at, (side, tile) in enumerate(tiles):
-                where = slice(tile * TILE, (tile + 1) * TILE)
-                copies.append(
-                    pltpu.make_async_copy(basis_refs[side].at[where], here_refs[side].at[where], semaphores[0].at[at])
-                )
-                copies[-1].start()
-        for place, ref in enumerate(query_refs):
-            query[place * columns : (place + 1) * columns, :] = ref[...]
-        begins = (0, basis_refs[0].shape[1], query.shape[1])
+            for at in range(min(AHEAD, len(tiles))):
+                copy(at).start()
+        for place, group in enumerate(groups):
+            block_of = query_refs.pop(0)[...]
+            for _ in group[1:]:
+                block_of = block_of + query_refs.pop(0)[...]
+            query[place * columns : (place + 1) * columns, :] = block_of
         for at, (side, tile) in enumerate(tiles):
             where = slice(tile * TILE, (tile + 1) * TILE)
             if not kept:
-                copies[at].wait()
+                copy(at).wait()
+            if keep and at + AHEAD < len(tiles):
+                copy(at + AHEAD).start()
             rotated = lax.dot_general(
-                here_refs[side][where, :],
-                query[:, begins[side] : begins[side + 1]],
+                block(at)[...],
+                query[:, begins[side] : begins[side] + basis_refs[side].shape[1]],
                 (((1,), (1,)), ((), ())),
                 preferred_element_type=jnp.float32,
             )
             scale = 1.0 / (eigen_refs[side][where, :] + damping)
             out_refs[side][where, :] = (rotated * scale).astype(jnp.bfloat16)
+            if not (keep or kept) and at + AHEAD < len(tiles):
+                copy(at + AHEAD).start()
 
     constrain = pltpu.with_memory_space_constraint
     in_vmem = pl.BlockSpec(memory_space=pltpu.VMEM)
-    here = [pltpu.VMEM(basis.shape, basis.dtype) for basis in bases]
-    copies = sum(basis.shape[0] for basis in bases) // TILE
+    scratch = [pltpu.VMEM((held, queries[0].shape[1]), jnp.bfloat16)]
+    if not (keep or kept):
+        scratch.append(pltpu.VMEM((AHEAD, TILE, max(basis.shape[1] for basis in bases)), jnp.bfloat16))
+    if not kept:
+        scratch.append(pltpu.SemaphoreType.DMA((len(tiles),)))
     return pl.pallas_call(
         kernel,
-        in_specs=[in_vmem if kept else pl.BlockSpec(memory_space=pltpu.HBM)] * 2 + [in_vmem] * (2 + count),
-        out_specs=[in_vmem] * (4 if keep else 2),
+        in_specs=[in_vmem if kept else pl.BlockSpec(memory_space=pltpu.HBM)] * sides + [in_vmem] * (sides + count),
+        out_specs=[in_vmem] * (2 * sides if keep else sides),
         out_shape=[jax.ShapeDtypeStruct((basis.shape[0], held), jnp.bfloat16) for basis in bases]
-        + (here if keep else []),
-        scratch_shapes=([] if keep or kept else here)
-        + [pltpu.VMEM((held, sum(basis.shape[1] for basis in bases)), jnp.bfloat16)]
-        + ([] if kept else [pltpu.SemaphoreType.DMA((copies,))]),
+        + ([pltpu.VMEM(basis.shape, basis.dtype) for basis in bases] if keep else []),
+        scratch_shapes=scratch,
         compiler_params=pltpu.CompilerParams(
-            vmem_limit_bytes=VMEM_LIMIT if keep or kept else VMEM_LIMIT + 28 * 1024 * 1024
+            vmem_limit_bytes=VMEM_LIMIT if keep or kept else VMEM_LIMIT + 8 * 1024 * 1024
         ),
         cost_estimate=pl.CostEstimate(flops=1, bytes_accessed=1, transcendentals=0),
     )(
@@ -141,23 +164,24 @@
 
 def along_four(query, bases, eigens, by_owner):
     row = lax.axis_index("rows")
-    columns = query.shape[0]
+    depth = bases[0].shape[1]
     eigens = [eigen.reshape(-1, 1) for eigen in eigens]
     after, before = along(query, -1), along(query, 1)
-    store = to_owners(by_owner)
-    *own, hidden_here, model_here = rotate(bases, eigens, [query], keep=True)
-    bases = [hidden_here, model_here]
-    own, store, after, before = lax.optimization_barrier((own, store, after, before))
-    stores = to_parts(store)
+    stores = to_parts(to_owners(by_owner))
     after_two, before_two = along(after, -1), along(before, 1)
-    near = rotate(bases, eigens, [after, before], kept=True)
-    near, stores, after_two, before_two = lax.optimization_barrier((near, stores, after_two, before_two))
-    two = jnp.where(row < 2, after_two, before_two)
-    three = lax.ppermute(two, "rows", [(1, 0), (2, 3)])
-    far = rotate(bases, eigens, [two], kept=True)
-    base = grams(stores, [own, near, far], [(0,), (1, 3), (2,)])
-    base, three = lax.optimization_barrier((base, three))
-    return grams(stores, [rotate(bases, eigens, [three], kept=True)], [(3,)], base)
+    near = rotate(bases, eigens, [query, after, before], (0, depth))
+    near, after_two, before_two = lax.optimization_barrier((near, after_two, before_two))
+    three_model, three_hidden = (
+        lax.ppermute(jnp.where(row < 2, after_two[:, side], before_two[:, side]), "rows", [(1, 0), (2, 3)])
+        for side in (slice(depth, None), slice(0, depth))
+    )
+    *far, hidden_here, model_here = rotate(bases, eigens, [(after_two, before_two)], (0, depth), keep=True)
+    base = grams(stores, [near, far], [(0, 1, 3), (2,)])
+    base, three_model = lax.optimization_barrier((base, three_model))
+    last_model = rotate([model_here], eigens[1:], [three_model], (0,), kept=True)
+    last_model, three_hidden = lax.optimization_barrier((last_model, three_hidden))
+    last_hidden = rotate([hidden_here], eigens[:1], [three_hidden], (0,), kept=True)
+    return grams(stores, [last_hidden + last_model], [(3,)], base)
 
 
 def to_owners(by_owner):

time: 131 us -> 131 us (level)
  local copies, waits for them, and re-layouts: 28.5 us -> 17.8 us
  blocking collectives: 13.7 us -> 19.8 us
  waiting for transfers between devices: 9.8 us -> 15 us
    ppermute x4, waiting for transfers between devices: 0.45 us -> 15 us  [along(): lax.ppermute(value, 'rows', [(i, i + by) for i in range(size) if 0 <= i +...]
    unnamed x56 -> x24, local copies, waits for them, and re-layouts: 24.9 us -> 15.2 us
    ppermute x1 -> x2, waiting for transfers between devices: 9.34 us -> 0.01 us  [along_four(): lax.ppermute(jnp.where(row < 2, after_two[:, side], before_two[:, side]),...]
    all_to_all x1, blocking collectives: 13.7 us -> 19.8 us  [per_device(): lax.all_to_all(partial.reshape((parts * rows * layers,) + partial.shape[3...]
    pallas_call x2, Pallas kernels: 4.54 us -> 1.76 us  [grams(): pl.pallas_call(kernel, out_shape=jax.ShapeDtypeStruct((parts, rows, rows,...]
    pallas_call x4, Pallas kernels: 42.7 us -> 45.1 us  [rotate(): pl.pallas_call(kernel, in_specs=[in_vmem if kept else pl.BlockSpec(memory...]
    another operation x4, local copies, waits for them, and re-layouts: 2.89 us -> 0.77 us  [per_device(): side[0].reshape(held, rows, -1).transpose(1, 0, 2)]
    all_to_all x1, starting transfers between devices: 6.32 us -> 4.22 us  [to_owners(): received = lax.all_to_all(by_owner, 'rows', 0, 0, tiled=True)]
  transfers between devices with their start and end apart: 7 -> 8, of which waited for: 2 -> 3; matrix products, arithmetic and copies ran while one was open for 1% -> 4% of each run, Pallas kernels for 28% -> 32%
where the time goes in v7:
time: 131 us
  Pallas kernels  46.9 us (36%)
  starting transfers between devices  26.7 us (20%)
  blocking collectives  19.8 us (15%)
  local copies, waits for them, and re-layouts  17.8 us (14%)
  waiting for transfers between devices  15 us (11%)
  other arithmetic  4.27 us (3%)
    pallas_call x4, Pallas kernels, rotate(): pl.pallas_call(kernel, in_specs=[in_vmem if kept else pl.BlockSpec(memory...  45.1 us
    all_to_all x1, blocking collectives, per_device(): lax.all_to_all(partial.reshape((parts * rows * layers,) + partial.shape[3...  19.8 us
    ppermute x4, starting transfers between devices, along(): lax.ppermute(value, 'rows', [(i, i + by) for i in range(size) if 0 <= i +...  18.1 us
    unnamed x24, local copies, waits for them, and re-layouts  15.2 us
    ppermute x4, waiting for transfers between devices, along(): lax.ppermute(value, 'rows', [(i, i + by) for i in range(size) if 0 <= i +...  15 us
    all_to_all x1, starting transfers between devices, to_owners(): received = lax.all_to_all(by_owner, 'rows', 0, 0, tiled=True)  4.22 us
    ppermute x2, starting transfers between devices, along_four(): lax.ppermute(jnp.where(row < 2, after_two[:, side], before_two[:, side]),...  2.9 us
  transfers between devices with their start and end apart: 8, of which 3 were waited for; matrix products, arithmetic and copies ran while one was open for 4% of the time, Pallas kernels for 32%

profile of v7, /device:TPU:0, one launch (start us, length us, event | category | flops | bytes accessed | tf_op | source)
XLA Modules:
  0.0 130.7 jit_solution(12101916513414981505)
XLA Ops:
  0.0 1.1 dynamic-slice_bitcast_fusion.1
  1.5 1.4 %collective-permute-start.1 = (bf16[48,10240]{1,0:T(8,128)(2,1)S(1)}, bf16[48,10240]{1,0:T(8,128)(2,1)}, u32[]{:S(2)}, u32[]{:S(2)}) collective-permute-start(bf16[48,10240]{1,0:T(8,128)(2,1)S(1)} %pad_maximum_fusion.refs_4_), channel_id=1, source_target_pairs={{4,0},{8,4},{12,8},{5,1},{9,5},{13,9},{6,2},{10,6},{14,10},{7,3},{... | collective-permute-start | bytes 2949128 | tf_op jit(solution)/shard_map/ppermute | solution.py:20
  3.0 6.6 %collective-permute-start.2 = (bf16[48,10240]{1,0:T(8,128)(2,1)S(1)}, bf16[48,10240]{1,0:T(8,128)(2,1)}, u32[]{:S(2)}, u32[]{:S(2)}) collective-permute-start(bf16[48,10240]{1,0:T(8,128)(2,1)S(1)} %pad_maximum_fusion.refs_4_), channel_id=1, source_target_pairs={{0,4},{4,8},{8,12},{1,5},{5,9},{9,13},{2,6},{6,10},{10,14},{3,7},{... | collective-permute-start | bytes 2949128 | tf_op jit(solution)/shard_map/ppermute | solution.py:20
  10.4 1.0 pad_maximum_fusion.1
  11.4 4.2 %all-to-all-start = ((bf16[4,40,2560]{2,1,0:T(8,128)(2,1)}), bf16[4,40,2560]{2,1,0:T(8,128)(2,1)S(1)}, u32[]{:S(2)}, u32[]{:S(2)}) async-start(bf16[4,40,2560]{2,1,0:T(8,128)(2,1)} %pad_maximum_fusion.1), calls=%async_computation | async-start | bytes 1638400 | tf_op jit(solution)/shard_map/all_to_all | solution.py:188
  15.6 13.7 %collective-permute-done.1.refs_5_ = bf16[48,10240]{1,0:T(8,128)(2,1)} collective-permute-done((bf16[48,10240]{1,0:T(8,128)(2,1)S(1)}, bf16[48,10240]{1,0:T(8,128)(2,1)}, u32[]{:S(2)}, u32[]{:S(2)}) %collective-permute-start.1) | collective-permute-done | bytes 983072 | tf_op jit(solution)/shard_map/ppermute | solution.py:20
  29.3 1.3 collective-permute-start.3
  30.7 8.8 %collective-permute-start.4 = (bf16[48,10240]{1,0:T(8,128)(2,1)}, bf16[48,10240]{1,0:T(8,128)(2,1)}, u32[]{:S(2)}, u32[]{:S(2)}) collective-permute-start(bf16[48,10240]{1,0:T(8,128)(2,1)} %collective-permute-done.2.refs_6_), channel_id=1, source_target_pairs={{0,4},{4,8},{8,12},{1,5},{5,9},{9,13},{2,6},{6,10},{10,14},{3,7},{... | collective-permute-start | bytes 2949128 | tf_op jit(solution)/shard_map/ppermute | solution.py:20
  40.0 1.2 copy-done.5
  41.2 19.1 %shard_map.82 = (bf16[1536,144]{1,0:T(8,128)(2,1)S(1)}, bf16[1024,144]{1,0:T(8,128)(2,1)S(1)}) custom-call(bf16[1536,6144]{1,0:T(8,128)(2,1)} %bitcast.26, bf16[1024,4096]{1,0:T(8,128)(2,1)} %bitcast.28, f32[1536,1]{1,0:T(8,128)S(1)} %copy.24.refs_2_.refs_1_, f32[1024,1]{1,0:T(8,128)S(1)} %copy.25.refs_3_.refs_1_, bf16[48,10240]{1,0:T(8,128)(2,1)S(1)} %copy-done.5, ...), custom_call_target="tpu_custom_call" | custom-call | flops 1 | bytes 1 | tf_op jit(solution)/shard_map/pallas_call | solution.py:86
  60.3 0.9 copy-done.6
  61.2 1.5 %collective-permute-start = (bf16[160,2560]{1,0:T(8,128)(2,1)S(1)}, bf16[160,2560]{1,0:T(8,128)(2,1)S(1)}, u32[]{:S(2)}, u32[]{:S(2)}) collective-permute-start(bf16[160,2560]{1,0:T(8,128)(2,1)S(1)} %bitcast.22), channel_id=1, source_target_pairs={{0,16},{16,0},{1,17},{17,1},{2,18},{18,2},{3,19},{19,3},{4,20},{20... | collective-permute-start | bytes 2457608 | tf_op jit(solution)/shard_map/ppermute | solution.py:195
  62.7 1.2 collective-permute-done.4.refs_5_
  63.9 1.3 slice_select_fusion
  65.2 1.3 collective-permute-start.6
  66.5 1.2 slice_select_fusion.1
  67.7 1.6 %collective-permute-start.5 = (bf16[48,4096]{1,0:T(8,128)(2,1)S(1)}, bf16[48,4096]{1,0:T(8,128)(2,1)S(1)}, u32[]{:S(2)}, u32[]{:S(2)}) collective-permute-start(bf16[48,4096]{1,0:T(8,128)(2,1)S(1)} %slice_select_fusion.1), channel_id=1, source_target_pairs={{4,0},{8,12},{5,1},{9,13},{6,2},{10,14},{7,3},{11,15},{20,16},{24,... | collective-permute-start | bytes 1179656 | tf_op jit(solution)/shard_map/ppermute | solution.py:175
  69.3 18.8 %shard_map.83 = (bf16[1536,48]{1,0:T(8,128)(2,1)S(1)}, bf16[1024,48]{1,0:T(8,128)(2,1)S(1)}, bf16[1536,6144]{1,0:T(8,128)(2,1)S(1)}, bf16[1024,4096]{1,0:T(8,128)(2,1)S(1)}) custom-call(bf16[1536,6144]{1,0:T(8,128)(2,1)} %bitcast.27, bf16[1024,4096]{1,0:T(8,128)(2,1)} %bitcast.29, f32[1536,1]{1,0:T(8,128)S(1)} %copy.24.refs_2_.refs_1_, ...), custom_call_target="tpu_custom_call" | custom-call | flops 1 | bytes 1 | tf_op jit(solution)/shard_map/pallas_call | solution.py:86
  88.1 6.4 %copy-done.2 = bf16[1536,6144]{1,0:T(8,128)(2,1)} copy-done((bf16[1536,6144]{1,0:T(8,128)(2,1)}, bf16[1536,6144]{1,0:T(8,128)(2,1)S(1)}, u32[]{:S(2)}) %copy-start.2) | copy-done | bytes 18874392
  94.5 1.1 shard_map.84.refs_4_
  95.6 2.3 %shard_map.85.refs_3_ = bf16[1024,48]{1,0:T(8,128)(2,1)S(1)} custom-call(bf16[1024,4096]{1,0:T(8,128)(2,1)S(1)} %get-tuple-element.24.refs_0_, f32[1024,1]{1,0:T(8,128)S(1)} %copy.25.refs_3_.refs_1_, bf16[48,4096]{1,0:T(8,128)(2,1)S(1)} %collective-permute-done.5.refs_2_), custom_call_target="tpu_custom_call" | custom-call | flops 1 | bytes 1 | tf_op jit(solution)/shard_map/pallas_call | solution.py:86
  98.0 6.4 %copy-done.3 = bf16[1536,6144]{1,0:T(8,128)(2,1)S(1)} copy-done((bf16[1536,6144]{1,0:T(8,128)(2,1)S(1)}, bf16[1536,6144]{1,0:T(8,128)(2,1)}, u32[]{:S(2)}) %copy-start.3) | copy-done | bytes 18874392
  104.3 5.0 %shard_map.86.refs_2_ = bf16[1536,48]{1,0:T(8,128)(2,1)S(1)} custom-call(bf16[1536,6144]{1,0:T(8,128)(2,1)S(1)} %copy-done.3, f32[1536,1]{1,0:T(8,128)S(1)} %copy.24.refs_2_.refs_1_, bf16[48,6144]{1,0:T(8,128)(2,1)S(1)} %collective-permute-done.6.refs_2_), custom_call_target="tpu_custom_call" | custom-call | flops 1 | bytes 1 | tf_op jit(solution)/shard_map/pallas_call | solution.py:86
  110.0 19.8 %all_to_all.10 = bf16[32,16,256]{2,1,0:T(8,128)(2,1)S(1)} all-to-all(bf16[32,16,256]{2,1,0:T(8,128)(2,1)S(1)} %bitcast.25), channel_id=1, replica_groups=mesh['parts'=2,'rows'=4,'layer'=4] {'parts','rows','layer'}, dimensions={0} | all-to-all | bytes 524288 | tf_op jit(solution)/shard_map/all_to_all | solution.py:250
  (41 shorter events, 3.4 us)
Async XLA Ops:
  0.0 1.4 %copy-start = (bf16[1,96,6144]{2,1,0:T(8,128)(2,1)S(1)}, bf16[1,96,6144]{2,1,0:T(8,128)(2,1)}, u32[]{:S(2)}) copy-start(bf16[1,96,6144]{2,1,0:T(8,128)(2,1)} %param.8) | copy-start | bytes 3538948
  0.0 9.5 %copy-start.9 = (bf16[1,40,4096]{2,1,0:T(8,128)(2,1)S(1)}, bf16[1,40,4096]{2,1,0:T(8,128)(2,1)}, u32[]{:S(2)}) copy-start(bf16[1,40,4096]{2,1,0:T(8,128)(2,1)} %param.11) | copy-start | bytes 983044
  1.4 8.5 %copy-start.8 = (bf16[1,40,6144]{2,1,0:T(8,128)(2,1)S(1)}, bf16[1,40,6144]{2,1,0:T(8,128)(2,1)}, u32[]{:S(2)}) copy-start(bf16[1,40,6144]{2,1,0:T(8,128)(2,1)} %param.10) | copy-start | bytes 1474564
  1.5 9.8 %copy-start.4 = (bf16[48,10240]{1,0:T(8,128)(2,1)}, bf16[48,10240]{1,0:T(8,128)(2,1)S(1)}, u32[]{:S(2)}) copy-start(bf16[48,10240]{1,0:T(8,128)(2,1)S(1)} %pad_maximum_fusion.refs_4_) | copy-start | bytes 2949124
  1.5 27.7 %collective-permute-start.1 = (bf16[48,10240]{1,0:T(8,128)(2,1)S(1)}, bf16[48,10240]{1,0:T(8,128)(2,1)}, u32[]{:S(2)}, u32[]{:S(2)}) collective-permute-start(bf16[48,10240]{1,0:T(8,128)(2,1)S(1)} %pad_maximum_fusion.refs_4_), channel_id=1, source_target_pairs={{4,0},{8,4},{12,8},{5,1},{9,5},{13,9},{6,2},{10,6},{14,10},{7,3},{... | collective-permute-start | bytes 2949128 | tf_op jit(solution)/shard_map/ppermute | solution.py:20
  3.0 27.7 %collective-permute-start.2 = (bf16[48,10240]{1,0:T(8,128)(2,1)S(1)}, bf16[48,10240]{1,0:T(8,128)(2,1)}, u32[]{:S(2)}, u32[]{:S(2)}) collective-permute-start(bf16[48,10240]{1,0:T(8,128)(2,1)S(1)} %pad_maximum_fusion.refs_4_), channel_id=1, source_target_pairs={{0,4},{4,8},{8,12},{1,5},{5,9},{9,13},{2,6},{6,10},{10,14},{3,7},{... | collective-permute-start | bytes 2949128 | tf_op jit(solution)/shard_map/ppermute | solution.py:20
  10.2 29.2 %copy-start.10 = (f32[1,1536]{1,0:T(1,128)S(1)}, f32[1,1536]{1,0:T(1,128)}, u32[]{:S(2)}) copy-start(f32[1,1536]{1,0:T(1,128)} %param.14) | copy-start | bytes 18436
  10.4 29.4 %copy-start.11 = (f32[1,1024]{1,0:T(1,128)S(1)}, f32[1,1024]{1,0:T(1,128)}, u32[]{:S(2)}) copy-start(f32[1,1024]{1,0:T(1,128)} %param.15) | copy-start | bytes 12292
  11.4 49.8 %all-to-all-start = ((bf16[4,40,2560]{2,1,0:T(8,128)(2,1)}), bf16[4,40,2560]{2,1,0:T(8,128)(2,1)S(1)}, u32[]{:S(2)}, u32[]{:S(2)}) async-start(bf16[4,40,2560]{2,1,0:T(8,128)(2,1)} %pad_maximum_fusion.1), calls=%async_computation | async-start | bytes 1638400 | tf_op jit(solution)/shard_map/all_to_all | solution.py:188
  29.3 33.4 %collective-permute-start.3 = (bf16[48,10240]{1,0:T(8,128)(2,1)}, bf16[48,10240]{1,0:T(8,128)(2,1)}, u32[]{:S(2)}, u32[]{:S(2)}) collective-permute-start(bf16[48,10240]{1,0:T(8,128)(2,1)} %collective-permute-done.1.refs_5_), channel_id=1, source_target_pairs={{4,0},{8,4},{12,8},{5,1},{9,5},{13,9},{6,2},{10,6},{14,10},{7,3},{... | collective-permute-start | bytes 2949128 | tf_op jit(solution)/shard_map/ppermute | solution.py:20
  30.7 33.2 %collective-permute-start.4 = (bf16[48,10240]{1,0:T(8,128)(2,1)}, bf16[48,10240]{1,0:T(8,128)(2,1)}, u32[]{:S(2)}, u32[]{:S(2)}) collective-permute-start(bf16[48,10240]{1,0:T(8,128)(2,1)} %collective-permute-done.2.refs_6_), channel_id=1, source_target_pairs={{0,4},{4,8},{8,12},{1,5},{5,9},{9,13},{2,6},{6,10},{10,14},{3,7},{... | collective-permute-start | bytes 2949128 | tf_op jit(solution)/shard_map/ppermute | solution.py:20
  40.0 1.2 copy-start.5
  60.3 0.9 copy-start.6
  61.2 33.3 %collective-permute-start = (bf16[160,2560]{1,0:T(8,128)(2,1)S(1)}, bf16[160,2560]{1,0:T(8,128)(2,1)S(1)}, u32[]{:S(2)}, u32[]{:S(2)}) collective-permute-start(bf16[160,2560]{1,0:T(8,128)(2,1)S(1)} %bitcast.22), channel_id=1, source_target_pairs={{0,16},{16,0},{1,17},{17,1},{2,18},{18,2},{3,19},{19,3},{4,20},{20... | collective-permute-start | bytes 2457608 | tf_op jit(solution)/shard_map/ppermute | solution.py:195
  65.2 32.7 %collective-permute-start.6 = (bf16[48,6144]{1,0:T(8,128)(2,1)S(1)}, bf16[48,6144]{1,0:T(8,128)(2,1)S(1)}, u32[]{:S(2)}, u32[]{:S(2)}) collective-permute-start(bf16[48,6144]{1,0:T(8,128)(2,1)S(1)} %slice_select_fusion), channel_id=1, source_target_pairs={{4,0},{8,12},{5,1},{9,13},{6,2},{10,14},{7,3},{11,15},{20,16},{24,... | collective-permute-start | bytes 1769480 | tf_op jit(solution)/shard_map/ppermute | solution.py:175
  67.7 26.9 %copy-start.7 = (bf16[1536,144]{1,0:T(8,128)(2,1)S(1)}, bf16[1536,144]{1,0:T(8,128)(2,1)}, u32[]{:S(2)}) copy-start(bf16[1536,144]{1,0:T(8,128)(2,1)} %copy-done.6) | copy-start | bytes 1327108
  67.7 28.0 %collective-permute-start.5 = (bf16[48,4096]{1,0:T(8,128)(2,1)S(1)}, bf16[48,4096]{1,0:T(8,128)(2,1)S(1)}, u32[]{:S(2)}, u32[]{:S(2)}) collective-permute-start(bf16[48,4096]{1,0:T(8,128)(2,1)S(1)} %slice_select_fusion.1), channel_id=1, source_target_pairs={{4,0},{8,12},{5,1},{9,13},{6,2},{10,14},{7,3},{11,15},{20,16},{24,... | collective-permute-start | bytes 1179656 | tf_op jit(solution)/shard_map/ppermute | solution.py:175
  88.1 6.5 %copy-start.2 = (bf16[1536,6144]{1,0:T(8,128)(2,1)}, bf16[1536,6144]{1,0:T(8,128)(2,1)S(1)}, u32[]{:S(2)}) copy-start(bf16[1536,6144]{1,0:T(8,128)(2,1)S(1)} %get-tuple-element.23.refs_0_) | copy-start | bytes 56623108
  98.0 6.4 %copy-start.3 = (bf16[1536,6144]{1,0:T(8,128)(2,1)S(1)}, bf16[1536,6144]{1,0:T(8,128)(2,1)}, u32[]{:S(2)}) copy-start(bf16[1536,6144]{1,0:T(8,128)(2,1)} %copy-done.2) | copy-start | bytes 56623108
  104.3 26.4 %copy-start.1 = (bf16[1,96,6144]{2,1,0:T(8,128)(2,1)S(1)}, bf16[1,96,6144]{2,1,0:T(8,128)(2,1)}, u32[]{:S(2)}) copy-start(bf16[1,96,6144]{2,1,0:T(8,128)(2,1)} %param.8) | copy-start | bytes 3538948

commit v8 on v7

--- a/solution.py
+++ b/solution.py
@@ -10,9 +10,9 @@
 
 damping = 0.1
 
-VMEM_LIMIT = 16 * 1024 * 1024
+MIB = 1024 * 1024
 TILE = 256
-AHEAD = 3
+AHEAD = 4
 
 
 def along(value, by):
@@ -53,7 +53,7 @@
 
         if not kept:
             for at in range(min(AHEAD, len(tiles))):
-                copy(at).start()
+                copy(at).start(priority=at % 2)
         for place, group in enumerate(groups):
             block_of = query_refs.pop(0)[...]
             for _ in group[1:]:
@@ -64,7 +64,7 @@
             if not kept:
                 copy(at).wait()
             if keep and at + AHEAD < len(tiles):
-                copy(at + AHEAD).start()
+                copy(at + AHEAD).start(priority=(at + AHEAD) % 2)
             rotated = lax.dot_general(
                 block(at)[...],
                 query[:, begins[side] : begins[side] + basis_refs[side].shape[1]],
@@ -74,7 +74,7 @@
             scale = 1.0 / (eigen_refs[side][where, :] + damping)
             out_refs[side][where, :] = (rotated * scale).astype(jnp.bfloat16)
             if not (keep or kept) and at + AHEAD < len(tiles):
-                copy(at + AHEAD).start()
+                copy(at + AHEAD).start(priority=(at + AHEAD) % 2)
 
     constrain = pltpu.with_memory_space_constraint
     in_vmem = pl.BlockSpec(memory_space=pltpu.VMEM)
@@ -90,9 +90,7 @@
         out_shape=[jax.ShapeDtypeStruct((basis.shape[0], held), jnp.bfloat16) for basis in bases]
         + ([pltpu.VMEM(basis.shape, basis.dtype) for basis in bases] if keep else []),
         scratch_shapes=scratch,
-        compiler_params=pltpu.CompilerParams(
-            vmem_limit_bytes=VMEM_LIMIT if keep or kept else VMEM_LIMIT + 8 * 1024 * 1024
-        ),
+        compiler_params=pltpu.CompilerParams(vmem_limit_bytes=(6 if keep or kept else 22) * MIB),
         cost_estimate=pl.CostEstimate(flops=1, bytes_accessed=1, transcendentals=0),
     )(
         *[constrain(basis, pltpu.VMEM if kept else pltpu.HBM) for basis in bases],
@@ -157,7 +155,7 @@
     return pl.pallas_call(
         kernel,
         out_shape=jax.ShapeDtypeStruct((parts, rows, rows, 2 * RANK, width), jnp.bfloat16),
-        compiler_params=pltpu.CompilerParams(vmem_limit_bytes=VMEM_LIMIT),
+        compiler_params=pltpu.CompilerParams(vmem_limit_bytes=6 * MIB),
         cost_estimate=pl.CostEstimate(flops=1, bytes_accessed=1, transcendentals=0),
     )(*operands, *([] if base is None else [base]))
 

time: 131 us -> 119 us (0.908)
  local copies, waits for them, and re-layouts: 17.8 us -> 4.97 us
  blocking collectives: 19.8 us -> 16.9 us
  waiting for transfers between devices: 15 us -> 17.9 us
    unnamed x24 -> x20, local copies, waits for them, and re-layouts: 15.2 us -> 2.35 us
    ppermute x2, waiting for transfers between devices: 0.01 us -> 2.96 us  [along_four(): lax.ppermute(jnp.where(row < 2, after_two[:, side], before_two[:, side]),...]
    all_to_all x1, blocking collectives: 19.8 us -> 16.9 us  [per_device(): lax.all_to_all(partial.reshape((parts * rows * layers,) + partial.shape[3...]
  transfers between devices with their start and end apart: 8 -> 8, of which waited for: 3 -> 4; matrix products, arithmetic and copies ran while one was open for 4% -> 4% of each run, Pallas kernels for 32% -> 36%
where the time goes in v8:
time: 119 us
  Pallas kernels  48 us (40%)
  starting transfers between devices  26.7 us (22%)
  waiting for transfers between devices  17.9 us (15%)
  blocking collectives  16.9 us (14%)
  local copies, waits for them, and re-layouts  4.97 us (4%)
  other arithmetic  4.26 us (4%)
    pallas_call x4, Pallas kernels, rotate(): pl.pallas_call(kernel, in_specs=[in_vmem if kept else pl.BlockSpec(memory...  46.2 us
    ppermute x4, starting transfers between devices, along(): lax.ppermute(value, 'rows', [(i, i + by) for i in range(size) if 0 <= i +...  18 us
    all_to_all x1, blocking collectives, per_device(): lax.all_to_all(partial.reshape((parts * rows * layers,) + partial.shape[3...  16.9 us
    ppermute x4, waiting for transfers between devices, along(): lax.ppermute(value, 'rows', [(i, i + by) for i in range(size) if 0 <= i +...  14.9 us
    all_to_all x1, starting transfers between devices, to_owners(): received = lax.all_to_all(by_owner, 'rows', 0, 0, tiled=True)  4.25 us
    ppermute x2, waiting for transfers between devices, along_four(): lax.ppermute(jnp.where(row < 2, after_two[:, side], before_two[:, side]),...  2.96 us
    ppermute x2, starting transfers between devices, along_four(): lax.ppermute(jnp.where(row < 2, after_two[:, side], before_two[:, side]),...  2.9 us
    select_n x2, other arithmetic, along_four(): jnp.where(row < 2, after_two[:, side], before_two[:, side])  2.47 us
  transfers between devices with their start and end apart: 8, of which 4 were waited for; matrix products, arithmetic and copies ran while one was open for 4% of the time, Pallas kernels for 36%

profile of v8, /device:TPU:0, one launch (start us, length us, event | category | flops | bytes accessed | tf_op | source)
XLA Modules:
  0.0 118.9 jit_solution(15409134902705807774)
XLA Ops:
  0.0 1.1 dynamic-slice_bitcast_fusion.1
  1.5 1.4 %collective-permute-start.1 = (bf16[48,10240]{1,0:T(8,128)(2,1)S(1)}, bf16[48,10240]{1,0:T(8,128)(2,1)}, u32[]{:S(2)}, u32[]{:S(2)}) collective-permute-start(bf16[48,10240]{1,0:T(8,128)(2,1)S(1)} %pad_maximum_fusion.refs_4_), channel_id=1, source_target_pairs={{4,0},{8,4},{12,8},{5,1},{9,5},{13,9},{6,2},{10,6},{14,10},{7,3},{... | collective-permute-start | bytes 2949128 | tf_op jit(solution)/shard_map/ppermute | solution.py:20
  3.0 6.6 %collective-permute-start.2 = (bf16[48,10240]{1,0:T(8,128)(2,1)S(1)}, bf16[48,10240]{1,0:T(8,128)(2,1)}, u32[]{:S(2)}, u32[]{:S(2)}) collective-permute-start(bf16[48,10240]{1,0:T(8,128)(2,1)S(1)} %pad_maximum_fusion.refs_4_), channel_id=1, source_target_pairs={{0,4},{4,8},{8,12},{1,5},{5,9},{9,13},{2,6},{6,10},{10,14},{3,7},{... | collective-permute-start | bytes 2949128 | tf_op jit(solution)/shard_map/ppermute | solution.py:20
  10.3 1.0 pad_maximum_fusion.1
  11.3 4.3 %all-to-all-start = ((bf16[4,40,2560]{2,1,0:T(8,128)(2,1)}), bf16[4,40,2560]{2,1,0:T(8,128)(2,1)S(1)}, u32[]{:S(2)}, u32[]{:S(2)}) async-start(bf16[4,40,2560]{2,1,0:T(8,128)(2,1)} %pad_maximum_fusion.1), calls=%async_computation | async-start | bytes 1638400 | tf_op jit(solution)/shard_map/all_to_all | solution.py:186
  15.6 13.7 %collective-permute-done.1.refs_5_ = bf16[48,10240]{1,0:T(8,128)(2,1)} collective-permute-done((bf16[48,10240]{1,0:T(8,128)(2,1)S(1)}, bf16[48,10240]{1,0:T(8,128)(2,1)}, u32[]{:S(2)}, u32[]{:S(2)}) %collective-permute-start.1) | collective-permute-done | bytes 983072 | tf_op jit(solution)/shard_map/ppermute | solution.py:20
  29.3 1.3 %collective-permute-start.3 = (bf16[48,10240]{1,0:T(8,128)(2,1)}, bf16[48,10240]{1,0:T(8,128)(2,1)}, u32[]{:S(2)}, u32[]{:S(2)}) collective-permute-start(bf16[48,10240]{1,0:T(8,128)(2,1)} %collective-permute-done.1.refs_5_), channel_id=1, source_target_pairs={{4,0},{8,4},{12,8},{5,1},{9,5},{13,9},{6,2},{10,6},{14,10},{7,3},{... | collective-permute-start | bytes 2949128 | tf_op jit(solution)/shard_map/ppermute | solution.py:20
  30.7 8.8 %collective-permute-start.4 = (bf16[48,10240]{1,0:T(8,128)(2,1)}, bf16[48,10240]{1,0:T(8,128)(2,1)}, u32[]{:S(2)}, u32[]{:S(2)}) collective-permute-start(bf16[48,10240]{1,0:T(8,128)(2,1)} %collective-permute-done.2.refs_6_), channel_id=1, source_target_pairs={{0,4},{4,8},{8,12},{1,5},{5,9},{9,13},{2,6},{6,10},{10,14},{3,7},{... | collective-permute-start | bytes 2949128 | tf_op jit(solution)/shard_map/ppermute | solution.py:20
  40.0 1.2 %copy-done.3 = bf16[48,10240]{1,0:T(8,128)(2,1)S(1)} copy-done((bf16[48,10240]{1,0:T(8,128)(2,1)S(1)}, bf16[48,10240]{1,0:T(8,128)(2,1)}, u32[]{:S(2)}) %copy-start.3) | copy-done | bytes 983064
  41.2 19.2 %shard_map.82 = (bf16[1536,144]{1,0:T(8,128)(2,1)S(1)}, bf16[1024,144]{1,0:T(8,128)(2,1)S(1)}) custom-call(bf16[1536,6144]{1,0:T(8,128)(2,1)} %bitcast.26, bf16[1024,4096]{1,0:T(8,128)(2,1)} %bitcast.28, f32[1536,1]{1,0:T(8,128)S(1)} %copy.24.refs_2_.refs_1_, f32[1024,1]{1,0:T(8,128)S(1)} %copy.25.refs_3_.refs_1_, bf16[48,10240]{1,0:T(8,128)(2,1)S(1)} %copy-done.3, ...), custom_call_target="tpu_custom_call" | custom-call | flops 1 | bytes 1 | tf_op jit(solution)/shard_map/pallas_call | solution.py:86
  60.4 0.9 copy-done.4
  61.2 1.5 %collective-permute-start = (bf16[160,2560]{1,0:T(8,128)(2,1)S(1)}, bf16[160,2560]{1,0:T(8,128)(2,1)S(1)}, u32[]{:S(2)}, u32[]{:S(2)}) collective-permute-start(bf16[160,2560]{1,0:T(8,128)(2,1)S(1)} %bitcast.22), channel_id=1, source_target_pairs={{0,16},{16,0},{1,17},{17,1},{2,18},{18,2},{3,19},{19,3},{4,20},{20... | collective-permute-start | bytes 2457608 | tf_op jit(solution)/shard_map/ppermute | solution.py:193
  62.8 1.1 collective-permute-done.4.refs_5_
  63.9 1.3 %slice_select_fusion = bf16[48,6144]{1,0:T(8,128)(2,1)S(1)} fusion(bf16[48,10240]{1,0:T(8,128)(2,1)} %collective-permute-done.4.refs_5_, bf16[48,10240]{1,0:T(8,128)(2,1)} %collective-permute-done.3.refs_4_, pred[]{:T(512)S(6)} %lt.9), kind=kLoop, calls=%fused_computation.2 | loop fusion | flops 294912 | bytes 1769473 | tf_op jit(solution)/shard_map/jit(_where)/select_n | solution.py:173
  65.2 1.3 %collective-permute-start.6 = (bf16[48,6144]{1,0:T(8,128)(2,1)S(1)}, bf16[48,6144]{1,0:T(8,128)(2,1)S(1)}, u32[]{:S(2)}, u32[]{:S(2)}) collective-permute-start(bf16[48,6144]{1,0:T(8,128)(2,1)S(1)} %slice_select_fusion), channel_id=1, source_target_pairs={{4,0},{8,12},{5,1},{9,13},{6,2},{10,14},{7,3},{11,15},{20,16},{24,... | collective-permute-start | bytes 1769480 | tf_op jit(solution)/shard_map/ppermute | solution.py:173
  66.5 1.2 slice_select_fusion.1
  67.7 1.6 %collective-permute-start.5 = (bf16[48,4096]{1,0:T(8,128)(2,1)S(1)}, bf16[48,4096]{1,0:T(8,128)(2,1)S(1)}, u32[]{:S(2)}, u32[]{:S(2)}) collective-permute-start(bf16[48,4096]{1,0:T(8,128)(2,1)S(1)} %slice_select_fusion.1), channel_id=1, source_target_pairs={{4,0},{8,12},{5,1},{9,13},{6,2},{10,14},{7,3},{11,15},{20,16},{24,... | collective-permute-start | bytes 1179656 | tf_op jit(solution)/shard_map/ppermute | solution.py:173
  69.3 19.8 %shard_map.83 = (bf16[1536,48]{1,0:T(8,128)(2,1)S(1)}, bf16[1024,48]{1,0:T(8,128)(2,1)S(1)}, bf16[1536,6144]{1,0:T(8,128)(2,1)S(1)}, bf16[1024,4096]{1,0:T(8,128)(2,1)S(1)}) custom-call(bf16[1536,6144]{1,0:T(8,128)(2,1)} %bitcast.27, bf16[1024,4096]{1,0:T(8,128)(2,1)} %bitcast.29, f32[1536,1]{1,0:T(8,128)S(1)} %copy.24.refs_2_.refs_1_, ...), custom_call_target="tpu_custom_call" | custom-call | flops 1 | bytes 1 | tf_op jit(solution)/shard_map/pallas_call | solution.py:86
  89.1 1.1 shard_map.84.refs_4_
  90.2 3.0 %collective-permute-done.5.refs_2_ = bf16[48,4096]{1,0:T(8,128)(2,1)S(1)} collective-permute-done((bf16[48,4096]{1,0:T(8,128)(2,1)S(1)}, bf16[48,4096]{1,0:T(8,128)(2,1)S(1)}, u32[]{:S(2)}, u32[]{:S(2)}) %collective-permute-start.5) | collective-permute-done | bytes 393248 | tf_op jit(solution)/shard_map/ppermute | solution.py:173
  93.2 2.3 %shard_map.85.refs_3_ = bf16[1024,48]{1,0:T(8,128)(2,1)S(1)} custom-call(bf16[1024,4096]{1,0:T(8,128)(2,1)S(1)} %get-tuple-element.24.refs_0_, f32[1024,1]{1,0:T(8,128)S(1)} %copy.25.refs_3_.refs_1_, bf16[48,4096]{1,0:T(8,128)(2,1)S(1)} %collective-permute-done.5.refs_2_), custom_call_target="tpu_custom_call" | custom-call | flops 1 | bytes 1 | tf_op jit(solution)/shard_map/pallas_call | solution.py:86
  95.5 5.0 %shard_map.86.refs_2_ = bf16[1536,48]{1,0:T(8,128)(2,1)S(1)} custom-call(bf16[1536,6144]{1,0:T(8,128)(2,1)S(1)} %get-tuple-element.23.refs_0_, f32[1536,1]{1,0:T(8,128)S(1)} %copy.24.refs_2_.refs_1_, bf16[48,6144]{1,0:T(8,128)(2,1)S(1)} %collective-permute-done.6.refs_2_), custom_call_target="tpu_custom_call" | custom-call | flops 1 | bytes 1 | tf_op jit(solution)/shard_map/pallas_call | solution.py:86
  101.2 16.9 %all_to_all.10 = bf16[32,16,256]{2,1,0:T(8,128)(2,1)S(1)} all-to-all(bf16[32,16,256]{2,1,0:T(8,128)(2,1)S(1)} %bitcast.25), channel_id=1, replica_groups=mesh['parts'=2,'rows'=4,'layer'=4] {'parts','rows','layer'}, dimensions={0} | all-to-all | bytes 524288 | tf_op jit(solution)/shard_map/all_to_all | solution.py:248
  118.3 0.7 reduce_sum.29
  (37 shorter events, 2.7 us)
Async XLA Ops:
  0.0 1.4 %copy-start = (bf16[1,96,6144]{2,1,0:T(8,128)(2,1)S(1)}, bf16[1,96,6144]{2,1,0:T(8,128)(2,1)}, u32[]{:S(2)}) copy-start(bf16[1,96,6144]{2,1,0:T(8,128)(2,1)} %param.8) | copy-start | bytes 3538948
  0.0 9.5 %copy-start.7 = (bf16[1,40,4096]{2,1,0:T(8,128)(2,1)S(1)}, bf16[1,40,4096]{2,1,0:T(8,128)(2,1)}, u32[]{:S(2)}) copy-start(bf16[1,40,4096]{2,1,0:T(8,128)(2,1)} %param.11) | copy-start | bytes 983044
  1.4 8.5 %copy-start.6 = (bf16[1,40,6144]{2,1,0:T(8,128)(2,1)S(1)}, bf16[1,40,6144]{2,1,0:T(8,128)(2,1)}, u32[]{:S(2)}) copy-start(bf16[1,40,6144]{2,1,0:T(8,128)(2,1)} %param.10) | copy-start | bytes 1474564
  1.5 9.8 %copy-start.2 = (bf16[48,10240]{1,0:T(8,128)(2,1)}, bf16[48,10240]{1,0:T(8,128)(2,1)S(1)}, u32[]{:S(2)}) copy-start(bf16[48,10240]{1,0:T(8,128)(2,1)S(1)} %pad_maximum_fusion.refs_4_) | copy-start | bytes 2949124
  1.5 27.7 %collective-permute-start.1 = (bf16[48,10240]{1,0:T(8,128)(2,1)S(1)}, bf16[48,10240]{1,0:T(8,128)(2,1)}, u32[]{:S(2)}, u32[]{:S(2)}) collective-permute-start(bf16[48,10240]{1,0:T(8,128)(2,1)S(1)} %pad_maximum_fusion.refs_4_), channel_id=1, source_target_pairs={{4,0},{8,4},{12,8},{5,1},{9,5},{13,9},{6,2},{10,6},{14,10},{7,3},{... | collective-permute-start | bytes 2949128 | tf_op jit(solution)/shard_map/ppermute | solution.py:20
  3.0 27.7 %collective-permute-start.2 = (bf16[48,10240]{1,0:T(8,128)(2,1)S(1)}, bf16[48,10240]{1,0:T(8,128)(2,1)}, u32[]{:S(2)}, u32[]{:S(2)}) collective-permute-start(bf16[48,10240]{1,0:T(8,128)(2,1)S(1)} %pad_maximum_fusion.refs_4_), channel_id=1, source_target_pairs={{0,4},{4,8},{8,12},{1,5},{5,9},{9,13},{2,6},{6,10},{10,14},{3,7},{... | collective-permute-start | bytes 2949128 | tf_op jit(solution)/shard_map/ppermute | solution.py:20
  10.2 29.2 %copy-start.8 = (f32[1,1536]{1,0:T(1,128)S(1)}, f32[1,1536]{1,0:T(1,128)}, u32[]{:S(2)}) copy-start(f32[1,1536]{1,0:T(1,128)} %param.14) | copy-start | bytes 18436
  10.3 29.4 %copy-start.9 = (f32[1,1024]{1,0:T(1,128)S(1)}, f32[1,1024]{1,0:T(1,128)}, u32[]{:S(2)}) copy-start(f32[1,1024]{1,0:T(1,128)} %param.15) | copy-start | bytes 12292
  11.3 49.9 %all-to-all-start = ((bf16[4,40,2560]{2,1,0:T(8,128)(2,1)}), bf16[4,40,2560]{2,1,0:T(8,128)(2,1)S(1)}, u32[]{:S(2)}, u32[]{:S(2)}) async-start(bf16[4,40,2560]{2,1,0:T(8,128)(2,1)} %pad_maximum_fusion.1), calls=%async_computation | async-start | bytes 1638400 | tf_op jit(solution)/shard_map/all_to_all | solution.py:186
  29.3 33.5 %collective-permute-start.3 = (bf16[48,10240]{1,0:T(8,128)(2,1)}, bf16[48,10240]{1,0:T(8,128)(2,1)}, u32[]{:S(2)}, u32[]{:S(2)}) collective-permute-start(bf16[48,10240]{1,0:T(8,128)(2,1)} %collective-permute-done.1.refs_5_), channel_id=1, source_target_pairs={{4,0},{8,4},{12,8},{5,1},{9,5},{13,9},{6,2},{10,6},{14,10},{7,3},{... | collective-permute-start | bytes 2949128 | tf_op jit(solution)/shard_map/ppermute | solution.py:20
  30.7 33.2 %collective-permute-start.4 = (bf16[48,10240]{1,0:T(8,128)(2,1)}, bf16[48,10240]{1,0:T(8,128)(2,1)}, u32[]{:S(2)}, u32[]{:S(2)}) collective-permute-start(bf16[48,10240]{1,0:T(8,128)(2,1)} %collective-permute-done.2.refs_6_), channel_id=1, source_target_pairs={{0,4},{4,8},{8,12},{1,5},{5,9},{9,13},{2,6},{6,10},{10,14},{3,7},{... | collective-permute-start | bytes 2949128 | tf_op jit(solution)/shard_map/ppermute | solution.py:20
  40.0 1.2 %copy-start.3 = (bf16[48,10240]{1,0:T(8,128)(2,1)S(1)}, bf16[48,10240]{1,0:T(8,128)(2,1)}, u32[]{:S(2)}) copy-start(bf16[48,10240]{1,0:T(8,128)(2,1)} %copy-done.2) | copy-start | bytes 2949124
  60.4 0.9 copy-start.4
  61.2 27.8 %collective-permute-start = (bf16[160,2560]{1,0:T(8,128)(2,1)S(1)}, bf16[160,2560]{1,0:T(8,128)(2,1)S(1)}, u32[]{:S(2)}, u32[]{:S(2)}) collective-permute-start(bf16[160,2560]{1,0:T(8,128)(2,1)S(1)} %bitcast.22), channel_id=1, source_target_pairs={{0,16},{16,0},{1,17},{17,1},{2,18},{18,2},{3,19},{19,3},{4,20},{20... | collective-permute-start | bytes 2457608 | tf_op jit(solution)/shard_map/ppermute | solution.py:193
  65.2 30.3 %collective-permute-start.6 = (bf16[48,6144]{1,0:T(8,128)(2,1)S(1)}, bf16[48,6144]{1,0:T(8,128)(2,1)S(1)}, u32[]{:S(2)}, u32[]{:S(2)}) collective-permute-start(bf16[48,6144]{1,0:T(8,128)(2,1)S(1)} %slice_select_fusion), channel_id=1, source_target_pairs={{4,0},{8,12},{5,1},{9,13},{6,2},{10,14},{7,3},{11,15},{20,16},{24,... | collective-permute-start | bytes 1769480 | tf_op jit(solution)/shard_map/ppermute | solution.py:173
  67.7 21.4 %copy-start.5 = (bf16[1536,144]{1,0:T(8,128)(2,1)S(1)}, bf16[1536,144]{1,0:T(8,128)(2,1)}, u32[]{:S(2)}) copy-start(bf16[1536,144]{1,0:T(8,128)(2,1)} %copy-done.4) | copy-start | bytes 1327108
  67.7 25.5 %collective-permute-start.5 = (bf16[48,4096]{1,0:T(8,128)(2,1)S(1)}, bf16[48,4096]{1,0:T(8,128)(2,1)S(1)}, u32[]{:S(2)}, u32[]{:S(2)}) collective-permute-start(bf16[48,4096]{1,0:T(8,128)(2,1)S(1)} %slice_select_fusion.1), channel_id=1, source_target_pairs={{4,0},{8,12},{5,1},{9,13},{6,2},{10,14},{7,3},{11,15},{20,16},{24,... | collective-permute-start | bytes 1179656 | tf_op jit(solution)/shard_map/ppermute | solution.py:173
  95.5 23.5 %copy-start.1 = (bf16[1,96,6144]{2,1,0:T(8,128)(2,1)S(1)}, bf16[1,96,6144]{2,1,0:T(8,128)(2,1)}, u32[]{:S(2)}) copy-start(bf16[1,96,6144]{2,1,0:T(8,128)(2,1)} %param.8) | copy-start | bytes 3538948

commit v9 on v8

--- a/solution.py
+++ b/solution.py
@@ -20,7 +20,7 @@
     return lax.ppermute(value, "rows", [(i, i + by) for i in range(size) if 0 <= i + by < size])
 
 
-def rotate(bases, eigens, queries, begins, keep=False, kept=False):
+def rotate(bases, eigens, queries, begins, kept):
     groups = [query if isinstance(query, tuple) else (query,) for query in queries]
     queries = [query for group in groups for query in group]
     columns = queries[0].shape[0]
@@ -32,9 +32,8 @@
         refs = list(refs)
         take = lambda many: [refs.pop(0) for _ in range(many)]
         basis_refs, eigen_refs, query_refs, out_refs = take(sides), take(sides), take(count), take(sides)
-        here_refs = take(sides) if keep else []
+        here_refs = [] if kept else take(sides)
         query = take(1)[0]
-        slots = None if keep or kept else take(1)[0]
         semaphores = None if kept else take(1)[0]
 
         def block(at):
@@ -42,9 +41,7 @@
             where = slice(tile * TILE, (tile + 1) * TILE)
             if kept:
                 return basis_refs[side].at[where]
-            if keep:
-                return here_refs[side].at[where]
-            return slots.at[at % AHEAD, :, : basis_refs[side].shape[1]]
+            return here_refs[side].at[where]
 
         def copy(at):
             side, tile = tiles[at]
@@ -63,7 +60,7 @@
             where = slice(tile * TILE, (tile + 1) * TILE)
             if not kept:
                 copy(at).wait()
-            if keep and at + AHEAD < len(tiles):
+            if not kept and at + AHEAD < len(tiles):
                 copy(at + AHEAD).start(priority=(at + AHEAD) % 2)
             rotated = lax.dot_general(
                 block(at)[...],
@@ -73,24 +70,20 @@
             )
             scale = 1.0 / (eigen_refs[side][where, :] + damping)
             out_refs[side][where, :] = (rotated * scale).astype(jnp.bfloat16)
-            if not (keep or kept) and at + AHEAD < len(tiles):
-                copy(at + AHEAD).start(priority=(at + AHEAD) % 2)
 
     constrain = pltpu.with_memory_space_constraint
     in_vmem = pl.BlockSpec(memory_space=pltpu.VMEM)
     scratch = [pltpu.VMEM((held, queries[0].shape[1]), jnp.bfloat16)]
-    if not (keep or kept):
-        scratch.append(pltpu.VMEM((AHEAD, TILE, max(basis.shape[1] for basis in bases)), jnp.bfloat16))
     if not kept:
         scratch.append(pltpu.SemaphoreType.DMA((len(tiles),)))
     return pl.pallas_call(
         kernel,
         in_specs=[in_vmem if kept else pl.BlockSpec(memory_space=pltpu.HBM)] * sides + [in_vmem] * (sides + count),
-        out_specs=[in_vmem] * (2 * sides if keep else sides),
+        out_specs=[in_vmem] * (sides if kept else 2 * sides),
         out_shape=[jax.ShapeDtypeStruct((basis.shape[0], held), jnp.bfloat16) for basis in bases]
-        + ([pltpu.VMEM(basis.shape, basis.dtype) for basis in bases] if keep else []),
+        + ([] if kept else [pltpu.VMEM(basis.shape, basis.dtype) for basis in bases]),
         scratch_shapes=scratch,
-        compiler_params=pltpu.CompilerParams(vmem_limit_bytes=(6 if keep or kept else 22) * MIB),
+        compiler_params=pltpu.CompilerParams(vmem_limit_bytes=8 * MIB),
         cost_estimate=pl.CostEstimate(flops=1, bytes_accessed=1, transcendentals=0),
     )(
         *[constrain(basis, pltpu.VMEM if kept else pltpu.HBM) for basis in bases],
@@ -144,7 +137,7 @@
                                 if fill:
                                     pieces.append(jnp.zeros((RANK, fill), jnp.float32))
                                 packed.append(jnp.concatenate(pieces, axis=1))
-                            out_ref[owner_part, owner, shard] = jnp.concatenate(packed, axis=0).astype(jnp.bfloat16)
+                            out_ref[owner_part, lax.rem(row + rows - owner, rows), shard] = jnp.concatenate(packed, axis=0).astype(jnp.bfloat16)
 
         if base is None:
             write()
@@ -164,27 +157,40 @@
     row = lax.axis_index("rows")
     depth = bases[0].shape[1]
     eigens = [eigen.reshape(-1, 1) for eigen in eigens]
-    after, before = along(query, -1), along(query, 1)
-    stores = to_parts(to_owners(by_owner))
-    after_two, before_two = along(after, -1), along(before, 1)
-    near = rotate(bases, eigens, [query, after, before], (0, depth))
+    after = lax.ppermute(query, "rows", [(1, 0), (2, 1), (3, 2)])
+    before = lax.ppermute(query, "rows", [(0, 1), (1, 2), (2, 3)])
+    sent = [lax.dynamic_index_in_dim(by_owner, (row + k) % 4, 0, False) for k in range(4)]
+    query, sent = lax.optimization_barrier((query, sent))
+    blocks = to_owners(sent)
+    *own, hidden_here, model_here = rotate(bases, eigens, [query], (0, depth), kept=False)
+    bases = [hidden_here, model_here]
+    own, bases, after, before = lax.optimization_barrier((own, bases, after, before))
+    after_two = lax.ppermute(after, "rows", [(1, 0), (2, 1)])
+    before_two = lax.ppermute(before, "rows", [(1, 2), (2, 3)])
+    near = rotate(bases, eigens, [after, before], (0, depth), kept=True)
+    near, blocks = lax.optimization_barrier((near, blocks))
+    stores = to_parts(jnp.concatenate(blocks, axis=0))
     near, after_two, before_two = lax.optimization_barrier((near, after_two, before_two))
-    three_model, three_hidden = (
-        lax.ppermute(jnp.where(row < 2, after_two[:, side], before_two[:, side]), "rows", [(1, 0), (2, 3)])
-        for side in (slice(depth, None), slice(0, depth))
-    )
-    *far, hidden_here, model_here = rotate(bases, eigens, [(after_two, before_two)], (0, depth), keep=True)
-    base = grams(stores, [near, far], [(0, 1, 3), (2,)])
-    base, three_model = lax.optimization_barrier((base, three_model))
-    last_model = rotate([model_here], eigens[1:], [three_model], (0,), kept=True)
-    last_model, three_hidden = lax.optimization_barrier((last_model, three_hidden))
-    last_hidden = rotate([hidden_here], eigens[:1], [three_hidden], (0,), kept=True)
+    two_hidden, two_model = (
+        jnp.where(row < 2, after_two[:, side], before_two[:, side]) for side in (slice(0, depth), slice(depth, None))
+    )
+    ends = [(1, 0), (2, 3)]
+    three_hidden = lax.ppermute(two_hidden, "rows", ends)
+    far = rotate(bases, eigens, [(after_two, before_two)], (0, depth), kept=True)
+    far, three_hidden, two_model = lax.optimization_barrier((far, three_hidden, two_model))
+    base = grams(stores, [own, near, far], [(0,), (1, 3), (2,)])
+    three_model = lax.ppermute(two_model, "rows", ends)
+    last_hidden = rotate(bases[:1], eigens[:1], [three_hidden], (0,), kept=True)
+    base, last_hidden, three_model = lax.optimization_barrier((base, last_hidden, three_model))
+    last_model = rotate(bases[1:], eigens[1:], [three_model], (0,), kept=True)
     return grams(stores, [last_hidden + last_model], [(3,)], base)
 
 
-def to_owners(by_owner):
-    received = lax.all_to_all(by_owner, "rows", 0, 0, tiled=True)
-    return received.reshape(-1, received.shape[-1])
+def to_owners(sent):
+    rows = lax.axis_size("rows")
+    return sent[:1] + [
+        lax.ppermute(sent[k], "rows", [(i, (i + k) % rows) for i in range(rows)]) for k in range(1, rows)
+    ]
 
 
 def to_parts(store):
@@ -227,7 +233,8 @@
     if rows == 4:
         partial = along_four(query, bases, eigens, by_owner)
     else:
-        stores = to_parts(to_owners(by_owner))
+        received = lax.all_to_all(by_owner, "rows", 0, 0, tiled=True)
+        stores = to_parts(received.reshape(rows * held, -1))
         every = lax.all_gather(query, "rows", axis=0, tiled=True)
         sides = []
         for basis, eigen, gathered, begin in zip(bases, eigens, (every[:, :depth], every[:, depth:]), (0, share)):

time: 119 us -> 116 us (0.975)
  local copies, waits for them, and re-layouts: 4.97 us -> 26.3 us
  waiting for transfers between devices: 17.9 us -> 9.52 us
  starting transfers between devices: 26.7 us -> 20.8 us
  Pallas kernels: 48 us -> 43.7 us
  blocking collectives: 16.9 us -> 13.1 us
  other arithmetic: 4.26 us -> 1.79 us
    unnamed x20 -> x29, local copies, waits for them, and re-layouts: 2.35 us -> 22.8 us
    ppermute x6 -> x9, waiting for transfers between devices: 17.9 us -> 9.51 us  [the longest x1 7.39 us: along_four(): three_hidden = lax.ppermute(two_hidden, 'rows', ends)]
    pallas_call x4 -> x5, Pallas kernels: 46.2 us -> 41.6 us  [rotate(): pl.pallas_call(kernel, in_specs=[in_vmem if kept else pl.BlockSpec(memory...]
    all_to_all x1 -> x0, starting transfers between devices: 4.25 us -> none  [to_owners(): received = lax.all_to_all(by_owner, 'rows', 0, 0, tiled=True)]
    all_to_all x1, blocking collectives: 16.9 us -> 13.1 us  [per_device(): lax.all_to_all(partial.reshape((parts * rows * layers,) + partial.shape[3...]
    select_n x2, other arithmetic: 2.47 us -> 0.11 us  [along_four(): jnp.where(row < 2, after_two[:, side], before_two[:, side])]
    ppermute x6 -> x9, starting transfers between devices: 20.9 us -> 19.2 us  [the longest x1 6.52 us: along_four(): before = lax.ppermute(query, 'rows', [(0, 1), (1, 2), (2, 3)])]
  transfers between devices with their start and end apart: 8 -> 10, of which waited for: 4 -> 2; matrix products, arithmetic and copies ran while one was open for 4% -> 4% of each run, Pallas kernels for 36% -> 35%
where the time goes in v9:
time: 116 us
  Pallas kernels  43.7 us (38%)
  local copies, waits for them, and re-layouts  26.3 us (23%)
  starting transfers between devices  20.8 us (18%)
  blocking collectives  13.1 us (11%)
  waiting for transfers between devices  9.52 us (8%)
  other arithmetic  1.79 us (2%)
    pallas_call x5, Pallas kernels, rotate(): pl.pallas_call(kernel, in_specs=[in_vmem if kept else pl.BlockSpec(memory...  41.6 us
    unnamed x29, local copies, waits for them, and re-layouts  22.8 us
    all_to_all x1, blocking collectives, per_device(): lax.all_to_all(partial.reshape((parts * rows * layers,) + partial.shape[3...  13.1 us
    ppermute x1, waiting for transfers between devices, along_four(): three_hidden = lax.ppermute(two_hidden, 'rows', ends)  7.39 us
    ppermute x1, starting transfers between devices, along_four(): before = lax.ppermute(query, 'rows', [(0, 1), (1, 2), (2, 3)])  6.52 us
    ppermute x3, starting transfers between devices, to_owners(): lax.ppermute(sent[k], 'rows', [(i, (i + k) % rows) for i in range(rows)])  6.02 us
  transfers between devices with their start and end apart: 10, of which 2 were waited for; matrix products, arithmetic and copies ran while one was open for 4% of the time, Pallas kernels for 35%

profile of v9, /device:TPU:0, one launch (start us, length us, event | category | flops | bytes accessed | tf_op | source)
XLA Modules:
  0.0 115.6 jit_solution(13519136834970543345)
XLA Ops:
  0.0 1.3 %copy-done = bf16[1,96,6144]{2,1,0:T(8,128)(2,1)S(1)} copy-done((bf16[1,96,6144]{2,1,0:T(8,128)(2,1)S(1)}, bf16[1,96,6144]{2,1,0:T(8,128)(2,1)}, u32[]{:S(2)}) %copy-start) | copy-done | bytes 1179672
  1.3 1.1 dynamic-slice_bitcast_fusion.1
  2.5 1.4 %collective-permute-start = (bf16[48,10240]{1,0:T(8,128)(2,1)S(1)}, bf16[48,10240]{1,0:T(8,128)(2,1)}, u32[]{:S(2)}, u32[]{:S(2)}) collective-permute-start(bf16[48,10240]{1,0:T(8,128)(2,1)S(1)} %pad_maximum_fusion.refs_4_), channel_id=1, source_target_pairs={{4,0},{8,4},{12,8},{5,1},{9,5},{13,9},{6,2},{10,6},{14,10},{7,3},{... | collective-permute-start | bytes 2949128 | tf_op jit(solution)/shard_map/ppermute | solution.py:160
  3.9 6.5 %collective-permute-start.1 = (bf16[48,10240]{1,0:T(8,128)(2,1)S(1)}, bf16[48,10240]{1,0:T(8,128)(2,1)}, u32[]{:S(2)}, u32[]{:S(2)}) collective-permute-start(bf16[48,10240]{1,0:T(8,128)(2,1)S(1)} %pad_maximum_fusion.refs_4_), channel_id=1, source_target_pairs={{0,4},{4,8},{8,12},{1,5},{5,9},{9,13},{2,6},{6,10},{10,14},{3,7},{... | collective-permute-start | bytes 2949128 | tf_op jit(solution)/shard_map/ppermute | solution.py:161
  12.2 1.1 collective-permute-start.2
  13.3 2.0 %collective-permute-start.3 = (bf16[40,2560]{1,0:T(8,128)(2,1)}, bf16[40,2560]{1,0:T(8,128)(2,1)}, u32[]{:S(2)}, u32[]{:S(2)}) collective-permute-start(bf16[40,2560]{1,0:T(8,128)(2,1)} %get-tuple-element.54), channel_id=1, source_target_pairs={{0,8},{4,12},{8,0},{12,4},{1,9},{5,13},{9,1},{13,5},{2,10},{6,14},... | collective-permute-start | bytes 614408 | tf_op jit(solution)/shard_map/ppermute | solution.py:192
  15.3 2.9 %collective-permute-start.4 = (bf16[40,2560]{1,0:T(8,128)(2,1)S(1)}, bf16[40,2560]{1,0:T(8,128)(2,1)}, u32[]{:S(2)}, u32[]{:S(2)}) collective-permute-start(bf16[40,2560]{1,0:T(8,128)(2,1)S(1)} %get-tuple-element.55), channel_id=1, source_target_pairs={{0,12},{4,0},{8,4},{12,8},{1,13},{5,1},{9,5},{13,9},{2,14},{6,2},{... | collective-permute-start | bytes 614408 | tf_op jit(solution)/shard_map/ppermute | solution.py:192
  18.7 18.3 %shard_map.82 = (bf16[1536,48]{1,0:T(8,128)(2,1)S(1)}, bf16[1024,48]{1,0:T(8,128)(2,1)S(1)}, bf16[1536,6144]{1,0:T(8,128)(2,1)S(1)}, bf16[1024,4096]{1,0:T(8,128)(2,1)S(1)}) custom-call(bf16[1536,6144]{1,0:T(8,128)(2,1)} %bitcast.32, bf16[1024,4096]{1,0:T(8,128)(2,1)} %bitcast.33, f32[1536,1]{1,0:T(8,128)S(1)} %copy.24.refs_2_.refs_1_, ...), custom_call_target="tpu_custom_call" | custom-call | flops 1 | bytes 1 | tf_op jit(solution)/shard_map/pallas_call | solution.py:79
  37.0 6.5 %copy-done.2 = bf16[1536,6144]{1,0:T(8,128)(2,1)} copy-done((bf16[1536,6144]{1,0:T(8,128)(2,1)}, bf16[1536,6144]{1,0:T(8,128)(2,1)S(1)}, u32[]{:S(2)}) %copy-start.2) | copy-done | bytes 18874392
  43.5 3.4 %copy-done.5 = bf16[1024,4096]{1,0:T(8,128)(2,1)} copy-done((bf16[1024,4096]{1,0:T(8,128)(2,1)}, bf16[1024,4096]{1,0:T(8,128)(2,1)S(1)}, u32[]{:S(2)}) %copy-start.5) | copy-done | bytes 8388632
  46.9 1.3 %collective-permute-start.6 = (bf16[48,10240]{1,0:T(8,128)(2,1)}, bf16[48,10240]{1,0:T(8,128)(2,1)S(1)}, u32[]{:S(2)}, u32[]{:S(2)}) collective-permute-start(bf16[48,10240]{1,0:T(8,128)(2,1)} %collective-permute-done.refs_4_), channel_id=1, source_target_pairs={{4,0},{8,4},{5,1},{9,5},{6,2},{10,6},{7,3},{11,7},{20,16},{24,20},... | collective-permute-start | bytes 2949128 | tf_op jit(solution)/shard_map/ppermute | solution.py:168
  49.1 6.4 %copy-done.3 = bf16[1536,6144]{1,0:T(8,128)(2,1)S(1)} copy-done((bf16[1536,6144]{1,0:T(8,128)(2,1)S(1)}, bf16[1536,6144]{1,0:T(8,128)(2,1)}, u32[]{:S(2)}) %copy-start.3) | copy-done | bytes 18874392
  55.4 3.4 %copy-done.6 = bf16[1024,4096]{1,0:T(8,128)(2,1)S(1)} copy-done((bf16[1024,4096]{1,0:T(8,128)(2,1)S(1)}, bf16[1024,4096]{1,0:T(8,128)(2,1)}, u32[]{:S(2)}) %copy-start.6) | copy-done | bytes 8388632
  58.8 8.8 %shard_map.83 = (bf16[1536,96]{1,0:T(8,128)(2,1)S(1)}, bf16[1024,96]{1,0:T(8,128)(2,1)S(1)}) custom-call(bf16[1536,6144]{1,0:T(8,128)(2,1)S(1)} %copy-done.3, bf16[1024,4096]{1,0:T(8,128)(2,1)S(1)} %copy-done.6, f32[1536,1]{1,0:T(8,128)S(1)} %copy.24.refs_2_.refs_1_, f32[1024,1]{1,0:T(8,128)S(1)} %copy.25.refs_3_.refs_1_, ...), custom_call_target="tpu_custom_call" | custom-call | flops 1 | bytes 1 | tf_op jit(solution)/shard_map/pallas_call | solution.py:79
  70.6 1.6 %collective-permute-start.5 = (bf16[160,2560]{1,0:T(8,128)(2,1)S(1)}, bf16[160,2560]{1,0:T(8,128)(2,1)S(1)}, u32[]{:S(2)}, u32[]{:S(2)}) collective-permute-start(bf16[160,2560]{1,0:T(8,128)(2,1)S(1)} %constant_dynamic-update-slice_fusion.refs_0_), channel_id=1, source_target_pairs={{0,16},{16,0},{1,17},{17,1},{2,18},{18,2},{3,19},{19,3},{4,20},{20... | collective-permute-start | bytes 2457608 | tf_op jit(solution)/shard_map/ppermute | solution.py:199
  72.2 1.3 %collective-permute-start.8 = (bf16[48,6144]{1,0:T(8,128)(2,1)S(1)}, bf16[48,6144]{1,0:T(8,128)(2,1)S(1)}, u32[]{:S(2)}, u32[]{:S(2)}) collective-permute-start(bf16[48,6144]{1,0:T(8,128)(2,1)S(1)} %slice_select_fusion), channel_id=1, source_target_pairs={{4,0},{8,12},{5,1},{9,13},{6,2},{10,14},{7,3},{11,15},{20,16},{24,... | collective-permute-start | bytes 1769480 | tf_op jit(solution)/shard_map/ppermute | solution.py:178
  73.6 7.2 %shard_map.84 = (bf16[1536,48]{1,0:T(8,128)(2,1)S(1)}, bf16[1024,48]{1,0:T(8,128)(2,1)S(1)}) custom-call(bf16[1536,6144]{1,0:T(8,128)(2,1)S(1)} %copy-done.4, bf16[1024,4096]{1,0:T(8,128)(2,1)S(1)} %copy-done.6, f32[1536,1]{1,0:T(8,128)S(1)} %copy.24.refs_2_.refs_1_, f32[1024,1]{1,0:T(8,128)S(1)} %copy.25.refs_3_.refs_1_, ...), custom_call_target="tpu_custom_call" | custom-call | flops 1 | bytes 1 | tf_op jit(solution)/shard_map/pallas_call | solution.py:79
  80.7 7.4 %collective-permute-done.8.refs_2_ = bf16[48,6144]{1,0:T(8,128)(2,1)S(1)} collective-permute-done((bf16[48,6144]{1,0:T(8,128)(2,1)S(1)}, bf16[48,6144]{1,0:T(8,128)(2,1)S(1)}, u32[]{:S(2)}, u32[]{:S(2)}) %collective-permute-start.8) | collective-permute-done | bytes 589856 | tf_op jit(solution)/shard_map/ppermute | solution.py:178
  88.1 1.8 %collective-permute-start.9 = (bf16[48,4096]{1,0:T(8,128)(2,1)S(1)}, bf16[48,4096]{1,0:T(8,128)(2,1)S(1)}, u32[]{:S(2)}, u32[]{:S(2)}) collective-permute-start(bf16[48,4096]{1,0:T(8,128)(2,1)S(1)} %slice_select_fusion.1), channel_id=1, source_target_pairs={{4,0},{8,12},{5,1},{9,13},{6,2},{10,14},{7,3},{11,15},{20,16},{24,... | collective-permute-start | bytes 1179656 | tf_op jit(solution)/shard_map/ppermute | solution.py:182
  89.9 5.0 %shard_map.86.refs_2_ = bf16[1536,48]{1,0:T(8,128)(2,1)S(1)} custom-call(bf16[1536,6144]{1,0:T(8,128)(2,1)S(1)} %copy-done.4, f32[1536,1]{1,0:T(8,128)S(1)} %copy.24.refs_2_.refs_1_, bf16[48,6144]{1,0:T(8,128)(2,1)S(1)} %collective-permute-done.8.refs_2_), custom_call_target="tpu_custom_call" | custom-call | flops 1 | bytes 1 | tf_op jit(solution)/shard_map/pallas_call | solution.py:79
  94.9 1.5 %shard_map.85.refs_4_ = bf16[2,4,4,16,256]{4,3,2,1,0:T(8,128)(2,1)S(1)} custom-call(bf16[160,2560]{1,0:T(8,128)(2,1)S(1)} %constant_dynamic-update-slice_fusion.refs_0_, bf16[160,2560]{1,0:T(8,128)(2,1)S(1)} %collective-permute-done.5.refs_1_, bf16[1536,48]{1,0:T(8,128)(2,1)S(1)} %get-tuple-element.60.refs_2_, ...), custom_call_target="tpu_custom_call" | custom-call | flops 1 | bytes 1 | tf_op jit(solution)/shard_map/pallas_call | solution.py:148
  96.4 2.1 %collective-permute-done.9.refs_2_ = bf16[48,4096]{1,0:T(8,128)(2,1)S(1)} collective-permute-done((bf16[48,4096]{1,0:T(8,128)(2,1)S(1)}, bf16[48,4096]{1,0:T(8,128)(2,1)S(1)}, u32[]{:S(2)}, u32[]{:S(2)}) %collective-permute-start.9) | collective-permute-done | bytes 393248 | tf_op jit(solution)/shard_map/ppermute | solution.py:182
  98.5 2.3 %shard_map.87.refs_3_ = bf16[1024,48]{1,0:T(8,128)(2,1)S(1)} custom-call(bf16[1024,4096]{1,0:T(8,128)(2,1)S(1)} %bitcast.30, f32[1024,1]{1,0:T(8,128)S(1)} %copy.25.refs_3_.refs_1_, bf16[48,4096]{1,0:T(8,128)(2,1)S(1)} %collective-permute-done.9.refs_2_), custom_call_target="tpu_custom_call" | custom-call | flops 1 | bytes 1 | tf_op jit(solution)/shard_map/pallas_call | solution.py:79
  101.5 13.1 %all_to_all.5 = bf16[32,16,256]{2,1,0:T(8,128)(2,1)S(1)} all-to-all(bf16[32,16,256]{2,1,0:T(8,128)(2,1)S(1)} %bitcast.31), channel_id=1, replica_groups=mesh['parts'=2,'rows'=4,'layer'=4] {'parts','rows','layer'}, dimensions={0} | all-to-all | bytes 524288 | tf_op jit(solution)/shard_map/all_to_all | solution.py:255
  (53 shorter events, 7.8 us)
Async XLA Ops:
  0.0 1.3 %copy-start = (bf16[1,96,6144]{2,1,0:T(8,128)(2,1)S(1)}, bf16[1,96,6144]{2,1,0:T(8,128)(2,1)}, u32[]{:S(2)}) copy-start(bf16[1,96,6144]{2,1,0:T(8,128)(2,1)} %param.8) | copy-start | bytes 3538948
  1.3 9.2 %copy-start.7 = (bf16[1,40,6144]{2,1,0:T(8,128)(2,1)S(1)}, bf16[1,40,6144]{2,1,0:T(8,128)(2,1)}, u32[]{:S(2)}) copy-start(bf16[1,40,6144]{2,1,0:T(8,128)(2,1)} %param.10) | copy-start | bytes 1474564
  2.4 8.5 %copy-start.8 = (bf16[1,40,4096]{2,1,0:T(8,128)(2,1)S(1)}, bf16[1,40,4096]{2,1,0:T(8,128)(2,1)}, u32[]{:S(2)}) copy-start(bf16[1,40,4096]{2,1,0:T(8,128)(2,1)} %param.11) | copy-start | bytes 983044
  2.5 44.4 %collective-permute-start = (bf16[48,10240]{1,0:T(8,128)(2,1)S(1)}, bf16[48,10240]{1,0:T(8,128)(2,1)}, u32[]{:S(2)}, u32[]{:S(2)}) collective-permute-start(bf16[48,10240]{1,0:T(8,128)(2,1)S(1)} %pad_maximum_fusion.refs_4_), channel_id=1, source_target_pairs={{4,0},{8,4},{12,8},{5,1},{9,5},{13,9},{6,2},{10,6},{14,10},{7,3},{... | collective-permute-start | bytes 2949128 | tf_op jit(solution)/shard_map/ppermute | solution.py:160
  3.9 43.0 %collective-permute-start.1 = (bf16[48,10240]{1,0:T(8,128)(2,1)S(1)}, bf16[48,10240]{1,0:T(8,128)(2,1)}, u32[]{:S(2)}, u32[]{:S(2)}) collective-permute-start(bf16[48,10240]{1,0:T(8,128)(2,1)S(1)} %pad_maximum_fusion.refs_4_), channel_id=1, source_target_pairs={{0,4},{4,8},{8,12},{1,5},{5,9},{9,13},{2,6},{6,10},{10,14},{3,7},{... | collective-permute-start | bytes 2949128 | tf_op jit(solution)/shard_map/ppermute | solution.py:161
  10.8 7.4 %copy-start.9 = (f32[1,1536]{1,0:T(1,128)S(1)}, f32[1,1536]{1,0:T(1,128)}, u32[]{:S(2)}) copy-start(f32[1,1536]{1,0:T(1,128)} %param.14) | copy-start | bytes 18436
  10.9 7.6 %copy-start.10 = (f32[1,1024]{1,0:T(1,128)S(1)}, f32[1,1024]{1,0:T(1,128)}, u32[]{:S(2)}) copy-start(f32[1,1024]{1,0:T(1,128)} %param.15) | copy-start | bytes 12292
  12.2 55.5 %collective-permute-start.2 = (bf16[40,2560]{1,0:T(8,128)(2,1)}, bf16[40,2560]{1,0:T(8,128)(2,1)}, u32[]{:S(2)}, u32[]{:S(2)}) collective-permute-start(bf16[40,2560]{1,0:T(8,128)(2,1)} %get-tuple-element.53), channel_id=1, source_target_pairs={{0,4},{4,8},{8,12},{12,0},{1,5},{5,9},{9,13},{13,1},{2,6},{6,10},{... | collective-permute-start | bytes 614408 | tf_op jit(solution)/shard_map/ppermute | solution.py:192
  13.3 54.4 %collective-permute-start.3 = (bf16[40,2560]{1,0:T(8,128)(2,1)}, bf16[40,2560]{1,0:T(8,128)(2,1)}, u32[]{:S(2)}, u32[]{:S(2)}) collective-permute-start(bf16[40,2560]{1,0:T(8,128)(2,1)} %get-tuple-element.54), channel_id=1, source_target_pairs={{0,8},{4,12},{8,0},{12,4},{1,9},{5,13},{9,1},{13,5},{2,10},{6,14},... | collective-permute-start | bytes 614408 | tf_op jit(solution)/shard_map/ppermute | solution.py:192
  15.3 52.4 %collective-permute-start.4 = (bf16[40,2560]{1,0:T(8,128)(2,1)S(1)}, bf16[40,2560]{1,0:T(8,128)(2,1)}, u32[]{:S(2)}, u32[]{:S(2)}) collective-permute-start(bf16[40,2560]{1,0:T(8,128)(2,1)S(1)} %get-tuple-element.55), channel_id=1, source_target_pairs={{0,12},{4,0},{8,4},{12,8},{1,13},{5,1},{9,5},{13,9},{2,14},{6,2},{... | collective-permute-start | bytes 614408 | tf_op jit(solution)/shard_map/ppermute | solution.py:192
  37.0 6.5 %copy-start.2 = (bf16[1536,6144]{1,0:T(8,128)(2,1)}, bf16[1536,6144]{1,0:T(8,128)(2,1)S(1)}, u32[]{:S(2)}) copy-start(bf16[1536,6144]{1,0:T(8,128)(2,1)S(1)} %get-tuple-element.46.refs_0_) | copy-start | bytes 56623108
  43.5 3.4 %copy-start.5 = (bf16[1024,4096]{1,0:T(8,128)(2,1)}, bf16[1024,4096]{1,0:T(8,128)(2,1)S(1)}, u32[]{:S(2)}) copy-start(bf16[1024,4096]{1,0:T(8,128)(2,1)S(1)} %get-tuple-element.47.refs_1_.refs_0_) | copy-start | bytes 25165828
  46.9 25.3 %collective-permute-start.6 = (bf16[48,10240]{1,0:T(8,128)(2,1)}, bf16[48,10240]{1,0:T(8,128)(2,1)S(1)}, u32[]{:S(2)}, u32[]{:S(2)}) collective-permute-start(bf16[48,10240]{1,0:T(8,128)(2,1)} %collective-permute-done.refs_4_), channel_id=1, source_target_pairs={{4,0},{8,4},{5,1},{9,5},{6,2},{10,6},{7,3},{11,7},{20,16},{24,20},... | collective-permute-start | bytes 2949128 | tf_op jit(solution)/shard_map/ppermute | solution.py:168
  48.2 24.0 %collective-permute-start.7 = (bf16[48,10240]{1,0:T(8,128)(2,1)}, bf16[48,10240]{1,0:T(8,128)(2,1)S(1)}, u32[]{:S(2)}, u32[]{:S(2)}) collective-permute-start(bf16[48,10240]{1,0:T(8,128)(2,1)} %collective-permute-done.1.refs_5_), channel_id=1, source_target_pairs={{4,8},{8,12},{5,9},{9,13},{6,10},{10,14},{7,11},{11,15},{20,24},{2... | collective-permute-start | bytes 2949128 | tf_op jit(solution)/shard_map/ppermute | solution.py:169
  49.1 6.4 %copy-start.3 = (bf16[1536,6144]{1,0:T(8,128)(2,1)S(1)}, bf16[1536,6144]{1,0:T(8,128)(2,1)}, u32[]{:S(2)}) copy-start(bf16[1536,6144]{1,0:T(8,128)(2,1)} %copy-done.2) | copy-start | bytes 56623108
  55.4 3.4 %copy-start.6 = (bf16[1024,4096]{1,0:T(8,128)(2,1)S(1)}, bf16[1024,4096]{1,0:T(8,128)(2,1)}, u32[]{:S(2)}) copy-start(bf16[1024,4096]{1,0:T(8,128)(2,1)} %copy-done.5) | copy-start | bytes 25165828
  58.8 14.7 %copy-start.4 = (bf16[1536,6144]{1,0:T(8,128)(2,1)S(1)}, bf16[1536,6144]{1,0:T(8,128)(2,1)}, u32[]{:S(2)}) copy-start(bf16[1536,6144]{1,0:T(8,128)(2,1)} %copy-done.2) | copy-start | bytes 56623108
  70.6 24.4 %collective-permute-start.5 = (bf16[160,2560]{1,0:T(8,128)(2,1)S(1)}, bf16[160,2560]{1,0:T(8,128)(2,1)S(1)}, u32[]{:S(2)}, u32[]{:S(2)}) collective-permute-start(bf16[160,2560]{1,0:T(8,128)(2,1)S(1)} %constant_dynamic-update-slice_fusion.refs_0_), channel_id=1, source_target_pairs={{0,16},{16,0},{1,17},{17,1},{2,18},{18,2},{3,19},{19,3},{4,20},{20... | collective-permute-start | bytes 2457608 | tf_op jit(solution)/shard_map/ppermute | solution.py:199
  72.2 15.9 %collective-permute-start.8 = (bf16[48,6144]{1,0:T(8,128)(2,1)S(1)}, bf16[48,6144]{1,0:T(8,128)(2,1)S(1)}, u32[]{:S(2)}, u32[]{:S(2)}) collective-permute-start(bf16[48,6144]{1,0:T(8,128)(2,1)S(1)} %slice_select_fusion), channel_id=1, source_target_pairs={{4,0},{8,12},{5,1},{9,13},{6,2},{10,14},{7,3},{11,15},{20,16},{24,... | collective-permute-start | bytes 1769480 | tf_op jit(solution)/shard_map/ppermute | solution.py:178
  88.1 10.4 %slice-start = ((s8[8388608]{0:T(1024)(128)(4,1)}), s8[4194304]{0:T(1024)(128)(4,1)S(1)}, s32[]{:S(2)}) async-start(s8[8388608]{0:T(1024)(128)(4,1)} %bitcast.29), calls=%async_computation.1 | async-start | bytes 8388608
  88.1 10.4 %slice-start.1 = ((s8[8388608]{0:T(1024)(128)(4,1)}), s8[4194304]{0:T(1024)(128)(4,1)S(1)}, s32[]{:S(2)}) async-start(s8[8388608]{0:T(1024)(128)(4,1)} %bitcast.29), calls=%async_computation.2 | async-start | bytes 8388608
  88.1 10.4 %collective-permute-start.9 = (bf16[48,4096]{1,0:T(8,128)(2,1)S(1)}, bf16[48,4096]{1,0:T(8,128)(2,1)S(1)}, u32[]{:S(2)}, u32[]{:S(2)}) collective-permute-start(bf16[48,4096]{1,0:T(8,128)(2,1)S(1)} %slice_select_fusion.1), channel_id=1, source_target_pairs={{4,0},{8,12},{5,1},{9,13},{6,2},{10,14},{7,3},{11,15},{20,16},{24,... | collective-permute-start | bytes 1179656 | tf_op jit(solution)/shard_map/ppermute | solution.py:182
  98.5 17.0 %copy-start.1 = (bf16[1,96,6144]{2,1,0:T(8,128)(2,1)S(1)}, bf16[1,96,6144]{2,1,0:T(8,128)(2,1)}, u32[]{:S(2)}) copy-start(bf16[1,96,6144]{2,1,0:T(8,128)(2,1)} %param.8) | copy-start | bytes 3538948

commit v10 on v9

--- a/solution.py
+++ b/solution.py
@@ -164,7 +164,7 @@
     blocks = to_owners(sent)
     *own, hidden_here, model_here = rotate(bases, eigens, [query], (0, depth), kept=False)
     bases = [hidden_here, model_here]
-    own, bases, after, before = lax.optimization_barrier((own, bases, after, before))
+    own, after, before = lax.optimization_barrier((own, after, before))
     after_two = lax.ppermute(after, "rows", [(1, 0), (2, 1)])
     before_two = lax.ppermute(before, "rows", [(1, 2), (2, 3)])
     near = rotate(bases, eigens, [after, before], (0, depth), kept=True)

time: 116 us -> 116 us (level)
  no operation moved by 1% of the time
where the time goes in v10:
time: 116 us
  Pallas kernels  43.7 us (38%)
  local copies, waits for them, and re-layouts  26.3 us (23%)
  starting transfers between devices  20.8 us (18%)
  blocking collectives  13.1 us (11%)
  waiting for transfers between devices  9.52 us (8%)
  other arithmetic  1.79 us (2%)
    pallas_call x5, Pallas kernels, rotate(): pl.pallas_call(kernel, in_specs=[in_vmem if kept else pl.BlockSpec(memory...  41.6 us
    unnamed x29, local copies, waits for them, and re-layouts  22.8 us
    all_to_all x1, blocking collectives, per_device(): lax.all_to_all(partial.reshape((parts * rows * layers,) + partial.shape[3...  13.1 us
    ppermute x1, waiting for transfers between devices, along_four(): three_hidden = lax.ppermute(two_hidden, 'rows', ends)  7.39 us
    ppermute x1, starting transfers between devices, along_four(): before = lax.ppermute(query, 'rows', [(0, 1), (1, 2), (2, 3)])  6.52 us
    ppermute x3, starting transfers between devices, to_owners(): lax.ppermute(sent[k], 'rows', [(i, (i + k) % rows) for i in range(rows)])  6.02 us
  transfers between devices with their start and end apart: 10, of which 2 were waited for; matrix products, arithmetic and copies ran while one was open for 4% of the time, Pallas kernels for 35%

profile of v10, /device:TPU:0, one launch (start us, length us, event | category | flops | bytes accessed | tf_op | source)
XLA Modules:
  0.0 115.6 jit_solution(13519136834970543345)
XLA Ops:
  0.0 1.3 %copy-done = bf16[1,96,6144]{2,1,0:T(8,128)(2,1)S(1)} copy-done((bf16[1,96,6144]{2,1,0:T(8,128)(2,1)S(1)}, bf16[1,96,6144]{2,1,0:T(8,128)(2,1)}, u32[]{:S(2)}) %copy-start) | copy-done | bytes 1179672
  1.3 1.1 dynamic-slice_bitcast_fusion.1
  2.5 1.4 %collective-permute-start = (bf16[48,10240]{1,0:T(8,128)(2,1)S(1)}, bf16[48,10240]{1,0:T(8,128)(2,1)}, u32[]{:S(2)}, u32[]{:S(2)}) collective-permute-start(bf16[48,10240]{1,0:T(8,128)(2,1)S(1)} %pad_maximum_fusion.refs_4_), channel_id=1, source_target_pairs={{4,0},{8,4},{12,8},{5,1},{9,5},{13,9},{6,2},{10,6},{14,10},{7,3},{... | collective-permute-start | bytes 2949128 | tf_op jit(solution)/shard_map/ppermute | solution.py:160
  3.9 6.5 %collective-permute-start.1 = (bf16[48,10240]{1,0:T(8,128)(2,1)S(1)}, bf16[48,10240]{1,0:T(8,128)(2,1)}, u32[]{:S(2)}, u32[]{:S(2)}) collective-permute-start(bf16[48,10240]{1,0:T(8,128)(2,1)S(1)} %pad_maximum_fusion.refs_4_), channel_id=1, source_target_pairs={{0,4},{4,8},{8,12},{1,5},{5,9},{9,13},{2,6},{6,10},{10,14},{3,7},{... | collective-permute-start | bytes 2949128 | tf_op jit(solution)/shard_map/ppermute | solution.py:161
  12.2 1.1 collective-permute-start.2
  13.3 2.0 %collective-permute-start.3 = (bf16[40,2560]{1,0:T(8,128)(2,1)}, bf16[40,2560]{1,0:T(8,128)(2,1)}, u32[]{:S(2)}, u32[]{:S(2)}) collective-permute-start(bf16[40,2560]{1,0:T(8,128)(2,1)} %get-tuple-element.50), channel_id=1, source_target_pairs={{0,8},{4,12},{8,0},{12,4},{1,9},{5,13},{9,1},{13,5},{2,10},{6,14},... | collective-permute-start | bytes 614408 | tf_op jit(solution)/shard_map/ppermute | solution.py:192
  15.3 2.9 %collective-permute-start.4 = (bf16[40,2560]{1,0:T(8,128)(2,1)S(1)}, bf16[40,2560]{1,0:T(8,128)(2,1)}, u32[]{:S(2)}, u32[]{:S(2)}) collective-permute-start(bf16[40,2560]{1,0:T(8,128)(2,1)S(1)} %get-tuple-element.51), channel_id=1, source_target_pairs={{0,12},{4,0},{8,4},{12,8},{1,13},{5,1},{9,5},{13,9},{2,14},{6,2},{... | collective-permute-start | bytes 614408 | tf_op jit(solution)/shard_map/ppermute | solution.py:192
  18.7 18.3 %shard_map.82 = (bf16[1536,48]{1,0:T(8,128)(2,1)S(1)}, bf16[1024,48]{1,0:T(8,128)(2,1)S(1)}, bf16[1536,6144]{1,0:T(8,128)(2,1)S(1)}, bf16[1024,4096]{1,0:T(8,128)(2,1)S(1)}) custom-call(bf16[1536,6144]{1,0:T(8,128)(2,1)} %bitcast.32, bf16[1024,4096]{1,0:T(8,128)(2,1)} %bitcast.33, f32[1536,1]{1,0:T(8,128)S(1)} %copy.24.refs_2_.refs_1_, ...), custom_call_target="tpu_custom_call" | custom-call | flops 1 | bytes 1 | tf_op jit(solution)/shard_map/pallas_call | solution.py:79
  37.0 6.5 %copy-done.2 = bf16[1536,6144]{1,0:T(8,128)(2,1)} copy-done((bf16[1536,6144]{1,0:T(8,128)(2,1)}, bf16[1536,6144]{1,0:T(8,128)(2,1)S(1)}, u32[]{:S(2)}) %copy-start.2) | copy-done | bytes 18874392
  43.5 3.4 %copy-done.5 = bf16[1024,4096]{1,0:T(8,128)(2,1)} copy-done((bf16[1024,4096]{1,0:T(8,128)(2,1)}, bf16[1024,4096]{1,0:T(8,128)(2,1)S(1)}, u32[]{:S(2)}) %copy-start.5) | copy-done | bytes 8388632
  46.9 1.3 %collective-permute-start.6 = (bf16[48,10240]{1,0:T(8,128)(2,1)}, bf16[48,10240]{1,0:T(8,128)(2,1)S(1)}, u32[]{:S(2)}, u32[]{:S(2)}) collective-permute-start(bf16[48,10240]{1,0:T(8,128)(2,1)} %collective-permute-done.refs_4_), channel_id=1, source_target_pairs={{4,0},{8,4},{5,1},{9,5},{6,2},{10,6},{7,3},{11,7},{20,16},{24,20},... | collective-permute-start | bytes 2949128 | tf_op jit(solution)/shard_map/ppermute | solution.py:168
  49.1 6.4 %copy-done.3 = bf16[1536,6144]{1,0:T(8,128)(2,1)S(1)} copy-done((bf16[1536,6144]{1,0:T(8,128)(2,1)S(1)}, bf16[1536,6144]{1,0:T(8,128)(2,1)}, u32[]{:S(2)}) %copy-start.3) | copy-done | bytes 18874392
  55.4 3.4 %copy-done.6 = bf16[1024,4096]{1,0:T(8,128)(2,1)S(1)} copy-done((bf16[1024,4096]{1,0:T(8,128)(2,1)S(1)}, bf16[1024,4096]{1,0:T(8,128)(2,1)}, u32[]{:S(2)}) %copy-start.6) | copy-done | bytes 8388632
  58.8 8.8 %shard_map.83 = (bf16[1536,96]{1,0:T(8,128)(2,1)S(1)}, bf16[1024,96]{1,0:T(8,128)(2,1)S(1)}) custom-call(bf16[1536,6144]{1,0:T(8,128)(2,1)S(1)} %copy-done.3, bf16[1024,4096]{1,0:T(8,128)(2,1)S(1)} %copy-done.6, f32[1536,1]{1,0:T(8,128)S(1)} %copy.24.refs_2_.refs_1_, f32[1024,1]{1,0:T(8,128)S(1)} %copy.25.refs_3_.refs_1_, ...), custom_call_target="tpu_custom_call" | custom-call | flops 1 | bytes 1 | tf_op jit(solution)/shard_map/pallas_call | solution.py:79
  70.6 1.6 %collective-permute-start.5 = (bf16[160,2560]{1,0:T(8,128)(2,1)S(1)}, bf16[160,2560]{1,0:T(8,128)(2,1)S(1)}, u32[]{:S(2)}, u32[]{:S(2)}) collective-permute-start(bf16[160,2560]{1,0:T(8,128)(2,1)S(1)} %constant_dynamic-update-slice_fusion.refs_0_), channel_id=1, source_target_pairs={{0,16},{16,0},{1,17},{17,1},{2,18},{18,2},{3,19},{19,3},{4,20},{20... | collective-permute-start | bytes 2457608 | tf_op jit(solution)/shard_map/ppermute | solution.py:199
  72.2 1.3 %collective-permute-start.8 = (bf16[48,6144]{1,0:T(8,128)(2,1)S(1)}, bf16[48,6144]{1,0:T(8,128)(2,1)S(1)}, u32[]{:S(2)}, u32[]{:S(2)}) collective-permute-start(bf16[48,6144]{1,0:T(8,128)(2,1)S(1)} %slice_select_fusion), channel_id=1, source_target_pairs={{4,0},{8,12},{5,1},{9,13},{6,2},{10,14},{7,3},{11,15},{20,16},{24,... | collective-permute-start | bytes 1769480 | tf_op jit(solution)/shard_map/ppermute | solution.py:178
  73.6 7.2 %shard_map.84 = (bf16[1536,48]{1,0:T(8,128)(2,1)S(1)}, bf16[1024,48]{1,0:T(8,128)(2,1)S(1)}) custom-call(bf16[1536,6144]{1,0:T(8,128)(2,1)S(1)} %copy-done.4, bf16[1024,4096]{1,0:T(8,128)(2,1)S(1)} %copy-done.6, f32[1536,1]{1,0:T(8,128)S(1)} %copy.24.refs_2_.refs_1_, f32[1024,1]{1,0:T(8,128)S(1)} %copy.25.refs_3_.refs_1_, ...), custom_call_target="tpu_custom_call" | custom-call | flops 1 | bytes 1 | tf_op jit(solution)/shard_map/pallas_call | solution.py:79
  80.7 7.4 %collective-permute-done.8.refs_2_ = bf16[48,6144]{1,0:T(8,128)(2,1)S(1)} collective-permute-done((bf16[48,6144]{1,0:T(8,128)(2,1)S(1)}, bf16[48,6144]{1,0:T(8,128)(2,1)S(1)}, u32[]{:S(2)}, u32[]{:S(2)}) %collective-permute-start.8) | collective-permute-done | bytes 589856 | tf_op jit(solution)/shard_map/ppermute | solution.py:178
  88.1 1.8 %collective-permute-start.9 = (bf16[48,4096]{1,0:T(8,128)(2,1)S(1)}, bf16[48,4096]{1,0:T(8,128)(2,1)S(1)}, u32[]{:S(2)}, u32[]{:S(2)}) collective-permute-start(bf16[48,4096]{1,0:T(8,128)(2,1)S(1)} %slice_select_fusion.1), channel_id=1, source_target_pairs={{4,0},{8,12},{5,1},{9,13},{6,2},{10,14},{7,3},{11,15},{20,16},{24,... | collective-permute-start | bytes 1179656 | tf_op jit(solution)/shard_map/ppermute | solution.py:182
  89.9 5.0 %shard_map.86.refs_2_ = bf16[1536,48]{1,0:T(8,128)(2,1)S(1)} custom-call(bf16[1536,6144]{1,0:T(8,128)(2,1)S(1)} %copy-done.4, f32[1536,1]{1,0:T(8,128)S(1)} %copy.24.refs_2_.refs_1_, bf16[48,6144]{1,0:T(8,128)(2,1)S(1)} %collective-permute-done.8.refs_2_), custom_call_target="tpu_custom_call" | custom-call | flops 1 | bytes 1 | tf_op jit(solution)/shard_map/pallas_call | solution.py:79
  94.9 1.5 %shard_map.85.refs_4_ = bf16[2,4,4,16,256]{4,3,2,1,0:T(8,128)(2,1)S(1)} custom-call(bf16[160,2560]{1,0:T(8,128)(2,1)S(1)} %constant_dynamic-update-slice_fusion.refs_0_, bf16[160,2560]{1,0:T(8,128)(2,1)S(1)} %collective-permute-done.5.refs_1_, bf16[1536,48]{1,0:T(8,128)(2,1)S(1)} %get-tuple-element.56.refs_2_, ...), custom_call_target="tpu_custom_call" | custom-call | flops 1 | bytes 1 | tf_op jit(solution)/shard_map/pallas_call | solution.py:148
  96.4 2.1 %collective-permute-done.9.refs_2_ = bf16[48,4096]{1,0:T(8,128)(2,1)S(1)} collective-permute-done((bf16[48,4096]{1,0:T(8,128)(2,1)S(1)}, bf16[48,4096]{1,0:T(8,128)(2,1)S(1)}, u32[]{:S(2)}, u32[]{:S(2)}) %collective-permute-start.9) | collective-permute-done | bytes 393248 | tf_op jit(solution)/shard_map/ppermute | solution.py:182
  98.5 2.3 %shard_map.87.refs_3_ = bf16[1024,48]{1,0:T(8,128)(2,1)S(1)} custom-call(bf16[1024,4096]{1,0:T(8,128)(2,1)S(1)} %bitcast.30, f32[1024,1]{1,0:T(8,128)S(1)} %copy.25.refs_3_.refs_1_, bf16[48,4096]{1,0:T(8,128)(2,1)S(1)} %collective-permute-done.9.refs_2_), custom_call_target="tpu_custom_call" | custom-call | flops 1 | bytes 1 | tf_op jit(solution)/shard_map/pallas_call | solution.py:79
  101.5 13.1 %all_to_all.5 = bf16[32,16,256]{2,1,0:T(8,128)(2,1)S(1)} all-to-all(bf16[32,16,256]{2,1,0:T(8,128)(2,1)S(1)} %bitcast.31), channel_id=1, replica_groups=mesh['parts'=2,'rows'=4,'layer'=4] {'parts','rows','layer'}, dimensions={0} | all-to-all | bytes 524288 | tf_op jit(solution)/shard_map/all_to_all | solution.py:255
  (53 shorter events, 7.8 us)
Async XLA Ops:
  0.0 1.3 %copy-start = (bf16[1,96,6144]{2,1,0:T(8,128)(2,1)S(1)}, bf16[1,96,6144]{2,1,0:T(8,128)(2,1)}, u32[]{:S(2)}) copy-start(bf16[1,96,6144]{2,1,0:T(8,128)(2,1)} %param.8) | copy-start | bytes 3538948
  1.3 9.2 %copy-start.7 = (bf16[1,40,6144]{2,1,0:T(8,128)(2,1)S(1)}, bf16[1,40,6144]{2,1,0:T(8,128)(2,1)}, u32[]{:S(2)}) copy-start(bf16[1,40,6144]{2,1,0:T(8,128)(2,1)} %param.10) | copy-start | bytes 1474564
  2.4 8.5 %copy-start.8 = (bf16[1,40,4096]{2,1,0:T(8,128)(2,1)S(1)}, bf16[1,40,4096]{2,1,0:T(8,128)(2,1)}, u32[]{:S(2)}) copy-start(bf16[1,40,4096]{2,1,0:T(8,128)(2,1)} %param.11) | copy-start | bytes 983044
  2.5 44.4 %collective-permute-start = (bf16[48,10240]{1,0:T(8,128)(2,1)S(1)}, bf16[48,10240]{1,0:T(8,128)(2,1)}, u32[]{:S(2)}, u32[]{:S(2)}) collective-permute-start(bf16[48,10240]{1,0:T(8,128)(2,1)S(1)} %pad_maximum_fusion.refs_4_), channel_id=1, source_target_pairs={{4,0},{8,4},{12,8},{5,1},{9,5},{13,9},{6,2},{10,6},{14,10},{7,3},{... | collective-permute-start | bytes 2949128 | tf_op jit(solution)/shard_map/ppermute | solution.py:160
  3.9 43.0 %collective-permute-start.1 = (bf16[48,10240]{1,0:T(8,128)(2,1)S(1)}, bf16[48,10240]{1,0:T(8,128)(2,1)}, u32[]{:S(2)}, u32[]{:S(2)}) collective-permute-start(bf16[48,10240]{1,0:T(8,128)(2,1)S(1)} %pad_maximum_fusion.refs_4_), channel_id=1, source_target_pairs={{0,4},{4,8},{8,12},{1,5},{5,9},{9,13},{2,6},{6,10},{10,14},{3,7},{... | collective-permute-start | bytes 2949128 | tf_op jit(solution)/shard_map/ppermute | solution.py:161
  10.8 7.4 %copy-start.9 = (f32[1,1536]{1,0:T(1,128)S(1)}, f32[1,1536]{1,0:T(1,128)}, u32[]{:S(2)}) copy-start(f32[1,1536]{1,0:T(1,128)} %param.14) | copy-start | bytes 18436
  10.9 7.6 %copy-start.10 = (f32[1,1024]{1,0:T(1,128)S(1)}, f32[1,1024]{1,0:T(1,128)}, u32[]{:S(2)}) copy-start(f32[1,1024]{1,0:T(1,128)} %param.15) | copy-start | bytes 12292
  12.2 55.5 %collective-permute-start.2 = (bf16[40,2560]{1,0:T(8,128)(2,1)}, bf16[40,2560]{1,0:T(8,128)(2,1)}, u32[]{:S(2)}, u32[]{:S(2)}) collective-permute-start(bf16[40,2560]{1,0:T(8,128)(2,1)} %get-tuple-element.49), channel_id=1, source_target_pairs={{0,4},{4,8},{8,12},{12,0},{1,5},{5,9},{9,13},{13,1},{2,6},{6,10},{... | collective-permute-start | bytes 614408 | tf_op jit(solution)/shard_map/ppermute | solution.py:192
  13.3 54.4 %collective-permute-start.3 = (bf16[40,2560]{1,0:T(8,128)(2,1)}, bf16[40,2560]{1,0:T(8,128)(2,1)}, u32[]{:S(2)}, u32[]{:S(2)}) collective-permute-start(bf16[40,2560]{1,0:T(8,128)(2,1)} %get-tuple-element.50), channel_id=1, source_target_pairs={{0,8},{4,12},{8,0},{12,4},{1,9},{5,13},{9,1},{13,5},{2,10},{6,14},... | collective-permute-start | bytes 614408 | tf_op jit(solution)/shard_map/ppermute | solution.py:192
  15.3 52.4 %collective-permute-start.4 = (bf16[40,2560]{1,0:T(8,128)(2,1)S(1)}, bf16[40,2560]{1,0:T(8,128)(2,1)}, u32[]{:S(2)}, u32[]{:S(2)}) collective-permute-start(bf16[40,2560]{1,0:T(8,128)(2,1)S(1)} %get-tuple-element.51), channel_id=1, source_target_pairs={{0,12},{4,0},{8,4},{12,8},{1,13},{5,1},{9,5},{13,9},{2,14},{6,2},{... | collective-permute-start | bytes 614408 | tf_op jit(solution)/shard_map/ppermute | solution.py:192
  37.0 6.5 %copy-start.2 = (bf16[1536,6144]{1,0:T(8,128)(2,1)}, bf16[1536,6144]{1,0:T(8,128)(2,1)S(1)}, u32[]{:S(2)}) copy-start(bf16[1536,6144]{1,0:T(8,128)(2,1)S(1)} %get-tuple-element.40.refs_0_) | copy-start | bytes 56623108
  43.5 3.4 %copy-start.5 = (bf16[1024,4096]{1,0:T(8,128)(2,1)}, bf16[1024,4096]{1,0:T(8,128)(2,1)S(1)}, u32[]{:S(2)}) copy-start(bf16[1024,4096]{1,0:T(8,128)(2,1)S(1)} %get-tuple-element.41.refs_1_.refs_0_) | copy-start | bytes 25165828
  46.9 25.3 %collective-permute-start.6 = (bf16[48,10240]{1,0:T(8,128)(2,1)}, bf16[48,10240]{1,0:T(8,128)(2,1)S(1)}, u32[]{:S(2)}, u32[]{:S(2)}) collective-permute-start(bf16[48,10240]{1,0:T(8,128)(2,1)} %collective-permute-done.refs_4_), channel_id=1, source_target_pairs={{4,0},{8,4},{5,1},{9,5},{6,2},{10,6},{7,3},{11,7},{20,16},{24,20},... | collective-permute-start | bytes 2949128 | tf_op jit(solution)/shard_map/ppermute | solution.py:168
  48.2 24.0 %collective-permute-start.7 = (bf16[48,10240]{1,0:T(8,128)(2,1)}, bf16[48,10240]{1,0:T(8,128)(2,1)S(1)}, u32[]{:S(2)}, u32[]{:S(2)}) collective-permute-start(bf16[48,10240]{1,0:T(8,128)(2,1)} %collective-permute-done.1.refs_5_), channel_id=1, source_target_pairs={{4,8},{8,12},{5,9},{9,13},{6,10},{10,14},{7,11},{11,15},{20,24},{2... | collective-permute-start | bytes 2949128 | tf_op jit(solution)/shard_map/ppermute | solution.py:169
  49.1 6.4 %copy-start.3 = (bf16[1536,6144]{1,0:T(8,128)(2,1)S(1)}, bf16[1536,6144]{1,0:T(8,128)(2,1)}, u32[]{:S(2)}) copy-start(bf16[1536,6144]{1,0:T(8,128)(2,1)} %copy-done.2) | copy-start | bytes 56623108
  55.4 3.4 %copy-start.6 = (bf16[1024,4096]{1,0:T(8,128)(2,1)S(1)}, bf16[1024,4096]{1,0:T(8,128)(2,1)}, u32[]{:S(2)}) copy-start(bf16[1024,4096]{1,0:T(8,128)(2,1)} %copy-done.5) | copy-start | bytes 25165828
  58.8 14.7 %copy-start.4 = (bf16[1536,6144]{1,0:T(8,128)(2,1)S(1)}, bf16[1536,6144]{1,0:T(8,128)(2,1)}, u32[]{:S(2)}) copy-start(bf16[1536,6144]{1,0:T(8,128)(2,1)} %copy-done.2) | copy-start | bytes 56623108
  70.6 24.4 %collective-permute-start.5 = (bf16[160,2560]{1,0:T(8,128)(2,1)S(1)}, bf16[160,2560]{1,0:T(8,128)(2,1)S(1)}, u32[]{:S(2)}, u32[]{:S(2)}) collective-permute-start(bf16[160,2560]{1,0:T(8,128)(2,1)S(1)} %constant_dynamic-update-slice_fusion.refs_0_), channel_id=1, source_target_pairs={{0,16},{16,0},{1,17},{17,1},{2,18},{18,2},{3,19},{19,3},{4,20},{20... | collective-permute-start | bytes 2457608 | tf_op jit(solution)/shard_map/ppermute | solution.py:199
  72.2 15.9 %collective-permute-start.8 = (bf16[48,6144]{1,0:T(8,128)(2,1)S(1)}, bf16[48,6144]{1,0:T(8,128)(2,1)S(1)}, u32[]{:S(2)}, u32[]{:S(2)}) collective-permute-start(bf16[48,6144]{1,0:T(8,128)(2,1)S(1)} %slice_select_fusion), channel_id=1, source_target_pairs={{4,0},{8,12},{5,1},{9,13},{6,2},{10,14},{7,3},{11,15},{20,16},{24,... | collective-permute-start | bytes 1769480 | tf_op jit(solution)/shard_map/ppermute | solution.py:178
  88.1 10.4 %slice-start = ((s8[8388608]{0:T(1024)(128)(4,1)}), s8[4194304]{0:T(1024)(128)(4,1)S(1)}, s32[]{:S(2)}) async-start(s8[8388608]{0:T(1024)(128)(4,1)} %bitcast.29), calls=%async_computation.1 | async-start | bytes 8388608
  88.1 10.4 %slice-start.1 = ((s8[8388608]{0:T(1024)(128)(4,1)}), s8[4194304]{0:T(1024)(128)(4,1)S(1)}, s32[]{:S(2)}) async-start(s8[8388608]{0:T(1024)(128)(4,1)} %bitcast.29), calls=%async_computation.2 | async-start | bytes 8388608
  88.1 10.4 %collective-permute-start.9 = (bf16[48,4096]{1,0:T(8,128)(2,1)S(1)}, bf16[48,4096]{1,0:T(8,128)(2,1)S(1)}, u32[]{:S(2)}, u32[]{:S(2)}) collective-permute-start(bf16[48,4096]{1,0:T(8,128)(2,1)S(1)} %slice_select_fusion.1), channel_id=1, source_target_pairs={{4,0},{8,12},{5,1},{9,13},{6,2},{10,14},{7,3},{11,15},{20,16},{24,... | collective-permute-start | bytes 1179656 | tf_op jit(solution)/shard_map/ppermute | solution.py:182
  98.5 17.0 %copy-start.1 = (bf16[1,96,6144]{2,1,0:T(8,128)(2,1)S(1)}, bf16[1,96,6144]{2,1,0:T(8,128)(2,1)}, u32[]{:S(2)}) copy-start(bf16[1,96,6144]{2,1,0:T(8,128)(2,1)} %param.8) | copy-start | bytes 3538948

commit v11 on v10

--- a/solution.py
+++ b/solution.py
@@ -1,3 +1,5 @@
+import typing
+
 import jax
 import jax.numpy as jnp
 from jax import lax
@@ -12,7 +14,6 @@
 
 MIB = 1024 * 1024
 TILE = 256
-AHEAD = 4
 
 
 def along(value, by):
@@ -20,75 +21,89 @@
     return lax.ppermute(value, "rows", [(i, i + by) for i in range(size) if 0 <= i + by < size])
 
 
-def rotate(bases, eigens, queries, begins, kept):
+class Side(typing.NamedTuple):
+    basis: jax.Array
+    eigen: jax.Array
+    begin: int | None
+    here: bool = False
+    keep: bool = False
+
+
+def rotate(queries, sides):
     groups = [query if isinstance(query, tuple) else (query,) for query in queries]
     queries = [query for group in groups for query in group]
     columns = queries[0].shape[0]
     held = columns * len(groups)
-    count, sides = len(queries), len(bases)
-    tiles = [(side, tile) for side in range(sides) for tile in range(bases[side].shape[0] // TILE)]
+    worked = [side for side in sides if side.begin is not None]
+    kept = [side for side in sides if side.keep]
+    tiles = [(side, tile) for side in sides for tile in range(side.basis.shape[0] // TILE)]
+    copied = [at for at, (side, _) in enumerate(tiles) if not side.here]
 
     def kernel(*refs):
         refs = list(refs)
-        take = lambda many: [refs.pop(0) for _ in range(many)]
-        basis_refs, eigen_refs, query_refs, out_refs = take(sides), take(sides), take(count), take(sides)
-        here_refs = [] if kept else take(sides)
-        query = take(1)[0]
-        semaphores = None if kept else take(1)[0]
-
-        def block(at):
-            side, tile = tiles[at]
-            where = slice(tile * TILE, (tile + 1) * TILE)
-            if kept:
-                return basis_refs[side].at[where]
-            return here_refs[side].at[where]
+        take = lambda sides: {id(side): refs.pop(0) for side in sides}
+        basis_refs, eigen_refs = take(sides), take(worked)
+        query_refs = [refs.pop(0) for _ in queries]
+        out_refs, here_refs, query = take(worked), take(kept), refs.pop(0)
+        here_refs.update(take([side for side in sides if not (side.here or side.keep)]))
+
+        def rows_of(at):
+            return slice(tiles[at][1] * TILE, (tiles[at][1] + 1) * TILE)
 
         def copy(at):
-            side, tile = tiles[at]
-            where = slice(tile * TILE, (tile + 1) * TILE)
-            return pltpu.make_async_copy(basis_refs[side].at[where], block(at), semaphores.at[at])
-
-        if not kept:
-            for at in range(min(AHEAD, len(tiles))):
-                copy(at).start(priority=at % 2)
+            side = tiles[at][0]
+            where = rows_of(at)
+            return pltpu.make_async_copy(
+                basis_refs[id(side)].at[where], here_refs[id(side)].at[where], refs[0].at[copied.index(at)]
+            )
+
+        for at in copied:
+            copy(at).start()
         for place, group in enumerate(groups):
-            block_of = query_refs.pop(0)[...]
+            block = query_refs.pop(0)[...]
             for _ in group[1:]:
-                block_of = block_of + query_refs.pop(0)[...]
-            query[place * columns : (place + 1) * columns, :] = block_of
-        for at, (side, tile) in enumerate(tiles):
-            where = slice(tile * TILE, (tile + 1) * TILE)
-            if not kept:
+                block = block + query_refs.pop(0)[...]
+            query[place * columns : (place + 1) * columns, :] = block
+        for at, (side, _) in enumerate(tiles):
+            where = rows_of(at)
+            if at in copied:
                 copy(at).wait()
-            if not kept and at + AHEAD < len(tiles):
-                copy(at + AHEAD).start(priority=(at + AHEAD) % 2)
+            if side.begin is None:
+                continue
+            basis_ref = (basis_refs if side.here else here_refs)[id(side)]
             rotated = lax.dot_general(
-                block(at)[...],
-                query[:, begins[side] : begins[side] + basis_refs[side].shape[1]],
+                basis_ref[where, :],
+                query[:, side.begin : side.begin + side.basis.shape[1]],
                 (((1,), (1,)), ((), ())),
                 preferred_element_type=jnp.float32,
             )
-            scale = 1.0 / (eigen_refs[side][where, :] + damping)
-            out_refs[side][where, :] = (rotated * scale).astype(jnp.bfloat16)
+            scale = 1.0 / (eigen_refs[id(side)][where, :] + damping)
+            out_refs[id(side)][where, :] = (rotated * scale).astype(jnp.bfloat16)
+
+    def here(side):
+        return pltpu.VMEM(side.basis.shape, side.basis.dtype)
 
     constrain = pltpu.with_memory_space_constraint
     in_vmem = pl.BlockSpec(memory_space=pltpu.VMEM)
-    scratch = [pltpu.VMEM((held, queries[0].shape[1]), jnp.bfloat16)]
-    if not kept:
-        scratch.append(pltpu.SemaphoreType.DMA((len(tiles),)))
+    operands = [constrain(side.basis, pltpu.VMEM if side.here else pltpu.HBM) for side in sides]
+    operands += [constrain(one, pltpu.VMEM) for one in (*[side.eigen for side in worked], *queries)]
+    streamed = [side for side in sides if not (side.here or side.keep)]
     return pl.pallas_call(
         kernel,
-        in_specs=[in_vmem if kept else pl.BlockSpec(memory_space=pltpu.HBM)] * sides + [in_vmem] * (sides + count),
-        out_specs=[in_vmem] * (sides if kept else 2 * sides),
-        out_shape=[jax.ShapeDtypeStruct((basis.shape[0], held), jnp.bfloat16) for basis in bases]
-        + ([] if kept else [pltpu.VMEM(basis.shape, basis.dtype) for basis in bases]),
-        scratch_shapes=scratch,
-        compiler_params=pltpu.CompilerParams(vmem_limit_bytes=8 * MIB),
+        in_specs=[in_vmem if side.here else pl.BlockSpec(memory_space=pltpu.HBM) for side in sides]
+        + [in_vmem] * (len(worked) + len(queries)),
+        out_specs=[in_vmem] * (len(worked) + len(kept)),
+        out_shape=[jax.ShapeDtypeStruct((side.basis.shape[0], held), jnp.bfloat16) for side in worked]
+        + [here(side) for side in kept],
+        input_output_aliases={
+            at: len(worked) + kept.index(side) for at, side in enumerate(sides) if side.here and side.keep
+        },
+        scratch_shapes=[pltpu.VMEM((held, queries[0].shape[1]), jnp.bfloat16)]
+        + [here(side) for side in streamed]
+        + ([pltpu.SemaphoreType.DMA((len(copied),))] if copied else []),
+        compiler_params=pltpu.CompilerParams(vmem_limit_bytes=(16 if streamed else 6) * MIB),
         cost_estimate=pl.CostEstimate(flops=1, bytes_accessed=1, transcendentals=0),
-    )(
-        *[constrain(basis, pltpu.VMEM if kept else pltpu.HBM) for basis in bases],
-        *[constrain(one, pltpu.VMEM) for one in (*eigens, *queries)],
-    )
+    )(*operands)
 
 
 def packed_width(examples, columns):
@@ -162,12 +177,14 @@
     sent = [lax.dynamic_index_in_dim(by_owner, (row + k) % 4, 0, False) for k in range(4)]
     query, sent = lax.optimization_barrier((query, sent))
     blocks = to_owners(sent)
-    *own, hidden_here, model_here = rotate(bases, eigens, [query], (0, depth), kept=False)
-    bases = [hidden_here, model_here]
+    hidden = Side(bases[0], eigens[0], 0, keep=True)
+    model = Side(bases[1], eigens[1], depth)
+    *own, basis = rotate([query], [hidden, model])
     own, after, before = lax.optimization_barrier((own, after, before))
     after_two = lax.ppermute(after, "rows", [(1, 0), (2, 1)])
     before_two = lax.ppermute(before, "rows", [(1, 2), (2, 3)])
-    near = rotate(bases, eigens, [after, before], (0, depth), kept=True)
+    hidden = hidden._replace(basis=basis, here=True)
+    *near, basis = rotate([after, before], [hidden, model])
     near, blocks = lax.optimization_barrier((near, blocks))
     stores = to_parts(jnp.concatenate(blocks, axis=0))
     near, after_two, before_two = lax.optimization_barrier((near, after_two, before_two))
@@ -176,14 +193,16 @@
     )
     ends = [(1, 0), (2, 3)]
     three_hidden = lax.ppermute(two_hidden, "rows", ends)
-    far = rotate(bases, eigens, [(after_two, before_two)], (0, depth), kept=True)
+    hidden = hidden._replace(basis=basis)
+    *far, basis = rotate([(after_two, before_two)], [hidden, model])
     far, three_hidden, two_model = lax.optimization_barrier((far, three_hidden, two_model))
     base = grams(stores, [own, near, far], [(0,), (1, 3), (2,)])
     three_model = lax.ppermute(two_model, "rows", ends)
-    last_hidden = rotate(bases[:1], eigens[:1], [three_hidden], (0,), kept=True)
+    hidden = hidden._replace(basis=basis, keep=False)
+    last_hidden, basis = rotate([three_hidden], [hidden, model._replace(begin=None, keep=True)])
     base, last_hidden, three_model = lax.optimization_barrier((base, last_hidden, three_model))
-    last_model = rotate(bases[1:], eigens[1:], [three_model], (0,), kept=True)
-    return grams(stores, [last_hidden + last_model], [(3,)], base)
+    last_model = rotate([three_model], [model._replace(basis=basis, begin=0, here=True)])
+    return grams(stores, [[last_hidden, *last_model]], [(3,)], base)
 
 
 def to_owners(sent):

time: 116 us -> 125 us (1.078)
  waiting for transfers between devices: 9.52 us -> 0.03 us
  Pallas kernels: 43.7 us -> 52.6 us
  local copies, waits for them, and re-layouts: 26.3 us -> 34.9 us
  blocking collectives: 13.1 us -> 15.8 us
  starting transfers between devices: 20.8 us -> 19.5 us
    pallas_call x5, Pallas kernels: 41.6 us -> 50.4 us  [rotate(): pl.pallas_call(kernel, in_specs=[in_vmem if side.here else pl.BlockSpec(m...]
    ppermute x1, waiting for transfers between devices: 7.39 us -> 0.01 us  [along_four(): three_hidden = lax.ppermute(two_hidden, 'rows', ends)]
    unnamed x29, local copies, waits for them, and re-layouts: 22.8 us -> 29.3 us
    all_to_all x1, blocking collectives: 13.1 us -> 15.8 us  [per_device(): lax.all_to_all(partial.reshape((parts * rows * layers,) + partial.shape[3...]
    ppermute x1, waiting for transfers between devices: 2.1 us -> 0.01 us  [along_four(): three_model = lax.ppermute(two_model, 'rows', ends)]
    another operation x4, local copies, waits for them, and re-layouts: 0.77 us -> 2.79 us  [per_device(): side[0].reshape(held, rows, -1).transpose(1, 0, 2)]
  transfers between devices with their start and end apart: 10 -> 10, of which waited for: 2 -> 0; matrix products, arithmetic and copies ran while one was open for 4% -> 6% of each run, Pallas kernels for 35% -> 40%
where the time goes in v11:
time: 125 us
  Pallas kernels  52.6 us (42%)
  local copies, waits for them, and re-layouts  34.9 us (28%)
  starting transfers between devices  19.5 us (16%)
  blocking collectives  15.8 us (13%)
  other arithmetic  1.85 us (1%)
    pallas_call x5, Pallas kernels, rotate(): pl.pallas_call(kernel, in_specs=[in_vmem if side.here else pl.BlockSpec(m...  50.4 us
    unnamed x29, local copies, waits for them, and re-layouts  29.3 us
    all_to_all x1, blocking collectives, per_device(): lax.all_to_all(partial.reshape((parts * rows * layers,) + partial.shape[3...  15.8 us
    ppermute x1, starting transfers between devices, along_four(): before = lax.ppermute(query, 'rows', [(0, 1), (1, 2), (2, 3)])  6.52 us
    ppermute x3, starting transfers between devices, to_owners(): lax.ppermute(sent[k], 'rows', [(i, (i + k) % rows) for i in range(rows)])  5.11 us
    another operation x4, local copies, waits for them, and re-layouts, per_device(): side[0].reshape(held, rows, -1).transpose(1, 0, 2)  2.79 us
  transfers between devices with their start and end apart: 10, of which 0 were waited for; matrix products, arithmetic and copies ran while one was open for 6% of the time, Pallas kernels for 40%

profile of v11, /device:TPU:0, one launch (start us, length us, event | category | flops | bytes accessed | tf_op | source)
XLA Modules:
  0.0 125.0 jit_solution(8799448969710805153)
XLA Ops:
  0.0 1.1 dynamic-slice_bitcast_fusion.1
  1.5 1.3 %collective-permute-start = (bf16[48,10240]{1,0:T(8,128)(2,1)S(1)}, bf16[48,10240]{1,0:T(8,128)(2,1)S(1)}, u32[]{:S(2)}, u32[]{:S(2)}) collective-permute-start(bf16[48,10240]{1,0:T(8,128)(2,1)S(1)} %pad_maximum_fusion.refs_4_), channel_id=1, source_target_pairs={{4,0},{8,4},{12,8},{5,1},{9,5},{13,9},{6,2},{10,6},{14,10},{7,3},{... | collective-permute-start | bytes 2949128 | tf_op jit(solution)/shard_map/ppermute | solution.py:175
  2.8 6.5 %collective-permute-start.1 = (bf16[48,10240]{1,0:T(8,128)(2,1)S(1)}, bf16[48,10240]{1,0:T(8,128)(2,1)}, u32[]{:S(2)}, u32[]{:S(2)}) collective-permute-start(bf16[48,10240]{1,0:T(8,128)(2,1)S(1)} %pad_maximum_fusion.refs_4_), channel_id=1, source_target_pairs={{0,4},{4,8},{8,12},{1,5},{5,9},{9,13},{2,6},{6,10},{10,14},{3,7},{... | collective-permute-start | bytes 2949128 | tf_op jit(solution)/shard_map/ppermute | solution.py:176
  9.3 1.4 %reshape_squeeze.6 = bf16[40,4,1536]{2,1,0:T(4,128)(2,1)S(1)} reshape(bf16[1,40,6144]{2,1,0:T(8,128)(2,1)} %param.10) | data formatting | bytes 983040 | tf_op jit(solution)/shard_map/reshape;squeeze | solution.py:250
  10.8 1.2 reshape_squeeze.7
  13.1 1.1 collective-permute-start.2
  14.2 1.1 collective-permute-start.3
  15.3 2.9 %collective-permute-start.4 = (bf16[40,2560]{1,0:T(8,128)(2,1)}, bf16[40,2560]{1,0:T(8,128)(2,1)}, u32[]{:S(2)}, u32[]{:S(2)}) collective-permute-start(bf16[40,2560]{1,0:T(8,128)(2,1)} %get-tuple-element.53), channel_id=1, source_target_pairs={{0,12},{4,0},{8,4},{12,8},{1,13},{5,1},{9,5},{13,9},{2,14},{6,2},{... | collective-permute-start | bytes 614408 | tf_op jit(solution)/shard_map/ppermute | solution.py:211
  18.7 17.3 %shard_map.82 = (bf16[1536,48]{1,0:T(8,128)(2,1)S(1)}, bf16[1024,48]{1,0:T(8,128)(2,1)S(1)}, bf16[1536,6144]{1,0:T(8,128)(2,1)S(1)}) custom-call(bf16[1536,6144]{1,0:T(8,128)(2,1)} %bitcast.34, bf16[1024,4096]{1,0:T(8,128)(2,1)} %bitcast.30, f32[1536,1]{1,0:T(8,128)S(1)} %copy.26.refs_2_, f32[1024,1]{1,0:T(8,128)S(1)} %copy.27.refs_3_.refs_1_, ...), custom_call_target="tpu_custom_call" | custom-call | flops 1 | bytes 1 | tf_op jit(solution)/shard_map/pallas_call | solution.py:91
  36.0 6.5 %copy-done.2 = bf16[1536,6144]{1,0:T(8,128)(2,1)} copy-done((bf16[1536,6144]{1,0:T(8,128)(2,1)}, bf16[1536,6144]{1,0:T(8,128)(2,1)S(1)}, u32[]{:S(2)}) %copy-start.2) | copy-done | bytes 18874392
  44.0 1.3 %collective-permute-start.6 = (bf16[48,10240]{1,0:T(8,128)(2,1)S(1)}, bf16[48,10240]{1,0:T(8,128)(2,1)S(1)}, u32[]{:S(2)}, u32[]{:S(2)}) collective-permute-start(bf16[48,10240]{1,0:T(8,128)(2,1)S(1)} %collective-permute-done.refs_4_), channel_id=1, source_target_pairs={{4,0},{8,4},{5,1},{9,5},{6,2},{10,6},{7,3},{11,7},{20,16},{24,20},... | collective-permute-start | bytes 2949128 | tf_op jit(solution)/shard_map/ppermute | solution.py:184
  46.2 6.4 %copy-done.3 = bf16[1536,6144]{1,0:T(8,128)(2,1)S(1)} copy-done((bf16[1536,6144]{1,0:T(8,128)(2,1)S(1)}, bf16[1536,6144]{1,0:T(8,128)(2,1)}, u32[]{:S(2)}) %copy-start.3) | copy-done | bytes 18874392
  52.5 12.6 %shard_map.83 = (bf16[1536,96]{1,0:T(8,128)(2,1)S(1)}, bf16[1024,96]{1,0:T(8,128)(2,1)S(1)}, bf16[1536,6144]{1,0:T(8,128)(2,1)S(1)}) custom-call(bf16[1536,6144]{1,0:T(8,128)(2,1)S(1)} %copy-done.3, bf16[1024,4096]{1,0:T(8,128)(2,1)} %bitcast.31, f32[1536,1]{1,0:T(8,128)S(1)} %copy.26.refs_2_, ...), custom_call_target="tpu_custom_call", output_to_operand_aliasing={{2}: (0, {})} | custom-call | flops 1 | bytes 1 | tf_op jit(solution)/shard_map/pallas_call | solution.py:91
  65.2 0.9 constant_dynamic-update-slice_fusion.2
  68.1 1.6 %collective-permute-start.5 = (bf16[160,2560]{1,0:T(8,128)(2,1)S(1)}, bf16[160,2560]{1,0:T(8,128)(2,1)S(1)}, u32[]{:S(2)}, u32[]{:S(2)}) collective-permute-start(bf16[160,2560]{1,0:T(8,128)(2,1)S(1)} %constant_dynamic-update-slice_fusion.refs_0_), channel_id=1, source_target_pairs={{0,16},{16,0},{1,17},{17,1},{2,18},{18,2},{3,19},{19,3},{4,20},{20... | collective-permute-start | bytes 2457608 | tf_op jit(solution)/shard_map/ppermute | solution.py:218
  69.7 1.3 %collective-permute-start.8 = (bf16[48,6144]{1,0:T(8,128)(2,1)S(1)}, bf16[48,6144]{1,0:T(8,128)(2,1)S(1)}, u32[]{:S(2)}, u32[]{:S(2)}) collective-permute-start(bf16[48,6144]{1,0:T(8,128)(2,1)S(1)} %slice_select_fusion), channel_id=1, source_target_pairs={{4,0},{8,12},{5,1},{9,13},{6,2},{10,14},{7,3},{11,15},{20,16},{24,... | collective-permute-start | bytes 1769480 | tf_op jit(solution)/shard_map/ppermute | solution.py:195
  71.1 11.3 %shard_map.84 = (bf16[1536,48]{1,0:T(8,128)(2,1)S(1)}, bf16[1024,48]{1,0:T(8,128)(2,1)S(1)}, bf16[1536,6144]{1,0:T(8,128)(2,1)S(1)}) custom-call(bf16[1536,6144]{1,0:T(8,128)(2,1)S(1)} %get-tuple-element.64.refs_0_, bf16[1024,4096]{1,0:T(8,128)(2,1)} %bitcast.32, f32[1536,1]{1,0:T(8,128)S(1)} %copy.26.refs_2_, ...), custom_call_target="tpu_custom_call", output_to_operand_aliasing={{2}: (0, {})} | custom-call | flops 1 | bytes 1 | tf_op jit(solution)/shard_map/pallas_call | solution.py:91
  82.4 6.5 %copy-done.4 = bf16[1536,6144]{1,0:T(8,128)(2,1)} copy-done((bf16[1536,6144]{1,0:T(8,128)(2,1)}, bf16[1536,6144]{1,0:T(8,128)(2,1)S(1)}, u32[]{:S(2)}) %copy-start.4) | copy-done | bytes 18874392
  88.9 1.5 %collective-permute-start.9 = (bf16[48,4096]{1,0:T(8,128)(2,1)S(1)}, bf16[48,4096]{1,0:T(8,128)(2,1)S(1)}, u32[]{:S(2)}, u32[]{:S(2)}) collective-permute-start(bf16[48,4096]{1,0:T(8,128)(2,1)S(1)} %slice_select_fusion.1), channel_id=1, source_target_pairs={{4,0},{8,12},{5,1},{9,13},{6,2},{10,14},{7,3},{11,15},{20,16},{24,... | collective-permute-start | bytes 1179656 | tf_op jit(solution)/shard_map/ppermute | solution.py:200
  90.4 6.4 %copy-done.5 = bf16[1536,6144]{1,0:T(8,128)(2,1)S(1)} copy-done((bf16[1536,6144]{1,0:T(8,128)(2,1)S(1)}, bf16[1536,6144]{1,0:T(8,128)(2,1)}, u32[]{:S(2)}) %copy-start.5) | copy-done | bytes 18874392
  96.8 6.9 %shard_map.86 = (bf16[1536,48]{1,0:T(8,128)(2,1)S(1)}, bf16[1024,4096]{1,0:T(8,128)(2,1)S(1)}) custom-call(bf16[1536,6144]{1,0:T(8,128)(2,1)S(1)} %copy-done.5, bf16[1024,4096]{1,0:T(8,128)(2,1)} %bitcast.33, f32[1536,1]{1,0:T(8,128)S(1)} %copy.26.refs_2_, bf16[48,6144]{1,0:T(8,128)(2,1)S(1)} %collective-permute-done.8.refs_3_), custom_call_target="tpu_custom_call" | custom-call | flops 1 | bytes 1 | tf_op jit(solution)/shard_map/pallas_call | solution.py:91
  103.7 1.5 %shard_map.85.refs_4_ = bf16[2,4,4,16,256]{4,3,2,1,0:T(8,128)(2,1)S(1)} custom-call(bf16[160,2560]{1,0:T(8,128)(2,1)S(1)} %constant_dynamic-update-slice_fusion.refs_0_, bf16[160,2560]{1,0:T(8,128)(2,1)S(1)} %collective-permute-done.5.refs_1_, bf16[1536,48]{1,0:T(8,128)(2,1)S(1)} %copy-done.7, bf16[1024,48]{1,0:T(8,128)(2,1)S(1)} %copy-done.9, ...), custom_call_target="tpu_custom_call" | custom-call | flops 1 | bytes 1 | tf_op jit(solution)/shard_map/pallas_call | solution.py:163
  105.2 2.3 %shard_map.87.refs_3_ = bf16[1024,48]{1,0:T(8,128)(2,1)S(1)} custom-call(bf16[1024,4096]{1,0:T(8,128)(2,1)S(1)} %get-tuple-element.76.refs_0_, f32[1024,1]{1,0:T(8,128)S(1)} %copy.27.refs_3_.refs_1_, bf16[48,4096]{1,0:T(8,128)(2,1)S(1)} %collective-permute-done.9.refs_2_), custom_call_target="tpu_custom_call" | custom-call | flops 1 | bytes 1 | tf_op jit(solution)/shard_map/pallas_call | solution.py:91
  108.2 15.8 %all_to_all.5 = bf16[32,16,256]{2,1,0:T(8,128)(2,1)S(1)} all-to-all(bf16[32,16,256]{2,1,0:T(8,128)(2,1)S(1)} %bitcast.29), channel_id=1, replica_groups=mesh['parts'=2,'rows'=4,'layer'=4] {'parts','rows','layer'}, dimensions={0} | all-to-all | bytes 524288 | tf_op jit(solution)/shard_map/all_to_all | solution.py:274
  (52 shorter events, 8.0 us)
Async XLA Ops:
  0.0 1.4 %copy-start = (bf16[1,96,6144]{2,1,0:T(8,128)(2,1)S(1)}, bf16[1,96,6144]{2,1,0:T(8,128)(2,1)}, u32[]{:S(2)}) copy-start(bf16[1,96,6144]{2,1,0:T(8,128)(2,1)} %param.8) | copy-start | bytes 3538948
  0.0 18.2 %copy-start.11 = (f32[1,1536]{1,0:T(1,128)S(1)}, f32[1,1536]{1,0:T(1,128)}, u32[]{:S(2)}) copy-start(f32[1,1536]{1,0:T(1,128)} %param.14) | copy-start | bytes 18436
  0.0 18.5 %copy-start.12 = (f32[1,1024]{1,0:T(1,128)S(1)}, f32[1,1024]{1,0:T(1,128)}, u32[]{:S(2)}) copy-start(f32[1,1024]{1,0:T(1,128)} %param.15) | copy-start | bytes 12292
  1.5 42.5 %collective-permute-start = (bf16[48,10240]{1,0:T(8,128)(2,1)S(1)}, bf16[48,10240]{1,0:T(8,128)(2,1)S(1)}, u32[]{:S(2)}, u32[]{:S(2)}) collective-permute-start(bf16[48,10240]{1,0:T(8,128)(2,1)S(1)} %pad_maximum_fusion.refs_4_), channel_id=1, source_target_pairs={{4,0},{8,4},{12,8},{5,1},{9,5},{13,9},{6,2},{10,6},{14,10},{7,3},{... | collective-permute-start | bytes 2949128 | tf_op jit(solution)/shard_map/ppermute | solution.py:175
  2.8 41.2 %collective-permute-start.1 = (bf16[48,10240]{1,0:T(8,128)(2,1)S(1)}, bf16[48,10240]{1,0:T(8,128)(2,1)}, u32[]{:S(2)}, u32[]{:S(2)}) collective-permute-start(bf16[48,10240]{1,0:T(8,128)(2,1)S(1)} %pad_maximum_fusion.refs_4_), channel_id=1, source_target_pairs={{0,4},{4,8},{8,12},{1,5},{5,9},{9,13},{2,6},{6,10},{10,14},{3,7},{... | collective-permute-start | bytes 2949128 | tf_op jit(solution)/shard_map/ppermute | solution.py:176
  13.1 52.1 %collective-permute-start.2 = (bf16[40,2560]{1,0:T(8,128)(2,1)}, bf16[40,2560]{1,0:T(8,128)(2,1)}, u32[]{:S(2)}, u32[]{:S(2)}) collective-permute-start(bf16[40,2560]{1,0:T(8,128)(2,1)} %get-tuple-element.51), channel_id=1, source_target_pairs={{0,4},{4,8},{8,12},{12,0},{1,5},{5,9},{9,13},{13,1},{2,6},{6,10},{... | collective-permute-start | bytes 614408 | tf_op jit(solution)/shard_map/ppermute | solution.py:211
  14.2 51.0 %collective-permute-start.3 = (bf16[40,2560]{1,0:T(8,128)(2,1)}, bf16[40,2560]{1,0:T(8,128)(2,1)}, u32[]{:S(2)}, u32[]{:S(2)}) collective-permute-start(bf16[40,2560]{1,0:T(8,128)(2,1)} %get-tuple-element.52), channel_id=1, source_target_pairs={{0,8},{4,12},{8,0},{12,4},{1,9},{5,13},{9,1},{13,5},{2,10},{6,14},... | collective-permute-start | bytes 614408 | tf_op jit(solution)/shard_map/ppermute | solution.py:211
  15.3 49.9 %collective-permute-start.4 = (bf16[40,2560]{1,0:T(8,128)(2,1)}, bf16[40,2560]{1,0:T(8,128)(2,1)}, u32[]{:S(2)}, u32[]{:S(2)}) collective-permute-start(bf16[40,2560]{1,0:T(8,128)(2,1)} %get-tuple-element.53), channel_id=1, source_target_pairs={{0,12},{4,0},{8,4},{12,8},{1,13},{5,1},{9,5},{13,9},{2,14},{6,2},{... | collective-permute-start | bytes 614408 | tf_op jit(solution)/shard_map/ppermute | solution.py:211
  36.0 6.5 %copy-start.2 = (bf16[1536,6144]{1,0:T(8,128)(2,1)}, bf16[1536,6144]{1,0:T(8,128)(2,1)S(1)}, u32[]{:S(2)}) copy-start(bf16[1536,6144]{1,0:T(8,128)(2,1)S(1)} %get-tuple-element.43.refs_0_) | copy-start | bytes 56623108
  42.5 0.8 copy-start.6
  43.3 0.7 copy-start.8
  44.0 25.7 %collective-permute-start.6 = (bf16[48,10240]{1,0:T(8,128)(2,1)S(1)}, bf16[48,10240]{1,0:T(8,128)(2,1)S(1)}, u32[]{:S(2)}, u32[]{:S(2)}) collective-permute-start(bf16[48,10240]{1,0:T(8,128)(2,1)S(1)} %collective-permute-done.refs_4_), channel_id=1, source_target_pairs={{4,0},{8,4},{5,1},{9,5},{6,2},{10,6},{7,3},{11,7},{20,16},{24,20},... | collective-permute-start | bytes 2949128 | tf_op jit(solution)/shard_map/ppermute | solution.py:184
  45.3 24.4 %collective-permute-start.7 = (bf16[48,10240]{1,0:T(8,128)(2,1)}, bf16[48,10240]{1,0:T(8,128)(2,1)S(1)}, u32[]{:S(2)}, u32[]{:S(2)}) collective-permute-start(bf16[48,10240]{1,0:T(8,128)(2,1)} %collective-permute-done.1.refs_5_), channel_id=1, source_target_pairs={{4,8},{8,12},{5,9},{9,13},{6,10},{10,14},{7,11},{11,15},{20,24},{2... | collective-permute-start | bytes 2949128 | tf_op jit(solution)/shard_map/ppermute | solution.py:185
  46.2 6.4 %copy-start.3 = (bf16[1536,6144]{1,0:T(8,128)(2,1)S(1)}, bf16[1536,6144]{1,0:T(8,128)(2,1)}, u32[]{:S(2)}) copy-start(bf16[1536,6144]{1,0:T(8,128)(2,1)} %copy-done.2) | copy-start | bytes 56623108
  52.5 12.7 %copy-start.10 = (bf16[40,2560]{1,0:T(8,128)(2,1)S(1)}, bf16[40,2560]{1,0:T(8,128)(2,1)}, u32[]{:S(2)}) copy-start(bf16[40,2560]{1,0:T(8,128)(2,1)} %get-tuple-element.54) | copy-start | bytes 614404
  68.1 35.6 %collective-permute-start.5 = (bf16[160,2560]{1,0:T(8,128)(2,1)S(1)}, bf16[160,2560]{1,0:T(8,128)(2,1)S(1)}, u32[]{:S(2)}, u32[]{:S(2)}) collective-permute-start(bf16[160,2560]{1,0:T(8,128)(2,1)S(1)} %constant_dynamic-update-slice_fusion.refs_0_), channel_id=1, source_target_pairs={{0,16},{16,0},{1,17},{17,1},{2,18},{18,2},{3,19},{19,3},{4,20},{20... | collective-permute-start | bytes 2457608 | tf_op jit(solution)/shard_map/ppermute | solution.py:218
  69.7 19.1 %collective-permute-start.8 = (bf16[48,6144]{1,0:T(8,128)(2,1)S(1)}, bf16[48,6144]{1,0:T(8,128)(2,1)S(1)}, u32[]{:S(2)}, u32[]{:S(2)}) collective-permute-start(bf16[48,6144]{1,0:T(8,128)(2,1)S(1)} %slice_select_fusion), channel_id=1, source_target_pairs={{4,0},{8,12},{5,1},{9,13},{6,2},{10,14},{7,3},{11,15},{20,16},{24,... | collective-permute-start | bytes 1769480 | tf_op jit(solution)/shard_map/ppermute | solution.py:195
  82.4 6.5 %copy-start.4 = (bf16[1536,6144]{1,0:T(8,128)(2,1)}, bf16[1536,6144]{1,0:T(8,128)(2,1)S(1)}, u32[]{:S(2)}) copy-start(bf16[1536,6144]{1,0:T(8,128)(2,1)S(1)} %get-tuple-element.71.refs_0_) | copy-start | bytes 56623108
  88.9 16.3 %collective-permute-start.9 = (bf16[48,4096]{1,0:T(8,128)(2,1)S(1)}, bf16[48,4096]{1,0:T(8,128)(2,1)S(1)}, u32[]{:S(2)}, u32[]{:S(2)}) collective-permute-start(bf16[48,4096]{1,0:T(8,128)(2,1)S(1)} %slice_select_fusion.1), channel_id=1, source_target_pairs={{4,0},{8,12},{5,1},{9,13},{6,2},{10,14},{7,3},{11,15},{20,16},{24,... | collective-permute-start | bytes 1179656 | tf_op jit(solution)/shard_map/ppermute | solution.py:200
  90.4 6.4 %copy-start.5 = (bf16[1536,6144]{1,0:T(8,128)(2,1)S(1)}, bf16[1536,6144]{1,0:T(8,128)(2,1)}, u32[]{:S(2)}) copy-start(bf16[1536,6144]{1,0:T(8,128)(2,1)} %copy-done.4) | copy-start | bytes 56623108
  96.8 6.9 %copy-start.7 = (bf16[1536,48]{1,0:T(8,128)(2,1)S(1)}, bf16[1536,48]{1,0:T(8,128)(2,1)}, u32[]{:S(2)}) copy-start(bf16[1536,48]{1,0:T(8,128)(2,1)} %copy-done.6) | copy-start | bytes 442372
  96.8 6.9 %copy-start.9 = (bf16[1024,48]{1,0:T(8,128)(2,1)S(1)}, bf16[1024,48]{1,0:T(8,128)(2,1)}, u32[]{:S(2)}) copy-start(bf16[1024,48]{1,0:T(8,128)(2,1)} %copy-done.8) | copy-start | bytes 294916
  96.8 28.2 %copy-start.1 = (bf16[1,96,6144]{2,1,0:T(8,128)(2,1)S(1)}, bf16[1,96,6144]{2,1,0:T(8,128)(2,1)}, u32[]{:S(2)}) copy-start(bf16[1,96,6144]{2,1,0:T(8,128)(2,1)} %param.8) | copy-start | bytes 3538948

commit v12 on v10

--- a/solution.py
+++ b/solution.py
@@ -12,7 +12,6 @@
 
 MIB = 1024 * 1024
 TILE = 256
-AHEAD = 4
 
 
 def along(value, by):
@@ -20,75 +19,41 @@
     return lax.ppermute(value, "rows", [(i, i + by) for i in range(size) if 0 <= i + by < size])
 
 
-def rotate(bases, eigens, queries, begins, kept):
+def rotate(bases, eigens, queries, begins):
     groups = [query if isinstance(query, tuple) else (query,) for query in queries]
     queries = [query for group in groups for query in group]
     columns = queries[0].shape[0]
     held = columns * len(groups)
-    count, sides = len(queries), len(bases)
-    tiles = [(side, tile) for side in range(sides) for tile in range(bases[side].shape[0] // TILE)]
+    sides = len(bases)
 
     def kernel(*refs):
-        refs = list(refs)
-        take = lambda many: [refs.pop(0) for _ in range(many)]
-        basis_refs, eigen_refs, query_refs, out_refs = take(sides), take(sides), take(count), take(sides)
-        here_refs = [] if kept else take(sides)
-        query = take(1)[0]
-        semaphores = None if kept else take(1)[0]
-
-        def block(at):
-            side, tile = tiles[at]
-            where = slice(tile * TILE, (tile + 1) * TILE)
-            if kept:
-                return basis_refs[side].at[where]
-            return here_refs[side].at[where]
-
-        def copy(at):
-            side, tile = tiles[at]
-            where = slice(tile * TILE, (tile + 1) * TILE)
-            return pltpu.make_async_copy(basis_refs[side].at[where], block(at), semaphores.at[at])
-
-        if not kept:
-            for at in range(min(AHEAD, len(tiles))):
-                copy(at).start(priority=at % 2)
+        basis_refs, eigen_refs = refs[:sides], refs[sides : 2 * sides]
+        query_refs = list(refs[2 * sides : 2 * sides + len(queries)])
+        out_refs, query = refs[2 * sides + len(queries) : -1], refs[-1]
         for place, group in enumerate(groups):
-            block_of = query_refs.pop(0)[...]
+            block = query_refs.pop(0)[...]
             for _ in group[1:]:
-                block_of = block_of + query_refs.pop(0)[...]
-            query[place * columns : (place + 1) * columns, :] = block_of
-        for at, (side, tile) in enumerate(tiles):
-            where = slice(tile * TILE, (tile + 1) * TILE)
-            if not kept:
-                copy(at).wait()
-            if not kept and at + AHEAD < len(tiles):
-                copy(at + AHEAD).start(priority=(at + AHEAD) % 2)
-            rotated = lax.dot_general(
-                block(at)[...],
-                query[:, begins[side] : begins[side] + basis_refs[side].shape[1]],
-                (((1,), (1,)), ((), ())),
-                preferred_element_type=jnp.float32,
-            )
-            scale = 1.0 / (eigen_refs[side][where, :] + damping)
-            out_refs[side][where, :] = (rotated * scale).astype(jnp.bfloat16)
-
-    constrain = pltpu.with_memory_space_constraint
-    in_vmem = pl.BlockSpec(memory_space=pltpu.VMEM)
-    scratch = [pltpu.VMEM((held, queries[0].shape[1]), jnp.bfloat16)]
-    if not kept:
-        scratch.append(pltpu.SemaphoreType.DMA((len(tiles),)))
+                block = block + query_refs.pop(0)[...]
+            query[place * columns : (place + 1) * columns, :] = block
+        for basis_ref, eigen_ref, out_ref, begin in zip(basis_refs, eigen_refs, out_refs, begins):
+            share, width = basis_ref.shape
+            for tile in range(share // TILE):
+                where = slice(tile * TILE, (tile + 1) * TILE)
+                rotated = lax.dot_general(
+                    basis_ref[where, :],
+                    query[:, begin : begin + width],
+                    (((1,), (1,)), ((), ())),
+                    preferred_element_type=jnp.float32,
+                )
+                out_ref[where, :] = (rotated * (1.0 / (eigen_ref[where, :] + damping))).astype(jnp.bfloat16)
+
     return pl.pallas_call(
         kernel,
-        in_specs=[in_vmem if kept else pl.BlockSpec(memory_space=pltpu.HBM)] * sides + [in_vmem] * (sides + count),
-        out_specs=[in_vmem] * (sides if kept else 2 * sides),
-        out_shape=[jax.ShapeDtypeStruct((basis.shape[0], held), jnp.bfloat16) for basis in bases]
-        + ([] if kept else [pltpu.VMEM(basis.shape, basis.dtype) for basis in bases]),
-        scratch_shapes=scratch,
+        out_shape=[jax.ShapeDtypeStruct((basis.shape[0], held), jnp.bfloat16) for basis in bases],
+        scratch_shapes=[pltpu.VMEM((held, queries[0].shape[1]), jnp.bfloat16)],
         compiler_params=pltpu.CompilerParams(vmem_limit_bytes=8 * MIB),
         cost_estimate=pl.CostEstimate(flops=1, bytes_accessed=1, transcendentals=0),
-    )(
-        *[constrain(basis, pltpu.VMEM if kept else pltpu.HBM) for basis in bases],
-        *[constrain(one, pltpu.VMEM) for one in (*eigens, *queries)],
-    )
+    )(*[pltpu.with_memory_space_constraint(one, pltpu.VMEM) for one in (*bases, *eigens, *queries)])
 
 
 def packed_width(examples, columns):
@@ -162,12 +127,10 @@
     sent = [lax.dynamic_index_in_dim(by_owner, (row + k) % 4, 0, False) for k in range(4)]
     query, sent = lax.optimization_barrier((query, sent))
     blocks = to_owners(sent)
-    *own, hidden_here, model_here = rotate(bases, eigens, [query], (0, depth), kept=False)
-    bases = [hidden_here, model_here]
-    own, after, before = lax.optimization_barrier((own, after, before))
+    query, after, before = lax.optimization_barrier((query, after, before))
     after_two = lax.ppermute(after, "rows", [(1, 0), (2, 1)])
     before_two = lax.ppermute(before, "rows", [(1, 2), (2, 3)])
-    near = rotate(bases, eigens, [after, before], (0, depth), kept=True)
+    near = rotate(bases, eigens, [query, after, before], (0, depth))
     near, blocks = lax.optimization_barrier((near, blocks))
     stores = to_parts(jnp.concatenate(blocks, axis=0))
     near, after_two, before_two = lax.optimization_barrier((near, after_two, before_two))
@@ -176,13 +139,13 @@
     )
     ends = [(1, 0), (2, 3)]
     three_hidden = lax.ppermute(two_hidden, "rows", ends)
-    far = rotate(bases, eigens, [(after_two, before_two)], (0, depth), kept=True)
+    far = rotate(bases, eigens, [(after_two, before_two)], (0, depth))
     far, three_hidden, two_model = lax.optimization_barrier((far, three_hidden, two_model))
-    base = grams(stores, [own, near, far], [(0,), (1, 3), (2,)])
+    base = grams(stores, [near, far], [(0, 1, 3), (2,)])
     three_model = lax.ppermute(two_model, "rows", ends)
-    last_hidden = rotate(bases[:1], eigens[:1], [three_hidden], (0,), kept=True)
+    last_hidden = rotate(bases[:1], eigens[:1], [three_hidden], (0,))
     base, last_hidden, three_model = lax.optimization_barrier((base, last_hidden, three_model))
-    last_model = rotate(bases[1:], eigens[1:], [three_model], (0,), kept=True)
+    last_model = rotate(bases[1:], eigens[1:], [three_model], (0,))
     return grams(stores, [last_hidden + last_model], [(3,)], base)
 
 

time: 116 us -> 116 us (level)
  Pallas kernels: 43.7 us -> 25 us
  waiting for transfers between devices: 9.52 us -> 24.6 us
  starting transfers between devices: 20.8 us -> 24.1 us
  local copies, waits for them, and re-layouts: 26.3 us -> 23.8 us
  blocking collectives: 13.1 us -> 15.6 us
    pallas_call x5 -> x4, Pallas kernels: 41.6 us -> 23.2 us  [rotate(): pl.pallas_call(kernel, out_shape=[jax.ShapeDtypeStruct((basis.shape[0], h...]
    ppermute x1, waiting for transfers between devices: 0.01 us -> 11.8 us  [along_four(): after = lax.ppermute(query, 'rows', [(1, 0), (2, 1), (3, 2)])]
    ppermute x1, starting transfers between devices: 1.58 us -> 5.18 us  [to_parts(): lax.ppermute(store, 'parts', [(i, (i + j) % parts) for i in range(parts)])]
    unnamed x29 -> x23, local copies, waits for them, and re-layouts: 22.8 us -> 19.3 us
    ppermute x1, waiting for transfers between devices: 0.01 us -> 3.31 us  [along_four(): after_two = lax.ppermute(after, 'rows', [(1, 0), (2, 1)])]
    all_to_all x1, blocking collectives: 13.1 us -> 15.6 us  [per_device(): lax.all_to_all(partial.reshape((parts * rows * layers,) + partial.shape[3...]
    ppermute x1, waiting for transfers between devices: 7.39 us -> 5.98 us  [along_four(): three_hidden = lax.ppermute(two_hidden, 'rows', ends)]
    ppermute x1, waiting for transfers between devices: 2.1 us -> 3.43 us  [along_four(): three_model = lax.ppermute(two_model, 'rows', ends)]
  transfers between devices with their start and end apart: 10 -> 10, of which waited for: 2 -> 4; matrix products, arithmetic and copies ran while one was open for 4% -> 5% of each run, Pallas kernels for 35% -> 19%
where the time goes in v12:
time: 116 us; the launch traced here: 115 us
  Pallas kernels  25 us (22%)
  waiting for transfers between devices  24.6 us (21%)
  starting transfers between devices  24.1 us (21%)
  local copies, waits for them, and re-layouts  23.8 us (21%)
  blocking collectives  15.6 us (13%)
  other arithmetic  1.86 us (2%)
    pallas_call x4, Pallas kernels, rotate(): pl.pallas_call(kernel, out_shape=[jax.ShapeDtypeStruct((basis.shape[0], h...  23.2 us
    unnamed x23, local copies, waits for them, and re-layouts  19.3 us
    all_to_all x1, blocking collectives, per_device(): lax.all_to_all(partial.reshape((parts * rows * layers,) + partial.shape[3...  15.6 us
    ppermute x1, waiting for transfers between devices, along_four(): after = lax.ppermute(query, 'rows', [(1, 0), (2, 1), (3, 2)])  11.8 us
    ppermute x1, starting transfers between devices, along_four(): before = lax.ppermute(query, 'rows', [(0, 1), (1, 2), (2, 3)])  6.52 us
    ppermute x3, starting transfers between devices, to_owners(): lax.ppermute(sent[k], 'rows', [(i, (i + k) % rows) for i in range(rows)])  6.04 us
    ppermute x1, waiting for transfers between devices, along_four(): three_hidden = lax.ppermute(two_hidden, 'rows', ends)  5.98 us
    ppermute x1, starting transfers between devices, to_parts(): lax.ppermute(store, 'parts', [(i, (i + j) % parts) for i in range(parts)])  5.18 us
  transfers between devices with their start and end apart: 10, of which 4 were waited for; matrix products, arithmetic and copies ran while one was open for 5% of the time, Pallas kernels for 19%

profile of v12, /device:TPU:0, one launch (start us, length us, event | category | flops | bytes accessed | tf_op | source)
XLA Modules:
  0.0 115.1 jit_solution(14942355145259935226)
XLA Ops:
  0.0 1.3 %copy-done = bf16[1,96,6144]{2,1,0:T(8,128)(2,1)S(1)} copy-done((bf16[1,96,6144]{2,1,0:T(8,128)(2,1)S(1)}, bf16[1,96,6144]{2,1,0:T(8,128)(2,1)}, u32[]{:S(2)}) %copy-start) | copy-done | bytes 1179672
  2.5 1.3 %collective-permute-start = (bf16[48,10240]{1,0:T(8,128)(2,1)S(1)}, bf16[48,10240]{1,0:T(8,128)(2,1)}, u32[]{:S(2)}, u32[]{:S(2)}) collective-permute-start(bf16[48,10240]{1,0:T(8,128)(2,1)S(1)} %pad_maximum_fusion.refs_4_), channel_id=1, source_target_pairs={{4,0},{8,4},{12,8},{5,1},{9,5},{13,9},{6,2},{10,6},{14,10},{7,3},{... | collective-permute-start | bytes 2949128 | tf_op jit(solution)/shard_map/ppermute | solution.py:125
  3.8 6.5 %collective-permute-start.1 = (bf16[48,10240]{1,0:T(8,128)(2,1)S(1)}, bf16[48,10240]{1,0:T(8,128)(2,1)}, u32[]{:S(2)}, u32[]{:S(2)}) collective-permute-start(bf16[48,10240]{1,0:T(8,128)(2,1)S(1)} %pad_maximum_fusion.refs_4_), channel_id=1, source_target_pairs={{0,4},{4,8},{8,12},{1,5},{5,9},{9,13},{2,6},{6,10},{10,14},{3,7},{... | collective-permute-start | bytes 2949128 | tf_op jit(solution)/shard_map/ppermute | solution.py:126
  10.8 1.2 %reshape_squeeze.7 = bf16[40,4,1024]{2,1,0:T(4,128)(2,1)S(1)} reshape(bf16[1,40,4096]{2,1,0:T(8,128)(2,1)} %param.11) | data formatting | bytes 655360 | tf_op jit(solution)/shard_map/reshape;squeeze | solution.py:194
  13.1 1.1 collective-permute-start.2
  14.2 2.0 %collective-permute-start.3 = (bf16[40,2560]{1,0:T(8,128)(2,1)}, bf16[40,2560]{1,0:T(8,128)(2,1)}, u32[]{:S(2)}, u32[]{:S(2)}) collective-permute-start(bf16[40,2560]{1,0:T(8,128)(2,1)} %get-tuple-element.42), channel_id=1, source_target_pairs={{0,8},{4,12},{8,0},{12,4},{1,9},{5,13},{9,1},{13,5},{2,10},{6,14},... | collective-permute-start | bytes 614408 | tf_op jit(solution)/shard_map/ppermute | solution.py:155
  16.2 2.9 %collective-permute-start.4 = (bf16[40,2560]{1,0:T(8,128)(2,1)}, bf16[40,2560]{1,0:T(8,128)(2,1)}, u32[]{:S(2)}, u32[]{:S(2)}) collective-permute-start(bf16[40,2560]{1,0:T(8,128)(2,1)} %get-tuple-element.43), channel_id=1, source_target_pairs={{0,12},{4,0},{8,4},{12,8},{1,13},{5,1},{9,5},{13,9},{2,14},{6,2},{... | collective-permute-start | bytes 614408 | tf_op jit(solution)/shard_map/ppermute | solution.py:155
  19.6 11.8 %collective-permute-done.refs_5_ = bf16[48,10240]{1,0:T(8,128)(2,1)} collective-permute-done((bf16[48,10240]{1,0:T(8,128)(2,1)S(1)}, bf16[48,10240]{1,0:T(8,128)(2,1)}, u32[]{:S(2)}, u32[]{:S(2)}) %collective-permute-start) | collective-permute-done | bytes 983072 | tf_op jit(solution)/shard_map/ppermute | solution.py:125
  31.5 1.3 %collective-permute-start.6 = (bf16[48,10240]{1,0:T(8,128)(2,1)}, bf16[48,10240]{1,0:T(8,128)(2,1)S(1)}, u32[]{:S(2)}, u32[]{:S(2)}) collective-permute-start(bf16[48,10240]{1,0:T(8,128)(2,1)} %collective-permute-done.refs_5_), channel_id=1, source_target_pairs={{4,0},{8,4},{5,1},{9,5},{6,2},{10,6},{7,3},{11,7},{20,16},{24,20},... | collective-permute-start | bytes 2949128 | tf_op jit(solution)/shard_map/ppermute | solution.py:131
  33.5 6.4 %copy-done.1 = bf16[1,1536,6144]{2,1,0:T(8,128)(2,1)S(1)} copy-done((bf16[1,1536,6144]{2,1,0:T(8,128)(2,1)S(1)}, bf16[1,1536,6144]{2,1,0:T(8,128)(2,1)}, u32[]{:S(2)}) %copy-start.1) | copy-done | bytes 18874392
  39.9 3.4 %copy-done.3 = bf16[1,1024,4096]{2,1,0:T(8,128)(2,1)S(1)} copy-done((bf16[1,1024,4096]{2,1,0:T(8,128)(2,1)S(1)}, bf16[1,1024,4096]{2,1,0:T(8,128)(2,1)}, u32[]{:S(2)}) %copy-start.3) | copy-done | bytes 8388632
  43.3 8.7 %shard_map.82 = (bf16[1536,144]{1,0:T(8,128)(2,1)S(1)}, bf16[1024,144]{1,0:T(8,128)(2,1)S(1)}) custom-call(bf16[1536,6144]{1,0:T(8,128)(2,1)S(1)} %bitcast.29, bf16[1024,4096]{1,0:T(8,128)(2,1)S(1)} %bitcast.32, f32[1536,1]{1,0:T(8,128)S(1)} %copy.22.refs_2_.refs_1_, f32[1024,1]{1,0:T(8,128)S(1)} %copy.23.refs_3_.refs_1_, ...), custom_call_target="tpu_custom_call" | custom-call | flops 1 | bytes 1 | tf_op jit(solution)/shard_map/pallas_call | solution.py:50
  54.9 5.2 %collective-permute-start.5 = (bf16[160,2560]{1,0:T(8,128)(2,1)S(1)}, bf16[160,2560]{1,0:T(8,128)(2,1)S(1)}, u32[]{:S(2)}, u32[]{:S(2)}) collective-permute-start(bf16[160,2560]{1,0:T(8,128)(2,1)S(1)} %constant_dynamic-update-slice_fusion.refs_0_), channel_id=1, source_target_pairs={{0,16},{16,0},{1,17},{17,1},{2,18},{18,2},{3,19},{19,3},{4,20},{20... | collective-permute-start | bytes 2457608 | tf_op jit(solution)/shard_map/ppermute | solution.py:162
  60.1 3.3 %collective-permute-done.6.refs_4_ = bf16[48,10240]{1,0:T(8,128)(2,1)S(1)} collective-permute-done((bf16[48,10240]{1,0:T(8,128)(2,1)}, bf16[48,10240]{1,0:T(8,128)(2,1)S(1)}, u32[]{:S(2)}, u32[]{:S(2)}) %collective-permute-start.6) | collective-permute-done | bytes 983072 | tf_op jit(solution)/shard_map/ppermute | solution.py:131
  63.5 1.3 %collective-permute-start.8 = (bf16[48,6144]{1,0:T(8,128)(2,1)S(1)}, bf16[48,6144]{1,0:T(8,128)(2,1)S(1)}, u32[]{:S(2)}, u32[]{:S(2)}) collective-permute-start(bf16[48,6144]{1,0:T(8,128)(2,1)S(1)} %slice_select_fusion), channel_id=1, source_target_pairs={{4,0},{8,12},{5,1},{9,13},{6,2},{10,14},{7,3},{11,15},{20,16},{24,... | collective-permute-start | bytes 1769480 | tf_op jit(solution)/shard_map/ppermute | solution.py:141
  64.8 6.4 %copy-done.2 = bf16[1,1536,6144]{2,1,0:T(8,128)(2,1)S(1)} copy-done((bf16[1,1536,6144]{2,1,0:T(8,128)(2,1)S(1)}, bf16[1,1536,6144]{2,1,0:T(8,128)(2,1)}, u32[]{:S(2)}) %copy-start.2) | copy-done | bytes 18874392
  71.2 7.2 %shard_map.83 = (bf16[1536,48]{1,0:T(8,128)(2,1)S(1)}, bf16[1024,48]{1,0:T(8,128)(2,1)S(1)}) custom-call(bf16[1536,6144]{1,0:T(8,128)(2,1)S(1)} %bitcast.30, bf16[1024,4096]{1,0:T(8,128)(2,1)S(1)} %bitcast.33, f32[1536,1]{1,0:T(8,128)S(1)} %copy.22.refs_2_.refs_1_, f32[1024,1]{1,0:T(8,128)S(1)} %copy.23.refs_3_.refs_1_, ...), custom_call_target="tpu_custom_call" | custom-call | flops 1 | bytes 1 | tf_op jit(solution)/shard_map/pallas_call | solution.py:50
  78.3 6.0 %collective-permute-done.8.refs_2_ = bf16[48,6144]{1,0:T(8,128)(2,1)S(1)} collective-permute-done((bf16[48,6144]{1,0:T(8,128)(2,1)S(1)}, bf16[48,6144]{1,0:T(8,128)(2,1)S(1)}, u32[]{:S(2)}, u32[]{:S(2)}) %collective-permute-start.8) | collective-permute-done | bytes 589856 | tf_op jit(solution)/shard_map/ppermute | solution.py:141
  84.3 1.7 %collective-permute-start.9 = (bf16[48,4096]{1,0:T(8,128)(2,1)S(1)}, bf16[48,4096]{1,0:T(8,128)(2,1)S(1)}, u32[]{:S(2)}, u32[]{:S(2)}) collective-permute-start(bf16[48,4096]{1,0:T(8,128)(2,1)S(1)} %slice_select_fusion.1), channel_id=1, source_target_pairs={{4,0},{8,12},{5,1},{9,13},{6,2},{10,14},{7,3},{11,15},{20,16},{24,... | collective-permute-start | bytes 1179656 | tf_op jit(solution)/shard_map/ppermute | solution.py:145
  86.1 5.0 %shard_map.85.refs_2_ = bf16[1536,48]{1,0:T(8,128)(2,1)S(1)} custom-call(bf16[1536,6144]{1,0:T(8,128)(2,1)S(1)} %bitcast.31, f32[1536,1]{1,0:T(8,128)S(1)} %copy.22.refs_2_.refs_1_, bf16[48,6144]{1,0:T(8,128)(2,1)S(1)} %collective-permute-done.8.refs_2_), custom_call_target="tpu_custom_call" | custom-call | flops 1 | bytes 1 | tf_op jit(solution)/shard_map/pallas_call | solution.py:50
  91.1 1.1 shard_map.84.refs_4_
  92.2 3.4 %collective-permute-done.9.refs_2_ = bf16[48,4096]{1,0:T(8,128)(2,1)S(1)} collective-permute-done((bf16[48,4096]{1,0:T(8,128)(2,1)S(1)}, bf16[48,4096]{1,0:T(8,128)(2,1)S(1)}, u32[]{:S(2)}, u32[]{:S(2)}) %collective-permute-start.9) | collective-permute-done | bytes 393248 | tf_op jit(solution)/shard_map/ppermute | solution.py:145
  95.6 2.3 %shard_map.86.refs_3_ = bf16[1024,48]{1,0:T(8,128)(2,1)S(1)} custom-call(bf16[1024,4096]{1,0:T(8,128)(2,1)S(1)} %bitcast.36, f32[1024,1]{1,0:T(8,128)S(1)} %copy.23.refs_3_.refs_1_, bf16[48,4096]{1,0:T(8,128)(2,1)S(1)} %collective-permute-done.9.refs_2_), custom_call_target="tpu_custom_call" | custom-call | flops 1 | bytes 1 | tf_op jit(solution)/shard_map/pallas_call | solution.py:50
  98.6 15.6 %all_to_all.5 = bf16[32,16,256]{2,1,0:T(8,128)(2,1)S(1)} all-to-all(bf16[32,16,256]{2,1,0:T(8,128)(2,1)S(1)} %bitcast.37), channel_id=1, replica_groups=mesh['parts'=2,'rows'=4,'layer'=4] {'parts','rows','layer'}, dimensions={0} | all-to-all | bytes 524288 | tf_op jit(solution)/shard_map/all_to_all | solution.py:218
  (46 shorter events, 8.5 us)
Async XLA Ops:
  0.0 1.3 %copy-start = (bf16[1,96,6144]{2,1,0:T(8,128)(2,1)S(1)}, bf16[1,96,6144]{2,1,0:T(8,128)(2,1)}, u32[]{:S(2)}) copy-start(bf16[1,96,6144]{2,1,0:T(8,128)(2,1)} %param.8) | copy-start | bytes 3538948
  1.3 9.0 %copy-start.5 = (bf16[1,40,6144]{2,1,0:T(8,128)(2,1)S(1)}, bf16[1,40,6144]{2,1,0:T(8,128)(2,1)}, u32[]{:S(2)}) copy-start(bf16[1,40,6144]{2,1,0:T(8,128)(2,1)} %param.10) | copy-start | bytes 1474564
  2.5 29.0 %collective-permute-start = (bf16[48,10240]{1,0:T(8,128)(2,1)S(1)}, bf16[48,10240]{1,0:T(8,128)(2,1)}, u32[]{:S(2)}, u32[]{:S(2)}) collective-permute-start(bf16[48,10240]{1,0:T(8,128)(2,1)S(1)} %pad_maximum_fusion.refs_4_), channel_id=1, source_target_pairs={{4,0},{8,4},{12,8},{5,1},{9,5},{13,9},{6,2},{10,6},{14,10},{7,3},{... | collective-permute-start | bytes 2949128 | tf_op jit(solution)/shard_map/ppermute | solution.py:125
  3.8 27.7 %collective-permute-start.1 = (bf16[48,10240]{1,0:T(8,128)(2,1)S(1)}, bf16[48,10240]{1,0:T(8,128)(2,1)}, u32[]{:S(2)}, u32[]{:S(2)}) collective-permute-start(bf16[48,10240]{1,0:T(8,128)(2,1)S(1)} %pad_maximum_fusion.refs_4_), channel_id=1, source_target_pairs={{0,4},{4,8},{8,12},{1,5},{5,9},{9,13},{2,6},{6,10},{10,14},{3,7},{... | collective-permute-start | bytes 2949128 | tf_op jit(solution)/shard_map/ppermute | solution.py:126
  10.7 8.5 %copy-start.6 = (f32[1,1536]{1,0:T(1,128)S(1)}, f32[1,1536]{1,0:T(1,128)}, u32[]{:S(2)}) copy-start(f32[1,1536]{1,0:T(1,128)} %param.14) | copy-start | bytes 18436
  10.8 8.6 %copy-start.7 = (f32[1,1024]{1,0:T(1,128)S(1)}, f32[1,1024]{1,0:T(1,128)}, u32[]{:S(2)}) copy-start(f32[1,1024]{1,0:T(1,128)} %param.15) | copy-start | bytes 12292
  13.1 38.9 %collective-permute-start.2 = (bf16[40,2560]{1,0:T(8,128)(2,1)}, bf16[40,2560]{1,0:T(8,128)(2,1)}, u32[]{:S(2)}, u32[]{:S(2)}) collective-permute-start(bf16[40,2560]{1,0:T(8,128)(2,1)} %get-tuple-element.41), channel_id=1, source_target_pairs={{0,4},{4,8},{8,12},{12,0},{1,5},{5,9},{9,13},{13,1},{2,6},{6,10},{... | collective-permute-start | bytes 614408 | tf_op jit(solution)/shard_map/ppermute | solution.py:155
  14.2 37.8 %collective-permute-start.3 = (bf16[40,2560]{1,0:T(8,128)(2,1)}, bf16[40,2560]{1,0:T(8,128)(2,1)}, u32[]{:S(2)}, u32[]{:S(2)}) collective-permute-start(bf16[40,2560]{1,0:T(8,128)(2,1)} %get-tuple-element.42), channel_id=1, source_target_pairs={{0,8},{4,12},{8,0},{12,4},{1,9},{5,13},{9,1},{13,5},{2,10},{6,14},... | collective-permute-start | bytes 614408 | tf_op jit(solution)/shard_map/ppermute | solution.py:155
  16.2 35.8 %collective-permute-start.4 = (bf16[40,2560]{1,0:T(8,128)(2,1)}, bf16[40,2560]{1,0:T(8,128)(2,1)}, u32[]{:S(2)}, u32[]{:S(2)}) collective-permute-start(bf16[40,2560]{1,0:T(8,128)(2,1)} %get-tuple-element.43), channel_id=1, source_target_pairs={{0,12},{4,0},{8,4},{12,8},{1,13},{5,1},{9,5},{13,9},{2,14},{6,2},{... | collective-permute-start | bytes 614408 | tf_op jit(solution)/shard_map/ppermute | solution.py:155
  31.5 31.9 %collective-permute-start.6 = (bf16[48,10240]{1,0:T(8,128)(2,1)}, bf16[48,10240]{1,0:T(8,128)(2,1)S(1)}, u32[]{:S(2)}, u32[]{:S(2)}) collective-permute-start(bf16[48,10240]{1,0:T(8,128)(2,1)} %collective-permute-done.refs_5_), channel_id=1, source_target_pairs={{4,0},{8,4},{5,1},{9,5},{6,2},{10,6},{7,3},{11,7},{20,16},{24,20},... | collective-permute-start | bytes 2949128 | tf_op jit(solution)/shard_map/ppermute | solution.py:131
  32.8 30.6 %collective-permute-start.7 = (bf16[48,10240]{1,0:T(8,128)(2,1)}, bf16[48,10240]{1,0:T(8,128)(2,1)S(1)}, u32[]{:S(2)}, u32[]{:S(2)}) collective-permute-start(bf16[48,10240]{1,0:T(8,128)(2,1)} %collective-permute-done.1.refs_6_), channel_id=1, source_target_pairs={{4,8},{8,12},{5,9},{9,13},{6,10},{10,14},{7,11},{11,15},{20,24},{2... | collective-permute-start | bytes 2949128 | tf_op jit(solution)/shard_map/ppermute | solution.py:132
  33.5 6.4 %copy-start.1 = (bf16[1,1536,6144]{2,1,0:T(8,128)(2,1)S(1)}, bf16[1,1536,6144]{2,1,0:T(8,128)(2,1)}, u32[]{:S(2)}) copy-start(bf16[1,1536,6144]{2,1,0:T(8,128)(2,1)} %param.12) | copy-start | bytes 56623108
  39.9 3.4 %copy-start.3 = (bf16[1,1024,4096]{2,1,0:T(8,128)(2,1)S(1)}, bf16[1,1024,4096]{2,1,0:T(8,128)(2,1)}, u32[]{:S(2)}) copy-start(bf16[1,1024,4096]{2,1,0:T(8,128)(2,1)} %param.13) | copy-start | bytes 25165828
  43.2 8.8 %copy-start.4 = (bf16[40,2560]{1,0:T(8,128)(2,1)S(1)}, bf16[40,2560]{1,0:T(8,128)(2,1)}, u32[]{:S(2)}) copy-start(bf16[40,2560]{1,0:T(8,128)(2,1)} %get-tuple-element.44) | copy-start | bytes 614404
  54.9 36.2 %collective-permute-start.5 = (bf16[160,2560]{1,0:T(8,128)(2,1)S(1)}, bf16[160,2560]{1,0:T(8,128)(2,1)S(1)}, u32[]{:S(2)}, u32[]{:S(2)}) collective-permute-start(bf16[160,2560]{1,0:T(8,128)(2,1)S(1)} %constant_dynamic-update-slice_fusion.refs_0_), channel_id=1, source_target_pairs={{0,16},{16,0},{1,17},{17,1},{2,18},{18,2},{3,19},{19,3},{4,20},{20... | collective-permute-start | bytes 2457608 | tf_op jit(solution)/shard_map/ppermute | solution.py:162
  63.5 20.9 %collective-permute-start.8 = (bf16[48,6144]{1,0:T(8,128)(2,1)S(1)}, bf16[48,6144]{1,0:T(8,128)(2,1)S(1)}, u32[]{:S(2)}, u32[]{:S(2)}) collective-permute-start(bf16[48,6144]{1,0:T(8,128)(2,1)S(1)} %slice_select_fusion), channel_id=1, source_target_pairs={{4,0},{8,12},{5,1},{9,13},{6,2},{10,14},{7,3},{11,15},{20,16},{24,... | collective-permute-start | bytes 1769480 | tf_op jit(solution)/shard_map/ppermute | solution.py:141
  64.8 6.4 %copy-start.2 = (bf16[1,1536,6144]{2,1,0:T(8,128)(2,1)S(1)}, bf16[1,1536,6144]{2,1,0:T(8,128)(2,1)}, u32[]{:S(2)}) copy-start(bf16[1,1536,6144]{2,1,0:T(8,128)(2,1)} %param.12) | copy-start | bytes 56623108
  84.3 11.3 %slice-start = ((s8[8388608]{0:T(1024)(128)(4,1)}), s8[4194304]{0:T(1024)(128)(4,1)S(1)}, s32[]{:S(2)}) async-start(s8[8388608]{0:T(1024)(128)(4,1)} %bitcast.34), calls=%async_computation.1 | async-start | bytes 8388608
  84.3 11.3 %slice-start.1 = ((s8[8388608]{0:T(1024)(128)(4,1)}), s8[4194304]{0:T(1024)(128)(4,1)S(1)}, s32[]{:S(2)}) async-start(s8[8388608]{0:T(1024)(128)(4,1)} %bitcast.34), calls=%async_computation.2 | async-start | bytes 8388608
  84.3 11.3 %collective-permute-start.9 = (bf16[48,4096]{1,0:T(8,128)(2,1)S(1)}, bf16[48,4096]{1,0:T(8,128)(2,1)S(1)}, u32[]{:S(2)}, u32[]{:S(2)}) collective-permute-start(bf16[48,4096]{1,0:T(8,128)(2,1)S(1)} %slice_select_fusion.1), channel_id=1, source_target_pairs={{4,0},{8,12},{5,1},{9,13},{6,2},{10,14},{7,3},{11,15},{20,16},{24,... | collective-permute-start | bytes 1179656 | tf_op jit(solution)/shard_map/ppermute | solution.py:145

commit v13 on v12

--- a/solution.py
+++ b/solution.py
@@ -102,7 +102,7 @@
                                 if fill:
                                     pieces.append(jnp.zeros((RANK, fill), jnp.float32))
                                 packed.append(jnp.concatenate(pieces, axis=1))
-                            out_ref[owner_part, lax.rem(row + rows - owner, rows), shard] = jnp.concatenate(packed, axis=0).astype(jnp.bfloat16)
+                            out_ref[owner_part, owner, shard] = jnp.concatenate(packed, axis=0).astype(jnp.bfloat16)
 
         if base is None:
             write()
@@ -118,42 +118,35 @@
     )(*operands, *([] if base is None else [base]))
 
 
-def along_four(query, bases, eigens, by_owner):
+def along_four(queries, bases, eigens, by_owner):
     row = lax.axis_index("rows")
-    depth = bases[0].shape[1]
     eigens = [eigen.reshape(-1, 1) for eigen in eigens]
-    after = lax.ppermute(query, "rows", [(1, 0), (2, 1), (3, 2)])
-    before = lax.ppermute(query, "rows", [(0, 1), (1, 2), (2, 3)])
-    sent = [lax.dynamic_index_in_dim(by_owner, (row + k) % 4, 0, False) for k in range(4)]
-    query, sent = lax.optimization_barrier((query, sent))
-    blocks = to_owners(sent)
-    query, after, before = lax.optimization_barrier((query, after, before))
-    after_two = lax.ppermute(after, "rows", [(1, 0), (2, 1)])
-    before_two = lax.ppermute(before, "rows", [(1, 2), (2, 3)])
-    near = rotate(bases, eigens, [query, after, before], (0, depth))
-    near, blocks = lax.optimization_barrier((near, blocks))
-    stores = to_parts(jnp.concatenate(blocks, axis=0))
-    near, after_two, before_two = lax.optimization_barrier((near, after_two, before_two))
-    two_hidden, two_model = (
-        jnp.where(row < 2, after_two[:, side], before_two[:, side]) for side in (slice(0, depth), slice(depth, None))
-    )
-    ends = [(1, 0), (2, 3)]
-    three_hidden = lax.ppermute(two_hidden, "rows", ends)
-    far = rotate(bases, eigens, [(after_two, before_two)], (0, depth))
-    far, three_hidden, two_model = lax.optimization_barrier((far, three_hidden, two_model))
+    one = [
+        (
+            query,
+            lax.ppermute(query, "rows", [(1, 0), (2, 1), (3, 2)]),
+            lax.ppermute(query, "rows", [(0, 1), (1, 2), (2, 3)]),
+        )
+        for query in queries
+    ]
+    store = lax.all_to_all(by_owner, "rows", 0, 0, tiled=True)
+    one = [lax.optimization_barrier(side) for side in one]
+    two = [
+        (lax.ppermute(after, "rows", [(1, 0), (2, 1)]), lax.ppermute(before, "rows", [(1, 2), (2, 3)]))
+        for _, after, before in one
+    ]
+    near = [rotate([basis], [eigen], side, (0,))[0] for basis, eigen, side in zip(bases, eigens, one)]
+    near, two, store = lax.optimization_barrier((near, two, store))
+    stores = to_parts(store.reshape(-1, store.shape[-1]))
+    model = jnp.where(row < 2, *two[1])
+    model, two[0] = lax.optimization_barrier((model, two[0]))
+    hidden = jnp.where(row < 2, *two[0])
+    three = [lax.ppermute(side, "rows", [(1, 0), (2, 3)]) for side in (hidden, model)]
+    far = [rotate([basis], [eigen], [pair], (0,))[0] for basis, eigen, pair in zip(bases, eigens, two)]
     base = grams(stores, [near, far], [(0, 1, 3), (2,)])
-    three_model = lax.ppermute(two_model, "rows", ends)
-    last_hidden = rotate(bases[:1], eigens[:1], [three_hidden], (0,))
-    base, last_hidden, three_model = lax.optimization_barrier((base, last_hidden, three_model))
-    last_model = rotate(bases[1:], eigens[1:], [three_model], (0,))
-    return grams(stores, [last_hidden + last_model], [(3,)], base)
-
-
-def to_owners(sent):
-    rows = lax.axis_size("rows")
-    return sent[:1] + [
-        lax.ppermute(sent[k], "rows", [(i, (i + k) % rows) for i in range(rows)]) for k in range(1, rows)
-    ]
+    base, three = lax.optimization_barrier((base, three))
+    last = [rotate([basis], [eigen], [side], (0,))[0] for basis, eigen, side in zip(bases, eigens, three)]
+    return grams(stores, [last], [(3,)], base)
 
 
 def to_parts(store):
@@ -186,19 +179,16 @@
     share = bases[0].shape[0]
     depth = bases[0].shape[1]
 
-    query = jnp.concatenate(
-        [lax.dynamic_slice_in_dim(side[0], part * columns, columns, 0) for side in (query_hidden, query_model)],
-        axis=1,
-    )
+    own = [lax.dynamic_slice_in_dim(side[0], part * columns, columns, 0) for side in (query_hidden, query_model)]
     by_owner = jnp.concatenate(
         [side[0].reshape(held, rows, -1).transpose(1, 0, 2) for side in (train_hidden, train_model)], axis=2
     )
     if rows == 4:
-        partial = along_four(query, bases, eigens, by_owner)
+        partial = along_four(own, bases, eigens, by_owner)
     else:
         received = lax.all_to_all(by_owner, "rows", 0, 0, tiled=True)
         stores = to_parts(received.reshape(rows * held, -1))
-        every = lax.all_gather(query, "rows", axis=0, tiled=True)
+        every = lax.all_gather(jnp.concatenate(own, axis=1), "rows", axis=0, tiled=True)
         sides = []
         for basis, eigen, gathered, begin in zip(bases, eigens, (every[:, :depth], every[:, depth:]), (0, share)):
             rotated = jnp.einsum("eh,qh->eq", basis, gathered, preferred_element_type=jnp.float32)

time: 116 us -> 128 us (1.10)
  starting transfers between devices: 24.1 us -> 28.7 us
  Pallas kernels: 25 us -> 28.8 us
  local copies, waits for them, and re-layouts: 23.8 us -> 26.8 us
  other arithmetic: 1.86 us -> 3.87 us
    unnamed x23 -> x48, local copies, waits for them, and re-layouts: 19.3 us -> 24.3 us
    all_to_all x0 -> x1, starting transfers between devices: none -> 4.42 us  [along_four(): store = lax.all_to_all(by_owner, 'rows', 0, 0, tiled=True)]
    pallas_call x4 -> x6, Pallas kernels: 23.2 us -> 27 us  [rotate(): pl.pallas_call(kernel, out_shape=[jax.ShapeDtypeStruct((basis.shape[0], h...]
    ppermute x9 -> x10, starting transfers between devices: 18.9 us -> 22.5 us  [the longest x2 11.7 us: along_four(): lax.ppermute(query, 'rows', [(0, 1), (1, 2), (2, 3)])]
    ppermute x1, starting transfers between devices: 5.18 us -> 1.77 us  [to_parts(): lax.ppermute(store, 'parts', [(i, (i + j) % parts) for i in range(parts)])]
    select_n x2, other arithmetic: 0.11 us -> 2.18 us  [the longest x1 1.13 us: along_four(): hidden = jnp.where(row < 2, *two[0])]
    ppermute x9 -> x10, waiting for transfers between devices: 24.6 us -> 24.1 us  [the longest x2 15.7 us: along_four(): lax.ppermute(query, 'rows', [(1, 0), (2, 1), (3, 2)])]
  transfers between devices with their start and end apart: 10 -> 12, of which waited for: 4 -> 3; matrix products, arithmetic and copies ran while one was open for 5% -> 3% of each run, Pallas kernels for 19% -> 16%
where the time goes in v13:
time: 128 us; the launch traced here: 127 us
  Pallas kernels  28.8 us (22%)
  starting transfers between devices  28.7 us (22%)
  local copies, waits for them, and re-layouts  26.8 us (21%)
  waiting for transfers between devices  24.1 us (19%)
  blocking collectives  14.8 us (12%)
  other arithmetic  3.87 us (3%)
    pallas_call x6, Pallas kernels, rotate(): pl.pallas_call(kernel, out_shape=[jax.ShapeDtypeStruct((basis.shape[0], h...  27 us
    unnamed x48, local copies, waits for them, and re-layouts  24.3 us
    ppermute x2, waiting for transfers between devices, along_four(): lax.ppermute(query, 'rows', [(1, 0), (2, 1), (3, 2)])  15.7 us
    all_to_all x1, blocking collectives, per_device(): lax.all_to_all(partial.reshape((parts * rows * layers,) + partial.shape[3...  14.8 us
    ppermute x2, starting transfers between devices, along_four(): lax.ppermute(query, 'rows', [(0, 1), (1, 2), (2, 3)])  11.7 us
    ppermute x2, waiting for transfers between devices, along_four(): lax.ppermute(side, 'rows', [(1, 0), (2, 3)])  8.11 us
    all_to_all x1, starting transfers between devices, along_four(): store = lax.all_to_all(by_owner, 'rows', 0, 0, tiled=True)  4.42 us
    ppermute x2, starting transfers between devices, along_four(): lax.ppermute(before, 'rows', [(1, 2), (2, 3)])  2.91 us
  transfers between devices with their start and end apart: 12, of which 3 were waited for; matrix products, arithmetic and copies ran while one was open for 3% of the time, Pallas kernels for 16%

profile of v13, /device:TPU:0, one launch (start us, length us, event | category | flops | bytes accessed | tf_op | source)
XLA Modules:
  0.0 127.5 jit_solution(8198174976330730209)
XLA Ops:
  1.3 1.3 %collective-permute-start = (bf16[48,6144]{1,0:T(8,128)(2,1)S(1)}, bf16[48,6144]{1,0:T(8,128)(2,1)}, u32[]{:S(2)}, u32[]{:S(2)}) collective-permute-start(bf16[48,6144]{1,0:T(8,128)(2,1)S(1)} %dynamic-slice_bitcast_fusion.refs_2_), channel_id=1, source_target_pairs={{4,0},{8,4},{12,8},{5,1},{9,5},{13,9},{6,2},{10,6},{14,10},{7,3},{... | collective-permute-start | bytes 1769480 | tf_op jit(solution)/shard_map/ppermute | solution.py:127
  2.6 6.4 %collective-permute-start.1 = (bf16[48,6144]{1,0:T(8,128)(2,1)S(1)}, bf16[48,6144]{1,0:T(8,128)(2,1)}, u32[]{:S(2)}, u32[]{:S(2)}) collective-permute-start(bf16[48,6144]{1,0:T(8,128)(2,1)S(1)} %dynamic-slice_bitcast_fusion.refs_2_), channel_id=1, source_target_pairs={{0,4},{4,8},{8,12},{1,5},{5,9},{9,13},{2,6},{6,10},{10,14},{3,7},{... | collective-permute-start | bytes 1769480 | tf_op jit(solution)/shard_map/ppermute | solution.py:128
  9.0 1.4 %reshape_squeeze.6 = bf16[40,4,1536]{2,1,0:T(4,128)(2,1)S(1)} reshape(bf16[1,40,6144]{2,1,0:T(8,128)(2,1)} %param.10) | data formatting | bytes 983040 | tf_op jit(solution)/shard_map/reshape;squeeze | solution.py:184
  11.8 4.4 %all-to-all-start = ((bf16[4,40,2560]{2,1,0:T(8,128)(2,1)}), bf16[4,40,2560]{2,1,0:T(8,128)(2,1)S(1)}, u32[]{:S(2)}, u32[]{:S(2)}) async-start(bf16[4,40,2560]{2,1,0:T(8,128)(2,1)} %pad_maximum_fusion), calls=%async_computation | async-start | bytes 1638400 | tf_op jit(solution)/shard_map/all_to_all | solution.py:132
  16.3 1.3 %collective-permute-start.2 = (bf16[48,4096]{1,0:T(8,128)(2,1)S(1)}, bf16[48,4096]{1,0:T(8,128)(2,1)}, u32[]{:S(2)}, u32[]{:S(2)}) collective-permute-start(bf16[48,4096]{1,0:T(8,128)(2,1)S(1)} %dynamic-slice_bitcast_fusion.1.refs_2_), channel_id=1, source_target_pairs={{4,0},{8,4},{12,8},{5,1},{9,5},{13,9},{6,2},{10,6},{14,10},{7,3},{... | collective-permute-start | bytes 1179656 | tf_op jit(solution)/shard_map/ppermute | solution.py:127
  17.6 5.3 %collective-permute-start.3 = (bf16[48,4096]{1,0:T(8,128)(2,1)S(1)}, bf16[48,4096]{1,0:T(8,128)(2,1)}, u32[]{:S(2)}, u32[]{:S(2)}) collective-permute-start(bf16[48,4096]{1,0:T(8,128)(2,1)S(1)} %dynamic-slice_bitcast_fusion.1.refs_2_), channel_id=1, source_target_pairs={{0,4},{4,8},{8,12},{1,5},{5,9},{9,13},{2,6},{6,10},{10,14},{3,7},{... | collective-permute-start | bytes 1179656 | tf_op jit(solution)/shard_map/ppermute | solution.py:128
  25.0 1.5 %collective-permute-start.5 = (bf16[48,6144]{1,0:T(8,128)(2,1)}, bf16[48,6144]{1,0:T(8,128)(2,1)}, u32[]{:S(2)}, u32[]{:S(2)}) collective-permute-start(bf16[48,6144]{1,0:T(8,128)(2,1)} %collective-permute-done.1.refs_4_), channel_id=1, source_target_pairs={{4,8},{8,12},{5,9},{9,13},{6,10},{10,14},{7,11},{11,15},{20,24},{2... | collective-permute-start | bytes 1769480 | tf_op jit(solution)/shard_map/ppermute | solution.py:135
  26.4 15.7 %collective-permute-done.2.refs_3_ = bf16[48,4096]{1,0:T(8,128)(2,1)} collective-permute-done((bf16[48,4096]{1,0:T(8,128)(2,1)S(1)}, bf16[48,4096]{1,0:T(8,128)(2,1)}, u32[]{:S(2)}, u32[]{:S(2)}) %collective-permute-start.2) | collective-permute-done | bytes 393248 | tf_op jit(solution)/shard_map/ppermute | solution.py:127
  43.7 1.4 %collective-permute-start.7 = (bf16[48,4096]{1,0:T(8,128)(2,1)}, bf16[48,4096]{1,0:T(8,128)(2,1)}, u32[]{:S(2)}, u32[]{:S(2)}) collective-permute-start(bf16[48,4096]{1,0:T(8,128)(2,1)} %collective-permute-done.3.refs_4_), channel_id=1, source_target_pairs={{4,8},{8,12},{5,9},{9,13},{6,10},{10,14},{7,11},{11,15},{20,24},{2... | collective-permute-start | bytes 1179656 | tf_op jit(solution)/shard_map/ppermute | solution.py:135
  45.7 3.4 %copy-done.3 = bf16[1,1024,4096]{2,1,0:T(8,128)(2,1)S(1)} copy-done((bf16[1,1024,4096]{2,1,0:T(8,128)(2,1)S(1)}, bf16[1,1024,4096]{2,1,0:T(8,128)(2,1)}, u32[]{:S(2)}) %copy-start.3) | copy-done | bytes 8388632
  50.1 3.5 %shard_map.83.refs_3_ = bf16[1024,144]{1,0:T(8,128)(2,1)S(1)} custom-call(bf16[1024,4096]{1,0:T(8,128)(2,1)S(1)} %bitcast.27, f32[1024,1]{1,0:T(8,128)S(1)} %copy.21.refs_1_, bf16[48,4096]{1,0:T(8,128)(2,1)S(1)} %copy-done.12, bf16[48,4096]{1,0:T(8,128)(2,1)} %collective-permute-done.2.refs_3_, bf16[48,4096]{1,0:T(8,128)(2,1)} %collective-permute-done.3.refs_4_), custom_call_target="tpu_custom_call" | custom-call | flops 1 | bytes 1 | tf_op jit(solution)/shard_map/pallas_call | solution.py:50
  54.4 6.4 %copy-done.1 = bf16[1,1536,6144]{2,1,0:T(8,128)(2,1)S(1)} copy-done((bf16[1,1536,6144]{2,1,0:T(8,128)(2,1)S(1)}, bf16[1,1536,6144]{2,1,0:T(8,128)(2,1)}, u32[]{:S(2)}) %copy-start.1) | copy-done | bytes 18874392
  60.7 6.3 %shard_map.82.refs_2_ = bf16[1536,144]{1,0:T(8,128)(2,1)S(1)} custom-call(bf16[1536,6144]{1,0:T(8,128)(2,1)S(1)} %bitcast.22, f32[1536,1]{1,0:T(8,128)S(1)} %copy.20.refs_1_, bf16[48,6144]{1,0:T(8,128)(2,1)S(1)} %copy-done.8, bf16[48,6144]{1,0:T(8,128)(2,1)} %collective-permute-done.refs_3_, bf16[48,6144]{1,0:T(8,128)(2,1)} %collective-permute-done.1.refs_4_), custom_call_target="tpu_custom_call" | custom-call | flops 1 | bytes 1 | tf_op jit(solution)/shard_map/pallas_call | solution.py:50
  69.0 1.8 %collective-permute-start.8 = (bf16[160,2560]{1,0:T(8,128)(2,1)S(1)}, bf16[160,2560]{1,0:T(8,128)(2,1)S(1)}, u32[]{:S(2)}, u32[]{:S(2)}) collective-permute-start(bf16[160,2560]{1,0:T(8,128)(2,1)S(1)} %bitcast.32), channel_id=1, source_target_pairs={{0,16},{16,0},{1,17},{17,1},{2,18},{18,2},{3,19},{19,3},{4,20},{20... | collective-permute-start | bytes 2457608 | tf_op jit(solution)/shard_map/ppermute | solution.py:155
  71.9 1.3 %collective-permute-start.9 = (bf16[48,6144]{1,0:T(8,128)(2,1)S(1)}, bf16[48,6144]{1,0:T(8,128)(2,1)S(1)}, u32[]{:S(2)}, u32[]{:S(2)}) collective-permute-start(bf16[48,6144]{1,0:T(8,128)(2,1)S(1)} %broadcast_select_fusion), channel_id=1, source_target_pairs={{4,0},{8,12},{5,1},{9,13},{6,2},{10,14},{7,3},{11,15},{20,16},{24,... | collective-permute-start | bytes 1769480 | tf_op jit(solution)/shard_map/ppermute | solution.py:144
  73.2 1.5 %collective-permute-start.10 = (bf16[48,4096]{1,0:T(8,128)(2,1)S(1)}, bf16[48,4096]{1,0:T(8,128)(2,1)S(1)}, u32[]{:S(2)}, u32[]{:S(2)}) collective-permute-start(bf16[48,4096]{1,0:T(8,128)(2,1)S(1)} %broadcast_select_fusion.1), channel_id=1, source_target_pairs={{4,0},{8,12},{5,1},{9,13},{6,2},{10,14},{7,3},{11,15},{20,16},{24,... | collective-permute-start | bytes 1179656 | tf_op jit(solution)/shard_map/ppermute | solution.py:144
  74.7 3.4 %copy-done.4 = bf16[1,1024,4096]{2,1,0:T(8,128)(2,1)S(1)} copy-done((bf16[1,1024,4096]{2,1,0:T(8,128)(2,1)S(1)}, bf16[1,1024,4096]{2,1,0:T(8,128)(2,1)}, u32[]{:S(2)}) %copy-start.4) | copy-done | bytes 8388632
  78.1 3.6 %shard_map.85.refs_5_ = bf16[1024,48]{1,0:T(8,128)(2,1)S(1)} custom-call(bf16[1024,4096]{1,0:T(8,128)(2,1)S(1)} %bitcast.28, f32[1024,1]{1,0:T(8,128)S(1)} %copy.21.refs_1_, bf16[48,4096]{1,0:T(8,128)(2,1)} %collective-permute-done.6.refs_2_, bf16[48,4096]{1,0:T(8,128)(2,1)} %collective-permute-done.7.refs_3_), custom_call_target="tpu_custom_call" | custom-call | flops 1 | bytes 1 | tf_op jit(solution)/shard_map/pallas_call | solution.py:50
  81.6 6.4 %copy-done.2 = bf16[1,1536,6144]{2,1,0:T(8,128)(2,1)S(1)} copy-done((bf16[1,1536,6144]{2,1,0:T(8,128)(2,1)S(1)}, bf16[1,1536,6144]{2,1,0:T(8,128)(2,1)}, u32[]{:S(2)}) %copy-start.2) | copy-done | bytes 18874392
  88.0 6.4 %shard_map.84.refs_4_ = bf16[1536,48]{1,0:T(8,128)(2,1)S(1)} custom-call(bf16[1536,6144]{1,0:T(8,128)(2,1)S(1)} %bitcast.23, f32[1536,1]{1,0:T(8,128)S(1)} %copy.20.refs_1_, bf16[48,6144]{1,0:T(8,128)(2,1)} %collective-permute-done.4.refs_2_, bf16[48,6144]{1,0:T(8,128)(2,1)} %collective-permute-done.5.refs_3_), custom_call_target="tpu_custom_call" | custom-call | flops 1 | bytes 1 | tf_op jit(solution)/shard_map/pallas_call | solution.py:50
  95.6 8.1 %collective-permute-done.10.refs_2_ = bf16[48,4096]{1,0:T(8,128)(2,1)S(1)} collective-permute-done((bf16[48,4096]{1,0:T(8,128)(2,1)S(1)}, bf16[48,4096]{1,0:T(8,128)(2,1)S(1)}, u32[]{:S(2)}, u32[]{:S(2)}) %collective-permute-start.10) | collective-permute-done | bytes 393248 | tf_op jit(solution)/shard_map/ppermute | solution.py:144
  103.7 2.3 %shard_map.88.refs_3_ = bf16[1024,48]{1,0:T(8,128)(2,1)S(1)} custom-call(bf16[1024,4096]{1,0:T(8,128)(2,1)S(1)} %bitcast.31, f32[1024,1]{1,0:T(8,128)S(1)} %copy.21.refs_1_, bf16[48,4096]{1,0:T(8,128)(2,1)S(1)} %collective-permute-done.10.refs_2_), custom_call_target="tpu_custom_call" | custom-call | flops 1 | bytes 1 | tf_op jit(solution)/shard_map/pallas_call | solution.py:50
  106.1 5.0 %shard_map.87.refs_2_ = bf16[1536,48]{1,0:T(8,128)(2,1)S(1)} custom-call(bf16[1536,6144]{1,0:T(8,128)(2,1)S(1)} %bitcast.26, f32[1536,1]{1,0:T(8,128)S(1)} %copy.20.refs_1_, bf16[48,6144]{1,0:T(8,128)(2,1)S(1)} %collective-permute-done.9.refs_2_), custom_call_target="tpu_custom_call" | custom-call | flops 1 | bytes 1 | tf_op jit(solution)/shard_map/pallas_call | solution.py:50
  111.8 14.8 %all_to_all.10 = bf16[32,16,256]{2,1,0:T(8,128)(2,1)S(1)} all-to-all(bf16[32,16,256]{2,1,0:T(8,128)(2,1)S(1)} %bitcast.35), channel_id=1, replica_groups=mesh['parts'=2,'rows'=4,'layer'=4] {'parts','rows','layer'}, dimensions={0} | all-to-all | bytes 524288 | tf_op jit(solution)/shard_map/all_to_all | solution.py:208
  (76 shorter events, 14.5 us)
Async XLA Ops:
  0.0 10.5 %copy-start.13 = (bf16[1,40,4096]{2,1,0:T(8,128)(2,1)S(1)}, bf16[1,40,4096]{2,1,0:T(8,128)(2,1)}, u32[]{:S(2)}) copy-start(bf16[1,40,4096]{2,1,0:T(8,128)(2,1)} %param.11) | copy-start | bytes 983044
  1.3 9.5 %copy-start.7 = (bf16[48,6144]{1,0:T(8,128)(2,1)}, bf16[48,6144]{1,0:T(8,128)(2,1)S(1)}, u32[]{:S(2)}) copy-start(bf16[48,6144]{1,0:T(8,128)(2,1)S(1)} %dynamic-slice_bitcast_fusion.refs_2_) | copy-start | bytes 1769476
  1.3 22.3 %collective-permute-start = (bf16[48,6144]{1,0:T(8,128)(2,1)S(1)}, bf16[48,6144]{1,0:T(8,128)(2,1)}, u32[]{:S(2)}, u32[]{:S(2)}) collective-permute-start(bf16[48,6144]{1,0:T(8,128)(2,1)S(1)} %dynamic-slice_bitcast_fusion.refs_2_), channel_id=1, source_target_pairs={{4,0},{8,4},{12,8},{5,1},{9,5},{13,9},{6,2},{10,6},{14,10},{7,3},{... | collective-permute-start | bytes 1769480 | tf_op jit(solution)/shard_map/ppermute | solution.py:127
  2.6 21.0 %collective-permute-start.1 = (bf16[48,6144]{1,0:T(8,128)(2,1)S(1)}, bf16[48,6144]{1,0:T(8,128)(2,1)}, u32[]{:S(2)}, u32[]{:S(2)}) collective-permute-start(bf16[48,6144]{1,0:T(8,128)(2,1)S(1)} %dynamic-slice_bitcast_fusion.refs_2_), channel_id=1, source_target_pairs={{0,4},{4,8},{8,12},{1,5},{5,9},{9,13},{2,6},{6,10},{10,14},{3,7},{... | collective-permute-start | bytes 1769480 | tf_op jit(solution)/shard_map/ppermute | solution.py:128
  10.9 34.2 %copy-start.16 = (f32[1,1024]{1,0:T(1,128)S(1)}, f32[1,1024]{1,0:T(1,128)}, u32[]{:S(2)}) copy-start(f32[1,1024]{1,0:T(1,128)} %param.15) | copy-start | bytes 12292
  11.8 33.5 %copy-start.15 = (f32[1,1536]{1,0:T(1,128)S(1)}, f32[1,1536]{1,0:T(1,128)}, u32[]{:S(2)}) copy-start(f32[1,1536]{1,0:T(1,128)} %param.14) | copy-start | bytes 18436
  11.8 56.1 %all-to-all-start = ((bf16[4,40,2560]{2,1,0:T(8,128)(2,1)}), bf16[4,40,2560]{2,1,0:T(8,128)(2,1)S(1)}, u32[]{:S(2)}, u32[]{:S(2)}) async-start(bf16[4,40,2560]{2,1,0:T(8,128)(2,1)} %pad_maximum_fusion), calls=%async_computation | async-start | bytes 1638400 | tf_op jit(solution)/shard_map/all_to_all | solution.py:132
  16.3 25.8 %collective-permute-start.2 = (bf16[48,4096]{1,0:T(8,128)(2,1)S(1)}, bf16[48,4096]{1,0:T(8,128)(2,1)}, u32[]{:S(2)}, u32[]{:S(2)}) collective-permute-start(bf16[48,4096]{1,0:T(8,128)(2,1)S(1)} %dynamic-slice_bitcast_fusion.1.refs_2_), channel_id=1, source_target_pairs={{4,0},{8,4},{12,8},{5,1},{9,5},{13,9},{6,2},{10,6},{14,10},{7,3},{... | collective-permute-start | bytes 1179656 | tf_op jit(solution)/shard_map/ppermute | solution.py:127
  17.6 24.8 %collective-permute-start.3 = (bf16[48,4096]{1,0:T(8,128)(2,1)S(1)}, bf16[48,4096]{1,0:T(8,128)(2,1)}, u32[]{:S(2)}, u32[]{:S(2)}) collective-permute-start(bf16[48,4096]{1,0:T(8,128)(2,1)S(1)} %dynamic-slice_bitcast_fusion.1.refs_2_), channel_id=1, source_target_pairs={{0,4},{4,8},{8,12},{1,5},{5,9},{9,13},{2,6},{6,10},{10,14},{3,7},{... | collective-permute-start | bytes 1179656 | tf_op jit(solution)/shard_map/ppermute | solution.py:128
  23.7 44.2 %collective-permute-start.4 = (bf16[48,6144]{1,0:T(8,128)(2,1)}, bf16[48,6144]{1,0:T(8,128)(2,1)}, u32[]{:S(2)}, u32[]{:S(2)}) collective-permute-start(bf16[48,6144]{1,0:T(8,128)(2,1)} %collective-permute-done.refs_3_), channel_id=1, source_target_pairs={{4,0},{8,4},{5,1},{9,5},{6,2},{10,6},{7,3},{11,7},{20,16},{24,20},... | collective-permute-start | bytes 1769480 | tf_op jit(solution)/shard_map/ppermute | solution.py:135
  25.0 43.0 %collective-permute-start.5 = (bf16[48,6144]{1,0:T(8,128)(2,1)}, bf16[48,6144]{1,0:T(8,128)(2,1)}, u32[]{:S(2)}, u32[]{:S(2)}) collective-permute-start(bf16[48,6144]{1,0:T(8,128)(2,1)} %collective-permute-done.1.refs_4_), channel_id=1, source_target_pairs={{4,8},{8,12},{5,9},{9,13},{6,10},{10,14},{7,11},{11,15},{20,24},{2... | collective-permute-start | bytes 1769480 | tf_op jit(solution)/shard_map/ppermute | solution.py:135
  42.4 25.5 %collective-permute-start.6 = (bf16[48,4096]{1,0:T(8,128)(2,1)}, bf16[48,4096]{1,0:T(8,128)(2,1)}, u32[]{:S(2)}, u32[]{:S(2)}) collective-permute-start(bf16[48,4096]{1,0:T(8,128)(2,1)} %collective-permute-done.2.refs_3_), channel_id=1, source_target_pairs={{4,0},{8,4},{5,1},{9,5},{6,2},{10,6},{7,3},{11,7},{20,16},{24,20},... | collective-permute-start | bytes 1179656 | tf_op jit(solution)/shard_map/ppermute | solution.py:135
  43.7 24.2 %collective-permute-start.7 = (bf16[48,4096]{1,0:T(8,128)(2,1)}, bf16[48,4096]{1,0:T(8,128)(2,1)}, u32[]{:S(2)}, u32[]{:S(2)}) collective-permute-start(bf16[48,4096]{1,0:T(8,128)(2,1)} %collective-permute-done.3.refs_4_), channel_id=1, source_target_pairs={{4,8},{8,12},{5,9},{9,13},{6,10},{10,14},{7,11},{11,15},{20,24},{2... | collective-permute-start | bytes 1179656 | tf_op jit(solution)/shard_map/ppermute | solution.py:135
  69.0 25.4 %collective-permute-start.8 = (bf16[160,2560]{1,0:T(8,128)(2,1)S(1)}, bf16[160,2560]{1,0:T(8,128)(2,1)S(1)}, u32[]{:S(2)}, u32[]{:S(2)}) collective-permute-start(bf16[160,2560]{1,0:T(8,128)(2,1)S(1)} %bitcast.32), channel_id=1, source_target_pairs={{0,16},{16,0},{1,17},{17,1},{2,18},{18,2},{3,19},{19,3},{4,20},{20... | collective-permute-start | bytes 2457608 | tf_op jit(solution)/shard_map/ppermute | solution.py:155
  71.9 31.8 %collective-permute-start.9 = (bf16[48,6144]{1,0:T(8,128)(2,1)S(1)}, bf16[48,6144]{1,0:T(8,128)(2,1)S(1)}, u32[]{:S(2)}, u32[]{:S(2)}) collective-permute-start(bf16[48,6144]{1,0:T(8,128)(2,1)S(1)} %broadcast_select_fusion), channel_id=1, source_target_pairs={{4,0},{8,12},{5,1},{9,13},{6,2},{10,14},{7,3},{11,15},{20,16},{24,... | collective-permute-start | bytes 1769480 | tf_op jit(solution)/shard_map/ppermute | solution.py:144
  73.2 30.5 %collective-permute-start.10 = (bf16[48,4096]{1,0:T(8,128)(2,1)S(1)}, bf16[48,4096]{1,0:T(8,128)(2,1)S(1)}, u32[]{:S(2)}, u32[]{:S(2)}) collective-permute-start(bf16[48,4096]{1,0:T(8,128)(2,1)S(1)} %broadcast_select_fusion.1), channel_id=1, source_target_pairs={{4,0},{8,12},{5,1},{9,13},{6,2},{10,14},{7,3},{11,15},{20,16},{24,... | collective-permute-start | bytes 1179656 | tf_op jit(solution)/shard_map/ppermute | solution.py:144
  78.1 25.6 %slice-start.5 = ((s8[8388608]{0:T(1024)(128)(4,1)}), s8[4194304]{0:T(1024)(128)(4,1)S(1)}, s32[]{:S(2)}) async-start(s8[8388608]{0:T(1024)(128)(4,1)} %bitcast.29), calls=%async_computation.7 | async-start | bytes 8388608
  88.0 6.5 %copy-start.10 = (bf16[1024,144]{1,0:T(8,128)(2,1)S(1)}, bf16[1024,144]{1,0:T(8,128)(2,1)}, u32[]{:S(2)}) copy-start(bf16[1024,144]{1,0:T(8,128)(2,1)} %copy-done.9) | copy-start | bytes 884740
  88.0 15.7 %slice-start.6 = ((s8[8388608]{0:T(1024)(128)(4,1)}), s8[4194304]{0:T(1024)(128)(4,1)S(1)}, s32[]{:S(2)}) async-start(s8[8388608]{0:T(1024)(128)(4,1)} %bitcast.29), calls=%async_computation.8 | async-start | bytes 8388608
  88.0 18.0 %slice-start = ((s8[18874368]{0:T(1024)(128)(4,1)}), s8[4194304]{0:T(1024)(128)(4,1)S(1)}, s32[]{:S(2)}) async-start(s8[18874368]{0:T(1024)(128)(4,1)} %bitcast.24), calls=%async_computation.2 | async-start | bytes 8388608
  88.0 18.0 %slice-start.1 = ((s8[18874368]{0:T(1024)(128)(4,1)}), s8[4194304]{0:T(1024)(128)(4,1)S(1)}, s32[]{:S(2)}) async-start(s8[18874368]{0:T(1024)(128)(4,1)} %bitcast.24), calls=%async_computation.3 | async-start | bytes 8388608
  88.0 18.0 %slice-start.2 = ((s8[18874368]{0:T(1024)(128)(4,1)}), s8[4194304]{0:T(1024)(128)(4,1)S(1)}, s32[]{:S(2)}) async-start(s8[18874368]{0:T(1024)(128)(4,1)} %bitcast.24), calls=%async_computation.4 | async-start | bytes 8388608
  88.0 18.0 %slice-start.3 = ((s8[18874368]{0:T(1024)(128)(4,1)}), s8[2097152]{0:T(1024)(128)(4,1)S(1)}, s32[]{:S(2)}) async-start(s8[18874368]{0:T(1024)(128)(4,1)} %bitcast.24), calls=%async_computation.5 | async-start | bytes 4194304
  95.6 10.5 %slice-start.4 = ((s8[18874368]{0:T(1024)(128)(4,1)}), s8[4194304]{0:T(1024)(128)(4,1)S(1)}, s32[]{:S(2)}) async-start(s8[18874368]{0:T(1024)(128)(4,1)} %bitcast.24), calls=%async_computation.6 | async-start | bytes 8388608
  (12 other events, 40.4 us)

commit v14 on v12

--- a/solution.py
+++ b/solution.py
@@ -102,7 +102,7 @@
                                 if fill:
                                     pieces.append(jnp.zeros((RANK, fill), jnp.float32))
                                 packed.append(jnp.concatenate(pieces, axis=1))
-                            out_ref[owner_part, lax.rem(row + rows - owner, rows), shard] = jnp.concatenate(packed, axis=0).astype(jnp.bfloat16)
+                            out_ref[owner_part, owner, shard] = jnp.concatenate(packed, axis=0).astype(jnp.bfloat16)
 
         if base is None:
             write()
@@ -124,15 +124,13 @@
     eigens = [eigen.reshape(-1, 1) for eigen in eigens]
     after = lax.ppermute(query, "rows", [(1, 0), (2, 1), (3, 2)])
     before = lax.ppermute(query, "rows", [(0, 1), (1, 2), (2, 3)])
-    sent = [lax.dynamic_index_in_dim(by_owner, (row + k) % 4, 0, False) for k in range(4)]
-    query, sent = lax.optimization_barrier((query, sent))
-    blocks = to_owners(sent)
-    query, after, before = lax.optimization_barrier((query, after, before))
+    by_owner, query, after, before = lax.optimization_barrier((by_owner, query, after, before))
+    store = lax.all_to_all(by_owner, "rows", 0, 0, tiled=True)
     after_two = lax.ppermute(after, "rows", [(1, 0), (2, 1)])
     before_two = lax.ppermute(before, "rows", [(1, 2), (2, 3)])
     near = rotate(bases, eigens, [query, after, before], (0, depth))
-    near, blocks = lax.optimization_barrier((near, blocks))
-    stores = to_parts(jnp.concatenate(blocks, axis=0))
+    near, store = lax.optimization_barrier((near, store))
+    stores = to_parts(store.reshape(-1, store.shape[-1]))
     near, after_two, before_two = lax.optimization_barrier((near, after_two, before_two))
     two_hidden, two_model = (
         jnp.where(row < 2, after_two[:, side], before_two[:, side]) for side in (slice(0, depth), slice(depth, None))
@@ -147,13 +145,6 @@
     base, last_hidden, three_model = lax.optimization_barrier((base, last_hidden, three_model))
     last_model = rotate(bases[1:], eigens[1:], [three_model], (0,))
     return grams(stores, [last_hidden + last_model], [(3,)], base)
-
-
-def to_owners(sent):
-    rows = lax.axis_size("rows")
-    return sent[:1] + [
-        lax.ppermute(sent[k], "rows", [(i, (i + k) % rows) for i in range(rows)]) for k in range(1, rows)
-    ]
 
 
 def to_parts(store):

time: 116 us -> 129 us (1.11)
  waiting for transfers between devices: 24.6 us -> 36.6 us
  blocking collectives: 15.6 us -> 12 us
  local copies, waits for them, and re-layouts: 23.8 us -> 26.2 us
  other arithmetic: 1.86 us -> 4.24 us
  starting transfers between devices: 24.1 us -> 22.3 us
  Pallas kernels: 25 us -> 26.5 us
    ppermute x1, waiting for transfers between devices: 3.31 us -> 10.7 us  [along_four(): after_two = lax.ppermute(after, 'rows', [(1, 0), (2, 1)])]
    all_to_all x0 -> x1, starting transfers between devices: none -> 6.99 us  [along_four(): store = lax.all_to_all(by_owner, 'rows', 0, 0, tiled=True)]
    ppermute x3 -> x0, starting transfers between devices: 6.04 us -> none  [to_owners(): lax.ppermute(sent[k], 'rows', [(i, (i + k) % rows) for i in range(rows)])]
    ppermute x1, waiting for transfers between devices: 5.98 us -> 0.01 us  [along_four(): three_hidden = lax.ppermute(two_hidden, 'rows', ends)]
    ppermute x1, waiting for transfers between devices: 11.8 us -> 17.2 us  [along_four(): after = lax.ppermute(query, 'rows', [(1, 0), (2, 1), (3, 2)])]
    unnamed x23 -> x34, local copies, waits for them, and re-layouts: 19.3 us -> 23.7 us
    ppermute x1, waiting for transfers between devices: 3.43 us -> 7.61 us  [along_four(): three_model = lax.ppermute(two_model, 'rows', ends)]
    all_to_all x1, blocking collectives: 15.6 us -> 12 us  [per_device(): lax.all_to_all(partial.reshape((parts * rows * layers,) + partial.shape[3...]
  transfers between devices with their start and end apart: 10 -> 8, of which waited for: 4 -> 4; matrix products, arithmetic and copies ran while one was open for 5% -> 3% of each run, Pallas kernels for 19% -> 18%
where the time goes in v14:
time: 129 us; the launch traced here: 128 us
  waiting for transfers between devices  36.6 us (28%)
  Pallas kernels  26.5 us (21%)
  local copies, waits for them, and re-layouts  26.2 us (20%)
  starting transfers between devices  22.3 us (17%)
  blocking collectives  12 us (9%)
  other arithmetic  4.24 us (3%)
    pallas_call x4, Pallas kernels, rotate(): pl.pallas_call(kernel, out_shape=[jax.ShapeDtypeStruct((basis.shape[0], h...  24.7 us
    unnamed x34, local copies, waits for them, and re-layouts  23.7 us
    ppermute x1, waiting for transfers between devices, along_four(): after = lax.ppermute(query, 'rows', [(1, 0), (2, 1), (3, 2)])  17.2 us
    all_to_all x1, blocking collectives, per_device(): lax.all_to_all(partial.reshape((parts * rows * layers,) + partial.shape[3...  12 us
    ppermute x1, waiting for transfers between devices, along_four(): after_two = lax.ppermute(after, 'rows', [(1, 0), (2, 1)])  10.7 us
    ppermute x1, waiting for transfers between devices, along_four(): three_model = lax.ppermute(two_model, 'rows', ends)  7.61 us
    all_to_all x1, starting transfers between devices, along_four(): store = lax.all_to_all(by_owner, 'rows', 0, 0, tiled=True)  6.99 us
    ppermute x1, starting transfers between devices, along_four(): before = lax.ppermute(query, 'rows', [(0, 1), (1, 2), (2, 3)])  6.53 us
  transfers between devices with their start and end apart: 8, of which 4 were waited for; matrix products, arithmetic and copies ran while one was open for 3% of the time, Pallas kernels for 18%

profile of v14, /device:TPU:0, one launch (start us, length us, event | category | flops | bytes accessed | tf_op | source)
XLA Modules:
  0.0 128.2 jit_solution(14880012051383250296)
XLA Ops:
  0.0 1.3 copy-done
  2.5 1.3 %collective-permute-start = (bf16[48,10240]{1,0:T(8,128)(2,1)S(1)}, bf16[48,10240]{1,0:T(8,128)(2,1)}, u32[]{:S(2)}, u32[]{:S(2)}) collective-permute-start(bf16[48,10240]{1,0:T(8,128)(2,1)S(1)} %pad_maximum_fusion.refs_4_), channel_id=1, source_target_pairs={{4,0},{8,4},{12,8},{5,1},{9,5},{13,9},{6,2},{10,6},{14,10},{7,3},{... | collective-permute-start | bytes 2949128 | tf_op jit(solution)/shard_map/ppermute | solution.py:125
  3.8 6.5 %collective-permute-start.1 = (bf16[48,10240]{1,0:T(8,128)(2,1)S(1)}, bf16[48,10240]{1,0:T(8,128)(2,1)}, u32[]{:S(2)}, u32[]{:S(2)}) collective-permute-start(bf16[48,10240]{1,0:T(8,128)(2,1)S(1)} %pad_maximum_fusion.refs_4_), channel_id=1, source_target_pairs={{0,4},{4,8},{8,12},{1,5},{5,9},{9,13},{2,6},{6,10},{10,14},{3,7},{... | collective-permute-start | bytes 2949128 | tf_op jit(solution)/shard_map/ppermute | solution.py:126
  12.1 17.2 %collective-permute-done.refs_5_ = bf16[48,10240]{1,0:T(8,128)(2,1)} collective-permute-done((bf16[48,10240]{1,0:T(8,128)(2,1)S(1)}, bf16[48,10240]{1,0:T(8,128)(2,1)}, u32[]{:S(2)}, u32[]{:S(2)}) %collective-permute-start) | collective-permute-done | bytes 983072 | tf_op jit(solution)/shard_map/ppermute | solution.py:125
  30.4 7.0 %all-to-all-start = ((bf16[4,40,2560]{2,1,0:T(8,128)(2,1)}), bf16[4,40,2560]{2,1,0:T(8,128)(2,1)S(1)}, u32[]{:S(2)}, u32[]{:S(2)}) async-start(bf16[4,40,2560]{2,1,0:T(8,128)(2,1)} %pad_maximum_fusion.1), calls=%async_computation | async-start | bytes 1638400 | tf_op jit(solution)/shard_map/all_to_all | solution.py:128
  37.3 1.3 collective-permute-start.3
  38.6 1.6 %collective-permute-start.4 = (bf16[48,10240]{1,0:T(8,128)(2,1)}, bf16[48,10240]{1,0:T(8,128)(2,1)}, u32[]{:S(2)}, u32[]{:S(2)}) collective-permute-start(bf16[48,10240]{1,0:T(8,128)(2,1)} %collective-permute-done.1.refs_6_), channel_id=1, source_target_pairs={{4,8},{8,12},{5,9},{9,13},{6,10},{10,14},{7,11},{11,15},{20,24},{2... | collective-permute-start | bytes 2949128 | tf_op jit(solution)/shard_map/ppermute | solution.py:130
  40.8 6.4 %copy-done.1 = bf16[1,1536,6144]{2,1,0:T(8,128)(2,1)S(1)} copy-done((bf16[1,1536,6144]{2,1,0:T(8,128)(2,1)S(1)}, bf16[1,1536,6144]{2,1,0:T(8,128)(2,1)}, u32[]{:S(2)}) %copy-start.1) | copy-done | bytes 18874392
  47.2 3.4 %copy-done.3 = bf16[1,1024,4096]{2,1,0:T(8,128)(2,1)S(1)} copy-done((bf16[1,1024,4096]{2,1,0:T(8,128)(2,1)S(1)}, bf16[1,1024,4096]{2,1,0:T(8,128)(2,1)}, u32[]{:S(2)}) %copy-start.3) | copy-done | bytes 8388632
  50.6 1.2 copy-done.6
  51.8 8.7 %shard_map.82 = (bf16[1536,144]{1,0:T(8,128)(2,1)S(1)}, bf16[1024,144]{1,0:T(8,128)(2,1)S(1)}) custom-call(bf16[1536,6144]{1,0:T(8,128)(2,1)S(1)} %bitcast.22, bf16[1024,4096]{1,0:T(8,128)(2,1)S(1)} %bitcast.25, f32[1536,1]{1,0:T(8,128)S(1)} %copy.22.refs_2_.refs_1_, f32[1024,1]{1,0:T(8,128)S(1)} %copy.23.refs_3_.refs_1_, bf16[48,10240]{1,0:T(8,128)(2,1)S(1)} %copy-done.6, ...), custom_call_target="tpu_custom_call" | custom-call | flops 1 | bytes 1 | tf_op jit(solution)/shard_map/pallas_call | solution.py:50
  62.1 10.7 %collective-permute-done.3.refs_4_ = bf16[48,10240]{1,0:T(8,128)(2,1)} collective-permute-done((bf16[48,10240]{1,0:T(8,128)(2,1)}, bf16[48,10240]{1,0:T(8,128)(2,1)}, u32[]{:S(2)}, u32[]{:S(2)}) %collective-permute-start.3) | collective-permute-done | bytes 983072 | tf_op jit(solution)/shard_map/ppermute | solution.py:129
  72.8 1.3 %slice_select_fusion = bf16[48,6144]{1,0:T(8,128)(2,1)S(1)} fusion(bf16[48,10240]{1,0:T(8,128)(2,1)} %collective-permute-done.4.refs_5_, bf16[48,10240]{1,0:T(8,128)(2,1)} %collective-permute-done.3.refs_4_, pred[]{:T(512)S(6)} %lt.9), kind=kLoop, calls=%fused_computation.2 | loop fusion | flops 294912 | bytes 1769473 | tf_op jit(solution)/shard_map/jit(_where)/select_n | solution.py:136
  74.2 1.3 %collective-permute-start.5 = (bf16[48,6144]{1,0:T(8,128)(2,1)S(1)}, bf16[48,6144]{1,0:T(8,128)(2,1)S(1)}, u32[]{:S(2)}, u32[]{:S(2)}) collective-permute-start(bf16[48,6144]{1,0:T(8,128)(2,1)S(1)} %slice_select_fusion), channel_id=1, source_target_pairs={{4,0},{8,12},{5,1},{9,13},{6,2},{10,14},{7,3},{11,15},{20,16},{24,... | collective-permute-start | bytes 1769480 | tf_op jit(solution)/shard_map/ppermute | solution.py:139
  75.5 1.6 %collective-permute-start.2 = (bf16[160,2560]{1,0:T(8,128)(2,1)S(1)}, bf16[160,2560]{1,0:T(8,128)(2,1)S(1)}, u32[]{:S(2)}, u32[]{:S(2)}) collective-permute-start(bf16[160,2560]{1,0:T(8,128)(2,1)S(1)} %bitcast.30), channel_id=1, source_target_pairs={{0,16},{16,0},{1,17},{17,1},{2,18},{18,2},{3,19},{19,3},{4,20},{20... | collective-permute-start | bytes 2457608 | tf_op jit(solution)/shard_map/ppermute | solution.py:153
  77.0 1.2 slice_select_fusion.1
  78.2 6.4 %copy-done.2 = bf16[1,1536,6144]{2,1,0:T(8,128)(2,1)S(1)} copy-done((bf16[1,1536,6144]{2,1,0:T(8,128)(2,1)S(1)}, bf16[1,1536,6144]{2,1,0:T(8,128)(2,1)}, u32[]{:S(2)}) %copy-start.2) | copy-done | bytes 18874392
  84.6 3.4 %copy-done.4 = bf16[1,1024,4096]{2,1,0:T(8,128)(2,1)S(1)} copy-done((bf16[1,1024,4096]{2,1,0:T(8,128)(2,1)S(1)}, bf16[1,1024,4096]{2,1,0:T(8,128)(2,1)}, u32[]{:S(2)}) %copy-start.4) | copy-done | bytes 8388632
  88.0 8.7 %shard_map.83 = (bf16[1536,48]{1,0:T(8,128)(2,1)S(1)}, bf16[1024,48]{1,0:T(8,128)(2,1)S(1)}) custom-call(bf16[1536,6144]{1,0:T(8,128)(2,1)S(1)} %bitcast.23, bf16[1024,4096]{1,0:T(8,128)(2,1)S(1)} %bitcast.26, f32[1536,1]{1,0:T(8,128)S(1)} %copy.22.refs_2_.refs_1_, f32[1024,1]{1,0:T(8,128)S(1)} %copy.23.refs_3_.refs_1_, ...), custom_call_target="tpu_custom_call" | custom-call | flops 1 | bytes 1 | tf_op jit(solution)/shard_map/pallas_call | solution.py:50
  96.7 1.7 %collective-permute-start.6 = (bf16[48,4096]{1,0:T(8,128)(2,1)S(1)}, bf16[48,4096]{1,0:T(8,128)(2,1)S(1)}, u32[]{:S(2)}, u32[]{:S(2)}) collective-permute-start(bf16[48,4096]{1,0:T(8,128)(2,1)S(1)} %slice_select_fusion.1), channel_id=1, source_target_pairs={{4,0},{8,12},{5,1},{9,13},{6,2},{10,14},{7,3},{11,15},{20,16},{24,... | collective-permute-start | bytes 1179656 | tf_op jit(solution)/shard_map/ppermute | solution.py:143
  98.5 5.0 %shard_map.85.refs_2_ = bf16[1536,48]{1,0:T(8,128)(2,1)S(1)} custom-call(bf16[1536,6144]{1,0:T(8,128)(2,1)S(1)} %bitcast.24, f32[1536,1]{1,0:T(8,128)S(1)} %copy.22.refs_2_.refs_1_, bf16[48,6144]{1,0:T(8,128)(2,1)S(1)} %collective-permute-done.5.refs_2_), custom_call_target="tpu_custom_call" | custom-call | flops 1 | bytes 1 | tf_op jit(solution)/shard_map/pallas_call | solution.py:50
  104.6 7.6 %collective-permute-done.6.refs_2_ = bf16[48,4096]{1,0:T(8,128)(2,1)S(1)} collective-permute-done((bf16[48,4096]{1,0:T(8,128)(2,1)S(1)}, bf16[48,4096]{1,0:T(8,128)(2,1)S(1)}, u32[]{:S(2)}, u32[]{:S(2)}) %collective-permute-start.6) | collective-permute-done | bytes 393248 | tf_op jit(solution)/shard_map/ppermute | solution.py:143
  112.2 2.3 %shard_map.86.refs_3_ = bf16[1024,48]{1,0:T(8,128)(2,1)S(1)} custom-call(bf16[1024,4096]{1,0:T(8,128)(2,1)S(1)} %bitcast.29, f32[1024,1]{1,0:T(8,128)S(1)} %copy.23.refs_3_.refs_1_, bf16[48,4096]{1,0:T(8,128)(2,1)S(1)} %collective-permute-done.6.refs_2_), custom_call_target="tpu_custom_call" | custom-call | flops 1 | bytes 1 | tf_op jit(solution)/shard_map/pallas_call | solution.py:50
  115.2 12.0 %all_to_all.10 = bf16[32,16,256]{2,1,0:T(8,128)(2,1)S(1)} all-to-all(bf16[32,16,256]{2,1,0:T(8,128)(2,1)S(1)} %bitcast.33), channel_id=1, replica_groups=mesh['parts'=2,'rows'=4,'layer'=4] {'parts','rows','layer'}, dimensions={0} | all-to-all | bytes 524288 | tf_op jit(solution)/shard_map/all_to_all | solution.py:209
  (52 shorter events, 8.9 us)
Async XLA Ops:
  0.0 1.3 copy-start
  1.3 9.1 %copy-start.11 = (bf16[1,40,6144]{2,1,0:T(8,128)(2,1)S(1)}, bf16[1,40,6144]{2,1,0:T(8,128)(2,1)}, u32[]{:S(2)}) copy-start(bf16[1,40,6144]{2,1,0:T(8,128)(2,1)} %param.10) | copy-start | bytes 1474564
  2.4 8.4 %copy-start.12 = (bf16[1,40,4096]{2,1,0:T(8,128)(2,1)S(1)}, bf16[1,40,4096]{2,1,0:T(8,128)(2,1)}, u32[]{:S(2)}) copy-start(bf16[1,40,4096]{2,1,0:T(8,128)(2,1)} %param.11) | copy-start | bytes 983044
  2.5 9.6 %copy-start.5 = (bf16[48,10240]{1,0:T(8,128)(2,1)}, bf16[48,10240]{1,0:T(8,128)(2,1)S(1)}, u32[]{:S(2)}) copy-start(bf16[48,10240]{1,0:T(8,128)(2,1)S(1)} %pad_maximum_fusion.refs_4_) | copy-start | bytes 2949124
  2.5 26.8 %collective-permute-start = (bf16[48,10240]{1,0:T(8,128)(2,1)S(1)}, bf16[48,10240]{1,0:T(8,128)(2,1)}, u32[]{:S(2)}, u32[]{:S(2)}) collective-permute-start(bf16[48,10240]{1,0:T(8,128)(2,1)S(1)} %pad_maximum_fusion.refs_4_), channel_id=1, source_target_pairs={{4,0},{8,4},{12,8},{5,1},{9,5},{13,9},{6,2},{10,6},{14,10},{7,3},{... | collective-permute-start | bytes 2949128 | tf_op jit(solution)/shard_map/ppermute | solution.py:125
  3.8 26.6 %collective-permute-start.1 = (bf16[48,10240]{1,0:T(8,128)(2,1)S(1)}, bf16[48,10240]{1,0:T(8,128)(2,1)}, u32[]{:S(2)}, u32[]{:S(2)}) collective-permute-start(bf16[48,10240]{1,0:T(8,128)(2,1)S(1)} %pad_maximum_fusion.refs_4_), channel_id=1, source_target_pairs={{0,4},{4,8},{8,12},{1,5},{5,9},{9,13},{2,6},{6,10},{10,14},{3,7},{... | collective-permute-start | bytes 2949128 | tf_op jit(solution)/shard_map/ppermute | solution.py:126
  11.0 29.2 %copy-start.13 = (f32[1,1536]{1,0:T(1,128)S(1)}, f32[1,1536]{1,0:T(1,128)}, u32[]{:S(2)}) copy-start(f32[1,1536]{1,0:T(1,128)} %param.14) | copy-start | bytes 18436
  11.1 29.4 %copy-start.14 = (f32[1,1024]{1,0:T(1,128)S(1)}, f32[1,1024]{1,0:T(1,128)}, u32[]{:S(2)}) copy-start(f32[1,1024]{1,0:T(1,128)} %param.15) | copy-start | bytes 12292
  30.4 31.8 %all-to-all-start = ((bf16[4,40,2560]{2,1,0:T(8,128)(2,1)}), bf16[4,40,2560]{2,1,0:T(8,128)(2,1)S(1)}, u32[]{:S(2)}, u32[]{:S(2)}) async-start(bf16[4,40,2560]{2,1,0:T(8,128)(2,1)} %pad_maximum_fusion.1), calls=%async_computation | async-start | bytes 1638400 | tf_op jit(solution)/shard_map/all_to_all | solution.py:128
  37.3 35.5 %collective-permute-start.3 = (bf16[48,10240]{1,0:T(8,128)(2,1)}, bf16[48,10240]{1,0:T(8,128)(2,1)}, u32[]{:S(2)}, u32[]{:S(2)}) collective-permute-start(bf16[48,10240]{1,0:T(8,128)(2,1)} %collective-permute-done.refs_5_), channel_id=1, source_target_pairs={{4,0},{8,4},{5,1},{9,5},{6,2},{10,6},{7,3},{11,7},{20,16},{24,20},... | collective-permute-start | bytes 2949128 | tf_op jit(solution)/shard_map/ppermute | solution.py:129
  38.6 34.2 %collective-permute-start.4 = (bf16[48,10240]{1,0:T(8,128)(2,1)}, bf16[48,10240]{1,0:T(8,128)(2,1)}, u32[]{:S(2)}, u32[]{:S(2)}) collective-permute-start(bf16[48,10240]{1,0:T(8,128)(2,1)} %collective-permute-done.1.refs_6_), channel_id=1, source_target_pairs={{4,8},{8,12},{5,9},{9,13},{6,10},{10,14},{7,11},{11,15},{20,24},{2... | collective-permute-start | bytes 2949128 | tf_op jit(solution)/shard_map/ppermute | solution.py:130
  40.8 6.4 %copy-start.1 = (bf16[1,1536,6144]{2,1,0:T(8,128)(2,1)S(1)}, bf16[1,1536,6144]{2,1,0:T(8,128)(2,1)}, u32[]{:S(2)}) copy-start(bf16[1,1536,6144]{2,1,0:T(8,128)(2,1)} %param.12) | copy-start | bytes 56623108
  47.2 3.4 %copy-start.3 = (bf16[1,1024,4096]{2,1,0:T(8,128)(2,1)S(1)}, bf16[1,1024,4096]{2,1,0:T(8,128)(2,1)}, u32[]{:S(2)}) copy-start(bf16[1,1024,4096]{2,1,0:T(8,128)(2,1)} %param.13) | copy-start | bytes 25165828
  50.5 1.2 copy-start.6
  60.4 0.9 copy-start.7
  74.2 22.5 %collective-permute-start.5 = (bf16[48,6144]{1,0:T(8,128)(2,1)S(1)}, bf16[48,6144]{1,0:T(8,128)(2,1)S(1)}, u32[]{:S(2)}, u32[]{:S(2)}) collective-permute-start(bf16[48,6144]{1,0:T(8,128)(2,1)S(1)} %slice_select_fusion), channel_id=1, source_target_pairs={{4,0},{8,12},{5,1},{9,13},{6,2},{10,14},{7,3},{11,15},{20,16},{24,... | collective-permute-start | bytes 1769480 | tf_op jit(solution)/shard_map/ppermute | solution.py:139
  75.5 28.0 %collective-permute-start.2 = (bf16[160,2560]{1,0:T(8,128)(2,1)S(1)}, bf16[160,2560]{1,0:T(8,128)(2,1)S(1)}, u32[]{:S(2)}, u32[]{:S(2)}) collective-permute-start(bf16[160,2560]{1,0:T(8,128)(2,1)S(1)} %bitcast.30), channel_id=1, source_target_pairs={{0,16},{16,0},{1,17},{17,1},{2,18},{18,2},{3,19},{19,3},{4,20},{20... | collective-permute-start | bytes 2457608 | tf_op jit(solution)/shard_map/ppermute | solution.py:153
  78.2 6.4 %copy-start.2 = (bf16[1,1536,6144]{2,1,0:T(8,128)(2,1)S(1)}, bf16[1,1536,6144]{2,1,0:T(8,128)(2,1)}, u32[]{:S(2)}) copy-start(bf16[1,1536,6144]{2,1,0:T(8,128)(2,1)} %param.12) | copy-start | bytes 56623108
  84.6 3.4 %copy-start.4 = (bf16[1,1024,4096]{2,1,0:T(8,128)(2,1)S(1)}, bf16[1,1024,4096]{2,1,0:T(8,128)(2,1)}, u32[]{:S(2)}) copy-start(bf16[1,1024,4096]{2,1,0:T(8,128)(2,1)} %param.13) | copy-start | bytes 25165828
  96.7 15.6 %slice-start = ((s8[8388608]{0:T(1024)(128)(4,1)}), s8[4194304]{0:T(1024)(128)(4,1)S(1)}, s32[]{:S(2)}) async-start(s8[8388608]{0:T(1024)(128)(4,1)} %bitcast.27), calls=%async_computation.2 | async-start | bytes 8388608
  96.7 6.8 %copy-start.8 = (bf16[1536,144]{1,0:T(8,128)(2,1)S(1)}, bf16[1536,144]{1,0:T(8,128)(2,1)}, u32[]{:S(2)}) copy-start(bf16[1536,144]{1,0:T(8,128)(2,1)} %copy-done.7) | copy-start | bytes 1327108
  96.7 6.8 %copy-start.10 = (bf16[1024,144]{1,0:T(8,128)(2,1)S(1)}, bf16[1024,144]{1,0:T(8,128)(2,1)}, u32[]{:S(2)}) copy-start(bf16[1024,144]{1,0:T(8,128)(2,1)} %copy-done.9) | copy-start | bytes 884740
  96.7 15.5 %slice-start.1 = ((s8[8388608]{0:T(1024)(128)(4,1)}), s8[4194304]{0:T(1024)(128)(4,1)S(1)}, s32[]{:S(2)}) async-start(s8[8388608]{0:T(1024)(128)(4,1)} %bitcast.27), calls=%async_computation.3 | async-start | bytes 8388608
  96.7 15.5 %collective-permute-start.6 = (bf16[48,4096]{1,0:T(8,128)(2,1)S(1)}, bf16[48,4096]{1,0:T(8,128)(2,1)S(1)}, u32[]{:S(2)}, u32[]{:S(2)}) collective-permute-start(bf16[48,4096]{1,0:T(8,128)(2,1)S(1)} %slice_select_fusion.1), channel_id=1, source_target_pairs={{4,0},{8,12},{5,1},{9,13},{6,2},{10,14},{7,3},{11,15},{20,16},{24,... | collective-permute-start | bytes 1179656 | tf_op jit(solution)/shard_map/ppermute | solution.py:143
  (1 other events, 0.8 us)

commit v15 on v14

--- a/solution.py
+++ b/solution.py
@@ -1,3 +1,5 @@
+import typing
+
 import jax
 import jax.numpy as jnp
 from jax import lax
@@ -60,62 +62,62 @@
     return -(-examples * columns // 128) * 128
 
 
-def grams(stores, blocks, offsets, base=None):
-    rows, parts = lax.axis_size("rows"), lax.axis_size("parts")
-    shares = [side.shape[0] for side in blocks[0]]
-    columns = blocks[0][0].shape[1] // len(offsets[0])
-    count = len(stores)
-    held = stores[0].shape[0] // rows
+class Store(typing.NamedTuple):
+    rows: jax.Array
+    shift: int
+    flips: tuple
+
+
+def grams(stores, near, two, three):
+    parts = lax.axis_size("parts")
+    shares = [side.shape[0] for side in near]
+    columns = two[0].shape[1]
+    held = stores[0].rows.shape[0] // len(stores[0].flips)
     examples = held // RANK
     width = packed_width(examples, columns)
+    fill = width - examples * columns
 
     def kernel(*refs):
-        store_refs, block_refs, out_ref = refs[:count], refs[count : count + 2 * len(blocks)], refs[-1]
+        store_refs, block_refs, out_ref = refs[: len(stores)], refs[len(stores) : -1], refs[-1]
         row, part = lax.axis_index("rows"), lax.axis_index("parts")
-        if base is not None:
-            base_ref = refs[-2]
-            out_ref[...] = base_ref[...]
-
-        def write():
-            for at, block_offsets in enumerate(offsets):
-                for j, store_ref in enumerate(store_refs):
-                    sides = []
-                    for side, begin in enumerate((0, shares[0])):
-                        store = store_ref[:, begin : begin + shares[side]]
-                        sides.append(
-                            jnp.dot(store, block_refs[2 * at + side][...], preferred_element_type=jnp.float32)
-                        )
-                    owner_part = lax.rem(part + parts - j, parts)
-                    for place, offset in enumerate(block_offsets):
-                        shard = lax.rem(row + offset, rows) if base is None else jnp.where(row == 0, rows - 1, 0)
-                        for owner in range(rows):
-                            packed = []
-                            for gram in sides:
-                                pieces = [
-                                    gram[
-                                        owner * held + i * RANK : owner * held + (i + 1) * RANK,
-                                        place * columns : (place + 1) * columns,
-                                    ]
-                                    for i in range(examples)
-                                ]
-                                fill = width - examples * columns
-                                if fill:
-                                    pieces.append(jnp.zeros((RANK, fill), jnp.float32))
-                                packed.append(jnp.concatenate(pieces, axis=1))
-                            out_ref[owner_part, owner, shard] = jnp.concatenate(packed, axis=0).astype(jnp.bfloat16)
-
-        if base is None:
-            write()
-        else:
-            pl.when(jnp.logical_or(row == 0, row == rows - 1))(write)
-
-    operands = [*stores, *[side for block in blocks for side in block]]
+
+        def packed(gram, block, place):
+            pieces = [
+                gram[
+                    block * held + i * RANK : block * held + (i + 1) * RANK, place * columns : (place + 1) * columns
+                ]
+                for i in range(examples)
+            ]
+            if fill:
+                pieces.append(jnp.zeros((RANK, fill), jnp.float32))
+            return jnp.concatenate(pieces, axis=1)
+
+        def write(sides, shards):
+            for store, store_ref in zip(stores, store_refs):
+                both = [
+                    jnp.dot(store_ref[:, begin : begin + share], side[...], preferred_element_type=jnp.float32)
+                    for side, begin, share in zip(sides, (0, shares[0]), shares)
+                ]
+                owner_part = lax.rem(part + parts - store.shift, parts)
+                for block, flip in enumerate(store.flips):
+                    for place, shard in enumerate(shards):
+                        out_ref[owner_part, lax.bitwise_xor(row, flip), shard] = jnp.concatenate(
+                            [packed(gram, block, place) for gram in both], axis=0
+                        ).astype(jnp.bfloat16)
+
+        write(block_refs[0:2], [row, lax.rem(row + 1, 4), lax.rem(row + 3, 4)])
+        write(block_refs[2:4], [lax.rem(row + 2, 4)])
+
+        @pl.when(jnp.logical_or(row == 0, row == 3))
+        def _():
+            write(block_refs[4:6], [jnp.where(row == 0, 3, 0)])
+
     return pl.pallas_call(
         kernel,
-        out_shape=jax.ShapeDtypeStruct((parts, rows, rows, 2 * RANK, width), jnp.bfloat16),
+        out_shape=jax.ShapeDtypeStruct((parts, 4, 4, 2 * RANK, width), jnp.bfloat16),
         compiler_params=pltpu.CompilerParams(vmem_limit_bytes=6 * MIB),
         cost_estimate=pl.CostEstimate(flops=1, bytes_accessed=1, transcendentals=0),
-    )(*operands, *([] if base is None else [base]))
+    )(*[store.rows for store in stores], *near, *two, *three)
 
 
 def along_four(query, bases, eigens, by_owner):
@@ -124,33 +126,41 @@
     eigens = [eigen.reshape(-1, 1) for eigen in eigens]
     after = lax.ppermute(query, "rows", [(1, 0), (2, 1), (3, 2)])
     before = lax.ppermute(query, "rows", [(0, 1), (1, 2), (2, 3)])
-    by_owner, query, after, before = lax.optimization_barrier((by_owner, query, after, before))
-    store = lax.all_to_all(by_owner, "rows", 0, 0, tiled=True)
+    sent = [lax.dynamic_index_in_dim(by_owner, lax.bitwise_xor(row, flip), 0, False) for flip in range(4)]
+    query, sent = lax.optimization_barrier((query, sent))
+    early = [sent[0], flipped(sent[1], 1)]
+    query, after, before = lax.optimization_barrier((query, after, before))
     after_two = lax.ppermute(after, "rows", [(1, 0), (2, 1)])
     before_two = lax.ppermute(before, "rows", [(1, 2), (2, 3)])
     near = rotate(bases, eigens, [query, after, before], (0, depth))
-    near, store = lax.optimization_barrier((near, store))
-    stores = to_parts(store.reshape(-1, store.shape[-1]))
-    near, after_two, before_two = lax.optimization_barrier((near, after_two, before_two))
+    near, early = lax.optimization_barrier((near, early))
+    stores = to_parts(jnp.concatenate(early, axis=0), (0, 1))
+    near, after_two, before_two, sent = lax.optimization_barrier((near, after_two, before_two, sent))
     two_hidden, two_model = (
         jnp.where(row < 2, after_two[:, side], before_two[:, side]) for side in (slice(0, depth), slice(depth, None))
     )
     ends = [(1, 0), (2, 3)]
     three_hidden = lax.ppermute(two_hidden, "rows", ends)
+    late = [flipped(sent[flip], flip) for flip in (2, 3)]
     far = rotate(bases, eigens, [(after_two, before_two)], (0, depth))
-    far, three_hidden, two_model = lax.optimization_barrier((far, three_hidden, two_model))
-    base = grams(stores, [near, far], [(0, 1, 3), (2,)])
+    far, three_hidden, two_model, late = lax.optimization_barrier((far, three_hidden, two_model, late))
     three_model = lax.ppermute(two_model, "rows", ends)
     last_hidden = rotate(bases[:1], eigens[:1], [three_hidden], (0,))
-    base, last_hidden, three_model = lax.optimization_barrier((base, last_hidden, three_model))
+    stores += to_parts(jnp.concatenate(late, axis=0), (2, 3))
+    last_hidden, three_model = lax.optimization_barrier((last_hidden, three_model))
     last_model = rotate(bases[1:], eigens[1:], [three_model], (0,))
-    return grams(stores, [last_hidden + last_model], [(3,)], base)
-
-
-def to_parts(store):
+    return grams(stores, near, far, last_hidden + last_model)
+
+
+def flipped(block, flip):
+    return lax.ppermute(block, "rows", [(i, i ^ flip) for i in range(4)])
+
+
+def to_parts(rows, flips):
     parts = lax.axis_size("parts")
-    return [store] + [
-        lax.ppermute(store, "parts", [(i, (i + j) % parts) for i in range(parts)]) for j in range(1, parts)
+    return [Store(rows, 0, flips)] + [
+        Store(lax.ppermute(rows, "parts", [(i, (i + j) % parts) for i in range(parts)]), j, flips)
+        for j in range(1, parts)
     ]
 
 
@@ -188,7 +198,7 @@
         partial = along_four(query, bases, eigens, by_owner)
     else:
         received = lax.all_to_all(by_owner, "rows", 0, 0, tiled=True)
-        stores = to_parts(received.reshape(rows * held, -1))
+        stores = [store.rows for store in to_parts(received.reshape(rows * held, -1), ())]
         every = lax.all_gather(query, "rows", axis=0, tiled=True)
         sides = []
         for basis, eigen, gathered, begin in zip(bases, eigens, (every[:, :depth], every[:, depth:]), (0, share)):

time: 129 us -> 129 us (level)
  waiting for transfers between devices: 36.6 us -> 21.2 us
  starting transfers between devices: 22.3 us -> 30.5 us
  blocking collectives: 12 us -> 17.4 us
    ppermute x1 -> x5, starting transfers between devices: 1.58 us -> 17 us  [the longest x3 15 us: flipped(): return lax.ppermute(block, 'rows', [(i, i ^ flip) for i in range(4)])]
    ppermute x1, waiting for transfers between devices: 10.7 us -> 0.01 us  [along_four(): after_two = lax.ppermute(after, 'rows', [(1, 0), (2, 1)])]
    all_to_all x1 -> x0, starting transfers between devices: 6.99 us -> none  [along_four(): store = lax.all_to_all(by_owner, 'rows', 0, 0, tiled=True)]
    all_to_all x1, blocking collectives: 12 us -> 17.4 us  [per_device(): lax.all_to_all(partial.reshape((parts * rows * layers,) + partial.shape[3...]
    ppermute x1, waiting for transfers between devices: 7.61 us -> 3.33 us  [along_four(): three_model = lax.ppermute(two_model, 'rows', ends)]
    unnamed x34 -> x32, local copies, waits for them, and re-layouts: 23.7 us -> 21.8 us
    concatenate x0 -> x2, local copies, waits for them, and re-layouts: none -> 1.89 us  [the longest x1 0.95 us: along_four(): stores = to_parts(jnp.concatenate(early, axis=0), (0, 1))]
  transfers between devices with their start and end apart: 8 -> 11, of which waited for: 4 -> 4; matrix products, arithmetic and copies ran while one was open for 3% -> 7% of each run, Pallas kernels for 18% -> 19%
where the time goes in v15:
time: 129 us
  starting transfers between devices  30.5 us (24%)
  local copies, waits for them, and re-layouts  27.2 us (21%)
  Pallas kernels  27.2 us (21%)
  waiting for transfers between devices  21.2 us (16%)
  blocking collectives  17.4 us (13%)
  other arithmetic  4.93 us (4%)
    pallas_call x4, Pallas kernels, rotate(): pl.pallas_call(kernel, out_shape=[jax.ShapeDtypeStruct((basis.shape[0], h...  24.9 us
    unnamed x32, local copies, waits for them, and re-layouts  21.8 us
    all_to_all x1, blocking collectives, per_device(): lax.all_to_all(partial.reshape((parts * rows * layers,) + partial.shape[3...  17.4 us
    ppermute x1, waiting for transfers between devices, along_four(): after = lax.ppermute(query, 'rows', [(1, 0), (2, 1), (3, 2)])  16.2 us
    ppermute x3, starting transfers between devices, flipped(): return lax.ppermute(block, 'rows', [(i, i ^ flip) for i in range(4)])  15 us
    ppermute x1, starting transfers between devices, along_four(): before = lax.ppermute(query, 'rows', [(0, 1), (1, 2), (2, 3)])  6.53 us
    ppermute x1, waiting for transfers between devices, along_four(): three_model = lax.ppermute(two_model, 'rows', ends)  3.33 us
    select_n x2, other arithmetic, along_four(): jnp.where(row < 2, after_two[:, side], before_two[:, side])  3.2 us
  transfers between devices with their start and end apart: 11, of which 4 were waited for; matrix products, arithmetic and copies ran while one was open for 7% of the time, Pallas kernels for 19%

profile of v15, /device:TPU:0, one launch (start us, length us, event | category | flops | bytes accessed | tf_op | source)
XLA Modules:
  0.0 128.7 jit_solution(13729099142378341785)
XLA Ops:
  0.0 1.3 copy-done
  2.5 1.3 %collective-permute-start = (bf16[48,10240]{1,0:T(8,128)(2,1)S(1)}, bf16[48,10240]{1,0:T(8,128)(2,1)}, u32[]{:S(2)}, u32[]{:S(2)}) collective-permute-start(bf16[48,10240]{1,0:T(8,128)(2,1)S(1)} %pad_maximum_fusion.refs_4_), channel_id=1, source_target_pairs={{4,0},{8,4},{12,8},{5,1},{9,5},{13,9},{6,2},{10,6},{14,10},{7,3},{... | collective-permute-start | bytes 2949128 | tf_op jit(solution)/shard_map/ppermute | solution.py:127
  3.8 6.5 %collective-permute-start.1 = (bf16[48,10240]{1,0:T(8,128)(2,1)S(1)}, bf16[48,10240]{1,0:T(8,128)(2,1)}, u32[]{:S(2)}, u32[]{:S(2)}) collective-permute-start(bf16[48,10240]{1,0:T(8,128)(2,1)S(1)} %pad_maximum_fusion.refs_4_), channel_id=1, source_target_pairs={{0,4},{4,8},{8,12},{1,5},{5,9},{9,13},{2,6},{6,10},{10,14},{3,7},{... | collective-permute-start | bytes 2949128 | tf_op jit(solution)/shard_map/ppermute | solution.py:128
  13.0 16.2 %collective-permute-done.refs_5_ = bf16[48,10240]{1,0:T(8,128)(2,1)} collective-permute-done((bf16[48,10240]{1,0:T(8,128)(2,1)S(1)}, bf16[48,10240]{1,0:T(8,128)(2,1)}, u32[]{:S(2)}, u32[]{:S(2)}) %collective-permute-start) | collective-permute-done | bytes 983072 | tf_op jit(solution)/shard_map/ppermute | solution.py:127
  30.3 1.3 collective-permute-start.4
  31.6 1.6 %collective-permute-start.5 = (bf16[48,10240]{1,0:T(8,128)(2,1)}, bf16[48,10240]{1,0:T(8,128)(2,1)}, u32[]{:S(2)}, u32[]{:S(2)}) collective-permute-start(bf16[48,10240]{1,0:T(8,128)(2,1)} %collective-permute-done.1.refs_6_), channel_id=1, source_target_pairs={{4,8},{8,12},{5,9},{9,13},{6,10},{10,14},{7,11},{11,15},{20,24},{2... | collective-permute-start | bytes 2949128 | tf_op jit(solution)/shard_map/ppermute | solution.py:134
  33.3 7.4 %collective-permute-start.2 = (bf16[40,2560]{1,0:T(8,128)(2,1)}, bf16[40,2560]{1,0:T(8,128)(2,1)}, u32[]{:S(2)}, u32[]{:S(2)}) collective-permute-start(bf16[40,2560]{1,0:T(8,128)(2,1)} %get-tuple-element.42), channel_id=1, source_target_pairs={{0,4},{4,0},{8,12},{12,8},{1,5},{5,1},{9,13},{13,9},{2,6},{6,2},{1... | collective-permute-start | bytes 614408 | tf_op jit(solution)/shard_map/ppermute | solution.py:156
  41.2 6.4 %copy-done.1 = bf16[1,1536,6144]{2,1,0:T(8,128)(2,1)S(1)} copy-done((bf16[1,1536,6144]{2,1,0:T(8,128)(2,1)S(1)}, bf16[1,1536,6144]{2,1,0:T(8,128)(2,1)}, u32[]{:S(2)}) %copy-start.1) | copy-done | bytes 18874392
  47.6 3.4 %copy-done.3 = bf16[1,1024,4096]{2,1,0:T(8,128)(2,1)S(1)} copy-done((bf16[1,1024,4096]{2,1,0:T(8,128)(2,1)S(1)}, bf16[1,1024,4096]{2,1,0:T(8,128)(2,1)}, u32[]{:S(2)}) %copy-start.3) | copy-done | bytes 8388632
  51.0 8.8 %shard_map.82 = (bf16[1536,144]{1,0:T(8,128)(2,1)S(1)}, bf16[1024,144]{1,0:T(8,128)(2,1)S(1)}) custom-call(bf16[1536,6144]{1,0:T(8,128)(2,1)S(1)} %bitcast.29, bf16[1024,4096]{1,0:T(8,128)(2,1)S(1)} %bitcast.34, f32[1536,1]{1,0:T(8,128)S(1)} %copy.22.refs_2_.refs_1_, f32[1024,1]{1,0:T(8,128)S(1)} %copy.23.refs_3_.refs_1_, ...), custom_call_target="tpu_custom_call" | custom-call | flops 1 | bytes 1 | tf_op jit(solution)/shard_map/pallas_call | solution.py:52
  61.4 1.4 %collective-permute-start.3 = (bf16[80,2560]{1,0:T(8,128)(2,1)S(1)}, bf16[80,2560]{1,0:T(8,128)(2,1)S(1)}, u32[]{:S(2)}, u32[]{:S(2)}) collective-permute-start(bf16[80,2560]{1,0:T(8,128)(2,1)S(1)} %constant_dynamic-update-slice_fusion.refs_0_), channel_id=1, source_target_pairs={{0,16},{16,0},{1,17},{17,1},{2,18},{18,2},{3,19},{19,3},{4,20},{20... | collective-permute-start | bytes 1228808 | tf_op jit(solution)/shard_map/ppermute | solution.py:162
  62.8 1.3 %slice_select_fusion = bf16[48,6144]{1,0:T(8,128)(2,1)S(1)} fusion(bf16[48,10240]{1,0:T(8,128)(2,1)} %collective-permute-done.5.refs_5_, bf16[48,10240]{1,0:T(8,128)(2,1)} %collective-permute-done.4.refs_4_, pred[]{:T(512)S(6)} %lt.26), kind=kLoop, calls=%fused_computation.9 | loop fusion | flops 294912 | bytes 1769473 | tf_op jit(solution)/shard_map/jit(_where)/select_n | solution.py:140
  64.1 1.3 %collective-permute-start.6 = (bf16[48,6144]{1,0:T(8,128)(2,1)S(1)}, bf16[48,6144]{1,0:T(8,128)(2,1)S(1)}, u32[]{:S(2)}, u32[]{:S(2)}) collective-permute-start(bf16[48,6144]{1,0:T(8,128)(2,1)S(1)} %slice_select_fusion), channel_id=1, source_target_pairs={{4,0},{8,12},{5,1},{9,13},{6,2},{10,14},{7,3},{11,15},{20,16},{24,... | collective-permute-start | bytes 1769480 | tf_op jit(solution)/shard_map/ppermute | solution.py:143
  65.4 7.6 %collective-permute-start.7 = (bf16[40,2560]{1,0:T(8,128)(2,1)}, bf16[40,2560]{1,0:T(8,128)(2,1)}, u32[]{:S(2)}, u32[]{:S(2)}) collective-permute-start(bf16[40,2560]{1,0:T(8,128)(2,1)} %get-tuple-element.53), channel_id=1, source_target_pairs={{0,8},{4,12},{8,0},{12,4},{1,9},{5,13},{9,1},{13,5},{2,10},{6,14},... | collective-permute-start | bytes 614408 | tf_op jit(solution)/shard_map/ppermute | solution.py:156
  73.0 1.9 %slice_select_fusion.1 = bf16[48,4096]{1,0:T(8,128)(2,1)} fusion(bf16[48,10240]{1,0:T(8,128)(2,1)} %collective-permute-done.5.refs_5_, bf16[48,10240]{1,0:T(8,128)(2,1)} %collective-permute-done.4.refs_4_, pred[]{:T(512)S(6)} %lt.26), kind=kLoop, calls=%fused_computation.13 | loop fusion | flops 196608 | bytes 1179649 | tf_op jit(solution)/shard_map/jit(_where)/select_n | solution.py:140
  74.9 6.4 %copy-done.2 = bf16[1,1536,6144]{2,1,0:T(8,128)(2,1)S(1)} copy-done((bf16[1,1536,6144]{2,1,0:T(8,128)(2,1)S(1)}, bf16[1,1536,6144]{2,1,0:T(8,128)(2,1)}, u32[]{:S(2)}) %copy-start.2) | copy-done | bytes 18874392
  81.3 8.8 %shard_map.83 = (bf16[1536,48]{1,0:T(8,128)(2,1)S(1)}, bf16[1024,48]{1,0:T(8,128)(2,1)S(1)}) custom-call(bf16[1536,6144]{1,0:T(8,128)(2,1)S(1)} %bitcast.30, bf16[1024,4096]{1,0:T(8,128)(2,1)S(1)} %bitcast.35, f32[1536,1]{1,0:T(8,128)S(1)} %copy.22.refs_2_.refs_1_, f32[1024,1]{1,0:T(8,128)S(1)} %copy.23.refs_3_.refs_1_, ...), custom_call_target="tpu_custom_call" | custom-call | flops 1 | bytes 1 | tf_op jit(solution)/shard_map/pallas_call | solution.py:52
  92.6 1.5 %collective-permute-start.10 = (bf16[48,4096]{1,0:T(8,128)(2,1)}, bf16[48,4096]{1,0:T(8,128)(2,1)S(1)}, u32[]{:S(2)}, u32[]{:S(2)}) collective-permute-start(bf16[48,4096]{1,0:T(8,128)(2,1)} %slice_select_fusion.1), channel_id=1, source_target_pairs={{4,0},{8,12},{5,1},{9,13},{6,2},{10,14},{7,3},{11,15},{20,16},{24,... | collective-permute-start | bytes 1179656 | tf_op jit(solution)/shard_map/ppermute | solution.py:147
  94.1 5.0 %shard_map.84.refs_8_ = bf16[1536,48]{1,0:T(8,128)(2,1)S(1)} custom-call(bf16[1536,6144]{1,0:T(8,128)(2,1)S(1)} %bitcast.33, f32[1536,1]{1,0:T(8,128)S(1)} %copy.22.refs_2_.refs_1_, bf16[48,6144]{1,0:T(8,128)(2,1)S(1)} %collective-permute-done.6.refs_2_), custom_call_target="tpu_custom_call" | custom-call | flops 1 | bytes 1 | tf_op jit(solution)/shard_map/pallas_call | solution.py:52
  99.1 3.3 %collective-permute-done.10.refs_2_ = bf16[48,4096]{1,0:T(8,128)(2,1)S(1)} collective-permute-done((bf16[48,4096]{1,0:T(8,128)(2,1)}, bf16[48,4096]{1,0:T(8,128)(2,1)S(1)}, u32[]{:S(2)}, u32[]{:S(2)}) %collective-permute-start.10) | collective-permute-done | bytes 393248 | tf_op jit(solution)/shard_map/ppermute | solution.py:147
  102.4 3.4 %copy-done.4 = bf16[1,1024,4096]{2,1,0:T(8,128)(2,1)S(1)} copy-done((bf16[1,1024,4096]{2,1,0:T(8,128)(2,1)S(1)}, bf16[1,1024,4096]{2,1,0:T(8,128)(2,1)}, u32[]{:S(2)}) %copy-start.4) | copy-done | bytes 8388632
  105.8 2.3 %shard_map.85.refs_9_ = bf16[1024,48]{1,0:T(8,128)(2,1)S(1)} custom-call(bf16[1024,4096]{1,0:T(8,128)(2,1)S(1)} %bitcast.36, f32[1024,1]{1,0:T(8,128)S(1)} %copy.23.refs_3_.refs_1_, bf16[48,4096]{1,0:T(8,128)(2,1)S(1)} %collective-permute-done.10.refs_2_), custom_call_target="tpu_custom_call" | custom-call | flops 1 | bytes 1 | tf_op jit(solution)/shard_map/pallas_call | solution.py:52
  108.2 2.3 %shard_map.86 = bf16[2,4,4,16,256]{4,3,2,1,0:T(8,128)(2,1)S(1)} custom-call(bf16[80,2560]{1,0:T(8,128)(2,1)S(1)} %constant_dynamic-update-slice_fusion.refs_0_, bf16[80,2560]{1,0:T(8,128)(2,1)S(1)} %collective-permute-done.3.refs_1_, bf16[80,2560]{1,0:T(8,128)(2,1)S(1)} %constant_dynamic-update-slice_fusion.2.refs_2_, ...), custom_call_target="tpu_custom_call" | custom-call | flops 1 | bytes 1 | tf_op jit(solution)/shard_map/pallas_call | solution.py:115
  110.4 17.4 %all_to_all.5 = bf16[32,16,256]{2,1,0:T(8,128)(2,1)S(1)} all-to-all(bf16[32,16,256]{2,1,0:T(8,128)(2,1)S(1)} %bitcast.37), channel_id=1, replica_groups=mesh['parts'=2,'rows'=4,'layer'=4] {'parts','rows','layer'}, dimensions={0} | all-to-all | bytes 524288 | tf_op jit(solution)/shard_map/all_to_all | solution.py:219
  (57 shorter events, 10.4 us)
Async XLA Ops:
  1.3 9.0 %copy-start.6 = (bf16[1,40,6144]{2,1,0:T(8,128)(2,1)S(1)}, bf16[1,40,6144]{2,1,0:T(8,128)(2,1)}, u32[]{:S(2)}) copy-start(bf16[1,40,6144]{2,1,0:T(8,128)(2,1)} %param.10) | copy-start | bytes 1474564
  2.5 26.8 %collective-permute-start = (bf16[48,10240]{1,0:T(8,128)(2,1)S(1)}, bf16[48,10240]{1,0:T(8,128)(2,1)}, u32[]{:S(2)}, u32[]{:S(2)}) collective-permute-start(bf16[48,10240]{1,0:T(8,128)(2,1)S(1)} %pad_maximum_fusion.refs_4_), channel_id=1, source_target_pairs={{4,0},{8,4},{12,8},{5,1},{9,5},{13,9},{6,2},{10,6},{14,10},{7,3},{... | collective-permute-start | bytes 2949128 | tf_op jit(solution)/shard_map/ppermute | solution.py:127
  3.8 26.6 %collective-permute-start.1 = (bf16[48,10240]{1,0:T(8,128)(2,1)S(1)}, bf16[48,10240]{1,0:T(8,128)(2,1)}, u32[]{:S(2)}, u32[]{:S(2)}) collective-permute-start(bf16[48,10240]{1,0:T(8,128)(2,1)S(1)} %pad_maximum_fusion.refs_4_), channel_id=1, source_target_pairs={{0,4},{4,8},{8,12},{1,5},{5,9},{9,13},{2,6},{6,10},{10,14},{3,7},{... | collective-permute-start | bytes 2949128 | tf_op jit(solution)/shard_map/ppermute | solution.py:128
  10.7 30.0 %copy-start.8 = (f32[1,1536]{1,0:T(1,128)S(1)}, f32[1,1536]{1,0:T(1,128)}, u32[]{:S(2)}) copy-start(f32[1,1536]{1,0:T(1,128)} %param.14) | copy-start | bytes 18436
  10.8 30.2 %copy-start.9 = (f32[1,1024]{1,0:T(1,128)S(1)}, f32[1,1024]{1,0:T(1,128)}, u32[]{:S(2)}) copy-start(f32[1,1024]{1,0:T(1,128)} %param.15) | copy-start | bytes 12292
  30.3 32.5 %collective-permute-start.4 = (bf16[48,10240]{1,0:T(8,128)(2,1)}, bf16[48,10240]{1,0:T(8,128)(2,1)}, u32[]{:S(2)}, u32[]{:S(2)}) collective-permute-start(bf16[48,10240]{1,0:T(8,128)(2,1)} %collective-permute-done.refs_5_), channel_id=1, source_target_pairs={{4,0},{8,4},{5,1},{9,5},{6,2},{10,6},{7,3},{11,7},{20,16},{24,20},... | collective-permute-start | bytes 2949128 | tf_op jit(solution)/shard_map/ppermute | solution.py:133
  31.6 31.2 %collective-permute-start.5 = (bf16[48,10240]{1,0:T(8,128)(2,1)}, bf16[48,10240]{1,0:T(8,128)(2,1)}, u32[]{:S(2)}, u32[]{:S(2)}) collective-permute-start(bf16[48,10240]{1,0:T(8,128)(2,1)} %collective-permute-done.1.refs_6_), channel_id=1, source_target_pairs={{4,8},{8,12},{5,9},{9,13},{6,10},{10,14},{7,11},{11,15},{20,24},{2... | collective-permute-start | bytes 2949128 | tf_op jit(solution)/shard_map/ppermute | solution.py:134
  33.3 27.1 %collective-permute-start.2 = (bf16[40,2560]{1,0:T(8,128)(2,1)}, bf16[40,2560]{1,0:T(8,128)(2,1)}, u32[]{:S(2)}, u32[]{:S(2)}) collective-permute-start(bf16[40,2560]{1,0:T(8,128)(2,1)} %get-tuple-element.42), channel_id=1, source_target_pairs={{0,4},{4,0},{8,12},{12,8},{1,5},{5,1},{9,13},{13,9},{2,6},{6,2},{1... | collective-permute-start | bytes 614408 | tf_op jit(solution)/shard_map/ppermute | solution.py:156
  41.2 6.4 %copy-start.1 = (bf16[1,1536,6144]{2,1,0:T(8,128)(2,1)S(1)}, bf16[1,1536,6144]{2,1,0:T(8,128)(2,1)}, u32[]{:S(2)}) copy-start(bf16[1,1536,6144]{2,1,0:T(8,128)(2,1)} %param.12) | copy-start | bytes 56623108
  51.0 9.4 %copy-start.5 = (bf16[40,2560]{1,0:T(8,128)(2,1)S(1)}, bf16[40,2560]{1,0:T(8,128)(2,1)}, u32[]{:S(2)}) copy-start(bf16[40,2560]{1,0:T(8,128)(2,1)} %get-tuple-element.43) | copy-start | bytes 614404
  51.0 43.1 %slice-start = ((s8[18874368]{0:T(1024)(128)(4,1)}), s8[4194304]{0:T(1024)(128)(4,1)S(1)}, s32[]{:S(2)}) async-start(s8[18874368]{0:T(1024)(128)(4,1)} %bitcast.31), calls=%async_computation.1 | async-start | bytes 8388608
  51.0 43.1 %slice-start.1 = ((s8[18874368]{0:T(1024)(128)(4,1)}), s8[4194304]{0:T(1024)(128)(4,1)S(1)}, s32[]{:S(2)}) async-start(s8[18874368]{0:T(1024)(128)(4,1)} %bitcast.31), calls=%async_computation.2 | async-start | bytes 8388608
  51.0 43.1 %slice-start.2 = ((s8[18874368]{0:T(1024)(128)(4,1)}), s8[2097152]{0:T(1024)(128)(4,1)S(1)}, s32[]{:S(2)}) async-start(s8[18874368]{0:T(1024)(128)(4,1)} %bitcast.31), calls=%async_computation.3 | async-start | bytes 4194304
  59.8 13.2 %copy-start.7 = (bf16[40,2560]{1,0:T(8,128)(2,1)S(1)}, bf16[40,2560]{1,0:T(8,128)(2,1)}, u32[]{:S(2)}) copy-start(bf16[40,2560]{1,0:T(8,128)(2,1)} %get-tuple-element.54) | copy-start | bytes 614404
  61.4 46.8 %collective-permute-start.3 = (bf16[80,2560]{1,0:T(8,128)(2,1)S(1)}, bf16[80,2560]{1,0:T(8,128)(2,1)S(1)}, u32[]{:S(2)}, u32[]{:S(2)}) collective-permute-start(bf16[80,2560]{1,0:T(8,128)(2,1)S(1)} %constant_dynamic-update-slice_fusion.refs_0_), channel_id=1, source_target_pairs={{0,16},{16,0},{1,17},{17,1},{2,18},{18,2},{3,19},{19,3},{4,20},{20... | collective-permute-start | bytes 1228808 | tf_op jit(solution)/shard_map/ppermute | solution.py:162
  64.1 26.0 %collective-permute-start.6 = (bf16[48,6144]{1,0:T(8,128)(2,1)S(1)}, bf16[48,6144]{1,0:T(8,128)(2,1)S(1)}, u32[]{:S(2)}, u32[]{:S(2)}) collective-permute-start(bf16[48,6144]{1,0:T(8,128)(2,1)S(1)} %slice_select_fusion), channel_id=1, source_target_pairs={{4,0},{8,12},{5,1},{9,13},{6,2},{10,14},{7,3},{11,15},{20,16},{24,... | collective-permute-start | bytes 1769480 | tf_op jit(solution)/shard_map/ppermute | solution.py:143
  65.4 24.7 %collective-permute-start.7 = (bf16[40,2560]{1,0:T(8,128)(2,1)}, bf16[40,2560]{1,0:T(8,128)(2,1)}, u32[]{:S(2)}, u32[]{:S(2)}) collective-permute-start(bf16[40,2560]{1,0:T(8,128)(2,1)} %get-tuple-element.53), channel_id=1, source_target_pairs={{0,8},{4,12},{8,0},{12,4},{1,9},{5,13},{9,1},{13,5},{2,10},{6,14},... | collective-permute-start | bytes 614408 | tf_op jit(solution)/shard_map/ppermute | solution.py:156
  73.0 17.1 %collective-permute-start.8 = (bf16[40,2560]{1,0:T(8,128)(2,1)S(1)}, bf16[40,2560]{1,0:T(8,128)(2,1)}, u32[]{:S(2)}, u32[]{:S(2)}) collective-permute-start(bf16[40,2560]{1,0:T(8,128)(2,1)S(1)} %copy-done.7), channel_id=1, source_target_pairs={{0,12},{4,8},{8,4},{12,0},{1,13},{5,9},{9,5},{13,1},{2,14},{6,10},... | collective-permute-start | bytes 614408 | tf_op jit(solution)/shard_map/ppermute | solution.py:156
  74.9 6.4 %copy-start.2 = (bf16[1,1536,6144]{2,1,0:T(8,128)(2,1)S(1)}, bf16[1,1536,6144]{2,1,0:T(8,128)(2,1)}, u32[]{:S(2)}) copy-start(bf16[1,1536,6144]{2,1,0:T(8,128)(2,1)} %param.12) | copy-start | bytes 56623108
  81.3 12.8 %slice-start.3 = ((s8[18874368]{0:T(1024)(128)(4,1)}), s8[4194304]{0:T(1024)(128)(4,1)S(1)}, s32[]{:S(2)}) async-start(s8[18874368]{0:T(1024)(128)(4,1)} %bitcast.31), calls=%async_computation.4 | async-start | bytes 8388608
  81.3 12.8 %slice-start.4 = ((s8[18874368]{0:T(1024)(128)(4,1)}), s8[4194304]{0:T(1024)(128)(4,1)S(1)}, s32[]{:S(2)}) async-start(s8[18874368]{0:T(1024)(128)(4,1)} %bitcast.31), calls=%async_computation.5 | async-start | bytes 8388608
  92.0 16.1 %collective-permute-start.9 = (bf16[80,2560]{1,0:T(8,128)(2,1)S(1)}, bf16[80,2560]{1,0:T(8,128)(2,1)S(1)}, u32[]{:S(2)}, u32[]{:S(2)}) collective-permute-start(bf16[80,2560]{1,0:T(8,128)(2,1)S(1)} %constant_dynamic-update-slice_fusion.2.refs_2_), channel_id=1, source_target_pairs={{0,16},{16,0},{1,17},{17,1},{2,18},{18,2},{3,19},{19,3},{4,20},{20... | collective-permute-start | bytes 1228808 | tf_op jit(solution)/shard_map/ppermute | solution.py:162
  92.6 9.9 %collective-permute-start.10 = (bf16[48,4096]{1,0:T(8,128)(2,1)}, bf16[48,4096]{1,0:T(8,128)(2,1)S(1)}, u32[]{:S(2)}, u32[]{:S(2)}) collective-permute-start(bf16[48,4096]{1,0:T(8,128)(2,1)} %slice_select_fusion.1), channel_id=1, source_target_pairs={{4,0},{8,12},{5,1},{9,13},{6,2},{10,14},{7,3},{11,15},{20,16},{24,... | collective-permute-start | bytes 1179656 | tf_op jit(solution)/shard_map/ppermute | solution.py:147
  102.4 3.4 %copy-start.4 = (bf16[1,1024,4096]{2,1,0:T(8,128)(2,1)S(1)}, bf16[1,1024,4096]{2,1,0:T(8,128)(2,1)}, u32[]{:S(2)}) copy-start(bf16[1,1024,4096]{2,1,0:T(8,128)(2,1)} %param.13) | copy-start | bytes 25165828
  (2 other events, 4.7 us)

commit v16 on v12

--- a/solution.py
+++ b/solution.py
@@ -118,35 +118,40 @@
     )(*operands, *([] if base is None else [base]))
 
 
-def along_four(query, bases, eigens, by_owner):
+def along_four(query, bases, eigens, train):
     row = lax.axis_index("rows")
     depth = bases[0].shape[1]
     eigens = [eigen.reshape(-1, 1) for eigen in eigens]
     after = lax.ppermute(query, "rows", [(1, 0), (2, 1), (3, 2)])
     before = lax.ppermute(query, "rows", [(0, 1), (1, 2), (2, 3)])
-    sent = [lax.dynamic_index_in_dim(by_owner, (row + k) % 4, 0, False) for k in range(4)]
-    query, sent = lax.optimization_barrier((query, sent))
-    blocks = to_owners(sent)
-    query, after, before = lax.optimization_barrier((query, after, before))
+    train, after, before = lax.optimization_barrier((train, after, before))
     after_two = lax.ppermute(after, "rows", [(1, 0), (2, 1)])
     before_two = lax.ppermute(before, "rows", [(1, 2), (2, 3)])
-    near = rotate(bases, eigens, [query, after, before], (0, depth))
-    near, blocks = lax.optimization_barrier((near, blocks))
-    stores = to_parts(jnp.concatenate(blocks, axis=0))
-    near, after_two, before_two = lax.optimization_barrier((near, after_two, before_two))
+    by_owner = cut_by_owner(*train)
+    blocks = to_owners([lax.dynamic_index_in_dim(by_owner, (row + k) % 4, 0, False) for k in range(4)])
     two_hidden, two_model = (
         jnp.where(row < 2, after_two[:, side], before_two[:, side]) for side in (slice(0, depth), slice(depth, None))
     )
     ends = [(1, 0), (2, 3)]
     three_hidden = lax.ppermute(two_hidden, "rows", ends)
-    far = rotate(bases, eigens, [(after_two, before_two)], (0, depth))
+    _, blocks = lax.optimization_barrier((two_hidden, blocks))
+    stores = to_parts(jnp.concatenate(blocks, axis=0))
+    far = rotate(bases, eigens, [query, after, before, (after_two, before_two)], (0, depth))
     far, three_hidden, two_model = lax.optimization_barrier((far, three_hidden, two_model))
-    base = grams(stores, [near, far], [(0, 1, 3), (2,)])
+    base = grams(stores, [far], [(0, 1, 3, 2)])
     three_model = lax.ppermute(two_model, "rows", ends)
     last_hidden = rotate(bases[:1], eigens[:1], [three_hidden], (0,))
     base, last_hidden, three_model = lax.optimization_barrier((base, last_hidden, three_model))
     last_model = rotate(bases[1:], eigens[1:], [three_model], (0,))
     return grams(stores, [last_hidden + last_model], [(3,)], base)
+
+
+def cut_by_owner(train_hidden, train_model):
+    rows = lax.axis_size("rows")
+    held = train_hidden.shape[0]
+    return jnp.concatenate(
+        [side.reshape(held, rows, -1).transpose(1, 0, 2) for side in (train_hidden, train_model)], axis=2
+    )
 
 
 def to_owners(sent):
@@ -190,12 +195,10 @@
         [lax.dynamic_slice_in_dim(side[0], part * columns, columns, 0) for side in (query_hidden, query_model)],
         axis=1,
     )
-    by_owner = jnp.concatenate(
-        [side[0].reshape(held, rows, -1).transpose(1, 0, 2) for side in (train_hidden, train_model)], axis=2
-    )
     if rows == 4:
-        partial = along_four(query, bases, eigens, by_owner)
+        partial = along_four(query, bases, eigens, (train_hidden[0], train_model[0]))
     else:
+        by_owner = cut_by_owner(train_hidden[0], train_model[0])
         received = lax.all_to_all(by_owner, "rows", 0, 0, tiled=True)
         stores = to_parts(received.reshape(rows * held, -1))
         every = lax.all_gather(query, "rows", axis=0, tiled=True)

time: 116 us -> 128 us (1.10)
  waiting for transfers between devices: 24.6 us -> 49.3 us
  local copies, waits for them, and re-layouts: 23.8 us -> 14.9 us
  Pallas kernels: 25 us -> 18 us
  other arithmetic: 1.86 us -> 3.34 us
    ppermute x1, waiting for transfers between devices: 3.31 us -> 16.3 us  [along_four(): after_two = lax.ppermute(after, 'rows', [(1, 0), (2, 1)])]
    unnamed x23 -> x17, local copies, waits for them, and re-layouts: 19.3 us -> 11.1 us
    ppermute x3, waiting for transfers between devices: 0.01 us -> 7.51 us  [to_owners(): lax.ppermute(sent[k], 'rows', [(i, (i + k) % rows) for i in range(rows)])]
    ppermute x1, waiting for transfers between devices: 11.8 us -> 19 us  [along_four(): after = lax.ppermute(query, 'rows', [(1, 0), (2, 1), (3, 2)])]
    pallas_call x4 -> x3, Pallas kernels: 23.2 us -> 16.6 us  [rotate(): pl.pallas_call(kernel, out_shape=[jax.ShapeDtypeStruct((basis.shape[0], h...]
    ppermute x1, waiting for transfers between devices: 5.98 us -> 0.01 us  [along_four(): three_hidden = lax.ppermute(two_hidden, 'rows', ends)]
    ppermute x3, starting transfers between devices: 6.04 us -> 9.91 us  [to_owners(): lax.ppermute(sent[k], 'rows', [(i, (i + k) % rows) for i in range(rows)])]
    ppermute x1, starting transfers between devices: 5.18 us -> 1.65 us  [to_parts(): lax.ppermute(store, 'parts', [(i, (i + j) % parts) for i in range(parts)])]
  transfers between devices with their start and end apart: 10 -> 10, of which waited for: 4 -> 5; matrix products, arithmetic and copies ran while one was open for 5% -> 4% of each run, Pallas kernels for 19% -> 12%
where the time goes in v16:
time: 128 us; the launch traced here: 127 us
  waiting for transfers between devices  49.3 us (39%)
  starting transfers between devices  25.2 us (20%)
  Pallas kernels  18 us (14%)
  blocking collectives  16.3 us (13%)
  local copies, waits for them, and re-layouts  14.9 us (12%)
  other arithmetic  3.34 us (3%)
    ppermute x1, waiting for transfers between devices, along_four(): after = lax.ppermute(query, 'rows', [(1, 0), (2, 1), (3, 2)])  19 us
    pallas_call x3, Pallas kernels, rotate(): pl.pallas_call(kernel, out_shape=[jax.ShapeDtypeStruct((basis.shape[0], h...  16.6 us
    ppermute x1, waiting for transfers between devices, along_four(): after_two = lax.ppermute(after, 'rows', [(1, 0), (2, 1)])  16.3 us
    all_to_all x1, blocking collectives, per_device(): lax.all_to_all(partial.reshape((parts * rows * layers,) + partial.shape[3...  16.3 us
    unnamed x17, local copies, waits for them, and re-layouts  11.1 us
    ppermute x3, starting transfers between devices, to_owners(): lax.ppermute(sent[k], 'rows', [(i, (i + k) % rows) for i in range(rows)])  9.91 us
    ppermute x3, waiting for transfers between devices, to_owners(): lax.ppermute(sent[k], 'rows', [(i, (i + k) % rows) for i in range(rows)])  7.51 us
    ppermute x1, starting transfers between devices, along_four(): before = lax.ppermute(query, 'rows', [(0, 1), (1, 2), (2, 3)])  6.52 us
  transfers between devices with their start and end apart: 10, of which 5 were waited for; matrix products, arithmetic and copies ran while one was open for 4% of the time, Pallas kernels for 12%

profile of v16, /device:TPU:0, one launch (start us, length us, event | category | flops | bytes accessed | tf_op | source)
XLA Modules:
  0.0 127.2 jit_solution(3605235055746416753)
XLA Ops:
  0.0 1.3 copy-done
  2.4 1.3 %collective-permute-start = (bf16[48,10240]{1,0:T(8,128)(2,1)S(1)}, bf16[48,10240]{1,0:T(8,128)(2,1)}, u32[]{:S(2)}, u32[]{:S(2)}) collective-permute-start(bf16[48,10240]{1,0:T(8,128)(2,1)S(1)} %pad_maximum_fusion.refs_4_), channel_id=1, source_target_pairs={{4,0},{8,4},{12,8},{5,1},{9,5},{13,9},{6,2},{10,6},{14,10},{7,3},{... | collective-permute-start | bytes 2949128 | tf_op jit(solution)/shard_map/ppermute | solution.py:125
  3.7 6.5 %collective-permute-start.1 = (bf16[48,10240]{1,0:T(8,128)(2,1)S(1)}, bf16[48,10240]{1,0:T(8,128)(2,1)}, u32[]{:S(2)}, u32[]{:S(2)}) collective-permute-start(bf16[48,10240]{1,0:T(8,128)(2,1)S(1)} %pad_maximum_fusion.refs_4_), channel_id=1, source_target_pairs={{0,4},{4,8},{8,12},{1,5},{5,9},{9,13},{2,6},{6,10},{10,14},{3,7},{... | collective-permute-start | bytes 2949128 | tf_op jit(solution)/shard_map/ppermute | solution.py:126
  10.3 19.0 %collective-permute-done.refs_5_ = bf16[48,10240]{1,0:T(8,128)(2,1)} collective-permute-done((bf16[48,10240]{1,0:T(8,128)(2,1)S(1)}, bf16[48,10240]{1,0:T(8,128)(2,1)}, u32[]{:S(2)}, u32[]{:S(2)}) %collective-permute-start) | collective-permute-done | bytes 983072 | tf_op jit(solution)/shard_map/ppermute | solution.py:125
  29.2 1.1 collective-permute-done.1.refs_6_
  30.3 1.3 %collective-permute-start.2 = (bf16[48,10240]{1,0:T(8,128)(2,1)}, bf16[48,10240]{1,0:T(8,128)(2,1)}, u32[]{:S(2)}, u32[]{:S(2)}) collective-permute-start(bf16[48,10240]{1,0:T(8,128)(2,1)} %collective-permute-done.refs_5_), channel_id=1, source_target_pairs={{4,0},{8,4},{5,1},{9,5},{6,2},{10,6},{7,3},{11,7},{20,16},{24,20},... | collective-permute-start | bytes 2949128 | tf_op jit(solution)/shard_map/ppermute | solution.py:128
  31.6 1.7 %collective-permute-start.3 = (bf16[48,10240]{1,0:T(8,128)(2,1)}, bf16[48,10240]{1,0:T(8,128)(2,1)}, u32[]{:S(2)}, u32[]{:S(2)}) collective-permute-start(bf16[48,10240]{1,0:T(8,128)(2,1)} %collective-permute-done.1.refs_6_), channel_id=1, source_target_pairs={{4,8},{8,12},{5,9},{9,13},{6,10},{10,14},{7,11},{11,15},{20,24},{2... | collective-permute-start | bytes 2949128 | tf_op jit(solution)/shard_map/ppermute | solution.py:129
  33.8 1.1 copy.29
  36.0 7.5 %collective-permute-start.4 = (bf16[40,2560]{1,0:T(8,128)(2,1)S(1)}, bf16[40,2560]{1,0:T(8,128)(2,1)S(1)}, u32[]{:S(2)}, u32[]{:S(2)}) collective-permute-start(bf16[40,2560]{1,0:T(8,128)(2,1)S(1)} %get-tuple-element.41), channel_id=1, source_target_pairs={{0,4},{4,8},{8,12},{12,0},{1,5},{5,9},{9,13},{13,1},{2,6},{6,10},{... | collective-permute-start | bytes 614408 | tf_op jit(solution)/shard_map/ppermute | solution.py:160
  43.4 2.4 %collective-permute-start.6 = (bf16[40,2560]{1,0:T(8,128)(2,1)S(1)}, bf16[40,2560]{1,0:T(8,128)(2,1)S(1)}, u32[]{:S(2)}, u32[]{:S(2)}) collective-permute-start(bf16[40,2560]{1,0:T(8,128)(2,1)S(1)} %get-tuple-element.39), channel_id=1, source_target_pairs={{0,12},{4,0},{8,4},{12,8},{1,13},{5,1},{9,5},{13,9},{2,14},{6,2},{... | collective-permute-start | bytes 614408 | tf_op jit(solution)/shard_map/ppermute | solution.py:160
  45.9 16.3 %collective-permute-done.2.refs_7_ = bf16[48,10240]{1,0:T(8,128)(2,1)} collective-permute-done((bf16[48,10240]{1,0:T(8,128)(2,1)}, bf16[48,10240]{1,0:T(8,128)(2,1)}, u32[]{:S(2)}, u32[]{:S(2)}) %collective-permute-start.2) | collective-permute-done | bytes 983072 | tf_op jit(solution)/shard_map/ppermute | solution.py:128
  62.2 1.3 %slice_select_fusion = bf16[48,6144]{1,0:T(8,128)(2,1)S(1)} fusion(bf16[48,10240]{1,0:T(8,128)(2,1)} %collective-permute-done.3.refs_8_, bf16[48,10240]{1,0:T(8,128)(2,1)} %collective-permute-done.2.refs_7_, pred[]{:T(512)S(6)} %lt.39), kind=kLoop, calls=%fused_computation.9 | loop fusion | flops 294912 | bytes 1769473 | tf_op jit(solution)/shard_map/jit(_where)/select_n | solution.py:133
  63.5 1.3 %collective-permute-start.8 = (bf16[48,6144]{1,0:T(8,128)(2,1)S(1)}, bf16[48,6144]{1,0:T(8,128)(2,1)S(1)}, u32[]{:S(2)}, u32[]{:S(2)}) collective-permute-start(bf16[48,6144]{1,0:T(8,128)(2,1)S(1)} %slice_select_fusion), channel_id=1, source_target_pairs={{4,0},{8,12},{5,1},{9,13},{6,2},{10,14},{7,3},{11,15},{20,16},{24,... | collective-permute-start | bytes 1769480 | tf_op jit(solution)/shard_map/ppermute | solution.py:136
  64.8 7.5 %collective-permute-done.5 = bf16[40,2560]{1,0:T(8,128)(2,1)S(1)} collective-permute-done((bf16[40,2560]{1,0:T(8,128)(2,1)S(1)}, bf16[40,2560]{1,0:T(8,128)(2,1)S(1)}, u32[]{:S(2)}, u32[]{:S(2)}) %collective-permute-start.5) | collective-permute-done | bytes 204832 | tf_op jit(solution)/shard_map/ppermute | solution.py:160
  72.4 1.7 %collective-permute-start.7 = (bf16[160,2560]{1,0:T(8,128)(2,1)S(1)}, bf16[160,2560]{1,0:T(8,128)(2,1)S(1)}, u32[]{:S(2)}, u32[]{:S(2)}) collective-permute-start(bf16[160,2560]{1,0:T(8,128)(2,1)S(1)} %constant_dynamic-update-slice_fusion.refs_0_), channel_id=1, source_target_pairs={{0,16},{16,0},{1,17},{17,1},{2,18},{18,2},{3,19},{19,3},{4,20},{20... | collective-permute-start | bytes 2457608 | tf_op jit(solution)/shard_map/ppermute | solution.py:167
  74.0 1.2 slice_select_fusion.1
  75.2 6.4 %copy-done.1 = bf16[1,1536,6144]{2,1,0:T(8,128)(2,1)S(1)} copy-done((bf16[1,1536,6144]{2,1,0:T(8,128)(2,1)S(1)}, bf16[1,1536,6144]{2,1,0:T(8,128)(2,1)}, u32[]{:S(2)}) %copy-start.1) | copy-done | bytes 18874392
  81.6 3.4 %copy-done.2 = bf16[1,1024,4096]{2,1,0:T(8,128)(2,1)S(1)} copy-done((bf16[1,1024,4096]{2,1,0:T(8,128)(2,1)S(1)}, bf16[1,1024,4096]{2,1,0:T(8,128)(2,1)}, u32[]{:S(2)}) %copy-start.2) | copy-done | bytes 8388632
  84.9 9.3 %shard_map.82 = (bf16[1536,192]{1,0:T(8,128)(2,1)S(1)}, bf16[1024,192]{1,0:T(8,128)(2,1)S(1)}) custom-call(bf16[1536,6144]{1,0:T(8,128)(2,1)S(1)} %bitcast.39, bf16[1024,4096]{1,0:T(8,128)(2,1)S(1)} %bitcast.41, f32[1536,1]{1,0:T(8,128)S(1)} %copy.20.refs_2_.refs_1_, f32[1024,1]{1,0:T(8,128)S(1)} %copy.21.refs_3_.refs_1_, ...), custom_call_target="tpu_custom_call" | custom-call | flops 1 | bytes 1 | tf_op jit(solution)/shard_map/pallas_call | solution.py:50
  94.3 1.6 %collective-permute-start.9 = (bf16[48,4096]{1,0:T(8,128)(2,1)S(1)}, bf16[48,4096]{1,0:T(8,128)(2,1)S(1)}, u32[]{:S(2)}, u32[]{:S(2)}) collective-permute-start(bf16[48,4096]{1,0:T(8,128)(2,1)S(1)} %slice_select_fusion.1), channel_id=1, source_target_pairs={{4,0},{8,12},{5,1},{9,13},{6,2},{10,14},{7,3},{11,15},{20,16},{24,... | collective-permute-start | bytes 1179656 | tf_op jit(solution)/shard_map/ppermute | solution.py:142
  95.8 5.0 %shard_map.84.refs_2_ = bf16[1536,48]{1,0:T(8,128)(2,1)S(1)} custom-call(bf16[1536,6144]{1,0:T(8,128)(2,1)S(1)} %bitcast.40, f32[1536,1]{1,0:T(8,128)S(1)} %copy.20.refs_2_.refs_1_, bf16[48,6144]{1,0:T(8,128)(2,1)S(1)} %collective-permute-done.8.refs_2_), custom_call_target="tpu_custom_call" | custom-call | flops 1 | bytes 1 | tf_op jit(solution)/shard_map/pallas_call | solution.py:50
  101.6 5.5 %collective-permute-done.9.refs_2_ = bf16[48,4096]{1,0:T(8,128)(2,1)S(1)} collective-permute-done((bf16[48,4096]{1,0:T(8,128)(2,1)S(1)}, bf16[48,4096]{1,0:T(8,128)(2,1)S(1)}, u32[]{:S(2)}, u32[]{:S(2)}) %collective-permute-start.9) | collective-permute-done | bytes 393248 | tf_op jit(solution)/shard_map/ppermute | solution.py:142
  107.0 2.3 %shard_map.85.refs_3_ = bf16[1024,48]{1,0:T(8,128)(2,1)S(1)} custom-call(bf16[1024,4096]{1,0:T(8,128)(2,1)S(1)} %bitcast.44, f32[1024,1]{1,0:T(8,128)S(1)} %copy.21.refs_3_.refs_1_, bf16[48,4096]{1,0:T(8,128)(2,1)S(1)} %collective-permute-done.9.refs_2_), custom_call_target="tpu_custom_call" | custom-call | flops 1 | bytes 1 | tf_op jit(solution)/shard_map/pallas_call | solution.py:50
  110.0 16.3 %all_to_all.5 = bf16[32,16,256]{2,1,0:T(8,128)(2,1)S(1)} all-to-all(bf16[32,16,256]{2,1,0:T(8,128)(2,1)S(1)} %bitcast.45), channel_id=1, replica_groups=mesh['parts'=2,'rows'=4,'layer'=4] {'parts','rows','layer'}, dimensions={0} | all-to-all | bytes 524288 | tf_op jit(solution)/shard_map/all_to_all | solution.py:221
  (37 shorter events, 5.1 us)
Async XLA Ops:
  0.0 1.3 copy-start
  1.3 32.0 %copy-start.3 = (f32[1,1536]{1,0:T(1,128)S(1)}, f32[1,1536]{1,0:T(1,128)}, u32[]{:S(2)}) copy-start(f32[1,1536]{1,0:T(1,128)} %param.14) | copy-start | bytes 18436
  1.3 32.2 %copy-start.4 = (f32[1,1024]{1,0:T(1,128)S(1)}, f32[1,1024]{1,0:T(1,128)}, u32[]{:S(2)}) copy-start(f32[1,1024]{1,0:T(1,128)} %param.15) | copy-start | bytes 12292
  2.4 26.8 %collective-permute-start = (bf16[48,10240]{1,0:T(8,128)(2,1)S(1)}, bf16[48,10240]{1,0:T(8,128)(2,1)}, u32[]{:S(2)}, u32[]{:S(2)}) collective-permute-start(bf16[48,10240]{1,0:T(8,128)(2,1)S(1)} %pad_maximum_fusion.refs_4_), channel_id=1, source_target_pairs={{4,0},{8,4},{12,8},{5,1},{9,5},{13,9},{6,2},{10,6},{14,10},{7,3},{... | collective-permute-start | bytes 2949128 | tf_op jit(solution)/shard_map/ppermute | solution.py:125
  3.7 26.6 %collective-permute-start.1 = (bf16[48,10240]{1,0:T(8,128)(2,1)S(1)}, bf16[48,10240]{1,0:T(8,128)(2,1)}, u32[]{:S(2)}, u32[]{:S(2)}) collective-permute-start(bf16[48,10240]{1,0:T(8,128)(2,1)S(1)} %pad_maximum_fusion.refs_4_), channel_id=1, source_target_pairs={{0,4},{4,8},{8,12},{1,5},{5,9},{9,13},{2,6},{6,10},{10,14},{3,7},{... | collective-permute-start | bytes 2949128 | tf_op jit(solution)/shard_map/ppermute | solution.py:126
  30.3 31.9 %collective-permute-start.2 = (bf16[48,10240]{1,0:T(8,128)(2,1)}, bf16[48,10240]{1,0:T(8,128)(2,1)}, u32[]{:S(2)}, u32[]{:S(2)}) collective-permute-start(bf16[48,10240]{1,0:T(8,128)(2,1)} %collective-permute-done.refs_5_), channel_id=1, source_target_pairs={{4,0},{8,4},{5,1},{9,5},{6,2},{10,6},{7,3},{11,7},{20,16},{24,20},... | collective-permute-start | bytes 2949128 | tf_op jit(solution)/shard_map/ppermute | solution.py:128
  31.6 30.6 %collective-permute-start.3 = (bf16[48,10240]{1,0:T(8,128)(2,1)}, bf16[48,10240]{1,0:T(8,128)(2,1)}, u32[]{:S(2)}, u32[]{:S(2)}) collective-permute-start(bf16[48,10240]{1,0:T(8,128)(2,1)} %collective-permute-done.1.refs_6_), channel_id=1, source_target_pairs={{4,8},{8,12},{5,9},{9,13},{6,10},{10,14},{7,11},{11,15},{20,24},{2... | collective-permute-start | bytes 2949128 | tf_op jit(solution)/shard_map/ppermute | solution.py:129
  36.0 28.8 %collective-permute-start.4 = (bf16[40,2560]{1,0:T(8,128)(2,1)S(1)}, bf16[40,2560]{1,0:T(8,128)(2,1)S(1)}, u32[]{:S(2)}, u32[]{:S(2)}) collective-permute-start(bf16[40,2560]{1,0:T(8,128)(2,1)S(1)} %get-tuple-element.41), channel_id=1, source_target_pairs={{0,4},{4,8},{8,12},{12,0},{1,5},{5,9},{9,13},{13,1},{2,6},{6,10},{... | collective-permute-start | bytes 614408 | tf_op jit(solution)/shard_map/ppermute | solution.py:160
  43.4 28.9 %collective-permute-start.5 = (bf16[40,2560]{1,0:T(8,128)(2,1)S(1)}, bf16[40,2560]{1,0:T(8,128)(2,1)S(1)}, u32[]{:S(2)}, u32[]{:S(2)}) collective-permute-start(bf16[40,2560]{1,0:T(8,128)(2,1)S(1)} %get-tuple-element.42), channel_id=1, source_target_pairs={{0,8},{4,12},{8,0},{12,4},{1,9},{5,13},{9,1},{13,5},{2,10},{6,14},... | collective-permute-start | bytes 614408 | tf_op jit(solution)/shard_map/ppermute | solution.py:160
  43.4 28.9 %collective-permute-start.6 = (bf16[40,2560]{1,0:T(8,128)(2,1)S(1)}, bf16[40,2560]{1,0:T(8,128)(2,1)S(1)}, u32[]{:S(2)}, u32[]{:S(2)}) collective-permute-start(bf16[40,2560]{1,0:T(8,128)(2,1)S(1)} %get-tuple-element.39), channel_id=1, source_target_pairs={{0,12},{4,0},{8,4},{12,8},{1,13},{5,1},{9,5},{13,9},{2,14},{6,2},{... | collective-permute-start | bytes 614408 | tf_op jit(solution)/shard_map/ppermute | solution.py:160
  63.5 30.8 %collective-permute-start.8 = (bf16[48,6144]{1,0:T(8,128)(2,1)S(1)}, bf16[48,6144]{1,0:T(8,128)(2,1)S(1)}, u32[]{:S(2)}, u32[]{:S(2)}) collective-permute-start(bf16[48,6144]{1,0:T(8,128)(2,1)S(1)} %slice_select_fusion), channel_id=1, source_target_pairs={{4,0},{8,12},{5,1},{9,13},{6,2},{10,14},{7,3},{11,15},{20,16},{24,... | collective-permute-start | bytes 1769480 | tf_op jit(solution)/shard_map/ppermute | solution.py:136
  72.4 28.5 %collective-permute-start.7 = (bf16[160,2560]{1,0:T(8,128)(2,1)S(1)}, bf16[160,2560]{1,0:T(8,128)(2,1)S(1)}, u32[]{:S(2)}, u32[]{:S(2)}) collective-permute-start(bf16[160,2560]{1,0:T(8,128)(2,1)S(1)} %constant_dynamic-update-slice_fusion.refs_0_), channel_id=1, source_target_pairs={{0,16},{16,0},{1,17},{17,1},{2,18},{18,2},{3,19},{19,3},{4,20},{20... | collective-permute-start | bytes 2457608 | tf_op jit(solution)/shard_map/ppermute | solution.py:167
  75.2 6.4 %copy-start.1 = (bf16[1,1536,6144]{2,1,0:T(8,128)(2,1)S(1)}, bf16[1,1536,6144]{2,1,0:T(8,128)(2,1)}, u32[]{:S(2)}) copy-start(bf16[1,1536,6144]{2,1,0:T(8,128)(2,1)} %param.12) | copy-start | bytes 56623108
  81.6 3.4 %copy-start.2 = (bf16[1,1024,4096]{2,1,0:T(8,128)(2,1)S(1)}, bf16[1,1024,4096]{2,1,0:T(8,128)(2,1)}, u32[]{:S(2)}) copy-start(bf16[1,1024,4096]{2,1,0:T(8,128)(2,1)} %param.13) | copy-start | bytes 25165828
  94.2 12.8 %slice-start = ((s8[8388608]{0:T(1024)(128)(4,1)}), s8[4194304]{0:T(1024)(128)(4,1)S(1)}, s32[]{:S(2)}) async-start(s8[8388608]{0:T(1024)(128)(4,1)} %bitcast.42), calls=%async_computation.1 | async-start | bytes 8388608
  94.3 12.8 %slice-start.1 = ((s8[8388608]{0:T(1024)(128)(4,1)}), s8[4194304]{0:T(1024)(128)(4,1)S(1)}, s32[]{:S(2)}) async-start(s8[8388608]{0:T(1024)(128)(4,1)} %bitcast.42), calls=%async_computation.2 | async-start | bytes 8388608
  94.3 12.8 %collective-permute-start.9 = (bf16[48,4096]{1,0:T(8,128)(2,1)S(1)}, bf16[48,4096]{1,0:T(8,128)(2,1)S(1)}, u32[]{:S(2)}, u32[]{:S(2)}) collective-permute-start(bf16[48,4096]{1,0:T(8,128)(2,1)S(1)} %slice_select_fusion.1), channel_id=1, source_target_pairs={{4,0},{8,12},{5,1},{9,13},{6,2},{10,14},{7,3},{11,15},{20,16},{24,... | collective-permute-start | bytes 1179656 | tf_op jit(solution)/shard_map/ppermute | solution.py:142

commit v17 on v12

--- a/solution.py
+++ b/solution.py
@@ -12,6 +12,7 @@
 
 MIB = 1024 * 1024
 TILE = 256
+AHEAD = 3
 
 
 def along(value, by):
@@ -19,7 +20,7 @@
     return lax.ppermute(value, "rows", [(i, i + by) for i in range(size) if 0 <= i + by < size])
 
 
-def rotate(bases, eigens, queries, begins):
+def rotate(bases, eigens, queries, begins, load=False):
     groups = [query if isinstance(query, tuple) else (query,) for query in queries]
     queries = [query for group in groups for query in group]
     columns = queries[0].shape[0]
@@ -29,16 +30,32 @@
     def kernel(*refs):
         basis_refs, eigen_refs = refs[:sides], refs[sides : 2 * sides]
         query_refs = list(refs[2 * sides : 2 * sides + len(queries)])
-        out_refs, query = refs[2 * sides + len(queries) : -1], refs[-1]
+        out_refs, rest = refs[2 * sides + len(queries) :][:sides], refs[3 * sides + len(queries) :]
+        copies = []
+        if load:
+            loaded, query, semaphores = rest
+            for tile in range(loaded.shape[0] // TILE):
+                where = slice(tile * TILE, (tile + 1) * TILE)
+                copies.append(pltpu.make_async_copy(basis_refs[0].at[where], loaded.at[where], semaphores.at[tile]))
+            for copy in copies[:AHEAD]:
+                copy.start()
+            basis_refs = [loaded, *basis_refs[1:]]
+        else:
+            (query,) = rest
         for place, group in enumerate(groups):
             block = query_refs.pop(0)[...]
             for _ in group[1:]:
                 block = block + query_refs.pop(0)[...]
             query[place * columns : (place + 1) * columns, :] = block
-        for basis_ref, eigen_ref, out_ref, begin in zip(basis_refs, eigen_refs, out_refs, begins):
+        for side in reversed(range(sides)):
+            basis_ref, eigen_ref, out_ref, begin = basis_refs[side], eigen_refs[side], out_refs[side], begins[side]
             share, width = basis_ref.shape
             for tile in range(share // TILE):
                 where = slice(tile * TILE, (tile + 1) * TILE)
+                if load and side == 0:
+                    copies[tile].wait()
+                    if tile + AHEAD < len(copies):
+                        copies[tile + AHEAD].start()
                 rotated = lax.dot_general(
                     basis_ref[where, :],
                     query[:, begin : begin + width],
@@ -47,13 +64,52 @@
                 )
                 out_ref[where, :] = (rotated * (1.0 / (eigen_ref[where, :] + damping))).astype(jnp.bfloat16)
 
+    spaces = [pltpu.HBM if load and side == 0 else pltpu.VMEM for side in range(sides)]
+    spaces += [pltpu.VMEM] * (sides + len(queries))
+    constrained = [
+        pltpu.with_memory_space_constraint(one, space) for one, space in zip((*bases, *eigens, *queries), spaces)
+    ]
     return pl.pallas_call(
         kernel,
-        out_shape=[jax.ShapeDtypeStruct((basis.shape[0], held), jnp.bfloat16) for basis in bases],
-        scratch_shapes=[pltpu.VMEM((held, queries[0].shape[1]), jnp.bfloat16)],
+        in_specs=[pl.BlockSpec(memory_space=space) for space in spaces],
+        out_specs=[pl.BlockSpec(memory_space=pltpu.VMEM)] * (sides + load),
+        out_shape=[jax.ShapeDtypeStruct((basis.shape[0], held), jnp.bfloat16) for basis in bases]
+        + ([pltpu.VMEM(bases[0].shape, bases[0].dtype)] if load else []),
+        scratch_shapes=[pltpu.VMEM((held, queries[0].shape[1]), jnp.bfloat16)]
+        + ([pltpu.SemaphoreType.DMA((bases[0].shape[0] // TILE,))] if load else []),
         compiler_params=pltpu.CompilerParams(vmem_limit_bytes=8 * MIB),
         cost_estimate=pl.CostEstimate(flops=1, bytes_accessed=1, transcendentals=0),
-    )(*[pltpu.with_memory_space_constraint(one, pltpu.VMEM) for one in (*bases, *eigens, *queries)])
+    )(*constrained)
+
+
+def own_rows(query_hidden, query_model, columns):
+    if columns % 16:
+        start = lax.axis_index("parts") * columns
+        return jnp.concatenate(
+            [lax.dynamic_slice_in_dim(side, start, columns, 0) for side in (query_hidden, query_model)], axis=1
+        )
+    depth = query_hidden.shape[1]
+
+    def kernel(hidden_ref, model_ref, out_ref, semaphores):
+        rows = pl.ds(pl.multiple_of(lax.axis_index("parts") * columns, columns), columns)
+        copies = [
+            pltpu.make_async_copy(hidden_ref.at[rows], out_ref.at[:, :depth], semaphores.at[0]),
+            pltpu.make_async_copy(model_ref.at[rows], out_ref.at[:, depth:], semaphores.at[1]),
+        ]
+        for copy in copies:
+            copy.start()
+        for copy in copies:
+            copy.wait()
+
+    return pl.pallas_call(
+        kernel,
+        in_specs=[pl.BlockSpec(memory_space=pltpu.HBM)] * 2,
+        out_specs=pl.BlockSpec(memory_space=pltpu.VMEM),
+        out_shape=pltpu.VMEM((columns, depth + query_model.shape[1]), query_hidden.dtype),
+        scratch_shapes=[pltpu.SemaphoreType.DMA((2,))],
+        compiler_params=pltpu.CompilerParams(vmem_limit_bytes=2 * MIB),
+        cost_estimate=pl.CostEstimate(flops=1, bytes_accessed=1, transcendentals=0),
+    )(*[pltpu.with_memory_space_constraint(side, pltpu.HBM) for side in (query_hidden, query_model)])
 
 
 def packed_width(examples, columns):
@@ -130,7 +186,8 @@
     query, after, before = lax.optimization_barrier((query, after, before))
     after_two = lax.ppermute(after, "rows", [(1, 0), (2, 1)])
     before_two = lax.ppermute(before, "rows", [(1, 2), (2, 3)])
-    near = rotate(bases, eigens, [query, after, before], (0, depth))
+    *near, hidden_here = rotate(bases, eigens, [query, after, before], (0, depth), load=True)
+    bases = [hidden_here, bases[1]]
     near, blocks = lax.optimization_barrier((near, blocks))
     stores = to_parts(jnp.concatenate(blocks, axis=0))
     near, after_two, before_two = lax.optimization_barrier((near, after_two, before_two))
@@ -186,10 +243,7 @@
     share = bases[0].shape[0]
     depth = bases[0].shape[1]
 
-    query = jnp.concatenate(
-        [lax.dynamic_slice_in_dim(side[0], part * columns, columns, 0) for side in (query_hidden, query_model)],
-        axis=1,
-    )
+    query = own_rows(query_hidden[0], query_model[0], columns)
     by_owner = jnp.concatenate(
         [side[0].reshape(held, rows, -1).transpose(1, 0, 2) for side in (train_hidden, train_model)], axis=2
     )

time: 116 us -> 114 us (0.983)
  local copies, waits for them, and re-layouts: 23.8 us -> 16.2 us
  Pallas kernels: 25 us -> 32.4 us
  waiting for transfers between devices: 24.6 us -> 22.3 us
  blocking collectives: 15.6 us -> 16.8 us
    unnamed x23 -> x19, local copies, waits for them, and re-layouts: 19.3 us -> 8.67 us
    pallas_call x4 -> x5, Pallas kernels: 23.2 us -> 30.6 us  [the longest x4 29.4 us: rotate(): pl.pallas_call(kernel, in_specs=[pl.BlockSpec(memory_space=space) for spa...]
    ppermute x1, waiting for transfers between devices: 5.98 us -> 12.1 us  [along_four(): three_hidden = lax.ppermute(two_hidden, 'rows', ends)]
    ppermute x1, waiting for transfers between devices: 11.8 us -> 7.83 us  [along_four(): after = lax.ppermute(query, 'rows', [(1, 0), (2, 1), (3, 2)])]
    ppermute x1, waiting for transfers between devices: 3.31 us -> 0.06 us  [along_four(): after_two = lax.ppermute(after, 'rows', [(1, 0), (2, 1)])]
    reshape x2, local copies, waits for them, and re-layouts: 0.51 us -> 3.59 us  [along_four(): eigens = [eigen.reshape(-1, 1) for eigen in eigens]]
    all_to_all x1, blocking collectives: 15.6 us -> 16.8 us  [per_device(): lax.all_to_all(partial.reshape((parts * rows * layers,) + partial.shape[3...]
    ppermute x1, waiting for transfers between devices: 3.43 us -> 2.26 us  [along_four(): three_model = lax.ppermute(two_model, 'rows', ends)]
  transfers between devices with their start and end apart: 10 -> 10, of which waited for: 4 -> 4; matrix products, arithmetic and copies ran while one was open for 5% -> 9% of each run, Pallas kernels for 19% -> 25%
where the time goes in v17:
time: 114 us; the launch traced here: 113 us
  Pallas kernels  32.4 us (28%)
  starting transfers between devices  23.7 us (21%)
  waiting for transfers between devices  22.3 us (20%)
  blocking collectives  16.8 us (15%)
  local copies, waits for them, and re-layouts  16.2 us (14%)
  other arithmetic  1.79 us (2%)
    pallas_call x4, Pallas kernels, rotate(): pl.pallas_call(kernel, in_specs=[pl.BlockSpec(memory_space=space) for spa...  29.4 us
    all_to_all x1, blocking collectives, per_device(): lax.all_to_all(partial.reshape((parts * rows * layers,) + partial.shape[3...  16.8 us
    ppermute x1, waiting for transfers between devices, along_four(): three_hidden = lax.ppermute(two_hidden, 'rows', ends)  12.1 us
    unnamed x19, local copies, waits for them, and re-layouts  8.67 us
    ppermute x1, waiting for transfers between devices, along_four(): after = lax.ppermute(query, 'rows', [(1, 0), (2, 1), (3, 2)])  7.83 us
    ppermute x1, starting transfers between devices, along_four(): before = lax.ppermute(query, 'rows', [(0, 1), (1, 2), (2, 3)])  6.56 us
    ppermute x3, starting transfers between devices, to_owners(): lax.ppermute(sent[k], 'rows', [(i, (i + k) % rows) for i in range(rows)])  5.95 us
    ppermute x1, starting transfers between devices, to_parts(): lax.ppermute(store, 'parts', [(i, (i + j) % parts) for i in range(parts)])  5.19 us
  transfers between devices with their start and end apart: 10, of which 4 were waited for; matrix products, arithmetic and copies ran while one was open for 9% of the time, Pallas kernels for 25%

profile of v17, /device:TPU:0, one launch (start us, length us, event | category | flops | bytes accessed | tf_op | source)
XLA Modules:
  0.0 113.5 jit_solution(8228662673820286730)
XLA Ops:
  0.0 1.2 %shard_map.82.refs_4_ = bf16[48,10240]{1,0:T(8,128)(2,1)S(1)} custom-call(bf16[96,6144]{1,0:T(8,128)(2,1)} %bitcast.34, bf16[96,4096]{1,0:T(8,128)(2,1)} %bitcast.36), custom_call_target="tpu_custom_call" | custom-call | flops 1 | bytes 1 | tf_op jit(solution)/shard_map/pallas_call | solution.py:104
  1.2 1.3 %collective-permute-start = (bf16[48,10240]{1,0:T(8,128)(2,1)S(1)}, bf16[48,10240]{1,0:T(8,128)(2,1)}, u32[]{:S(2)}, u32[]{:S(2)}) collective-permute-start(bf16[48,10240]{1,0:T(8,128)(2,1)S(1)} %shard_map.82.refs_4_), channel_id=1, source_target_pairs={{4,0},{8,4},{12,8},{5,1},{9,5},{13,9},{6,2},{10,6},{14,10},{7,3},{... | collective-permute-start | bytes 2949128 | tf_op jit(solution)/shard_map/ppermute | solution.py:181
  2.5 6.6 %collective-permute-start.1 = (bf16[48,10240]{1,0:T(8,128)(2,1)S(1)}, bf16[48,10240]{1,0:T(8,128)(2,1)}, u32[]{:S(2)}, u32[]{:S(2)}) collective-permute-start(bf16[48,10240]{1,0:T(8,128)(2,1)S(1)} %shard_map.82.refs_4_), channel_id=1, source_target_pairs={{0,4},{4,8},{8,12},{1,5},{5,9},{9,13},{2,6},{6,10},{10,14},{3,7},{... | collective-permute-start | bytes 2949128 | tf_op jit(solution)/shard_map/ppermute | solution.py:182
  9.1 1.4 %reshape_squeeze.6 = bf16[40,4,1536]{2,1,0:T(4,128)(2,1)S(1)} reshape(bf16[1,40,6144]{2,1,0:T(8,128)(2,1)} %param.10) | data formatting | bytes 983040 | tf_op jit(solution)/shard_map/reshape;squeeze | solution.py:248
  10.6 1.2 %reshape_squeeze.7 = bf16[40,4,1024]{2,1,0:T(4,128)(2,1)S(1)} reshape(bf16[1,40,4096]{2,1,0:T(8,128)(2,1)} %param.11) | data formatting | bytes 655360 | tf_op jit(solution)/shard_map/reshape;squeeze | solution.py:248
  13.9 1.9 %collective-permute-start.3 = (bf16[40,2560]{1,0:T(8,128)(2,1)}, bf16[40,2560]{1,0:T(8,128)(2,1)}, u32[]{:S(2)}, u32[]{:S(2)}) collective-permute-start(bf16[40,2560]{1,0:T(8,128)(2,1)} %get-tuple-element.43), channel_id=1, source_target_pairs={{0,8},{4,12},{8,0},{12,4},{1,9},{5,13},{9,1},{13,5},{2,10},{6,14},... | collective-permute-start | bytes 614408 | tf_op jit(solution)/shard_map/ppermute | solution.py:212
  15.9 2.9 %collective-permute-start.4 = (bf16[40,2560]{1,0:T(8,128)(2,1)}, bf16[40,2560]{1,0:T(8,128)(2,1)}, u32[]{:S(2)}, u32[]{:S(2)}) collective-permute-start(bf16[40,2560]{1,0:T(8,128)(2,1)} %get-tuple-element.44), channel_id=1, source_target_pairs={{0,12},{4,0},{8,4},{12,8},{1,13},{5,1},{9,5},{13,9},{2,14},{6,2},{... | collective-permute-start | bytes 614408 | tf_op jit(solution)/shard_map/ppermute | solution.py:212
  18.8 1.9 %copy.22.refs_2_.refs_1_ = f32[1536,1]{1,0:T(8,128)} copy(f32[1536,1]{0,1:T(1,128)} %bitcast.39) | data formatting | bytes 12288 | tf_op jit(solution)/shard_map/reshape | solution.py:180
  20.7 1.7 %copy.23.refs_3_.refs_1_ = f32[1024,1]{1,0:T(8,128)} copy(f32[1024,1]{0,1:T(1,128)} %bitcast.40) | data formatting | bytes 8192 | tf_op jit(solution)/shard_map/reshape | solution.py:180
  22.4 7.8 %collective-permute-done.refs_5_ = bf16[48,10240]{1,0:T(8,128)(2,1)} collective-permute-done((bf16[48,10240]{1,0:T(8,128)(2,1)S(1)}, bf16[48,10240]{1,0:T(8,128)(2,1)}, u32[]{:S(2)}, u32[]{:S(2)}) %collective-permute-start) | collective-permute-done | bytes 983072 | tf_op jit(solution)/shard_map/ppermute | solution.py:181
  30.2 1.3 %collective-permute-start.6 = (bf16[48,10240]{1,0:T(8,128)(2,1)}, bf16[48,10240]{1,0:T(8,128)(2,1)S(1)}, u32[]{:S(2)}, u32[]{:S(2)}) collective-permute-start(bf16[48,10240]{1,0:T(8,128)(2,1)} %collective-permute-done.refs_5_), channel_id=1, source_target_pairs={{4,0},{8,4},{5,1},{9,5},{6,2},{10,6},{7,3},{11,7},{20,16},{24,20},... | collective-permute-start | bytes 2949128 | tf_op jit(solution)/shard_map/ppermute | solution.py:187
  32.3 3.4 %copy-done = bf16[1,1024,4096]{2,1,0:T(8,128)(2,1)S(1)} copy-done((bf16[1,1024,4096]{2,1,0:T(8,128)(2,1)S(1)}, bf16[1,1024,4096]{2,1,0:T(8,128)(2,1)}, u32[]{:S(2)}) %copy-start) | copy-done | bytes 8388632
  35.6 1.1 copy-done.2
  37.8 1.2 %copy-done.6 = bf16[48,10240]{1,0:T(8,128)(2,1)S(1)} copy-done((bf16[48,10240]{1,0:T(8,128)(2,1)S(1)}, bf16[48,10240]{1,0:T(8,128)(2,1)}, u32[]{:S(2)}) %copy-start.6) | copy-done | bytes 983064
  39.0 14.9 %shard_map.83 = (bf16[1536,144]{1,0:T(8,128)(2,1)S(1)}, bf16[1024,144]{1,0:T(8,128)(2,1)S(1)}, bf16[1536,6144]{1,0:T(8,128)(2,1)S(1)}) custom-call(bf16[1536,6144]{1,0:T(8,128)(2,1)} %bitcast.31, bf16[1024,4096]{1,0:T(8,128)(2,1)S(1)} %bitcast.27, f32[1536,1]{1,0:T(8,128)S(1)} %copy-done.2, f32[1024,1]{1,0:T(8,128)S(1)} %copy-done.4, ...), custom_call_target="tpu_custom_call" | custom-call | flops 1 | bytes 1 | tf_op jit(solution)/shard_map/pallas_call | solution.py:72
  56.9 5.2 %collective-permute-start.5 = (bf16[160,2560]{1,0:T(8,128)(2,1)S(1)}, bf16[160,2560]{1,0:T(8,128)(2,1)S(1)}, u32[]{:S(2)}, u32[]{:S(2)}) collective-permute-start(bf16[160,2560]{1,0:T(8,128)(2,1)S(1)} %constant_dynamic-update-slice_fusion.refs_0_), channel_id=1, source_target_pairs={{0,16},{16,0},{1,17},{17,1},{2,18},{18,2},{3,19},{19,3},{4,20},{20... | collective-permute-start | bytes 2457608 | tf_op jit(solution)/shard_map/ppermute | solution.py:219
  62.2 1.5 %collective-permute-start.8 = (bf16[48,6144]{1,0:T(8,128)(2,1)S(1)}, bf16[48,6144]{1,0:T(8,128)(2,1)S(1)}, u32[]{:S(2)}, u32[]{:S(2)}) collective-permute-start(bf16[48,6144]{1,0:T(8,128)(2,1)S(1)} %slice_select_fusion), channel_id=1, source_target_pairs={{4,0},{8,12},{5,1},{9,13},{6,2},{10,14},{7,3},{11,15},{20,16},{24,... | collective-permute-start | bytes 1769480 | tf_op jit(solution)/shard_map/ppermute | solution.py:198
  63.7 7.2 %shard_map.84 = (bf16[1536,48]{1,0:T(8,128)(2,1)S(1)}, bf16[1024,48]{1,0:T(8,128)(2,1)S(1)}) custom-call(bf16[1536,6144]{1,0:T(8,128)(2,1)S(1)} %get-tuple-element.53.refs_0_, bf16[1024,4096]{1,0:T(8,128)(2,1)S(1)} %bitcast.28, f32[1536,1]{1,0:T(8,128)S(1)} %copy-done.3, f32[1024,1]{1,0:T(8,128)S(1)} %copy-done.4, ...), custom_call_target="tpu_custom_call" | custom-call | flops 1 | bytes 1 | tf_op jit(solution)/shard_map/pallas_call | solution.py:72
  70.9 12.1 %collective-permute-done.8.refs_2_ = bf16[48,6144]{1,0:T(8,128)(2,1)S(1)} collective-permute-done((bf16[48,6144]{1,0:T(8,128)(2,1)S(1)}, bf16[48,6144]{1,0:T(8,128)(2,1)S(1)}, u32[]{:S(2)}, u32[]{:S(2)}) %collective-permute-start.8) | collective-permute-done | bytes 589856 | tf_op jit(solution)/shard_map/ppermute | solution.py:198
  83.1 1.3 %collective-permute-start.9 = (bf16[48,4096]{1,0:T(8,128)(2,1)S(1)}, bf16[48,4096]{1,0:T(8,128)(2,1)S(1)}, u32[]{:S(2)}, u32[]{:S(2)}) collective-permute-start(bf16[48,4096]{1,0:T(8,128)(2,1)S(1)} %slice_select_fusion.1), channel_id=1, source_target_pairs={{4,0},{8,12},{5,1},{9,13},{6,2},{10,14},{7,3},{11,15},{20,16},{24,... | collective-permute-start | bytes 1179656 | tf_op jit(solution)/shard_map/ppermute | solution.py:202
  84.3 5.0 %shard_map.86.refs_2_ = bf16[1536,48]{1,0:T(8,128)(2,1)S(1)} custom-call(bf16[1536,6144]{1,0:T(8,128)(2,1)S(1)} %get-tuple-element.53.refs_0_, f32[1536,1]{1,0:T(8,128)S(1)} %copy-done.3, bf16[48,6144]{1,0:T(8,128)(2,1)S(1)} %collective-permute-done.8.refs_2_), custom_call_target="tpu_custom_call" | custom-call | flops 1 | bytes 1 | tf_op jit(solution)/shard_map/pallas_call | solution.py:72
  90.5 2.3 %collective-permute-done.9.refs_2_ = bf16[48,4096]{1,0:T(8,128)(2,1)S(1)} collective-permute-done((bf16[48,4096]{1,0:T(8,128)(2,1)S(1)}, bf16[48,4096]{1,0:T(8,128)(2,1)S(1)}, u32[]{:S(2)}, u32[]{:S(2)}) %collective-permute-start.9) | collective-permute-done | bytes 393248 | tf_op jit(solution)/shard_map/ppermute | solution.py:202
  92.7 2.3 %shard_map.87.refs_3_ = bf16[1024,48]{1,0:T(8,128)(2,1)S(1)} custom-call(bf16[1024,4096]{1,0:T(8,128)(2,1)S(1)} %bitcast.29, f32[1024,1]{1,0:T(8,128)S(1)} %copy-done.4, bf16[48,4096]{1,0:T(8,128)(2,1)S(1)} %collective-permute-done.9.refs_2_), custom_call_target="tpu_custom_call" | custom-call | flops 1 | bytes 1 | tf_op jit(solution)/shard_map/pallas_call | solution.py:72
  95.7 16.8 %all_to_all.5 = bf16[32,16,256]{2,1,0:T(8,128)(2,1)S(1)} all-to-all(bf16[32,16,256]{2,1,0:T(8,128)(2,1)S(1)} %bitcast.30), channel_id=1, replica_groups=mesh['parts'=2,'rows'=4,'layer'=4] {'parts','rows','layer'}, dimensions={0} | all-to-all | bytes 524288 | tf_op jit(solution)/shard_map/all_to_all | solution.py:272
  (39 shorter events, 9.7 us)
Async XLA Ops:
  1.2 31.0 %copy-start.5 = (bf16[48,10240]{1,0:T(8,128)(2,1)}, bf16[48,10240]{1,0:T(8,128)(2,1)S(1)}, u32[]{:S(2)}) copy-start(bf16[48,10240]{1,0:T(8,128)(2,1)S(1)} %shard_map.82.refs_4_) | copy-start | bytes 2949124
  1.2 29.0 %collective-permute-start = (bf16[48,10240]{1,0:T(8,128)(2,1)S(1)}, bf16[48,10240]{1,0:T(8,128)(2,1)}, u32[]{:S(2)}, u32[]{:S(2)}) collective-permute-start(bf16[48,10240]{1,0:T(8,128)(2,1)S(1)} %shard_map.82.refs_4_), channel_id=1, source_target_pairs={{4,0},{8,4},{12,8},{5,1},{9,5},{13,9},{6,2},{10,6},{14,10},{7,3},{... | collective-permute-start | bytes 2949128 | tf_op jit(solution)/shard_map/ppermute | solution.py:181
  2.5 27.7 %collective-permute-start.1 = (bf16[48,10240]{1,0:T(8,128)(2,1)S(1)}, bf16[48,10240]{1,0:T(8,128)(2,1)}, u32[]{:S(2)}, u32[]{:S(2)}) collective-permute-start(bf16[48,10240]{1,0:T(8,128)(2,1)S(1)} %shard_map.82.refs_4_), channel_id=1, source_target_pairs={{0,4},{4,8},{8,12},{1,5},{5,9},{9,13},{2,6},{6,10},{10,14},{3,7},{... | collective-permute-start | bytes 2949128 | tf_op jit(solution)/shard_map/ppermute | solution.py:182
  12.8 41.1 %collective-permute-start.2 = (bf16[40,2560]{1,0:T(8,128)(2,1)}, bf16[40,2560]{1,0:T(8,128)(2,1)}, u32[]{:S(2)}, u32[]{:S(2)}) collective-permute-start(bf16[40,2560]{1,0:T(8,128)(2,1)} %get-tuple-element.42), channel_id=1, source_target_pairs={{0,4},{4,8},{8,12},{12,0},{1,5},{5,9},{9,13},{13,1},{2,6},{6,10},{... | collective-permute-start | bytes 614408 | tf_op jit(solution)/shard_map/ppermute | solution.py:212
  13.9 40.1 %collective-permute-start.3 = (bf16[40,2560]{1,0:T(8,128)(2,1)}, bf16[40,2560]{1,0:T(8,128)(2,1)}, u32[]{:S(2)}, u32[]{:S(2)}) collective-permute-start(bf16[40,2560]{1,0:T(8,128)(2,1)} %get-tuple-element.43), channel_id=1, source_target_pairs={{0,8},{4,12},{8,0},{12,4},{1,9},{5,13},{9,1},{13,5},{2,10},{6,14},... | collective-permute-start | bytes 614408 | tf_op jit(solution)/shard_map/ppermute | solution.py:212
  15.9 38.1 %collective-permute-start.4 = (bf16[40,2560]{1,0:T(8,128)(2,1)}, bf16[40,2560]{1,0:T(8,128)(2,1)}, u32[]{:S(2)}, u32[]{:S(2)}) collective-permute-start(bf16[40,2560]{1,0:T(8,128)(2,1)} %get-tuple-element.44), channel_id=1, source_target_pairs={{0,12},{4,0},{8,4},{12,8},{1,13},{5,1},{9,5},{13,9},{2,14},{6,2},{... | collective-permute-start | bytes 614408 | tf_op jit(solution)/shard_map/ppermute | solution.py:212
  30.2 31.9 %collective-permute-start.6 = (bf16[48,10240]{1,0:T(8,128)(2,1)}, bf16[48,10240]{1,0:T(8,128)(2,1)S(1)}, u32[]{:S(2)}, u32[]{:S(2)}) collective-permute-start(bf16[48,10240]{1,0:T(8,128)(2,1)} %collective-permute-done.refs_5_), channel_id=1, source_target_pairs={{4,0},{8,4},{5,1},{9,5},{6,2},{10,6},{7,3},{11,7},{20,16},{24,20},... | collective-permute-start | bytes 2949128 | tf_op jit(solution)/shard_map/ppermute | solution.py:187
  31.5 30.6 %collective-permute-start.7 = (bf16[48,10240]{1,0:T(8,128)(2,1)}, bf16[48,10240]{1,0:T(8,128)(2,1)S(1)}, u32[]{:S(2)}, u32[]{:S(2)}) collective-permute-start(bf16[48,10240]{1,0:T(8,128)(2,1)} %collective-permute-done.1.refs_6_), channel_id=1, source_target_pairs={{4,8},{8,12},{5,9},{9,13},{6,10},{10,14},{7,11},{11,15},{20,24},{2... | collective-permute-start | bytes 2949128 | tf_op jit(solution)/shard_map/ppermute | solution.py:188
  32.2 3.4 %copy-start = (bf16[1,1024,4096]{2,1,0:T(8,128)(2,1)S(1)}, bf16[1,1024,4096]{2,1,0:T(8,128)(2,1)}, u32[]{:S(2)}) copy-start(bf16[1,1024,4096]{2,1,0:T(8,128)(2,1)} %param.13) | copy-start | bytes 25165828
  35.6 1.1 copy-start.2
  36.8 1.0 copy-start.4
  37.8 1.2 %copy-start.6 = (bf16[48,10240]{1,0:T(8,128)(2,1)S(1)}, bf16[48,10240]{1,0:T(8,128)(2,1)}, u32[]{:S(2)}) copy-start(bf16[48,10240]{1,0:T(8,128)(2,1)} %copy-done.5) | copy-start | bytes 2949124
  39.0 15.0 %copy-start.7 = (bf16[40,2560]{1,0:T(8,128)(2,1)S(1)}, bf16[40,2560]{1,0:T(8,128)(2,1)}, u32[]{:S(2)}) copy-start(bf16[40,2560]{1,0:T(8,128)(2,1)} %get-tuple-element.45) | copy-start | bytes 614404
  39.0 24.7 %copy-start.1 = (bf16[1,1024,4096]{2,1,0:T(8,128)(2,1)S(1)}, bf16[1,1024,4096]{2,1,0:T(8,128)(2,1)}, u32[]{:S(2)}) copy-start(bf16[1,1024,4096]{2,1,0:T(8,128)(2,1)} %param.13) | copy-start | bytes 25165828
  39.0 24.7 %copy-start.3 = (f32[1536,1]{1,0:T(8,128)S(1)}, f32[1536,1]{1,0:T(8,128)}, u32[]{:S(2)}) copy-start(f32[1536,1]{1,0:T(8,128)} %copy.22.refs_2_.refs_1_) | copy-start | bytes 18436
  56.9 32.5 %collective-permute-start.5 = (bf16[160,2560]{1,0:T(8,128)(2,1)S(1)}, bf16[160,2560]{1,0:T(8,128)(2,1)S(1)}, u32[]{:S(2)}, u32[]{:S(2)}) collective-permute-start(bf16[160,2560]{1,0:T(8,128)(2,1)S(1)} %constant_dynamic-update-slice_fusion.refs_0_), channel_id=1, source_target_pairs={{0,16},{16,0},{1,17},{17,1},{2,18},{18,2},{3,19},{19,3},{4,20},{20... | collective-permute-start | bytes 2457608 | tf_op jit(solution)/shard_map/ppermute | solution.py:219
  62.2 20.9 %collective-permute-start.8 = (bf16[48,6144]{1,0:T(8,128)(2,1)S(1)}, bf16[48,6144]{1,0:T(8,128)(2,1)S(1)}, u32[]{:S(2)}, u32[]{:S(2)}) collective-permute-start(bf16[48,6144]{1,0:T(8,128)(2,1)S(1)} %slice_select_fusion), channel_id=1, source_target_pairs={{4,0},{8,12},{5,1},{9,13},{6,2},{10,14},{7,3},{11,15},{20,16},{24,... | collective-permute-start | bytes 1769480 | tf_op jit(solution)/shard_map/ppermute | solution.py:198
  83.1 9.7 %collective-permute-start.9 = (bf16[48,4096]{1,0:T(8,128)(2,1)S(1)}, bf16[48,4096]{1,0:T(8,128)(2,1)S(1)}, u32[]{:S(2)}, u32[]{:S(2)}) collective-permute-start(bf16[48,4096]{1,0:T(8,128)(2,1)S(1)} %slice_select_fusion.1), channel_id=1, source_target_pairs={{4,0},{8,12},{5,1},{9,13},{6,2},{10,14},{7,3},{11,15},{20,16},{24,... | collective-permute-start | bytes 1179656 | tf_op jit(solution)/shard_map/ppermute | solution.py:202

commit v18 on v17

--- a/solution.py
+++ b/solution.py
@@ -13,11 +13,6 @@
 MIB = 1024 * 1024
 TILE = 256
 AHEAD = 3
-
-
-def along(value, by):
-    size = lax.axis_size("rows")
-    return lax.ppermute(value, "rows", [(i, i + by) for i in range(size) if 0 <= i + by < size])
 
 
 def rotate(bases, eigens, queries, begins, load=False):
@@ -143,7 +138,7 @@
                         )
                     owner_part = lax.rem(part + parts - j, parts)
                     for place, offset in enumerate(block_offsets):
-                        shard = lax.rem(row + offset, rows) if base is None else jnp.where(row == 0, rows - 1, 0)
+                        shard = lax.bitwise_xor(row, offset)
                         for owner in range(rows):
                             packed = []
                             for gram in sides:
@@ -178,28 +173,27 @@
     row = lax.axis_index("rows")
     depth = bases[0].shape[1]
     eigens = [eigen.reshape(-1, 1) for eigen in eigens]
-    after = lax.ppermute(query, "rows", [(1, 0), (2, 1), (3, 2)])
-    before = lax.ppermute(query, "rows", [(0, 1), (1, 2), (2, 3)])
+    across, outwards = [(1, 2), (2, 1)], [(1, 0), (2, 3)]
+    beside = lax.ppermute(query, "rows", [(0, 1), (1, 0), (2, 3), (3, 2)])
+    opposite = lax.ppermute(query, "rows", across)
     sent = [lax.dynamic_index_in_dim(by_owner, (row + k) % 4, 0, False) for k in range(4)]
     query, sent = lax.optimization_barrier((query, sent))
     blocks = to_owners(sent)
-    query, after, before = lax.optimization_barrier((query, after, before))
-    after_two = lax.ppermute(after, "rows", [(1, 0), (2, 1)])
-    before_two = lax.ppermute(before, "rows", [(1, 2), (2, 3)])
-    *near, hidden_here = rotate(bases, eigens, [query, after, before], (0, depth), load=True)
+    query, beside = lax.optimization_barrier((query, beside))
+    two_across = lax.ppermute(beside, "rows", across)
+    query, beside, opposite = lax.optimization_barrier((query, beside, opposite))
+    two_outwards = lax.ppermute(opposite, "rows", outwards)
+    *near, hidden_here = rotate(bases, eigens, [query, beside, opposite], (0, depth), load=True)
     bases = [hidden_here, bases[1]]
     near, blocks = lax.optimization_barrier((near, blocks))
     stores = to_parts(jnp.concatenate(blocks, axis=0))
-    near, after_two, before_two = lax.optimization_barrier((near, after_two, before_two))
-    two_hidden, two_model = (
-        jnp.where(row < 2, after_two[:, side], before_two[:, side]) for side in (slice(0, depth), slice(depth, None))
-    )
-    ends = [(1, 0), (2, 3)]
-    three_hidden = lax.ppermute(two_hidden, "rows", ends)
-    far = rotate(bases, eigens, [(after_two, before_two)], (0, depth))
+    near, two_across = lax.optimization_barrier((near, two_across))
+    two_model = two_across[:, depth:]
+    three_hidden = lax.ppermute(two_across[:, :depth], "rows", outwards)
+    far = rotate(bases, eigens, [(two_across, two_outwards)], (0, depth))
     far, three_hidden, two_model = lax.optimization_barrier((far, three_hidden, two_model))
     base = grams(stores, [near, far], [(0, 1, 3), (2,)])
-    three_model = lax.ppermute(two_model, "rows", ends)
+    three_model = lax.ppermute(two_model, "rows", outwards)
     last_hidden = rotate(bases[:1], eigens[:1], [three_hidden], (0,))
     base, last_hidden, three_model = lax.optimization_barrier((base, last_hidden, three_model))
     last_model = rotate(bases[1:], eigens[1:], [three_model], (0,))

time: 114 us -> 113 us (level)
  waiting for transfers between devices: 22.3 us -> 30.1 us
  starting transfers between devices: 23.7 us -> 17.7 us
  blocking collectives: 16.8 us -> 14.4 us
    ppermute x6, waiting for transfers between devices: 22.3 us -> 30.1 us  [the longest x1 11.5 us: along_four(): three_hidden = lax.ppermute(two_across[:, :depth], 'rows', outwards)]
    ppermute x6, starting transfers between devices: 12.6 us -> 9.45 us  [the longest x1 3.09 us: along_four(): beside = lax.ppermute(query, 'rows', [(0, 1), (1, 0), (2, 3), (3, 2)])]
    ppermute x1, starting transfers between devices: 5.19 us -> 2.33 us  [to_parts(): lax.ppermute(store, 'parts', [(i, (i + j) % parts) for i in range(parts)])]
    all_to_all x1, blocking collectives: 16.8 us -> 14.4 us  [per_device(): lax.all_to_all(partial.reshape((parts * rows * layers,) + partial.shape[3...]
where the time goes in v18:
time: 113 us
  Pallas kernels  32.4 us (29%)
  waiting for transfers between devices  30.1 us (27%)
  starting transfers between devices  17.7 us (16%)
  local copies, waits for them, and re-layouts  16.2 us (14%)
  blocking collectives  14.4 us (13%)
  other arithmetic  1.69 us (1%)
    pallas_call x4, Pallas kernels, rotate(): pl.pallas_call(kernel, in_specs=[pl.BlockSpec(memory_space=space) for spa...  29.4 us
    all_to_all x1, blocking collectives, per_device(): lax.all_to_all(partial.reshape((parts * rows * layers,) + partial.shape[3...  14.4 us
    ppermute x1, waiting for transfers between devices, along_four(): three_hidden = lax.ppermute(two_across[:, :depth], 'rows', outwards)  11.5 us
    unnamed x19, local copies, waits for them, and re-layouts  8.67 us
    ppermute x1, waiting for transfers between devices, along_four(): beside = lax.ppermute(query, 'rows', [(0, 1), (1, 0), (2, 3), (3, 2)])  7.83 us
    ppermute x1, waiting for transfers between devices, along_four(): two_outwards = lax.ppermute(opposite, 'rows', outwards)  6.95 us
    ppermute x3, starting transfers between devices, to_owners(): lax.ppermute(sent[k], 'rows', [(i, (i + k) % rows) for i in range(rows)])  5.88 us
    ppermute x1, waiting for transfers between devices, along_four(): three_model = lax.ppermute(two_model, 'rows', outwards)  3.81 us
  transfers between devices with their start and end apart: 10, of which 4 were waited for; matrix products, arithmetic and copies ran while one was open for 9% of the time, Pallas kernels for 25%

profile of v18, /device:TPU:0, one launch (start us, length us, event | category | flops | bytes accessed | tf_op | source)
XLA Modules:
  0.0 112.7 jit_solution(7372730248921408022)
XLA Ops:
  0.0 1.2 %shard_map.82.refs_4_ = bf16[48,10240]{1,0:T(8,128)(2,1)S(1)} custom-call(bf16[96,6144]{1,0:T(8,128)(2,1)} %bitcast.34, bf16[96,4096]{1,0:T(8,128)(2,1)} %bitcast.36), custom_call_target="tpu_custom_call" | custom-call | flops 1 | bytes 1 | tf_op jit(solution)/shard_map/pallas_call | solution.py:99
  1.2 3.1 %collective-permute-start = (bf16[48,10240]{1,0:T(8,128)(2,1)S(1)}, bf16[48,10240]{1,0:T(8,128)(2,1)}, u32[]{:S(2)}, u32[]{:S(2)}) collective-permute-start(bf16[48,10240]{1,0:T(8,128)(2,1)S(1)} %shard_map.82.refs_4_), channel_id=1, source_target_pairs={{0,4},{4,0},{8,12},{12,8},{1,5},{5,1},{9,13},{13,9},{2,6},{6,2},{1... | collective-permute-start | bytes 2949128 | tf_op jit(solution)/shard_map/ppermute | solution.py:177
  4.3 1.6 %collective-permute-start.1 = (bf16[48,10240]{1,0:T(8,128)(2,1)S(1)}, bf16[48,10240]{1,0:T(8,128)(2,1)}, u32[]{:S(2)}, u32[]{:S(2)}) collective-permute-start(bf16[48,10240]{1,0:T(8,128)(2,1)S(1)} %shard_map.82.refs_4_), channel_id=1, source_target_pairs={{4,8},{8,4},{5,9},{9,5},{6,10},{10,6},{7,11},{11,7},{20,24},{24,20... | collective-permute-start | bytes 2949128 | tf_op jit(solution)/shard_map/ppermute | solution.py:178
  5.9 1.4 %reshape_squeeze.6 = bf16[40,4,1536]{2,1,0:T(4,128)(2,1)S(1)} reshape(bf16[1,40,6144]{2,1,0:T(8,128)(2,1)} %param.10) | data formatting | bytes 983040 | tf_op jit(solution)/shard_map/reshape;squeeze | solution.py:242
  7.4 1.2 %reshape_squeeze.7 = bf16[40,4,1024]{2,1,0:T(4,128)(2,1)S(1)} reshape(bf16[1,40,4096]{2,1,0:T(8,128)(2,1)} %param.11) | data formatting | bytes 655360 | tf_op jit(solution)/shard_map/reshape;squeeze | solution.py:242
  9.7 3.5 %collective-permute-start.2 = (bf16[40,2560]{1,0:T(8,128)(2,1)}, bf16[40,2560]{1,0:T(8,128)(2,1)}, u32[]{:S(2)}, u32[]{:S(2)}) collective-permute-start(bf16[40,2560]{1,0:T(8,128)(2,1)} %get-tuple-element.45), channel_id=1, source_target_pairs={{0,4},{4,8},{8,12},{12,0},{1,5},{5,9},{9,13},{13,1},{2,6},{6,10},{... | collective-permute-start | bytes 614408 | tf_op jit(solution)/shard_map/ppermute | solution.py:206
  13.2 2.4 %collective-permute-start.4 = (bf16[40,2560]{1,0:T(8,128)(2,1)}, bf16[40,2560]{1,0:T(8,128)(2,1)}, u32[]{:S(2)}, u32[]{:S(2)}) collective-permute-start(bf16[40,2560]{1,0:T(8,128)(2,1)} %get-tuple-element.47), channel_id=1, source_target_pairs={{0,12},{4,0},{8,4},{12,8},{1,13},{5,1},{9,5},{13,9},{2,14},{6,2},{... | collective-permute-start | bytes 614408 | tf_op jit(solution)/shard_map/ppermute | solution.py:206
  15.6 1.9 %copy.22.refs_2_.refs_1_ = f32[1536,1]{1,0:T(8,128)} copy(f32[1536,1]{0,1:T(1,128)} %bitcast.39) | data formatting | bytes 12288 | tf_op jit(solution)/shard_map/reshape | solution.py:175
  17.4 1.7 %copy.23.refs_3_.refs_1_ = f32[1024,1]{1,0:T(8,128)} copy(f32[1024,1]{0,1:T(1,128)} %bitcast.40) | data formatting | bytes 8192 | tf_op jit(solution)/shard_map/reshape | solution.py:175
  19.2 7.8 %collective-permute-done.refs_5_ = bf16[48,10240]{1,0:T(8,128)(2,1)} collective-permute-done((bf16[48,10240]{1,0:T(8,128)(2,1)S(1)}, bf16[48,10240]{1,0:T(8,128)(2,1)}, u32[]{:S(2)}, u32[]{:S(2)}) %collective-permute-start) | collective-permute-done | bytes 983072 | tf_op jit(solution)/shard_map/ppermute | solution.py:177
  27.7 1.3 %collective-permute-start.7 = (bf16[48,10240]{1,0:T(8,128)(2,1)}, bf16[48,10240]{1,0:T(8,128)(2,1)S(1)}, u32[]{:S(2)}, u32[]{:S(2)}) collective-permute-start(bf16[48,10240]{1,0:T(8,128)(2,1)} %collective-permute-done.1.refs_6_), channel_id=1, source_target_pairs={{4,0},{8,12},{5,1},{9,13},{6,2},{10,14},{7,3},{11,15},{20,16},{24,... | collective-permute-start | bytes 2949128 | tf_op jit(solution)/shard_map/ppermute | solution.py:185
  29.0 3.4 %copy-done = bf16[1,1024,4096]{2,1,0:T(8,128)(2,1)S(1)} copy-done((bf16[1,1024,4096]{2,1,0:T(8,128)(2,1)S(1)}, bf16[1,1024,4096]{2,1,0:T(8,128)(2,1)}, u32[]{:S(2)}) %copy-start) | copy-done | bytes 8388632
  34.6 1.2 %copy-done.6 = bf16[48,10240]{1,0:T(8,128)(2,1)S(1)} copy-done((bf16[48,10240]{1,0:T(8,128)(2,1)S(1)}, bf16[48,10240]{1,0:T(8,128)(2,1)}, u32[]{:S(2)}) %copy-start.6) | copy-done | bytes 983064
  35.8 14.9 %shard_map.83 = (bf16[1536,144]{1,0:T(8,128)(2,1)S(1)}, bf16[1024,144]{1,0:T(8,128)(2,1)S(1)}, bf16[1536,6144]{1,0:T(8,128)(2,1)S(1)}) custom-call(bf16[1536,6144]{1,0:T(8,128)(2,1)} %bitcast.31, bf16[1024,4096]{1,0:T(8,128)(2,1)S(1)} %bitcast.27, f32[1536,1]{1,0:T(8,128)S(1)} %copy-done.2, f32[1024,1]{1,0:T(8,128)S(1)} %copy-done.4, ...), custom_call_target="tpu_custom_call" | custom-call | flops 1 | bytes 1 | tf_op jit(solution)/shard_map/pallas_call | solution.py:67
  52.8 1.5 %collective-permute-start.8 = (bf16[48,6144]{1,0:T(8,128)(2,1)S(1)}, bf16[48,6144]{1,0:T(8,128)(2,1)S(1)}, u32[]{:S(2)}, u32[]{:S(2)}) collective-permute-start(bf16[48,6144]{1,0:T(8,128)(2,1)S(1)} %slice.15), channel_id=1, source_target_pairs={{4,0},{8,12},{5,1},{9,13},{6,2},{10,14},{7,3},{11,15},{20,16},{24,... | collective-permute-start | bytes 1769480 | tf_op jit(solution)/shard_map/ppermute | solution.py:192
  55.2 2.3 %collective-permute-start.5 = (bf16[160,2560]{1,0:T(8,128)(2,1)S(1)}, bf16[160,2560]{1,0:T(8,128)(2,1)S(1)}, u32[]{:S(2)}, u32[]{:S(2)}) collective-permute-start(bf16[160,2560]{1,0:T(8,128)(2,1)S(1)} %constant_dynamic-update-slice_fusion.refs_0_), channel_id=1, source_target_pairs={{0,16},{16,0},{1,17},{17,1},{2,18},{18,2},{3,19},{19,3},{4,20},{20... | collective-permute-start | bytes 2457608 | tf_op jit(solution)/shard_map/ppermute | solution.py:213
  57.5 7.0 %collective-permute-done.7.refs_5_ = bf16[48,10240]{1,0:T(8,128)(2,1)S(1)} collective-permute-done((bf16[48,10240]{1,0:T(8,128)(2,1)}, bf16[48,10240]{1,0:T(8,128)(2,1)S(1)}, u32[]{:S(2)}, u32[]{:S(2)}) %collective-permute-start.7) | collective-permute-done | bytes 983072 | tf_op jit(solution)/shard_map/ppermute | solution.py:185
  64.5 7.2 %shard_map.84 = (bf16[1536,48]{1,0:T(8,128)(2,1)S(1)}, bf16[1024,48]{1,0:T(8,128)(2,1)S(1)}) custom-call(bf16[1536,6144]{1,0:T(8,128)(2,1)S(1)} %get-tuple-element.56.refs_0_, bf16[1024,4096]{1,0:T(8,128)(2,1)S(1)} %bitcast.28, f32[1536,1]{1,0:T(8,128)S(1)} %copy-done.3, f32[1024,1]{1,0:T(8,128)S(1)} %copy-done.4, ...), custom_call_target="tpu_custom_call" | custom-call | flops 1 | bytes 1 | tf_op jit(solution)/shard_map/pallas_call | solution.py:67
  71.7 11.5 %collective-permute-done.8.refs_2_ = bf16[48,6144]{1,0:T(8,128)(2,1)S(1)} collective-permute-done((bf16[48,6144]{1,0:T(8,128)(2,1)S(1)}, bf16[48,6144]{1,0:T(8,128)(2,1)S(1)}, u32[]{:S(2)}, u32[]{:S(2)}) %collective-permute-start.8) | collective-permute-done | bytes 589856 | tf_op jit(solution)/shard_map/ppermute | solution.py:192
  83.2 1.3 %collective-permute-start.9 = (bf16[48,4096]{1,0:T(8,128)(2,1)S(1)}, bf16[48,4096]{1,0:T(8,128)(2,1)S(1)}, u32[]{:S(2)}, u32[]{:S(2)}) collective-permute-start(bf16[48,4096]{1,0:T(8,128)(2,1)S(1)} %slice.16), channel_id=1, source_target_pairs={{4,0},{8,12},{5,1},{9,13},{6,2},{10,14},{7,3},{11,15},{20,16},{24,... | collective-permute-start | bytes 1179656 | tf_op jit(solution)/shard_map/ppermute | solution.py:196
  84.5 5.0 %shard_map.86.refs_2_ = bf16[1536,48]{1,0:T(8,128)(2,1)S(1)} custom-call(bf16[1536,6144]{1,0:T(8,128)(2,1)S(1)} %get-tuple-element.56.refs_0_, f32[1536,1]{1,0:T(8,128)S(1)} %copy-done.3, bf16[48,6144]{1,0:T(8,128)(2,1)S(1)} %collective-permute-done.8.refs_2_), custom_call_target="tpu_custom_call" | custom-call | flops 1 | bytes 1 | tf_op jit(solution)/shard_map/pallas_call | solution.py:67
  90.6 3.8 %collective-permute-done.9.refs_2_ = bf16[48,4096]{1,0:T(8,128)(2,1)S(1)} collective-permute-done((bf16[48,4096]{1,0:T(8,128)(2,1)S(1)}, bf16[48,4096]{1,0:T(8,128)(2,1)S(1)}, u32[]{:S(2)}, u32[]{:S(2)}) %collective-permute-start.9) | collective-permute-done | bytes 393248 | tf_op jit(solution)/shard_map/ppermute | solution.py:196
  94.4 2.3 %shard_map.87.refs_3_ = bf16[1024,48]{1,0:T(8,128)(2,1)S(1)} custom-call(bf16[1024,4096]{1,0:T(8,128)(2,1)S(1)} %bitcast.29, f32[1024,1]{1,0:T(8,128)S(1)} %copy-done.4, bf16[48,4096]{1,0:T(8,128)(2,1)S(1)} %collective-permute-done.9.refs_2_), custom_call_target="tpu_custom_call" | custom-call | flops 1 | bytes 1 | tf_op jit(solution)/shard_map/pallas_call | solution.py:67
  97.4 14.4 %all_to_all.5 = bf16[32,16,256]{2,1,0:T(8,128)(2,1)S(1)} all-to-all(bf16[32,16,256]{2,1,0:T(8,128)(2,1)S(1)} %bitcast.30), channel_id=1, replica_groups=mesh['parts'=2,'rows'=4,'layer'=4] {'parts','rows','layer'}, dimensions={0} | all-to-all | bytes 524288 | tf_op jit(solution)/shard_map/all_to_all | solution.py:266
  (39 shorter events, 9.7 us)
Async XLA Ops:
  1.2 27.8 %copy-start.5 = (bf16[48,10240]{1,0:T(8,128)(2,1)}, bf16[48,10240]{1,0:T(8,128)(2,1)S(1)}, u32[]{:S(2)}) copy-start(bf16[48,10240]{1,0:T(8,128)(2,1)S(1)} %shard_map.82.refs_4_) | copy-start | bytes 2949124
  1.2 25.8 %collective-permute-start = (bf16[48,10240]{1,0:T(8,128)(2,1)S(1)}, bf16[48,10240]{1,0:T(8,128)(2,1)}, u32[]{:S(2)}, u32[]{:S(2)}) collective-permute-start(bf16[48,10240]{1,0:T(8,128)(2,1)S(1)} %shard_map.82.refs_4_), channel_id=1, source_target_pairs={{0,4},{4,0},{8,12},{12,8},{1,5},{5,1},{9,13},{13,9},{2,6},{6,2},{1... | collective-permute-start | bytes 2949128 | tf_op jit(solution)/shard_map/ppermute | solution.py:177
  4.3 23.4 %collective-permute-start.1 = (bf16[48,10240]{1,0:T(8,128)(2,1)S(1)}, bf16[48,10240]{1,0:T(8,128)(2,1)}, u32[]{:S(2)}, u32[]{:S(2)}) collective-permute-start(bf16[48,10240]{1,0:T(8,128)(2,1)S(1)} %shard_map.82.refs_4_), channel_id=1, source_target_pairs={{4,8},{8,4},{5,9},{9,5},{6,10},{10,6},{7,11},{11,7},{20,24},{24,20... | collective-permute-start | bytes 2949128 | tf_op jit(solution)/shard_map/ppermute | solution.py:178
  9.7 41.1 %collective-permute-start.2 = (bf16[40,2560]{1,0:T(8,128)(2,1)}, bf16[40,2560]{1,0:T(8,128)(2,1)}, u32[]{:S(2)}, u32[]{:S(2)}) collective-permute-start(bf16[40,2560]{1,0:T(8,128)(2,1)} %get-tuple-element.45), channel_id=1, source_target_pairs={{0,4},{4,8},{8,12},{12,0},{1,5},{5,9},{9,13},{13,1},{2,6},{6,10},{... | collective-permute-start | bytes 614408 | tf_op jit(solution)/shard_map/ppermute | solution.py:206
  13.2 37.6 %collective-permute-start.3 = (bf16[40,2560]{1,0:T(8,128)(2,1)}, bf16[40,2560]{1,0:T(8,128)(2,1)}, u32[]{:S(2)}, u32[]{:S(2)}) collective-permute-start(bf16[40,2560]{1,0:T(8,128)(2,1)} %get-tuple-element.46), channel_id=1, source_target_pairs={{0,8},{4,12},{8,0},{12,4},{1,9},{5,13},{9,1},{13,5},{2,10},{6,14},... | collective-permute-start | bytes 614408 | tf_op jit(solution)/shard_map/ppermute | solution.py:206
  13.2 37.6 %collective-permute-start.4 = (bf16[40,2560]{1,0:T(8,128)(2,1)}, bf16[40,2560]{1,0:T(8,128)(2,1)}, u32[]{:S(2)}, u32[]{:S(2)}) collective-permute-start(bf16[40,2560]{1,0:T(8,128)(2,1)} %get-tuple-element.47), channel_id=1, source_target_pairs={{0,12},{4,0},{8,4},{12,8},{1,13},{5,1},{9,5},{13,9},{2,14},{6,2},{... | collective-permute-start | bytes 614408 | tf_op jit(solution)/shard_map/ppermute | solution.py:206
  27.0 25.7 %collective-permute-start.6 = (bf16[48,10240]{1,0:T(8,128)(2,1)}, bf16[48,10240]{1,0:T(8,128)(2,1)S(1)}, u32[]{:S(2)}, u32[]{:S(2)}) collective-permute-start(bf16[48,10240]{1,0:T(8,128)(2,1)} %collective-permute-done.refs_5_), channel_id=1, source_target_pairs={{4,8},{8,4},{5,9},{9,5},{6,10},{10,6},{7,11},{11,7},{20,24},{24,20... | collective-permute-start | bytes 2949128 | tf_op jit(solution)/shard_map/ppermute | solution.py:183
  27.7 36.8 %collective-permute-start.7 = (bf16[48,10240]{1,0:T(8,128)(2,1)}, bf16[48,10240]{1,0:T(8,128)(2,1)S(1)}, u32[]{:S(2)}, u32[]{:S(2)}) collective-permute-start(bf16[48,10240]{1,0:T(8,128)(2,1)} %collective-permute-done.1.refs_6_), channel_id=1, source_target_pairs={{4,0},{8,12},{5,1},{9,13},{6,2},{10,14},{7,3},{11,15},{20,16},{24,... | collective-permute-start | bytes 2949128 | tf_op jit(solution)/shard_map/ppermute | solution.py:185
  29.0 3.4 %copy-start = (bf16[1,1024,4096]{2,1,0:T(8,128)(2,1)S(1)}, bf16[1,1024,4096]{2,1,0:T(8,128)(2,1)}, u32[]{:S(2)}) copy-start(bf16[1,1024,4096]{2,1,0:T(8,128)(2,1)} %param.13) | copy-start | bytes 25165828
  32.4 1.1 %copy-start.2 = (f32[1536,1]{1,0:T(8,128)S(1)}, f32[1536,1]{1,0:T(8,128)}, u32[]{:S(2)}) copy-start(f32[1536,1]{1,0:T(8,128)} %copy.22.refs_2_.refs_1_) | copy-start | bytes 18436
  33.5 1.0 copy-start.4
  34.6 1.2 %copy-start.6 = (bf16[48,10240]{1,0:T(8,128)(2,1)S(1)}, bf16[48,10240]{1,0:T(8,128)(2,1)}, u32[]{:S(2)}) copy-start(bf16[48,10240]{1,0:T(8,128)(2,1)} %copy-done.5) | copy-start | bytes 2949124
  35.8 15.0 %copy-start.7 = (bf16[40,2560]{1,0:T(8,128)(2,1)S(1)}, bf16[40,2560]{1,0:T(8,128)(2,1)}, u32[]{:S(2)}) copy-start(bf16[40,2560]{1,0:T(8,128)(2,1)} %get-tuple-element.48) | copy-start | bytes 614404
  35.8 28.7 %copy-start.1 = (bf16[1,1024,4096]{2,1,0:T(8,128)(2,1)S(1)}, bf16[1,1024,4096]{2,1,0:T(8,128)(2,1)}, u32[]{:S(2)}) copy-start(bf16[1,1024,4096]{2,1,0:T(8,128)(2,1)} %param.13) | copy-start | bytes 25165828
  35.8 28.7 %copy-start.3 = (f32[1536,1]{1,0:T(8,128)S(1)}, f32[1536,1]{1,0:T(8,128)}, u32[]{:S(2)}) copy-start(f32[1536,1]{1,0:T(8,128)} %copy.22.refs_2_.refs_1_) | copy-start | bytes 18436
  52.8 30.5 %collective-permute-start.8 = (bf16[48,6144]{1,0:T(8,128)(2,1)S(1)}, bf16[48,6144]{1,0:T(8,128)(2,1)S(1)}, u32[]{:S(2)}, u32[]{:S(2)}) collective-permute-start(bf16[48,6144]{1,0:T(8,128)(2,1)S(1)} %slice.15), channel_id=1, source_target_pairs={{4,0},{8,12},{5,1},{9,13},{6,2},{10,14},{7,3},{11,15},{20,16},{24,... | collective-permute-start | bytes 1769480 | tf_op jit(solution)/shard_map/ppermute | solution.py:192
  55.2 34.3 %collective-permute-start.5 = (bf16[160,2560]{1,0:T(8,128)(2,1)S(1)}, bf16[160,2560]{1,0:T(8,128)(2,1)S(1)}, u32[]{:S(2)}, u32[]{:S(2)}) collective-permute-start(bf16[160,2560]{1,0:T(8,128)(2,1)S(1)} %constant_dynamic-update-slice_fusion.refs_0_), channel_id=1, source_target_pairs={{0,16},{16,0},{1,17},{17,1},{2,18},{18,2},{3,19},{19,3},{4,20},{20... | collective-permute-start | bytes 2457608 | tf_op jit(solution)/shard_map/ppermute | solution.py:213
  83.2 11.2 %collective-permute-start.9 = (bf16[48,4096]{1,0:T(8,128)(2,1)S(1)}, bf16[48,4096]{1,0:T(8,128)(2,1)S(1)}, u32[]{:S(2)}, u32[]{:S(2)}) collective-permute-start(bf16[48,4096]{1,0:T(8,128)(2,1)S(1)} %slice.16), channel_id=1, source_target_pairs={{4,0},{8,12},{5,1},{9,13},{6,2},{10,14},{7,3},{11,15},{20,16},{24,... | collective-permute-start | bytes 1179656 | tf_op jit(solution)/shard_map/ppermute | solution.py:196

commit v19 on v18

--- a/solution.py
+++ b/solution.py
@@ -116,7 +116,7 @@
     shares = [side.shape[0] for side in blocks[0]]
     columns = blocks[0][0].shape[1] // len(offsets[0])
     count = len(stores)
-    held = stores[0].shape[0] // rows
+    held = stores[0][0].shape[0] // len(stores[0][2])
     examples = held // RANK
     width = packed_width(examples, columns)
 
@@ -129,7 +129,7 @@
 
         def write():
             for at, block_offsets in enumerate(offsets):
-                for j, store_ref in enumerate(store_refs):
+                for (_, j, ks), store_ref in zip(stores, store_refs):
                     sides = []
                     for side, begin in enumerate((0, shares[0])):
                         store = store_ref[:, begin : begin + shares[side]]
@@ -139,12 +139,12 @@
                     owner_part = lax.rem(part + parts - j, parts)
                     for place, offset in enumerate(block_offsets):
                         shard = lax.bitwise_xor(row, offset)
-                        for owner in range(rows):
+                        for place_of, k in enumerate(ks):
                             packed = []
                             for gram in sides:
                                 pieces = [
                                     gram[
-                                        owner * held + i * RANK : owner * held + (i + 1) * RANK,
+                                        place_of * held + i * RANK : place_of * held + (i + 1) * RANK,
                                         place * columns : (place + 1) * columns,
                                     ]
                                     for i in range(examples)
@@ -153,14 +153,14 @@
                                 if fill:
                                     pieces.append(jnp.zeros((RANK, fill), jnp.float32))
                                 packed.append(jnp.concatenate(pieces, axis=1))
-                            out_ref[owner_part, lax.rem(row + rows - owner, rows), shard] = jnp.concatenate(packed, axis=0).astype(jnp.bfloat16)
+                            out_ref[owner_part, lax.rem(row + rows - k, rows), shard] = jnp.concatenate(packed, axis=0).astype(jnp.bfloat16)
 
         if base is None:
             write()
         else:
             pl.when(jnp.logical_or(row == 0, row == rows - 1))(write)
 
-    operands = [*stores, *[side for block in blocks for side in block]]
+    operands = [*[store for store, _, _ in stores], *[side for block in blocks for side in block]]
     return pl.pallas_call(
         kernel,
         out_shape=jax.ShapeDtypeStruct((parts, rows, rows, 2 * RANK, width), jnp.bfloat16),
@@ -178,7 +178,7 @@
     opposite = lax.ppermute(query, "rows", across)
     sent = [lax.dynamic_index_in_dim(by_owner, (row + k) % 4, 0, False) for k in range(4)]
     query, sent = lax.optimization_barrier((query, sent))
-    blocks = to_owners(sent)
+    blocks = [sent[0], further(sent[1], 1), further(sent[3], 3)]
     query, beside = lax.optimization_barrier((query, beside))
     two_across = lax.ppermute(beside, "rows", across)
     query, beside, opposite = lax.optimization_barrier((query, beside, opposite))
@@ -186,11 +186,14 @@
     *near, hidden_here = rotate(bases, eigens, [query, beside, opposite], (0, depth), load=True)
     bases = [hidden_here, bases[1]]
     near, blocks = lax.optimization_barrier((near, blocks))
-    stores = to_parts(jnp.concatenate(blocks, axis=0))
-    near, two_across = lax.optimization_barrier((near, two_across))
+    stores = [(store, j, (0, 1, 3)) for j, store in enumerate(to_parts(jnp.concatenate(blocks, axis=0)))]
+    near, two_across, late = lax.optimization_barrier((near, two_across, sent[2]))
     two_model = two_across[:, depth:]
     three_hidden = lax.ppermute(two_across[:, :depth], "rows", outwards)
+    late = further(late, 2)
     far = rotate(bases, eigens, [(two_across, two_outwards)], (0, depth))
+    far, late = lax.optimization_barrier((far, late))
+    stores += [(store, j, (2,)) for j, store in enumerate(to_parts(late))]
     far, three_hidden, two_model = lax.optimization_barrier((far, three_hidden, two_model))
     base = grams(stores, [near, far], [(0, 1, 3), (2,)])
     three_model = lax.ppermute(two_model, "rows", outwards)
@@ -200,11 +203,9 @@
     return grams(stores, [last_hidden + last_model], [(3,)], base)
 
 
-def to_owners(sent):
+def further(block, k):
     rows = lax.axis_size("rows")
-    return sent[:1] + [
-        lax.ppermute(sent[k], "rows", [(i, (i + k) % rows) for i in range(rows)]) for k in range(1, rows)
-    ]
+    return lax.ppermute(block, "rows", [(i, (i + k) % rows) for i in range(rows)])
 
 
 def to_parts(store):

time: 113 us -> 110 us (0.973)
  waiting for transfers between devices: 30.1 us -> 21.4 us
  starting transfers between devices: 17.7 us -> 21.7 us
  Pallas kernels: 32.4 us -> 34.2 us
  blocking collectives: 14.4 us -> 13.1 us
    ppermute x1, waiting for transfers between devices: 7.83 us -> 16.5 us  [along_four(): beside = lax.ppermute(query, 'rows', [(0, 1), (1, 0), (2, 3), (3, 2)])]
    ppermute x1, waiting for transfers between devices: 11.5 us -> 2.98 us  [along_four(): three_hidden = lax.ppermute(two_across[:, :depth], 'rows', outwards)]
    ppermute x1, waiting for transfers between devices: 6.95 us -> 0.01 us  [along_four(): two_outwards = lax.ppermute(opposite, 'rows', outwards)]
    ppermute x3, starting transfers between devices: 5.88 us -> 7.91 us  [further(): lax.ppermute(block, 'rows', [(i, (i + k) % rows) for i in range(rows)])]
    ppermute x1, waiting for transfers between devices: 3.81 us -> 1.96 us  [along_four(): three_model = lax.ppermute(two_model, 'rows', outwards)]
    all_to_all x1, blocking collectives: 14.4 us -> 13.1 us  [per_device(): lax.all_to_all(partial.reshape((parts * rows * layers,) + partial.shape[3...]
    pallas_call x4, Pallas kernels: 29.4 us -> 30.6 us  [rotate(): pl.pallas_call(kernel, in_specs=[pl.BlockSpec(memory_space=space) for spa...]
    ppermute x1 -> x2, starting transfers between devices: 2.33 us -> 3.42 us  [to_parts(): lax.ppermute(store, 'parts', [(i, (i + j) % parts) for i in range(parts)])]
  transfers between devices with their start and end apart: 10 -> 11, of which waited for: 4 -> 3; matrix products, arithmetic and copies ran while one was open for 9% -> 10% of each run, Pallas kernels for 25% -> 27%
where the time goes in v19:
time: 110 us
  Pallas kernels  34.2 us (31%)
  starting transfers between devices  21.7 us (20%)
  waiting for transfers between devices  21.4 us (19%)
  local copies, waits for them, and re-layouts  17.3 us (16%)
  blocking collectives  13.1 us (12%)
  other arithmetic  1.71 us (2%)
    pallas_call x4, Pallas kernels, rotate(): pl.pallas_call(kernel, in_specs=[pl.BlockSpec(memory_space=space) for spa...  30.6 us
    ppermute x1, waiting for transfers between devices, along_four(): beside = lax.ppermute(query, 'rows', [(0, 1), (1, 0), (2, 3), (3, 2)])  16.5 us
    all_to_all x1, blocking collectives, per_device(): lax.all_to_all(partial.reshape((parts * rows * layers,) + partial.shape[3...  13.1 us
    ppermute x3, starting transfers between devices, further(): lax.ppermute(block, 'rows', [(i, (i + k) % rows) for i in range(rows)])  7.91 us
    unnamed x20, local copies, waits for them, and re-layouts  7.73 us
    reshape x2, local copies, waits for them, and re-layouts, along_four(): eigens = [eigen.reshape(-1, 1) for eigen in eigens]  3.58 us
    ppermute x2, starting transfers between devices, to_parts(): lax.ppermute(store, 'parts', [(i, (i + j) % parts) for i in range(parts)])  3.42 us
    ppermute x1, starting transfers between devices, along_four(): beside = lax.ppermute(query, 'rows', [(0, 1), (1, 0), (2, 3), (3, 2)])  3.09 us
  transfers between devices with their start and end apart: 11, of which 3 were waited for; matrix products, arithmetic and copies ran while one was open for 10% of the time, Pallas kernels for 27%

profile of v19, /device:TPU:0, one launch (start us, length us, event | category | flops | bytes accessed | tf_op | source)
XLA Modules:
  0.0 109.7 jit_solution(2496298686269518379)
XLA Ops:
  1.2 3.1 %collective-permute-start = (bf16[48,10240]{1,0:T(8,128)(2,1)S(1)}, bf16[48,10240]{1,0:T(8,128)(2,1)}, u32[]{:S(2)}, u32[]{:S(2)}) collective-permute-start(bf16[48,10240]{1,0:T(8,128)(2,1)S(1)} %shard_map.82.refs_4_), channel_id=1, source_target_pairs={{0,4},{4,0},{8,12},{12,8},{1,5},{5,1},{9,13},{13,9},{2,6},{6,2},{1... | collective-permute-start | bytes 2949128 | tf_op jit(solution)/shard_map/ppermute | solution.py:177
  4.3 1.6 %collective-permute-start.1 = (bf16[48,10240]{1,0:T(8,128)(2,1)S(1)}, bf16[48,10240]{1,0:T(8,128)(2,1)}, u32[]{:S(2)}, u32[]{:S(2)}) collective-permute-start(bf16[48,10240]{1,0:T(8,128)(2,1)S(1)} %shard_map.82.refs_4_), channel_id=1, source_target_pairs={{4,8},{8,4},{5,9},{9,5},{6,10},{10,6},{7,11},{11,7},{20,24},{24,20... | collective-permute-start | bytes 2949128 | tf_op jit(solution)/shard_map/ppermute | solution.py:178
  5.9 1.4 %reshape_squeeze.6 = bf16[40,4,1536]{2,1,0:T(4,128)(2,1)S(1)} reshape(bf16[1,40,6144]{2,1,0:T(8,128)(2,1)} %param.10) | data formatting | bytes 983040 | tf_op jit(solution)/shard_map/reshape;squeeze | solution.py:243
  7.4 1.2 %reshape_squeeze.7 = bf16[40,4,1024]{2,1,0:T(4,128)(2,1)S(1)} reshape(bf16[1,40,4096]{2,1,0:T(8,128)(2,1)} %param.11) | data formatting | bytes 655360 | tf_op jit(solution)/shard_map/reshape;squeeze | solution.py:243
  9.7 16.5 %collective-permute-done.refs_5_ = bf16[48,10240]{1,0:T(8,128)(2,1)} collective-permute-done((bf16[48,10240]{1,0:T(8,128)(2,1)S(1)}, bf16[48,10240]{1,0:T(8,128)(2,1)}, u32[]{:S(2)}, u32[]{:S(2)}) %collective-permute-start) | collective-permute-done | bytes 983072 | tf_op jit(solution)/shard_map/ppermute | solution.py:177
  26.2 1.6 %collective-permute-start.5 = (bf16[48,10240]{1,0:T(8,128)(2,1)}, bf16[48,10240]{1,0:T(8,128)(2,1)}, u32[]{:S(2)}, u32[]{:S(2)}) collective-permute-start(bf16[48,10240]{1,0:T(8,128)(2,1)} %collective-permute-done.refs_5_), channel_id=1, source_target_pairs={{4,8},{8,4},{5,9},{9,5},{6,10},{10,6},{7,11},{11,7},{20,24},{24,20... | collective-permute-start | bytes 2949128 | tf_op jit(solution)/shard_map/ppermute | solution.py:183
  27.8 3.6 %collective-permute-start.2 = (bf16[40,2560]{1,0:T(8,128)(2,1)}, bf16[40,2560]{1,0:T(8,128)(2,1)}, u32[]{:S(2)}, u32[]{:S(2)}) collective-permute-start(bf16[40,2560]{1,0:T(8,128)(2,1)} %get-tuple-element.48), channel_id=1, source_target_pairs={{0,4},{4,8},{8,12},{12,0},{1,5},{5,9},{9,13},{13,1},{2,6},{6,10},{... | collective-permute-start | bytes 614408 | tf_op jit(solution)/shard_map/ppermute | solution.py:208
  31.6 1.9 %copy.22.refs_2_.refs_1_ = f32[1536,1]{1,0:T(8,128)} copy(f32[1536,1]{0,1:T(1,128)} %bitcast.39) | data formatting | bytes 12288 | tf_op jit(solution)/shard_map/reshape | solution.py:175
  33.5 1.7 %copy.23.refs_3_.refs_1_ = f32[1024,1]{1,0:T(8,128)} copy(f32[1024,1]{0,1:T(1,128)} %bitcast.40) | data formatting | bytes 8192 | tf_op jit(solution)/shard_map/reshape | solution.py:175
  35.2 1.3 %collective-permute-start.6 = (bf16[48,10240]{1,0:T(8,128)(2,1)}, bf16[48,10240]{1,0:T(8,128)(2,1)S(1)}, u32[]{:S(2)}, u32[]{:S(2)}) collective-permute-start(bf16[48,10240]{1,0:T(8,128)(2,1)} %collective-permute-done.1.refs_6_), channel_id=1, source_target_pairs={{4,0},{8,12},{5,1},{9,13},{6,2},{10,14},{7,3},{11,15},{20,16},{24,... | collective-permute-start | bytes 2949128 | tf_op jit(solution)/shard_map/ppermute | solution.py:185
  36.5 3.4 %copy-done = bf16[1,1024,4096]{2,1,0:T(8,128)(2,1)S(1)} copy-done((bf16[1,1024,4096]{2,1,0:T(8,128)(2,1)S(1)}, bf16[1,1024,4096]{2,1,0:T(8,128)(2,1)}, u32[]{:S(2)}) %copy-start) | copy-done | bytes 8388632
  43.3 15.0 %shard_map.83 = (bf16[1536,144]{1,0:T(8,128)(2,1)S(1)}, bf16[1024,144]{1,0:T(8,128)(2,1)S(1)}, bf16[1536,6144]{1,0:T(8,128)(2,1)S(1)}) custom-call(bf16[1536,6144]{1,0:T(8,128)(2,1)} %bitcast.31, bf16[1024,4096]{1,0:T(8,128)(2,1)S(1)} %bitcast.27, f32[1536,1]{1,0:T(8,128)S(1)} %copy-done.2, f32[1024,1]{1,0:T(8,128)S(1)} %copy-done.4, ...), custom_call_target="tpu_custom_call" | custom-call | flops 1 | bytes 1 | tf_op jit(solution)/shard_map/pallas_call | solution.py:67
  59.4 1.5 %collective-permute-start.9 = (bf16[48,6144]{1,0:T(8,128)(2,1)S(1)}, bf16[48,6144]{1,0:T(8,128)(2,1)S(1)}, u32[]{:S(2)}, u32[]{:S(2)}) collective-permute-start(bf16[48,6144]{1,0:T(8,128)(2,1)S(1)} %slice.15), channel_id=1, source_target_pairs={{4,0},{8,12},{5,1},{9,13},{6,2},{10,14},{7,3},{11,15},{20,16},{24,... | collective-permute-start | bytes 1769480 | tf_op jit(solution)/shard_map/ppermute | solution.py:192
  62.8 1.7 %collective-permute-start.4 = (bf16[120,2560]{1,0:T(8,128)(2,1)S(1)}, bf16[120,2560]{1,0:T(8,128)(2,1)S(1)}, u32[]{:S(2)}, u32[]{:S(2)}) collective-permute-start(bf16[120,2560]{1,0:T(8,128)(2,1)S(1)} %constant_dynamic-update-slice_fusion.refs_0_), channel_id=1, source_target_pairs={{0,16},{16,0},{1,17},{17,1},{2,18},{18,2},{3,19},{19,3},{4,20},{20... | collective-permute-start | bytes 1843208 | tf_op jit(solution)/shard_map/ppermute | solution.py:214
  64.6 4.1 %collective-permute-start.7 = (bf16[40,2560]{1,0:T(8,128)(2,1)S(1)}, bf16[40,2560]{1,0:T(8,128)(2,1)S(1)}, u32[]{:S(2)}, u32[]{:S(2)}) collective-permute-start(bf16[40,2560]{1,0:T(8,128)(2,1)S(1)} %copy-done.8), channel_id=1, source_target_pairs={{0,8},{4,12},{8,0},{12,4},{1,9},{5,13},{9,1},{13,5},{2,10},{6,14},... | collective-permute-start | bytes 614408 | tf_op jit(solution)/shard_map/ppermute | solution.py:208
  68.7 8.4 %shard_map.84 = (bf16[1536,48]{1,0:T(8,128)(2,1)S(1)}, bf16[1024,48]{1,0:T(8,128)(2,1)S(1)}) custom-call(bf16[1536,6144]{1,0:T(8,128)(2,1)S(1)} %get-tuple-element.53.refs_0_, bf16[1024,4096]{1,0:T(8,128)(2,1)S(1)} %bitcast.28, f32[1536,1]{1,0:T(8,128)S(1)} %copy-done.3, f32[1024,1]{1,0:T(8,128)S(1)} %copy-done.4, ...), custom_call_target="tpu_custom_call" | custom-call | flops 1 | bytes 1 | tf_op jit(solution)/shard_map/pallas_call | solution.py:67
  78.1 3.0 %collective-permute-done.9.refs_2_ = bf16[48,6144]{1,0:T(8,128)(2,1)S(1)} collective-permute-done((bf16[48,6144]{1,0:T(8,128)(2,1)S(1)}, bf16[48,6144]{1,0:T(8,128)(2,1)S(1)}, u32[]{:S(2)}, u32[]{:S(2)}) %collective-permute-start.9) | collective-permute-done | bytes 589856 | tf_op jit(solution)/shard_map/ppermute | solution.py:192
  81.0 1.3 %collective-permute-start.10 = (bf16[48,4096]{1,0:T(8,128)(2,1)S(1)}, bf16[48,4096]{1,0:T(8,128)(2,1)S(1)}, u32[]{:S(2)}, u32[]{:S(2)}) collective-permute-start(bf16[48,4096]{1,0:T(8,128)(2,1)S(1)} %slice.16), channel_id=1, source_target_pairs={{4,0},{8,12},{5,1},{9,13},{6,2},{10,14},{7,3},{11,15},{20,16},{24,... | collective-permute-start | bytes 1179656 | tf_op jit(solution)/shard_map/ppermute | solution.py:199
  82.3 1.7 %collective-permute-start.8 = (bf16[40,2560]{1,0:T(8,128)(2,1)S(1)}, bf16[40,2560]{1,0:T(8,128)(2,1)S(1)}, u32[]{:S(2)}, u32[]{:S(2)}) collective-permute-start(bf16[40,2560]{1,0:T(8,128)(2,1)S(1)} %collective-permute-done.7.refs_2_), channel_id=1, source_target_pairs={{0,16},{16,0},{1,17},{17,1},{2,18},{18,2},{3,19},{19,3},{4,20},{20... | collective-permute-start | bytes 614408 | tf_op jit(solution)/shard_map/ppermute | solution.py:214
  84.0 5.0 %shard_map.86.refs_4_ = bf16[1536,48]{1,0:T(8,128)(2,1)S(1)} custom-call(bf16[1536,6144]{1,0:T(8,128)(2,1)S(1)} %get-tuple-element.53.refs_0_, f32[1536,1]{1,0:T(8,128)S(1)} %copy-done.3, bf16[48,6144]{1,0:T(8,128)(2,1)S(1)} %collective-permute-done.9.refs_2_), custom_call_target="tpu_custom_call" | custom-call | flops 1 | bytes 1 | tf_op jit(solution)/shard_map/pallas_call | solution.py:67
  89.0 1.6 %shard_map.85.refs_6_ = bf16[2,4,4,16,256]{4,3,2,1,0:T(8,128)(2,1)S(1)} custom-call(bf16[120,2560]{1,0:T(8,128)(2,1)S(1)} %constant_dynamic-update-slice_fusion.refs_0_, bf16[120,2560]{1,0:T(8,128)(2,1)S(1)} %collective-permute-done.4.refs_1_, bf16[40,2560]{1,0:T(8,128)(2,1)S(1)} %collective-permute-done.7.refs_2_, ...), custom_call_target="tpu_custom_call" | custom-call | flops 1 | bytes 1 | tf_op jit(solution)/shard_map/pallas_call | solution.py:164
  90.6 2.0 %collective-permute-done.10.refs_2_ = bf16[48,4096]{1,0:T(8,128)(2,1)S(1)} collective-permute-done((bf16[48,4096]{1,0:T(8,128)(2,1)S(1)}, bf16[48,4096]{1,0:T(8,128)(2,1)S(1)}, u32[]{:S(2)}, u32[]{:S(2)}) %collective-permute-start.10) | collective-permute-done | bytes 393248 | tf_op jit(solution)/shard_map/ppermute | solution.py:199
  92.6 2.3 %shard_map.87.refs_5_ = bf16[1024,48]{1,0:T(8,128)(2,1)S(1)} custom-call(bf16[1024,4096]{1,0:T(8,128)(2,1)S(1)} %bitcast.29, f32[1024,1]{1,0:T(8,128)S(1)} %copy-done.4, bf16[48,4096]{1,0:T(8,128)(2,1)S(1)} %collective-permute-done.10.refs_2_), custom_call_target="tpu_custom_call" | custom-call | flops 1 | bytes 1 | tf_op jit(solution)/shard_map/pallas_call | solution.py:67
  95.6 13.1 %all_to_all.5 = bf16[32,16,256]{2,1,0:T(8,128)(2,1)S(1)} all-to-all(bf16[32,16,256]{2,1,0:T(8,128)(2,1)S(1)} %bitcast.30), channel_id=1, replica_groups=mesh['parts'=2,'rows'=4,'layer'=4] {'parts','rows','layer'}, dimensions={0} | all-to-all | bytes 524288 | tf_op jit(solution)/shard_map/all_to_all | solution.py:267
  (42 shorter events, 11.7 us)
Async XLA Ops:
  1.2 35.3 %copy-start.5 = (bf16[48,10240]{1,0:T(8,128)(2,1)}, bf16[48,10240]{1,0:T(8,128)(2,1)S(1)}, u32[]{:S(2)}) copy-start(bf16[48,10240]{1,0:T(8,128)(2,1)S(1)} %shard_map.82.refs_4_) | copy-start | bytes 2949124
  1.2 24.9 %collective-permute-start = (bf16[48,10240]{1,0:T(8,128)(2,1)S(1)}, bf16[48,10240]{1,0:T(8,128)(2,1)}, u32[]{:S(2)}, u32[]{:S(2)}) collective-permute-start(bf16[48,10240]{1,0:T(8,128)(2,1)S(1)} %shard_map.82.refs_4_), channel_id=1, source_target_pairs={{0,4},{4,0},{8,12},{12,8},{1,5},{5,1},{9,13},{13,9},{2,6},{6,2},{1... | collective-permute-start | bytes 2949128 | tf_op jit(solution)/shard_map/ppermute | solution.py:177
  4.3 30.9 %collective-permute-start.1 = (bf16[48,10240]{1,0:T(8,128)(2,1)S(1)}, bf16[48,10240]{1,0:T(8,128)(2,1)}, u32[]{:S(2)}, u32[]{:S(2)}) collective-permute-start(bf16[48,10240]{1,0:T(8,128)(2,1)S(1)} %shard_map.82.refs_4_), channel_id=1, source_target_pairs={{4,8},{8,4},{5,9},{9,5},{6,10},{10,6},{7,11},{11,7},{20,24},{24,20... | collective-permute-start | bytes 2949128 | tf_op jit(solution)/shard_map/ppermute | solution.py:178
  26.2 32.2 %collective-permute-start.5 = (bf16[48,10240]{1,0:T(8,128)(2,1)}, bf16[48,10240]{1,0:T(8,128)(2,1)}, u32[]{:S(2)}, u32[]{:S(2)}) collective-permute-start(bf16[48,10240]{1,0:T(8,128)(2,1)} %collective-permute-done.refs_5_), channel_id=1, source_target_pairs={{4,8},{8,4},{5,9},{9,5},{6,10},{10,6},{7,11},{11,7},{20,24},{24,20... | collective-permute-start | bytes 2949128 | tf_op jit(solution)/shard_map/ppermute | solution.py:183
  27.8 30.5 %collective-permute-start.2 = (bf16[40,2560]{1,0:T(8,128)(2,1)}, bf16[40,2560]{1,0:T(8,128)(2,1)}, u32[]{:S(2)}, u32[]{:S(2)}) collective-permute-start(bf16[40,2560]{1,0:T(8,128)(2,1)} %get-tuple-element.48), channel_id=1, source_target_pairs={{0,4},{4,8},{8,12},{12,0},{1,5},{5,9},{9,13},{13,1},{2,6},{6,10},{... | collective-permute-start | bytes 614408 | tf_op jit(solution)/shard_map/ppermute | solution.py:208
  31.4 26.8 %collective-permute-start.3 = (bf16[40,2560]{1,0:T(8,128)(2,1)}, bf16[40,2560]{1,0:T(8,128)(2,1)}, u32[]{:S(2)}, u32[]{:S(2)}) collective-permute-start(bf16[40,2560]{1,0:T(8,128)(2,1)} %get-tuple-element.49), channel_id=1, source_target_pairs={{0,12},{4,0},{8,4},{12,8},{1,13},{5,1},{9,5},{13,9},{2,14},{6,2},{... | collective-permute-start | bytes 614408 | tf_op jit(solution)/shard_map/ppermute | solution.py:208
  35.2 33.4 %collective-permute-start.6 = (bf16[48,10240]{1,0:T(8,128)(2,1)}, bf16[48,10240]{1,0:T(8,128)(2,1)S(1)}, u32[]{:S(2)}, u32[]{:S(2)}) collective-permute-start(bf16[48,10240]{1,0:T(8,128)(2,1)} %collective-permute-done.1.refs_6_), channel_id=1, source_target_pairs={{4,0},{8,12},{5,1},{9,13},{6,2},{10,14},{7,3},{11,15},{20,16},{24,... | collective-permute-start | bytes 2949128 | tf_op jit(solution)/shard_map/ppermute | solution.py:185
  36.5 3.4 %copy-start = (bf16[1,1024,4096]{2,1,0:T(8,128)(2,1)S(1)}, bf16[1,1024,4096]{2,1,0:T(8,128)(2,1)}, u32[]{:S(2)}) copy-start(bf16[1,1024,4096]{2,1,0:T(8,128)(2,1)} %param.13) | copy-start | bytes 25165828
  39.9 1.1 %copy-start.2 = (f32[1536,1]{1,0:T(8,128)S(1)}, f32[1536,1]{1,0:T(8,128)}, u32[]{:S(2)}) copy-start(f32[1536,1]{1,0:T(8,128)} %copy.22.refs_2_.refs_1_) | copy-start | bytes 18436
  41.0 1.0 copy-start.4
  42.1 1.2 %copy-start.6 = (bf16[48,10240]{1,0:T(8,128)(2,1)S(1)}, bf16[48,10240]{1,0:T(8,128)(2,1)}, u32[]{:S(2)}) copy-start(bf16[48,10240]{1,0:T(8,128)(2,1)} %copy-done.5) | copy-start | bytes 2949124
  43.3 15.0 %copy-start.7 = (bf16[40,2560]{1,0:T(8,128)(2,1)S(1)}, bf16[40,2560]{1,0:T(8,128)(2,1)}, u32[]{:S(2)}) copy-start(bf16[40,2560]{1,0:T(8,128)(2,1)} %get-tuple-element.50) | copy-start | bytes 614404
  43.3 21.3 %copy-start.8 = (bf16[40,2560]{1,0:T(8,128)(2,1)S(1)}, bf16[40,2560]{1,0:T(8,128)(2,1)}, u32[]{:S(2)}) copy-start(bf16[40,2560]{1,0:T(8,128)(2,1)} %get-tuple-element.60) | copy-start | bytes 614404
  43.3 25.4 %copy-start.1 = (bf16[1,1024,4096]{2,1,0:T(8,128)(2,1)S(1)}, bf16[1,1024,4096]{2,1,0:T(8,128)(2,1)}, u32[]{:S(2)}) copy-start(bf16[1,1024,4096]{2,1,0:T(8,128)(2,1)} %param.13) | copy-start | bytes 25165828
  43.3 25.4 %copy-start.3 = (f32[1536,1]{1,0:T(8,128)S(1)}, f32[1536,1]{1,0:T(8,128)}, u32[]{:S(2)}) copy-start(f32[1536,1]{1,0:T(8,128)} %copy.22.refs_2_.refs_1_) | copy-start | bytes 18436
  59.4 21.6 %collective-permute-start.9 = (bf16[48,6144]{1,0:T(8,128)(2,1)S(1)}, bf16[48,6144]{1,0:T(8,128)(2,1)S(1)}, u32[]{:S(2)}, u32[]{:S(2)}) collective-permute-start(bf16[48,6144]{1,0:T(8,128)(2,1)S(1)} %slice.15), channel_id=1, source_target_pairs={{4,0},{8,12},{5,1},{9,13},{6,2},{10,14},{7,3},{11,15},{20,16},{24,... | collective-permute-start | bytes 1769480 | tf_op jit(solution)/shard_map/ppermute | solution.py:192
  62.8 26.2 %collective-permute-start.4 = (bf16[120,2560]{1,0:T(8,128)(2,1)S(1)}, bf16[120,2560]{1,0:T(8,128)(2,1)S(1)}, u32[]{:S(2)}, u32[]{:S(2)}) collective-permute-start(bf16[120,2560]{1,0:T(8,128)(2,1)S(1)} %constant_dynamic-update-slice_fusion.refs_0_), channel_id=1, source_target_pairs={{0,16},{16,0},{1,17},{17,1},{2,18},{18,2},{3,19},{19,3},{4,20},{20... | collective-permute-start | bytes 1843208 | tf_op jit(solution)/shard_map/ppermute | solution.py:214
  64.6 13.5 %collective-permute-start.7 = (bf16[40,2560]{1,0:T(8,128)(2,1)S(1)}, bf16[40,2560]{1,0:T(8,128)(2,1)S(1)}, u32[]{:S(2)}, u32[]{:S(2)}) collective-permute-start(bf16[40,2560]{1,0:T(8,128)(2,1)S(1)} %copy-done.8), channel_id=1, source_target_pairs={{0,8},{4,12},{8,0},{12,4},{1,9},{5,13},{9,1},{13,5},{2,10},{6,14},... | collective-permute-start | bytes 614408 | tf_op jit(solution)/shard_map/ppermute | solution.py:208
  81.0 11.5 %collective-permute-start.10 = (bf16[48,4096]{1,0:T(8,128)(2,1)S(1)}, bf16[48,4096]{1,0:T(8,128)(2,1)S(1)}, u32[]{:S(2)}, u32[]{:S(2)}) collective-permute-start(bf16[48,4096]{1,0:T(8,128)(2,1)S(1)} %slice.16), channel_id=1, source_target_pairs={{4,0},{8,12},{5,1},{9,13},{6,2},{10,14},{7,3},{11,15},{20,16},{24,... | collective-permute-start | bytes 1179656 | tf_op jit(solution)/shard_map/ppermute | solution.py:199
  82.3 6.7 %collective-permute-start.8 = (bf16[40,2560]{1,0:T(8,128)(2,1)S(1)}, bf16[40,2560]{1,0:T(8,128)(2,1)S(1)}, u32[]{:S(2)}, u32[]{:S(2)}) collective-permute-start(bf16[40,2560]{1,0:T(8,128)(2,1)S(1)} %collective-permute-done.7.refs_2_), channel_id=1, source_target_pairs={{0,16},{16,0},{1,17},{17,1},{2,18},{18,2},{3,19},{19,3},{4,20},{20... | collective-permute-start | bytes 614408 | tf_op jit(solution)/shard_map/ppermute | solution.py:214

commit v20 on v19

--- a/solution.py
+++ b/solution.py
@@ -15,7 +15,20 @@
 AHEAD = 3
 
 
-def rotate(bases, eigens, queries, begins, load=False):
+def inverses(eigens):
+    def kernel(*refs):
+        for eigen_ref, out_ref in zip(refs[: len(eigens)], refs[len(eigens) :]):
+            out_ref[...] = 1.0 / (eigen_ref[...] + damping)
+
+    return pl.pallas_call(
+        kernel,
+        out_shape=[jax.ShapeDtypeStruct(eigen.shape, eigen.dtype) for eigen in eigens],
+        compiler_params=pltpu.CompilerParams(vmem_limit_bytes=2 * MIB),
+        cost_estimate=pl.CostEstimate(flops=1, bytes_accessed=1, transcendentals=0),
+    )(*eigens)
+
+
+def rotate(bases, inverses, queries, begins, load=False):
     groups = [query if isinstance(query, tuple) else (query,) for query in queries]
     queries = [query for group in groups for query in group]
     columns = queries[0].shape[0]
@@ -23,7 +36,7 @@
     sides = len(bases)
 
     def kernel(*refs):
-        basis_refs, eigen_refs = refs[:sides], refs[sides : 2 * sides]
+        basis_refs, inverse_refs = refs[:sides], refs[sides : 2 * sides]
         query_refs = list(refs[2 * sides : 2 * sides + len(queries)])
         out_refs, rest = refs[2 * sides + len(queries) :][:sides], refs[3 * sides + len(queries) :]
         copies = []
@@ -43,7 +56,7 @@
                 block = block + query_refs.pop(0)[...]
             query[place * columns : (place + 1) * columns, :] = block
         for side in reversed(range(sides)):
-            basis_ref, eigen_ref, out_ref, begin = basis_refs[side], eigen_refs[side], out_refs[side], begins[side]
+            basis_ref, inverse_ref, out_ref, begin = basis_refs[side], inverse_refs[side], out_refs[side], begins[side]
             share, width = basis_ref.shape
             for tile in range(share // TILE):
                 where = slice(tile * TILE, (tile + 1) * TILE)
@@ -57,12 +70,12 @@
                     (((1,), (1,)), ((), ())),
                     preferred_element_type=jnp.float32,
                 )
-                out_ref[where, :] = (rotated * (1.0 / (eigen_ref[where, :] + damping))).astype(jnp.bfloat16)
+                out_ref[where, :] = (rotated * inverse_ref[where, :]).astype(jnp.bfloat16)
 
     spaces = [pltpu.HBM if load and side == 0 else pltpu.VMEM for side in range(sides)]
     spaces += [pltpu.VMEM] * (sides + len(queries))
     constrained = [
-        pltpu.with_memory_space_constraint(one, space) for one, space in zip((*bases, *eigens, *queries), spaces)
+        pltpu.with_memory_space_constraint(one, space) for one, space in zip((*bases, *inverses, *queries), spaces)
     ]
     return pl.pallas_call(
         kernel,
@@ -172,14 +185,14 @@
 def along_four(query, bases, eigens, by_owner):
     row = lax.axis_index("rows")
     depth = bases[0].shape[1]
-    eigens = [eigen.reshape(-1, 1) for eigen in eigens]
     across, outwards = [(1, 2), (2, 1)], [(1, 0), (2, 3)]
     beside = lax.ppermute(query, "rows", [(0, 1), (1, 0), (2, 3), (3, 2)])
     opposite = lax.ppermute(query, "rows", across)
     sent = [lax.dynamic_index_in_dim(by_owner, (row + k) % 4, 0, False) for k in range(4)]
-    query, sent = lax.optimization_barrier((query, sent))
+    query, sent, eigens = lax.optimization_barrier((query, sent, eigens))
+    eigens = inverses([eigen.reshape(-1, 1) for eigen in eigens])
     blocks = [sent[0], further(sent[1], 1), further(sent[3], 3)]
-    query, beside = lax.optimization_barrier((query, beside))
+    query, beside, eigens = lax.optimization_barrier((query, beside, eigens))
     two_across = lax.ppermute(beside, "rows", across)
     query, beside, opposite = lax.optimization_barrier((query, beside, opposite))
     two_outwards = lax.ppermute(opposite, "rows", outwards)

time: 110 us -> 111 us (level)
  starting transfers between devices: 21.7 us -> 28 us
  local copies, waits for them, and re-layouts: 17.3 us -> 11.7 us
  Pallas kernels: 34.2 us -> 32.5 us
  waiting for transfers between devices: 21.4 us -> 22.7 us
    ppermute x3, starting transfers between devices: 7.91 us -> 16.5 us  [further(): lax.ppermute(block, 'rows', [(i, (i + k) % rows) for i in range(rows)])]
    pallas_call x4, Pallas kernels: 30.6 us -> 28.8 us  [rotate(): pl.pallas_call(kernel, in_specs=[pl.BlockSpec(memory_space=space) for spa...]
    reshape x2, local copies, waits for them, and re-layouts: 3.58 us -> 1.88 us  [along_four(): eigens = inverses([eigen.reshape(-1, 1) for eigen in eigens])]
    ppermute x1, waiting for transfers between devices: 2.98 us -> 4.21 us  [along_four(): three_hidden = lax.ppermute(two_across[:, :depth], 'rows', outwards)]
    ppermute x1, waiting for transfers between devices: 16.5 us -> 15.3 us  [along_four(): beside = lax.ppermute(query, 'rows', [(0, 1), (1, 0), (2, 3), (3, 2)])]
    unnamed x20 -> x12, local copies, waits for them, and re-layouts: 7.73 us -> 6.81 us
  transfers between devices with their start and end apart: 11 -> 11, of which waited for: 3 -> 4; matrix products, arithmetic and copies ran while one was open for 10% -> 5% of each run, Pallas kernels for 27% -> 26%
where the time goes in v20:
time: 111 us; the launch traced here: 110 us
  Pallas kernels  32.5 us (29%)
  starting transfers between devices  28 us (25%)
  waiting for transfers between devices  22.7 us (20%)
  blocking collectives  13.3 us (12%)
  local copies, waits for them, and re-layouts  11.7 us (11%)
  other arithmetic  1.63 us (1%)
    pallas_call x4, Pallas kernels, rotate(): pl.pallas_call(kernel, in_specs=[pl.BlockSpec(memory_space=space) for spa...  28.8 us
    ppermute x3, starting transfers between devices, further(): lax.ppermute(block, 'rows', [(i, (i + k) % rows) for i in range(rows)])  16.5 us
    ppermute x1, waiting for transfers between devices, along_four(): beside = lax.ppermute(query, 'rows', [(0, 1), (1, 0), (2, 3), (3, 2)])  15.3 us
    all_to_all x1, blocking collectives, per_device(): lax.all_to_all(partial.reshape((parts * rows * layers,) + partial.shape[3...  13.3 us
    unnamed x12, local copies, waits for them, and re-layouts  6.81 us
    ppermute x1, waiting for transfers between devices, along_four(): three_hidden = lax.ppermute(two_across[:, :depth], 'rows', outwards)  4.21 us
    ppermute x1, starting transfers between devices, along_four(): beside = lax.ppermute(query, 'rows', [(0, 1), (1, 0), (2, 3), (3, 2)])  3.09 us
    ppermute x2, starting transfers between devices, to_parts(): lax.ppermute(store, 'parts', [(i, (i + j) % parts) for i in range(parts)])  2.96 us
  transfers between devices with their start and end apart: 11, of which 4 were waited for; matrix products, arithmetic and copies ran while one was open for 5% of the time, Pallas kernels for 26%

profile of v20, /device:TPU:0, one launch (start us, length us, event | category | flops | bytes accessed | tf_op | source)
XLA Modules:
  0.0 110.1 jit_solution(15148845680724166591)
XLA Ops:
  0.0 1.2 %shard_map.82.refs_4_ = bf16[48,10240]{1,0:T(8,128)(2,1)S(1)} custom-call(bf16[96,6144]{1,0:T(8,128)(2,1)} %bitcast.36, bf16[96,4096]{1,0:T(8,128)(2,1)} %bitcast.38), custom_call_target="tpu_custom_call" | custom-call | flops 1 | bytes 1 | tf_op jit(solution)/shard_map/pallas_call | solution.py:112
  1.2 3.1 %collective-permute-start = (bf16[48,10240]{1,0:T(8,128)(2,1)S(1)}, bf16[48,10240]{1,0:T(8,128)(2,1)}, u32[]{:S(2)}, u32[]{:S(2)}) collective-permute-start(bf16[48,10240]{1,0:T(8,128)(2,1)S(1)} %shard_map.82.refs_4_), channel_id=1, source_target_pairs={{0,4},{4,0},{8,12},{12,8},{1,5},{5,1},{9,13},{13,9},{2,6},{6,2},{1... | collective-permute-start | bytes 2949128 | tf_op jit(solution)/shard_map/ppermute | solution.py:189
  5.1 1.4 %reshape_squeeze.6 = bf16[40,4,1536]{2,1,0:T(4,128)(2,1)S(1)} reshape(bf16[1,40,6144]{2,1,0:T(8,128)(2,1)} %param.10) | data formatting | bytes 983040 | tf_op jit(solution)/shard_map/reshape;squeeze | solution.py:256
  6.5 1.2 %reshape_squeeze.7 = bf16[40,4,1024]{2,1,0:T(4,128)(2,1)S(1)} reshape(bf16[1,40,4096]{2,1,0:T(8,128)(2,1)} %param.11) | data formatting | bytes 655360 | tf_op jit(solution)/shard_map/reshape;squeeze | solution.py:256
  8.8 1.0 copy.18.refs_0_
  9.8 0.9 copy.19.refs_1_
  10.9 15.3 %collective-permute-done.refs_5_ = bf16[48,10240]{1,0:T(8,128)(2,1)} collective-permute-done((bf16[48,10240]{1,0:T(8,128)(2,1)S(1)}, bf16[48,10240]{1,0:T(8,128)(2,1)}, u32[]{:S(2)}, u32[]{:S(2)}) %collective-permute-start) | collective-permute-done | bytes 983072 | tf_op jit(solution)/shard_map/ppermute | solution.py:189
  26.9 4.6 %collective-permute-start.2 = (bf16[40,2560]{1,0:T(8,128)(2,1)}, bf16[40,2560]{1,0:T(8,128)(2,1)S(1)}, u32[]{:S(2)}, u32[]{:S(2)}) collective-permute-start(bf16[40,2560]{1,0:T(8,128)(2,1)} %get-tuple-element.60), channel_id=1, source_target_pairs={{0,4},{4,8},{8,12},{12,0},{1,5},{5,9},{9,13},{13,1},{2,6},{6,10},{... | collective-permute-start | bytes 614408 | tf_op jit(solution)/shard_map/ppermute | solution.py:221
  31.4 1.3 %collective-permute-start.6 = (bf16[48,10240]{1,0:T(8,128)(2,1)S(1)}, bf16[48,10240]{1,0:T(8,128)(2,1)S(1)}, u32[]{:S(2)}, u32[]{:S(2)}) collective-permute-start(bf16[48,10240]{1,0:T(8,128)(2,1)S(1)} %collective-permute-done.1.refs_6_), channel_id=1, source_target_pairs={{4,0},{8,12},{5,1},{9,13},{6,2},{10,14},{7,3},{11,15},{20,16},{24,... | collective-permute-start | bytes 2949128 | tf_op jit(solution)/shard_map/ppermute | solution.py:198
  32.7 3.4 %copy-done = bf16[1,1024,4096]{2,1,0:T(8,128)(2,1)S(1)} copy-done((bf16[1,1024,4096]{2,1,0:T(8,128)(2,1)S(1)}, bf16[1,1024,4096]{2,1,0:T(8,128)(2,1)}, u32[]{:S(2)}) %copy-start) | copy-done | bytes 8388632
  36.1 14.3 %shard_map.84 = (bf16[1536,144]{1,0:T(8,128)(2,1)S(1)}, bf16[1024,144]{1,0:T(8,128)(2,1)S(1)}, bf16[1536,6144]{1,0:T(8,128)(2,1)S(1)}) custom-call(bf16[1536,6144]{1,0:T(8,128)(2,1)} %bitcast.33, bf16[1024,4096]{1,0:T(8,128)(2,1)S(1)} %bitcast.27, f32[1536,1]{1,0:T(8,128)S(1)} %get-tuple-element.50.refs_2_.refs_1_, ...), custom_call_target="tpu_custom_call" | custom-call | flops 1 | bytes 1 | tf_op jit(solution)/shard_map/pallas_call | solution.py:80
  50.5 1.5 %collective-permute-start.9 = (bf16[48,6144]{1,0:T(8,128)(2,1)S(1)}, bf16[48,6144]{1,0:T(8,128)(2,1)S(1)}, u32[]{:S(2)}, u32[]{:S(2)}) collective-permute-start(bf16[48,6144]{1,0:T(8,128)(2,1)S(1)} %slice.15), channel_id=1, source_target_pairs={{4,0},{8,12},{5,1},{9,13},{6,2},{10,14},{7,3},{11,15},{20,16},{24,... | collective-permute-start | bytes 1769480 | tf_op jit(solution)/shard_map/ppermute | solution.py:205
  52.1 1.6 %collective-permute-start.4 = (bf16[120,2560]{1,0:T(8,128)(2,1)S(1)}, bf16[120,2560]{1,0:T(8,128)(2,1)S(1)}, u32[]{:S(2)}, u32[]{:S(2)}) collective-permute-start(bf16[120,2560]{1,0:T(8,128)(2,1)S(1)} %constant_dynamic-update-slice_fusion.refs_0_), channel_id=1, source_target_pairs={{0,16},{16,0},{1,17},{17,1},{2,18},{18,2},{3,19},{19,3},{4,20},{20... | collective-permute-start | bytes 1843208 | tf_op jit(solution)/shard_map/ppermute | solution.py:227
  53.7 12.0 %collective-permute-start.7 = (bf16[40,2560]{1,0:T(8,128)(2,1)S(1)}, bf16[40,2560]{1,0:T(8,128)(2,1)S(1)}, u32[]{:S(2)}, u32[]{:S(2)}) collective-permute-start(bf16[40,2560]{1,0:T(8,128)(2,1)S(1)} %copy-done.2), channel_id=1, source_target_pairs={{0,8},{4,12},{8,0},{12,4},{1,9},{5,13},{9,1},{13,5},{2,10},{6,14},... | collective-permute-start | bytes 614408 | tf_op jit(solution)/shard_map/ppermute | solution.py:221
  65.6 3.4 %copy-done.1 = bf16[1,1024,4096]{2,1,0:T(8,128)(2,1)S(1)} copy-done((bf16[1,1024,4096]{2,1,0:T(8,128)(2,1)S(1)}, bf16[1,1024,4096]{2,1,0:T(8,128)(2,1)}, u32[]{:S(2)}) %copy-start.1) | copy-done | bytes 8388632
  69.0 7.2 %shard_map.85 = (bf16[1536,48]{1,0:T(8,128)(2,1)S(1)}, bf16[1024,48]{1,0:T(8,128)(2,1)S(1)}) custom-call(bf16[1536,6144]{1,0:T(8,128)(2,1)S(1)} %get-tuple-element.65.refs_0_, bf16[1024,4096]{1,0:T(8,128)(2,1)S(1)} %bitcast.28, f32[1536,1]{1,0:T(8,128)S(1)} %get-tuple-element.50.refs_2_.refs_1_, f32[1024,1]{1,0:T(8,128)S(1)} %get-tuple-element.51.refs_3_.refs_1_, ...), custom_call_target="tpu_custom_call" | custom-call | flops 1 | bytes 1 | tf_op jit(solution)/shard_map/pallas_call | solution.py:80
  76.3 4.2 %collective-permute-done.9.refs_2_ = bf16[48,6144]{1,0:T(8,128)(2,1)S(1)} collective-permute-done((bf16[48,6144]{1,0:T(8,128)(2,1)S(1)}, bf16[48,6144]{1,0:T(8,128)(2,1)S(1)}, u32[]{:S(2)}, u32[]{:S(2)}) %collective-permute-start.9) | collective-permute-done | bytes 589856 | tf_op jit(solution)/shard_map/ppermute | solution.py:205
  80.5 1.3 %collective-permute-start.10 = (bf16[48,4096]{1,0:T(8,128)(2,1)S(1)}, bf16[48,4096]{1,0:T(8,128)(2,1)S(1)}, u32[]{:S(2)}, u32[]{:S(2)}) collective-permute-start(bf16[48,4096]{1,0:T(8,128)(2,1)S(1)} %slice.16), channel_id=1, source_target_pairs={{4,0},{8,12},{5,1},{9,13},{6,2},{10,14},{7,3},{11,15},{20,16},{24,... | collective-permute-start | bytes 1179656 | tf_op jit(solution)/shard_map/ppermute | solution.py:212
  81.7 1.4 %collective-permute-start.8 = (bf16[40,2560]{1,0:T(8,128)(2,1)S(1)}, bf16[40,2560]{1,0:T(8,128)(2,1)S(1)}, u32[]{:S(2)}, u32[]{:S(2)}) collective-permute-start(bf16[40,2560]{1,0:T(8,128)(2,1)S(1)} %collective-permute-done.7.refs_2_), channel_id=1, source_target_pairs={{0,16},{16,0},{1,17},{17,1},{2,18},{18,2},{3,19},{19,3},{4,20},{20... | collective-permute-start | bytes 614408 | tf_op jit(solution)/shard_map/ppermute | solution.py:227
  83.1 5.0 %shard_map.87.refs_4_ = bf16[1536,48]{1,0:T(8,128)(2,1)S(1)} custom-call(bf16[1536,6144]{1,0:T(8,128)(2,1)S(1)} %get-tuple-element.65.refs_0_, f32[1536,1]{1,0:T(8,128)S(1)} %get-tuple-element.50.refs_2_.refs_1_, bf16[48,6144]{1,0:T(8,128)(2,1)S(1)} %collective-permute-done.9.refs_2_), custom_call_target="tpu_custom_call" | custom-call | flops 1 | bytes 1 | tf_op jit(solution)/shard_map/pallas_call | solution.py:80
  88.4 1.6 %shard_map.86.refs_6_ = bf16[2,4,4,16,256]{4,3,2,1,0:T(8,128)(2,1)S(1)} custom-call(bf16[120,2560]{1,0:T(8,128)(2,1)S(1)} %constant_dynamic-update-slice_fusion.refs_0_, bf16[120,2560]{1,0:T(8,128)(2,1)S(1)} %collective-permute-done.4.refs_1_, bf16[40,2560]{1,0:T(8,128)(2,1)S(1)} %collective-permute-done.7.refs_2_, ...), custom_call_target="tpu_custom_call" | custom-call | flops 1 | bytes 1 | tf_op jit(solution)/shard_map/pallas_call | solution.py:177
  90.0 2.9 %collective-permute-done.10.refs_2_ = bf16[48,4096]{1,0:T(8,128)(2,1)S(1)} collective-permute-done((bf16[48,4096]{1,0:T(8,128)(2,1)S(1)}, bf16[48,4096]{1,0:T(8,128)(2,1)S(1)}, u32[]{:S(2)}, u32[]{:S(2)}) %collective-permute-start.10) | collective-permute-done | bytes 393248 | tf_op jit(solution)/shard_map/ppermute | solution.py:212
  92.9 2.3 %shard_map.88.refs_5_ = bf16[1024,48]{1,0:T(8,128)(2,1)S(1)} custom-call(bf16[1024,4096]{1,0:T(8,128)(2,1)S(1)} %bitcast.31, f32[1024,1]{1,0:T(8,128)S(1)} %get-tuple-element.51.refs_3_.refs_1_, bf16[48,4096]{1,0:T(8,128)(2,1)S(1)} %collective-permute-done.10.refs_2_), custom_call_target="tpu_custom_call" | custom-call | flops 1 | bytes 1 | tf_op jit(solution)/shard_map/pallas_call | solution.py:80
  95.9 13.3 %all_to_all.5 = bf16[32,16,256]{2,1,0:T(8,128)(2,1)S(1)} all-to-all(bf16[32,16,256]{2,1,0:T(8,128)(2,1)S(1)} %bitcast.32), channel_id=1, replica_groups=mesh['parts'=2,'rows'=4,'layer'=4] {'parts','rows','layer'}, dimensions={0} | all-to-all | bytes 524288 | tf_op jit(solution)/shard_map/all_to_all | solution.py:280
  (36 shorter events, 4.8 us)
Async XLA Ops:
  1.2 24.9 %collective-permute-start = (bf16[48,10240]{1,0:T(8,128)(2,1)S(1)}, bf16[48,10240]{1,0:T(8,128)(2,1)}, u32[]{:S(2)}, u32[]{:S(2)}) collective-permute-start(bf16[48,10240]{1,0:T(8,128)(2,1)S(1)} %shard_map.82.refs_4_), channel_id=1, source_target_pairs={{0,4},{4,0},{8,12},{12,8},{1,5},{5,1},{9,13},{13,9},{2,6},{6,2},{1... | collective-permute-start | bytes 2949128 | tf_op jit(solution)/shard_map/ppermute | solution.py:189
  4.3 27.1 %collective-permute-start.1 = (bf16[48,10240]{1,0:T(8,128)(2,1)S(1)}, bf16[48,10240]{1,0:T(8,128)(2,1)S(1)}, u32[]{:S(2)}, u32[]{:S(2)}) collective-permute-start(bf16[48,10240]{1,0:T(8,128)(2,1)S(1)} %shard_map.82.refs_4_), channel_id=1, source_target_pairs={{4,8},{8,4},{5,9},{9,5},{6,10},{10,6},{7,11},{11,7},{20,24},{24,20... | collective-permute-start | bytes 2949128 | tf_op jit(solution)/shard_map/ppermute | solution.py:190
  10.7 43.0 %copy-start.2 = (bf16[40,2560]{1,0:T(8,128)(2,1)S(1)}, bf16[40,2560]{1,0:T(8,128)(2,1)}, u32[]{:S(2)}) copy-start(bf16[40,2560]{1,0:T(8,128)(2,1)} %get-tuple-element.72) | copy-start | bytes 614404
  26.1 24.3 %collective-permute-start.5 = (bf16[48,10240]{1,0:T(8,128)(2,1)}, bf16[48,10240]{1,0:T(8,128)(2,1)S(1)}, u32[]{:S(2)}, u32[]{:S(2)}) collective-permute-start(bf16[48,10240]{1,0:T(8,128)(2,1)} %collective-permute-done.refs_5_), channel_id=1, source_target_pairs={{4,8},{8,4},{5,9},{9,5},{6,10},{10,6},{7,11},{11,7},{20,24},{24,20... | collective-permute-start | bytes 2949128 | tf_op jit(solution)/shard_map/ppermute | solution.py:196
  26.9 23.6 %collective-permute-start.2 = (bf16[40,2560]{1,0:T(8,128)(2,1)}, bf16[40,2560]{1,0:T(8,128)(2,1)S(1)}, u32[]{:S(2)}, u32[]{:S(2)}) collective-permute-start(bf16[40,2560]{1,0:T(8,128)(2,1)} %get-tuple-element.60), channel_id=1, source_target_pairs={{0,4},{4,8},{8,12},{12,0},{1,5},{5,9},{9,13},{13,1},{2,6},{6,10},{... | collective-permute-start | bytes 614408 | tf_op jit(solution)/shard_map/ppermute | solution.py:221
  31.4 19.0 %collective-permute-start.3 = (bf16[40,2560]{1,0:T(8,128)(2,1)}, bf16[40,2560]{1,0:T(8,128)(2,1)S(1)}, u32[]{:S(2)}, u32[]{:S(2)}) collective-permute-start(bf16[40,2560]{1,0:T(8,128)(2,1)} %get-tuple-element.61), channel_id=1, source_target_pairs={{0,12},{4,0},{8,4},{12,8},{1,13},{5,1},{9,5},{13,9},{2,14},{6,2},{... | collective-permute-start | bytes 614408 | tf_op jit(solution)/shard_map/ppermute | solution.py:221
  31.4 34.2 %collective-permute-start.6 = (bf16[48,10240]{1,0:T(8,128)(2,1)S(1)}, bf16[48,10240]{1,0:T(8,128)(2,1)S(1)}, u32[]{:S(2)}, u32[]{:S(2)}) collective-permute-start(bf16[48,10240]{1,0:T(8,128)(2,1)S(1)} %collective-permute-done.1.refs_6_), channel_id=1, source_target_pairs={{4,0},{8,12},{5,1},{9,13},{6,2},{10,14},{7,3},{11,15},{20,16},{24,... | collective-permute-start | bytes 2949128 | tf_op jit(solution)/shard_map/ppermute | solution.py:198
  32.7 3.4 %copy-start = (bf16[1,1024,4096]{2,1,0:T(8,128)(2,1)S(1)}, bf16[1,1024,4096]{2,1,0:T(8,128)(2,1)}, u32[]{:S(2)}) copy-start(bf16[1,1024,4096]{2,1,0:T(8,128)(2,1)} %param.13) | copy-start | bytes 25165828
  50.5 29.9 %collective-permute-start.9 = (bf16[48,6144]{1,0:T(8,128)(2,1)S(1)}, bf16[48,6144]{1,0:T(8,128)(2,1)S(1)}, u32[]{:S(2)}, u32[]{:S(2)}) collective-permute-start(bf16[48,6144]{1,0:T(8,128)(2,1)S(1)} %slice.15), channel_id=1, source_target_pairs={{4,0},{8,12},{5,1},{9,13},{6,2},{10,14},{7,3},{11,15},{20,16},{24,... | collective-permute-start | bytes 1769480 | tf_op jit(solution)/shard_map/ppermute | solution.py:205
  52.1 36.1 %collective-permute-start.4 = (bf16[120,2560]{1,0:T(8,128)(2,1)S(1)}, bf16[120,2560]{1,0:T(8,128)(2,1)S(1)}, u32[]{:S(2)}, u32[]{:S(2)}) collective-permute-start(bf16[120,2560]{1,0:T(8,128)(2,1)S(1)} %constant_dynamic-update-slice_fusion.refs_0_), channel_id=1, source_target_pairs={{0,16},{16,0},{1,17},{17,1},{2,18},{18,2},{3,19},{19,3},{4,20},{20... | collective-permute-start | bytes 1843208 | tf_op jit(solution)/shard_map/ppermute | solution.py:227
  53.7 22.6 %collective-permute-start.7 = (bf16[40,2560]{1,0:T(8,128)(2,1)S(1)}, bf16[40,2560]{1,0:T(8,128)(2,1)S(1)}, u32[]{:S(2)}, u32[]{:S(2)}) collective-permute-start(bf16[40,2560]{1,0:T(8,128)(2,1)S(1)} %copy-done.2), channel_id=1, source_target_pairs={{0,8},{4,12},{8,0},{12,4},{1,9},{5,13},{9,1},{13,5},{2,10},{6,14},... | collective-permute-start | bytes 614408 | tf_op jit(solution)/shard_map/ppermute | solution.py:221
  65.6 3.4 %copy-start.1 = (bf16[1,1024,4096]{2,1,0:T(8,128)(2,1)S(1)}, bf16[1,1024,4096]{2,1,0:T(8,128)(2,1)}, u32[]{:S(2)}) copy-start(bf16[1,1024,4096]{2,1,0:T(8,128)(2,1)} %param.13) | copy-start | bytes 25165828
  76.2 16.7 %slice-start = ((s8[8388608]{0:T(1024)(128)(4,1)}), s8[4194304]{0:T(1024)(128)(4,1)S(1)}, s32[]{:S(2)}) async-start(s8[8388608]{0:T(1024)(128)(4,1)} %bitcast.29), calls=%async_computation.1 | async-start | bytes 8388608
  76.2 16.6 %slice-start.1 = ((s8[8388608]{0:T(1024)(128)(4,1)}), s8[4194304]{0:T(1024)(128)(4,1)S(1)}, s32[]{:S(2)}) async-start(s8[8388608]{0:T(1024)(128)(4,1)} %bitcast.29), calls=%async_computation.2 | async-start | bytes 8388608
  80.5 12.4 %collective-permute-start.10 = (bf16[48,4096]{1,0:T(8,128)(2,1)S(1)}, bf16[48,4096]{1,0:T(8,128)(2,1)S(1)}, u32[]{:S(2)}, u32[]{:S(2)}) collective-permute-start(bf16[48,4096]{1,0:T(8,128)(2,1)S(1)} %slice.16), channel_id=1, source_target_pairs={{4,0},{8,12},{5,1},{9,13},{6,2},{10,14},{7,3},{11,15},{20,16},{24,... | collective-permute-start | bytes 1179656 | tf_op jit(solution)/shard_map/ppermute | solution.py:212
  81.7 6.7 %collective-permute-start.8 = (bf16[40,2560]{1,0:T(8,128)(2,1)S(1)}, bf16[40,2560]{1,0:T(8,128)(2,1)S(1)}, u32[]{:S(2)}, u32[]{:S(2)}) collective-permute-start(bf16[40,2560]{1,0:T(8,128)(2,1)S(1)} %collective-permute-done.7.refs_2_), channel_id=1, source_target_pairs={{0,16},{16,0},{1,17},{17,1},{2,18},{18,2},{3,19},{19,3},{4,20},{20... | collective-permute-start | bytes 614408 | tf_op jit(solution)/shard_map/ppermute | solution.py:227

commit v21 on v20

--- a/solution.py
+++ b/solution.py
@@ -198,11 +198,12 @@
     two_outwards = lax.ppermute(opposite, "rows", outwards)
     *near, hidden_here = rotate(bases, eigens, [query, beside, opposite], (0, depth), load=True)
     bases = [hidden_here, bases[1]]
-    near, blocks = lax.optimization_barrier((near, blocks))
-    stores = [(store, j, (0, 1, 3)) for j, store in enumerate(to_parts(jnp.concatenate(blocks, axis=0)))]
     near, two_across, late = lax.optimization_barrier((near, two_across, sent[2]))
     two_model = two_across[:, depth:]
-    three_hidden = lax.ppermute(two_across[:, :depth], "rows", outwards)
+    two_hidden = two_across[:, :depth]
+    three_hidden = lax.ppermute(two_hidden, "rows", outwards)
+    _, blocks = lax.optimization_barrier((two_hidden, blocks))
+    stores = [(store, j, (0, 1, 3)) for j, store in enumerate(to_parts(jnp.concatenate(blocks, axis=0)))]
     late = further(late, 2)
     far = rotate(bases, eigens, [(two_across, two_outwards)], (0, depth))
     far, late = lax.optimization_barrier((far, late))

time: 111 us -> 107 us (0.964)
  waiting for transfers between devices: 22.7 us -> 21.2 us
  starting transfers between devices: 28 us -> 26.6 us
    ppermute x3, starting transfers between devices: 16.5 us -> 15 us  [further(): lax.ppermute(block, 'rows', [(i, (i + k) % rows) for i in range(rows)])]
    ppermute x1, waiting for transfers between devices: 4.21 us -> 3.1 us  [along_four(): three_hidden = lax.ppermute(two_hidden, 'rows', outwards)]
  transfers between devices with their start and end apart: 11 -> 11, of which waited for: 4 -> 3; matrix products, arithmetic and copies ran while one was open for 5% -> 5% of each run, Pallas kernels for 26% -> 26%
where the time goes in v21:
time: 107 us
  Pallas kernels  32.5 us (30%)
  starting transfers between devices  26.6 us (25%)
  waiting for transfers between devices  21.2 us (20%)
  blocking collectives  12.7 us (12%)
  local copies, waits for them, and re-layouts  11.7 us (11%)
  other arithmetic  1.64 us (2%)
    pallas_call x4, Pallas kernels, rotate(): pl.pallas_call(kernel, in_specs=[pl.BlockSpec(memory_space=space) for spa...  28.8 us
    ppermute x1, waiting for transfers between devices, along_four(): beside = lax.ppermute(query, 'rows', [(0, 1), (1, 0), (2, 3), (3, 2)])  15.3 us
    ppermute x3, starting transfers between devices, further(): lax.ppermute(block, 'rows', [(i, (i + k) % rows) for i in range(rows)])  15 us
    all_to_all x1, blocking collectives, per_device(): lax.all_to_all(partial.reshape((parts * rows * layers,) + partial.shape[3...  12.7 us
    unnamed x12, local copies, waits for them, and re-layouts  6.81 us
    ppermute x1, waiting for transfers between devices, along_four(): three_hidden = lax.ppermute(two_hidden, 'rows', outwards)  3.1 us
    ppermute x1, starting transfers between devices, along_four(): beside = lax.ppermute(query, 'rows', [(0, 1), (1, 0), (2, 3), (3, 2)])  3.09 us
    ppermute x2, starting transfers between devices, to_parts(): lax.ppermute(store, 'parts', [(i, (i + j) % parts) for i in range(parts)])  3.08 us
  transfers between devices with their start and end apart: 11, of which 3 were waited for; matrix products, arithmetic and copies ran while one was open for 5% of the time, Pallas kernels for 26%

profile of v21, /device:TPU:0, one launch (start us, length us, event | category | flops | bytes accessed | tf_op | source)
XLA Modules:
  0.0 106.7 jit_solution(10249974855971033744)
XLA Ops:
  0.0 1.2 %shard_map.82.refs_4_ = bf16[48,10240]{1,0:T(8,128)(2,1)S(1)} custom-call(bf16[96,6144]{1,0:T(8,128)(2,1)} %bitcast.36, bf16[96,4096]{1,0:T(8,128)(2,1)} %bitcast.38), custom_call_target="tpu_custom_call" | custom-call | flops 1 | bytes 1 | tf_op jit(solution)/shard_map/pallas_call | solution.py:112
  1.2 3.1 %collective-permute-start = (bf16[48,10240]{1,0:T(8,128)(2,1)S(1)}, bf16[48,10240]{1,0:T(8,128)(2,1)}, u32[]{:S(2)}, u32[]{:S(2)}) collective-permute-start(bf16[48,10240]{1,0:T(8,128)(2,1)S(1)} %shard_map.82.refs_4_), channel_id=1, source_target_pairs={{0,4},{4,0},{8,12},{12,8},{1,5},{5,1},{9,13},{13,9},{2,6},{6,2},{1... | collective-permute-start | bytes 2949128 | tf_op jit(solution)/shard_map/ppermute | solution.py:189
  5.1 1.4 %reshape_squeeze.6 = bf16[40,4,1536]{2,1,0:T(4,128)(2,1)S(1)} reshape(bf16[1,40,6144]{2,1,0:T(8,128)(2,1)} %param.10) | data formatting | bytes 983040 | tf_op jit(solution)/shard_map/reshape;squeeze | solution.py:257
  6.5 1.2 %reshape_squeeze.7 = bf16[40,4,1024]{2,1,0:T(4,128)(2,1)S(1)} reshape(bf16[1,40,4096]{2,1,0:T(8,128)(2,1)} %param.11) | data formatting | bytes 655360 | tf_op jit(solution)/shard_map/reshape;squeeze | solution.py:257
  8.8 1.0 copy.18.refs_0_
  9.8 0.9 copy.19.refs_1_
  10.9 15.3 %collective-permute-done.refs_5_ = bf16[48,10240]{1,0:T(8,128)(2,1)} collective-permute-done((bf16[48,10240]{1,0:T(8,128)(2,1)S(1)}, bf16[48,10240]{1,0:T(8,128)(2,1)}, u32[]{:S(2)}, u32[]{:S(2)}) %collective-permute-start) | collective-permute-done | bytes 983072 | tf_op jit(solution)/shard_map/ppermute | solution.py:189
  26.9 4.6 %collective-permute-start.3 = (bf16[40,2560]{1,0:T(8,128)(2,1)}, bf16[40,2560]{1,0:T(8,128)(2,1)S(1)}, u32[]{:S(2)}, u32[]{:S(2)}) collective-permute-start(bf16[40,2560]{1,0:T(8,128)(2,1)} %get-tuple-element.60), channel_id=1, source_target_pairs={{0,4},{4,8},{8,12},{12,0},{1,5},{5,9},{9,13},{13,1},{2,6},{6,10},{... | collective-permute-start | bytes 614408 | tf_op jit(solution)/shard_map/ppermute | solution.py:222
  31.4 1.3 %collective-permute-start.6 = (bf16[48,10240]{1,0:T(8,128)(2,1)S(1)}, bf16[48,10240]{1,0:T(8,128)(2,1)S(1)}, u32[]{:S(2)}, u32[]{:S(2)}) collective-permute-start(bf16[48,10240]{1,0:T(8,128)(2,1)S(1)} %collective-permute-done.1.refs_6_), channel_id=1, source_target_pairs={{4,0},{8,12},{5,1},{9,13},{6,2},{10,14},{7,3},{11,15},{20,16},{24,... | collective-permute-start | bytes 2949128 | tf_op jit(solution)/shard_map/ppermute | solution.py:198
  32.7 3.4 %copy-done = bf16[1,1024,4096]{2,1,0:T(8,128)(2,1)S(1)} copy-done((bf16[1,1024,4096]{2,1,0:T(8,128)(2,1)S(1)}, bf16[1,1024,4096]{2,1,0:T(8,128)(2,1)}, u32[]{:S(2)}) %copy-start) | copy-done | bytes 8388632
  36.1 14.3 %shard_map.84 = (bf16[1536,144]{1,0:T(8,128)(2,1)S(1)}, bf16[1024,144]{1,0:T(8,128)(2,1)S(1)}, bf16[1536,6144]{1,0:T(8,128)(2,1)S(1)}) custom-call(bf16[1536,6144]{1,0:T(8,128)(2,1)} %bitcast.33, bf16[1024,4096]{1,0:T(8,128)(2,1)S(1)} %bitcast.27, f32[1536,1]{1,0:T(8,128)S(1)} %get-tuple-element.48.refs_2_.refs_1_, ...), custom_call_target="tpu_custom_call" | custom-call | flops 1 | bytes 1 | tf_op jit(solution)/shard_map/pallas_call | solution.py:80
  50.5 1.5 %collective-permute-start.9 = (bf16[48,6144]{1,0:T(8,128)(2,1)S(1)}, bf16[48,6144]{1,0:T(8,128)(2,1)S(1)}, u32[]{:S(2)}, u32[]{:S(2)}) collective-permute-start(bf16[48,6144]{1,0:T(8,128)(2,1)S(1)} %slice.15), channel_id=1, source_target_pairs={{4,0},{8,12},{5,1},{9,13},{6,2},{10,14},{7,3},{11,15},{20,16},{24,... | collective-permute-start | bytes 1769480 | tf_op jit(solution)/shard_map/ppermute | solution.py:204
  52.1 1.6 %collective-permute-start.5 = (bf16[120,2560]{1,0:T(8,128)(2,1)S(1)}, bf16[120,2560]{1,0:T(8,128)(2,1)S(1)}, u32[]{:S(2)}, u32[]{:S(2)}) collective-permute-start(bf16[120,2560]{1,0:T(8,128)(2,1)S(1)} %constant_dynamic-update-slice_fusion.refs_0_), channel_id=1, source_target_pairs={{0,16},{16,0},{1,17},{17,1},{2,18},{18,2},{3,19},{19,3},{4,20},{20... | collective-permute-start | bytes 1843208 | tf_op jit(solution)/shard_map/ppermute | solution.py:228
  53.7 10.4 %collective-permute-start.7 = (bf16[40,2560]{1,0:T(8,128)(2,1)S(1)}, bf16[40,2560]{1,0:T(8,128)(2,1)S(1)}, u32[]{:S(2)}, u32[]{:S(2)}) collective-permute-start(bf16[40,2560]{1,0:T(8,128)(2,1)S(1)} %copy-done.2), channel_id=1, source_target_pairs={{0,8},{4,12},{8,0},{12,4},{1,9},{5,13},{9,1},{13,5},{2,10},{6,14},... | collective-permute-start | bytes 614408 | tf_op jit(solution)/shard_map/ppermute | solution.py:222
  64.1 3.4 %copy-done.1 = bf16[1,1024,4096]{2,1,0:T(8,128)(2,1)S(1)} copy-done((bf16[1,1024,4096]{2,1,0:T(8,128)(2,1)S(1)}, bf16[1,1024,4096]{2,1,0:T(8,128)(2,1)}, u32[]{:S(2)}) %copy-start.1) | copy-done | bytes 8388632
  67.4 7.2 %shard_map.85 = (bf16[1536,48]{1,0:T(8,128)(2,1)S(1)}, bf16[1024,48]{1,0:T(8,128)(2,1)S(1)}) custom-call(bf16[1536,6144]{1,0:T(8,128)(2,1)S(1)} %get-tuple-element.65.refs_0_, bf16[1024,4096]{1,0:T(8,128)(2,1)S(1)} %bitcast.28, f32[1536,1]{1,0:T(8,128)S(1)} %get-tuple-element.48.refs_2_.refs_1_, f32[1024,1]{1,0:T(8,128)S(1)} %get-tuple-element.49.refs_3_.refs_1_, ...), custom_call_target="tpu_custom_call" | custom-call | flops 1 | bytes 1 | tf_op jit(solution)/shard_map/pallas_call | solution.py:80
  74.7 3.1 %collective-permute-done.9.refs_2_ = bf16[48,6144]{1,0:T(8,128)(2,1)S(1)} collective-permute-done((bf16[48,6144]{1,0:T(8,128)(2,1)S(1)}, bf16[48,6144]{1,0:T(8,128)(2,1)S(1)}, u32[]{:S(2)}, u32[]{:S(2)}) %collective-permute-start.9) | collective-permute-done | bytes 589856 | tf_op jit(solution)/shard_map/ppermute | solution.py:204
  77.8 1.3 %collective-permute-start.10 = (bf16[48,4096]{1,0:T(8,128)(2,1)S(1)}, bf16[48,4096]{1,0:T(8,128)(2,1)S(1)}, u32[]{:S(2)}, u32[]{:S(2)}) collective-permute-start(bf16[48,4096]{1,0:T(8,128)(2,1)S(1)} %slice.16), channel_id=1, source_target_pairs={{4,0},{8,12},{5,1},{9,13},{6,2},{10,14},{7,3},{11,15},{20,16},{24,... | collective-permute-start | bytes 1179656 | tf_op jit(solution)/shard_map/ppermute | solution.py:213
  79.1 1.5 %collective-permute-start.8 = (bf16[40,2560]{1,0:T(8,128)(2,1)S(1)}, bf16[40,2560]{1,0:T(8,128)(2,1)S(1)}, u32[]{:S(2)}, u32[]{:S(2)}) collective-permute-start(bf16[40,2560]{1,0:T(8,128)(2,1)S(1)} %collective-permute-done.7.refs_2_), channel_id=1, source_target_pairs={{0,16},{16,0},{1,17},{17,1},{2,18},{18,2},{3,19},{19,3},{4,20},{20... | collective-permute-start | bytes 614408 | tf_op jit(solution)/shard_map/ppermute | solution.py:228
  80.6 5.0 %shard_map.87.refs_4_ = bf16[1536,48]{1,0:T(8,128)(2,1)S(1)} custom-call(bf16[1536,6144]{1,0:T(8,128)(2,1)S(1)} %get-tuple-element.65.refs_0_, f32[1536,1]{1,0:T(8,128)S(1)} %get-tuple-element.48.refs_2_.refs_1_, bf16[48,6144]{1,0:T(8,128)(2,1)S(1)} %collective-permute-done.9.refs_2_), custom_call_target="tpu_custom_call" | custom-call | flops 1 | bytes 1 | tf_op jit(solution)/shard_map/pallas_call | solution.py:80
  85.6 1.6 %shard_map.86.refs_6_ = bf16[2,4,4,16,256]{4,3,2,1,0:T(8,128)(2,1)S(1)} custom-call(bf16[120,2560]{1,0:T(8,128)(2,1)S(1)} %constant_dynamic-update-slice_fusion.refs_0_, bf16[120,2560]{1,0:T(8,128)(2,1)S(1)} %collective-permute-done.5.refs_1_, bf16[40,2560]{1,0:T(8,128)(2,1)S(1)} %collective-permute-done.7.refs_2_, ...), custom_call_target="tpu_custom_call" | custom-call | flops 1 | bytes 1 | tf_op jit(solution)/shard_map/pallas_call | solution.py:177
  87.1 2.8 %collective-permute-done.10.refs_2_ = bf16[48,4096]{1,0:T(8,128)(2,1)S(1)} collective-permute-done((bf16[48,4096]{1,0:T(8,128)(2,1)S(1)}, bf16[48,4096]{1,0:T(8,128)(2,1)S(1)}, u32[]{:S(2)}, u32[]{:S(2)}) %collective-permute-start.10) | collective-permute-done | bytes 393248 | tf_op jit(solution)/shard_map/ppermute | solution.py:213
  89.9 2.3 %shard_map.88.refs_5_ = bf16[1024,48]{1,0:T(8,128)(2,1)S(1)} custom-call(bf16[1024,4096]{1,0:T(8,128)(2,1)S(1)} %bitcast.31, f32[1024,1]{1,0:T(8,128)S(1)} %get-tuple-element.49.refs_3_.refs_1_, bf16[48,4096]{1,0:T(8,128)(2,1)S(1)} %collective-permute-done.10.refs_2_), custom_call_target="tpu_custom_call" | custom-call | flops 1 | bytes 1 | tf_op jit(solution)/shard_map/pallas_call | solution.py:80
  93.0 12.7 %all_to_all.5 = bf16[32,16,256]{2,1,0:T(8,128)(2,1)S(1)} all-to-all(bf16[32,16,256]{2,1,0:T(8,128)(2,1)S(1)} %bitcast.32), channel_id=1, replica_groups=mesh['parts'=2,'rows'=4,'layer'=4] {'parts','rows','layer'}, dimensions={0} | all-to-all | bytes 524288 | tf_op jit(solution)/shard_map/all_to_all | solution.py:281
  (36 shorter events, 4.5 us)
Async XLA Ops:
  1.2 24.9 %collective-permute-start = (bf16[48,10240]{1,0:T(8,128)(2,1)S(1)}, bf16[48,10240]{1,0:T(8,128)(2,1)}, u32[]{:S(2)}, u32[]{:S(2)}) collective-permute-start(bf16[48,10240]{1,0:T(8,128)(2,1)S(1)} %shard_map.82.refs_4_), channel_id=1, source_target_pairs={{0,4},{4,0},{8,12},{12,8},{1,5},{5,1},{9,13},{13,9},{2,6},{6,2},{1... | collective-permute-start | bytes 2949128 | tf_op jit(solution)/shard_map/ppermute | solution.py:189
  4.3 27.1 %collective-permute-start.1 = (bf16[48,10240]{1,0:T(8,128)(2,1)S(1)}, bf16[48,10240]{1,0:T(8,128)(2,1)S(1)}, u32[]{:S(2)}, u32[]{:S(2)}) collective-permute-start(bf16[48,10240]{1,0:T(8,128)(2,1)S(1)} %shard_map.82.refs_4_), channel_id=1, source_target_pairs={{4,8},{8,4},{5,9},{9,5},{6,10},{10,6},{7,11},{11,7},{20,24},{24,20... | collective-permute-start | bytes 2949128 | tf_op jit(solution)/shard_map/ppermute | solution.py:190
  10.7 43.0 %copy-start.2 = (bf16[40,2560]{1,0:T(8,128)(2,1)S(1)}, bf16[40,2560]{1,0:T(8,128)(2,1)}, u32[]{:S(2)}) copy-start(bf16[40,2560]{1,0:T(8,128)(2,1)} %get-tuple-element.68) | copy-start | bytes 614404
  26.1 24.3 %collective-permute-start.2 = (bf16[48,10240]{1,0:T(8,128)(2,1)}, bf16[48,10240]{1,0:T(8,128)(2,1)S(1)}, u32[]{:S(2)}, u32[]{:S(2)}) collective-permute-start(bf16[48,10240]{1,0:T(8,128)(2,1)} %collective-permute-done.refs_5_), channel_id=1, source_target_pairs={{4,8},{8,4},{5,9},{9,5},{6,10},{10,6},{7,11},{11,7},{20,24},{24,20... | collective-permute-start | bytes 2949128 | tf_op jit(solution)/shard_map/ppermute | solution.py:196
  26.9 25.1 %collective-permute-start.3 = (bf16[40,2560]{1,0:T(8,128)(2,1)}, bf16[40,2560]{1,0:T(8,128)(2,1)S(1)}, u32[]{:S(2)}, u32[]{:S(2)}) collective-permute-start(bf16[40,2560]{1,0:T(8,128)(2,1)} %get-tuple-element.60), channel_id=1, source_target_pairs={{0,4},{4,8},{8,12},{12,0},{1,5},{5,9},{9,13},{13,1},{2,6},{6,10},{... | collective-permute-start | bytes 614408 | tf_op jit(solution)/shard_map/ppermute | solution.py:222
  31.4 20.6 %collective-permute-start.4 = (bf16[40,2560]{1,0:T(8,128)(2,1)}, bf16[40,2560]{1,0:T(8,128)(2,1)S(1)}, u32[]{:S(2)}, u32[]{:S(2)}) collective-permute-start(bf16[40,2560]{1,0:T(8,128)(2,1)} %get-tuple-element.61), channel_id=1, source_target_pairs={{0,12},{4,0},{8,4},{12,8},{1,13},{5,1},{9,5},{13,9},{2,14},{6,2},{... | collective-permute-start | bytes 614408 | tf_op jit(solution)/shard_map/ppermute | solution.py:222
  31.4 32.6 %collective-permute-start.6 = (bf16[48,10240]{1,0:T(8,128)(2,1)S(1)}, bf16[48,10240]{1,0:T(8,128)(2,1)S(1)}, u32[]{:S(2)}, u32[]{:S(2)}) collective-permute-start(bf16[48,10240]{1,0:T(8,128)(2,1)S(1)} %collective-permute-done.1.refs_6_), channel_id=1, source_target_pairs={{4,0},{8,12},{5,1},{9,13},{6,2},{10,14},{7,3},{11,15},{20,16},{24,... | collective-permute-start | bytes 2949128 | tf_op jit(solution)/shard_map/ppermute | solution.py:198
  32.7 3.4 %copy-start = (bf16[1,1024,4096]{2,1,0:T(8,128)(2,1)S(1)}, bf16[1,1024,4096]{2,1,0:T(8,128)(2,1)}, u32[]{:S(2)}) copy-start(bf16[1,1024,4096]{2,1,0:T(8,128)(2,1)} %param.13) | copy-start | bytes 25165828
  50.5 27.3 %collective-permute-start.9 = (bf16[48,6144]{1,0:T(8,128)(2,1)S(1)}, bf16[48,6144]{1,0:T(8,128)(2,1)S(1)}, u32[]{:S(2)}, u32[]{:S(2)}) collective-permute-start(bf16[48,6144]{1,0:T(8,128)(2,1)S(1)} %slice.15), channel_id=1, source_target_pairs={{4,0},{8,12},{5,1},{9,13},{6,2},{10,14},{7,3},{11,15},{20,16},{24,... | collective-permute-start | bytes 1769480 | tf_op jit(solution)/shard_map/ppermute | solution.py:204
  52.1 33.5 %collective-permute-start.5 = (bf16[120,2560]{1,0:T(8,128)(2,1)S(1)}, bf16[120,2560]{1,0:T(8,128)(2,1)S(1)}, u32[]{:S(2)}, u32[]{:S(2)}) collective-permute-start(bf16[120,2560]{1,0:T(8,128)(2,1)S(1)} %constant_dynamic-update-slice_fusion.refs_0_), channel_id=1, source_target_pairs={{0,16},{16,0},{1,17},{17,1},{2,18},{18,2},{3,19},{19,3},{4,20},{20... | collective-permute-start | bytes 1843208 | tf_op jit(solution)/shard_map/ppermute | solution.py:228
  53.7 21.0 %collective-permute-start.7 = (bf16[40,2560]{1,0:T(8,128)(2,1)S(1)}, bf16[40,2560]{1,0:T(8,128)(2,1)S(1)}, u32[]{:S(2)}, u32[]{:S(2)}) collective-permute-start(bf16[40,2560]{1,0:T(8,128)(2,1)S(1)} %copy-done.2), channel_id=1, source_target_pairs={{0,8},{4,12},{8,0},{12,4},{1,9},{5,13},{9,1},{13,5},{2,10},{6,14},... | collective-permute-start | bytes 614408 | tf_op jit(solution)/shard_map/ppermute | solution.py:222
  64.1 3.4 %copy-start.1 = (bf16[1,1024,4096]{2,1,0:T(8,128)(2,1)S(1)}, bf16[1,1024,4096]{2,1,0:T(8,128)(2,1)}, u32[]{:S(2)}) copy-start(bf16[1,1024,4096]{2,1,0:T(8,128)(2,1)} %param.13) | copy-start | bytes 25165828
  74.6 15.3 %slice-start = ((s8[8388608]{0:T(1024)(128)(4,1)}), s8[4194304]{0:T(1024)(128)(4,1)S(1)}, s32[]{:S(2)}) async-start(s8[8388608]{0:T(1024)(128)(4,1)} %bitcast.29), calls=%async_computation.1 | async-start | bytes 8388608
  74.7 15.3 %slice-start.1 = ((s8[8388608]{0:T(1024)(128)(4,1)}), s8[4194304]{0:T(1024)(128)(4,1)S(1)}, s32[]{:S(2)}) async-start(s8[8388608]{0:T(1024)(128)(4,1)} %bitcast.29), calls=%async_computation.2 | async-start | bytes 8388608
  77.8 12.2 %collective-permute-start.10 = (bf16[48,4096]{1,0:T(8,128)(2,1)S(1)}, bf16[48,4096]{1,0:T(8,128)(2,1)S(1)}, u32[]{:S(2)}, u32[]{:S(2)}) collective-permute-start(bf16[48,4096]{1,0:T(8,128)(2,1)S(1)} %slice.16), channel_id=1, source_target_pairs={{4,0},{8,12},{5,1},{9,13},{6,2},{10,14},{7,3},{11,15},{20,16},{24,... | collective-permute-start | bytes 1179656 | tf_op jit(solution)/shard_map/ppermute | solution.py:213
  79.1 6.5 %collective-permute-start.8 = (bf16[40,2560]{1,0:T(8,128)(2,1)S(1)}, bf16[40,2560]{1,0:T(8,128)(2,1)S(1)}, u32[]{:S(2)}, u32[]{:S(2)}) collective-permute-start(bf16[40,2560]{1,0:T(8,128)(2,1)S(1)} %collective-permute-done.7.refs_2_), channel_id=1, source_target_pairs={{0,16},{16,0},{1,17},{17,1},{2,18},{18,2},{3,19},{19,3},{4,20},{20... | collective-permute-start | bytes 614408 | tf_op jit(solution)/shard_map/ppermute | solution.py:228
